TPU v7x, 256 devices: a whole 4x4x8 slice. The times are simulated.
256 devices in a mesh: leaf: 16 (over y, x), top: 16 (over z, core).
Axes of the slice: x: 4, y: 4, z: 8, core: 2. Of those that a mesh axis runs over, the one named last changes fastest.
Arguments:
- rhs: bfloat16 [2, 262144, 256], P(None, ('leaf', 'top')), may hold values from -6 to 6
- diag_blocks: bfloat16 [2, 512, 512, 512], P(None, ('leaf', 'top')), may hold values from -0.1875 to 0.1875
- row_basis: bfloat16 [2, 512, 512, 256], P(None, ('leaf', 'top')), may hold values from -0.125 to 0.125
- col_basis: bfloat16 [2, 512, 512, 256], P(None, ('leaf', 'top')), may hold values from -0.1875 to 0.1875
- local_pair: bfloat16 [2, 256, 2, 256, 256], P(None, ('leaf', 'top')), may hold values from -0.21875 to 0.21875
- local_couple: bfloat16 [2, 256, 256, 256], P(None, ('leaf', 'top')), may hold values from -0.25 to 0.25
- cross_pair: bfloat16 [2, 256, 8, 2, 256, 256], P(None, ('leaf', 'top')), may hold values from -0.21650635 to 0.21650635, as said below
- cross_couple: bfloat16 [2, 256, 8, 256, 256], P(None, ('leaf', 'top')), may hold values from -0.42474313 to 0.42474313, as said below
- leaf_map: int32 [256, 2], P(('leaf', 'top')), may hold values from 0 to 1, each once within a row
Outputs:
- applied: bfloat16 [2, 262144, 256], P(None, ('leaf', 'top'))
Inputs may be any that keep to these rules, and one draw needn't show every extreme that they name: `leaf_map`: each row lists the 2 row blocks of one device, each once. `cross_pair`: the slices [:, d, k] of all devices d with the same d // 2^(k+1) are equal. `cross_couple`: the slices [:, d, k] of all devices d with the same d // 2^(k+1) are equal.
All inputs are finite; a program needn't handle non-finite values.
Results may differ from a plain program's by a relative error of at most 0.023.
Values may be sent and summed in bfloat16 or wider, within the bound.
No kernel may reach another device: no remote copies, remote signals or barrier semaphores. Data moves between devices by JAX's collectives and lax.ppermute only.
A program may use at most 64 MiB of HBM per device.

v0:
```python
import jax
import jax.numpy as jnp
from jax import lax
from jax.sharding import PartitionSpec as P


def swapped(value, axis, apart):
    mask = 2**apart
    pairs = [(source, source ^ mask) for source in range(lax.axis_size(axis))]
    return lax.ppermute(value, axis, pairs)


def complex_einsum(pattern, first_arg, second_arg):
    real_part = jnp.einsum(
        pattern, first_arg[0], second_arg[0], preferred_element_type=jnp.float32
    ) - jnp.einsum(pattern, first_arg[1], second_arg[1], preferred_element_type=jnp.float32)
    imag_part = jnp.einsum(
        pattern, first_arg[0], second_arg[1], preferred_element_type=jnp.float32
    ) + jnp.einsum(pattern, first_arg[1], second_arg[0], preferred_element_type=jnp.float32)
    return jnp.stack([real_part, imag_part])


def climb(q_now, q_other, half_bit, w_pair, b_mat, is_last):
    b_use = jnp.where(half_bit == 0, b_mat, jnp.swapaxes(b_mat, 1, 2))
    coupled = complex_einsum("ij,jn->in", b_use, q_other)
    if is_last:
        return (coupled, q_now)
    q_left = jnp.where(half_bit == 0, q_now, q_other)
    q_right = jnp.where(half_bit == 0, q_other, q_now)
    parent = complex_einsum("ij,in->jn", w_pair[:, 0], q_left) + complex_einsum(
        "ij,in->jn", w_pair[:, 1], q_right
    )
    return (coupled, parent.astype(jnp.bfloat16))


def descend(coupled, half_bit, w_pair, upper_sum):
    w_own = jnp.where(half_bit == 0, w_pair[:, 0], w_pair[:, 1])
    return coupled + complex_einsum("ij,jn->in", w_own, upper_sum.astype(jnp.bfloat16))


def shards(
    rhs,
    diag_blocks,
    row_basis,
    col_basis,
    local_pair,
    local_couple,
    cross_pair,
    cross_couple,
    leaf_map,
):
    leaf_count = diag_blocks.shape[1]
    leaf_rows = diag_blocks.shape[2]
    columns = rhs.shape[2]
    rank_size = col_basis.shape[3]
    slot_order = leaf_map[0]
    blocks = rhs.reshape(2, leaf_count, leaf_rows, columns)[:, slot_order]
    skeleton = complex_einsum("lkr,lkn->lrn", col_basis, blocks)
    height = 0
    parent_count = skeleton.shape[1] // 2
    rounded = skeleton.astype(jnp.bfloat16).reshape(2, parent_count, 2, rank_size, columns)
    w_pairs = local_pair
    coupled = jnp.stack(
        [
            complex_einsum("pij,pjn->pin", local_couple, rounded[:, :, 1]),
            complex_einsum("pji,pjn->pin", local_couple, rounded[:, :, 0]),
        ],
        axis=2,
    )
    skeleton = complex_einsum("pcij,pcin->pjn", w_pairs, rounded)
    local_steps = [(coupled, w_pairs)]
    current = skeleton[:, 0].astype(jnp.bfloat16)
    bits_top = lax.axis_size("top").bit_length() - 1
    bits_leaf = lax.axis_size("leaf").bit_length() - 1
    total_bits = bits_top + bits_leaf
    top_pos = lax.axis_index("top")
    leaf_pos = lax.axis_index("leaf")
    climbed = []
    for height in range(bits_top):
        partner = swapped(current, "top", height)
        half_bit = top_pos >> height & 1
        coupled, current = climb(
            current,
            partner,
            half_bit,
            cross_pair[:, 0, height],
            cross_couple[:, 0, height],
            height == total_bits - 1,
        )
        climbed.append((coupled, half_bit))
    upper_steps = []
    for leaf_bit in range(bits_leaf):
        height = bits_top + leaf_bit
        partner = swapped(current, "leaf", leaf_bit)
        half_bit = leaf_pos >> leaf_bit & 1
        coupled, current = climb(
            current,
            partner,
            half_bit,
            cross_pair[:, 0, height],
            cross_couple[:, 0, height],
            height == total_bits - 1,
        )
        upper_steps.append((coupled, half_bit, height))
    group_part = jnp.zeros((2, rank_size, columns), jnp.float32)
    for coupled, half_bit, height in reversed(upper_steps):
        group_part = descend(coupled, half_bit, cross_pair[:, 0, height], group_part)
    above_node = group_part
    for height in reversed(range(bits_top)):
        coupled, half_bit = climbed[height]
        above_node = descend(coupled, half_bit, cross_pair[:, 0, height], above_node)
    hidden = above_node[:, None]
    for coupled, w_pairs in reversed(local_steps):
        children = coupled + complex_einsum("pcij,pjn->pcin", w_pairs, hidden.astype(jnp.bfloat16))
        hidden = children.reshape(2, -1, rank_size, columns)
    direct = complex_einsum("lij,ljn->lin", diag_blocks, blocks)
    result = (
        direct + complex_einsum("lkr,lrn->lkn", row_basis, hidden.astype(jnp.bfloat16))
    ).astype(jnp.bfloat16)
    placed = jnp.zeros_like(result).at[:, slot_order].set(result)
    return placed.reshape(2, leaf_count * leaf_rows, columns)


def solution(mesh):
    return jax.shard_map(
        shards,
        mesh=mesh,
        in_specs=(
            P(None, ("leaf", "top"), None),
            P(None, ("leaf", "top"), None, None),
            P(None, ("leaf", "top"), None, None),
            P(None, ("leaf", "top"), None, None),
            P(None, ("leaf", "top"), None, None, None),
            P(None, ("leaf", "top"), None, None),
            P(None, ("leaf", "top"), None, None, None, None),
            P(None, ("leaf", "top"), None, None, None),
            P(("leaf", "top"), None),
        ),
        out_specs=P(None, ("leaf", "top"), None),
        check_vma=False,
    )
```

profile of v0, /device:TPU:22, one launch (start us, length us, event | category | flops | bytes accessed | tf_op | source)
XLA Modules:
  0.0 154.4 jit_solution(10041819962255078084)
XLA Ops:
  0.0 0.7 fusion.228
  0.8 0.5 copy-done
  1.2 0.6 gather_fusion
  1.9 0.5 copy.29
  3.1 0.3 fusion.7
  3.4 0.3 fusion.8
  3.7 0.4 copy-done.3
  5.1 0.7 maximum_bitcast_fusion
  5.8 1.8 %fusion.158 = f32[256,256]{1,0:T(8,128)} fusion(bf16[1,1,2,256,256]{3,4,2,1,0:T(8,128)(2,1)S(1)} %bitcast.948, bf16[2,1,256,256]{3,2,1,0:T(8,128)(2,1)} %param.14), kind=kOutput, calls=%fused_computation.428 | convolution fusion | flops 33554432 | bytes 524288 | tf_op jit(solution)/shard_map/pij,pjn->pin/dot_general | solution.py:14
  7.6 1.8 %fusion.154 = f32[256,256]{1,0:T(8,128)} fusion(bf16[1,1,2,256,256]{3,4,2,1,0:T(8,128)(2,1)S(1)} %bitcast.949, bf16[2,1,256,256]{3,2,1,0:T(8,128)(2,1)} %param.14), kind=kOutput, calls=%fused_computation.424 | convolution fusion | flops 33554432 | bytes 524288 | tf_op jit(solution)/shard_map/pji,pjn->pin/dot_general | solution.py:14
  9.4 1.9 %fusion.156 = f32[256,256]{1,0:T(8,128)} fusion(bf16[1,1,2,256,256]{3,4,2,1,0:T(8,128)(2,1)} %bitcast.952, bf16[2,1,256,256]{3,2,1,0:T(8,128)(2,1)} %param.14), kind=kOutput, calls=%fused_computation.426 | convolution fusion | flops 33554432 | bytes 524288 | tf_op jit(solution)/shard_map/pij,pjn->pin/dot_general | solution.py:17
  11.3 1.9 %fusion.152 = f32[256,256]{1,0:T(8,128)} fusion(bf16[1,1,2,256,256]{3,4,2,1,0:T(8,128)(2,1)} %bitcast.953, bf16[2,1,256,256]{3,2,1,0:T(8,128)(2,1)} %param.14), kind=kOutput, calls=%fused_computation.422 | convolution fusion | flops 33554432 | bytes 524288 | tf_op jit(solution)/shard_map/pji,pjn->pin/dot_general | solution.py:17
  13.2 1.4 fusion.81
  14.6 1.5 fusion.83
  16.1 4.2 %slice_bitcast_fusion.2 = (bf16[2,2,256,256]{3,2,1,0:T(8,128)(2,1)}, bf16[2,2,256,256]{3,2,1,0:T(8,128)(2,1)}, bf16[2,2,256,256]{3,2,1,0:T(8,128)(2,1)}, bf16[2,...) fusion(bf16[2,1,8,2,256,256]{5,4,3,2,1,0:T(8,128)(2,1)} %param.15), kind=kLoop, calls=%fused_computation.211 | loop fusion | bytes 8388608 | tf_op jit(solution)/shard_map/squeeze | solution.py:107
  20.3 2.9 %slice_bitcast_fusion.20 = (bf16[2,256,256]{2,1,0:T(8,128)(2,1)}, bf16[2,256,256]{2,1,0:T(8,128)(2,1)}, bf16[2,256,256]{2,1,0:T(8,128)(2,1)}, bf16[2,256,256]{2,...) fusion(bf16[2,1,8,256,256]{4,3,2,1,0:T(8,128)(2,1)} %param.16), kind=kLoop, calls=%fused_computation.262 | loop fusion | bytes 4194304 | tf_op jit(solution)/shard_map/squeeze | solution.py:101
  23.1 1.8 %copy.44 = bf16[2,256,256]{1,2,0:T(8,128)(2,1)} copy(bf16[2,256,256]{2,1,0:T(8,128)(2,1)} %get-tuple-element.13) | data formatting | bytes 524288 | tf_op jit(solution)/shard_map/squeeze | solution.py:101
  24.9 1.8 %bitcast_select_fusion.7 = bf16[2,256,256]{2,1,0:T(8,128)(2,1)} fusion(bf16[2,256,256]{1,2,0:T(8,128)(2,1)} %copy.44, pred[]{:T(512)S(6)} %eq.23, bf16[2,1,8,256,256]{4,3,2,1,0:T(8,128)(2,1)} %param.16), kind=kLoop, calls=%fused_computation.245 | loop fusion | flops 131072 | bytes 786433 | tf_op jit(solution)/shard_map/jit(_where)/select_n | solution.py:24
  26.7 1.9 %slice_select_fusion = (bf16[2,1,256,256]{3,2,1,0:T(8,128)(2,1)S(1)}, bf16[2,1,256,256]{3,2,1,0:T(8,128)(2,1)}) fusion(bf16[2,2,256,256]{3,2,1,0:T(8,128)(2,1)} %get-tuple-element.5, pred[]{:T(512)S(6)} %eq.23, bf16[2,2,256,256]{3,2,1,0:T(8,128)(2,1)} %get-tuple-element.12, pred[]{:T(512)S(6)} %eq.22), kind=kLoop, calls=%fused_computation.229 | loop fusion | flops 262144 | bytes 1572866 | tf_op jit(solution)/shard_map/jit(_where)/select_n | solution.py:37
  28.6 0.7 copy-done.35
  29.3 0.9 fusion.146
  30.2 1.8 %copy.33 = bf16[2,256,256]{1,2,0:T(8,128)(2,1)} copy(bf16[2,256,256]{2,1,0:T(8,128)(2,1)} %get-tuple-element.15) | data formatting | bytes 524288 | tf_op jit(solution)/shard_map/squeeze | solution.py:87
  32.0 1.8 %copy.35 = bf16[2,256,256]{1,2,0:T(8,128)(2,1)} copy(bf16[2,256,256]{2,1,0:T(8,128)(2,1)} %get-tuple-element.16) | data formatting | bytes 524288 | tf_op jit(solution)/shard_map/squeeze | solution.py:87
  33.8 1.8 %copy.37 = bf16[2,256,256]{1,2,0:T(8,128)(2,1)} copy(bf16[2,256,256]{2,1,0:T(8,128)(2,1)} %get-tuple-element.17) | data formatting | bytes 524288 | tf_op jit(solution)/shard_map/squeeze | solution.py:87
  35.6 1.8 %copy.39 = bf16[2,256,256]{1,2,0:T(8,128)(2,1)} copy(bf16[2,256,256]{2,1,0:T(8,128)(2,1)} %get-tuple-element.18) | data formatting | bytes 524288 | tf_op jit(solution)/shard_map/squeeze | solution.py:101
  37.4 1.8 %copy.41 = bf16[2,256,256]{1,2,0:T(8,128)(2,1)} copy(bf16[2,256,256]{2,1,0:T(8,128)(2,1)} %get-tuple-element.19) | data formatting | bytes 524288 | tf_op jit(solution)/shard_map/squeeze | solution.py:101
  39.2 1.8 %copy.43 = bf16[2,256,256]{1,2,0:T(8,128)(2,1)} copy(bf16[2,256,256]{2,1,0:T(8,128)(2,1)} %get-tuple-element.20) | data formatting | bytes 524288 | tf_op jit(solution)/shard_map/squeeze | solution.py:101
  41.0 1.8 %copy.31 = bf16[2,256,256]{1,2,0:T(8,128)(2,1)} copy(bf16[2,256,256]{2,1,0:T(8,128)(2,1)} %get-tuple-element.14) | data formatting | bytes 524288 | tf_op jit(solution)/shard_map/squeeze | solution.py:87
  42.8 1.2 slice_select_fusion.7
  44.0 1.2 bitcast_select_fusion.6
  45.2 1.3 fusion.70
  47.2 0.5 fusion.3
  47.6 0.5 copy-done.15
  48.2 0.5 fusion.4
  48.7 0.5 copy-done.5
  49.9 0.9 copy-done.7
  51.0 0.7 copy-done.28
  52.2 0.6 copy-done.23
  52.8 1.0 broadcast_select_fusion.12
  55.4 2.0 %collective-permute-start.1 = (bf16[2,256,256]{1,2,0:T(8,128)(2,1)S(1)}, bf16[2,256,256]{1,2,0:T(8,128)(2,1)S(1)}, u32[]{:S(2)}, u32[]{:S(2)}) collective-permute-start(bf16[2,256,256]{1,2,0:T(8,128)(2,1)S(1)} %fusion.90), channel_id=1, source_target_pairs={{0,2},{1,3},{2,0},{3,1},{4,6},{5,7},{6,4},{7,5},{8,10},{9,11},{10,... | collective-permute-start | bytes 786440 | tf_op jit(solution)/shard_map/ppermute | solution.py:10
  57.5 1.1 fusion.161
  58.6 1.1 fusion.160
  59.7 1.1 fusion.66
  60.9 1.1 fusion.65
  62.0 2.3 %collective-permute-done.1 = bf16[2,256,256]{1,2,0:T(8,128)(2,1)S(1)} collective-permute-done((bf16[2,256,256]{1,2,0:T(8,128)(2,1)S(1)}, bf16[2,256,256]{1,2,0:T(8,128)(2,1)S(1)}, u32[]{:S(2)}, u32[]{:S(2)}) %collective-permute-start.1) | collective-permute-done | bytes 262176 | tf_op jit(solution)/shard_map/ppermute | solution.py:10
  66.1 3.4 %collective-permute-start.2 = (bf16[2,256,256]{1,2,0:T(8,128)(2,1)S(1)}, bf16[2,256,256]{1,2,0:T(8,128)(2,1)S(1)}, u32[]{:S(2)}, u32[]{:S(2)}) collective-permute-start(bf16[2,256,256]{1,2,0:T(8,128)(2,1)S(1)} %fusion.92), channel_id=1, source_target_pairs={{0,4},{1,5},{2,6},{3,7},{4,0},{5,1},{6,2},{7,3},{8,12},{9,13},{10,... | collective-permute-start | bytes 786440 | tf_op jit(solution)/shard_map/ppermute | solution.py:10
  70.4 11.0 %collective-permute-done.2 = bf16[2,256,256]{1,2,0:T(8,128)(2,1)S(1)} collective-permute-done((bf16[2,256,256]{1,2,0:T(8,128)(2,1)S(1)}, bf16[2,256,256]{1,2,0:T(8,128)(2,1)S(1)}, u32[]{:S(2)}, u32[]{:S(2)}) %collective-permute-start.2) | collective-permute-done | bytes 262176 | tf_op jit(solution)/shard_map/ppermute | solution.py:10
  83.1 6.3 %collective-permute-start.3 = (bf16[2,256,256]{1,2,0:T(8,128)(2,1)S(1)}, bf16[2,256,256]{1,2,0:T(8,128)(2,1)S(1)}, u32[]{:S(2)}, u32[]{:S(2)}) collective-permute-start(bf16[2,256,256]{1,2,0:T(8,128)(2,1)S(1)} %fusion.94), channel_id=1, source_target_pairs={{0,8},{1,9},{2,10},{3,11},{4,12},{5,13},{6,14},{7,15},{8,0},{9,1},... | collective-permute-start | bytes 786440 | tf_op jit(solution)/shard_map/ppermute | solution.py:10
  90.3 10.7 %collective-permute-done.3 = bf16[2,256,256]{1,2,0:T(8,128)(2,1)S(1)} collective-permute-done((bf16[2,256,256]{1,2,0:T(8,128)(2,1)S(1)}, bf16[2,256,256]{1,2,0:T(8,128)(2,1)S(1)}, u32[]{:S(2)}, u32[]{:S(2)}) %collective-permute-start.3) | collective-permute-done | bytes 262176 | tf_op jit(solution)/shard_map/ppermute | solution.py:10
  102.8 1.1 collective-permute-start.4
  104.8 5.8 %collective-permute-done.4 = bf16[2,256,256]{1,2,0:T(8,128)(2,1)S(1)} collective-permute-done((bf16[2,256,256]{1,2,0:T(8,128)(2,1)S(1)}, bf16[2,256,256]{1,2,0:T(8,128)(2,1)S(1)}, u32[]{:S(2)}, u32[]{:S(2)}) %collective-permute-start.4) | collective-permute-done | bytes 262176 | tf_op jit(solution)/shard_map/ppermute | solution.py:10
  113.6 6.7 %collective-permute-done.5 = bf16[2,256,256]{1,2,0:T(8,128)(2,1)S(1)} collective-permute-done((bf16[2,256,256]{1,2,0:T(8,128)(2,1)S(1)}, bf16[2,256,256]{1,2,0:T(8,128)(2,1)S(1)}, u32[]{:S(2)}, u32[]{:S(2)}) %collective-permute-start.5) | collective-permute-done | bytes 262176 | tf_op jit(solution)/shard_map/ppermute | solution.py:10
  122.2 1.4 collective-permute-start.6
  124.5 6.6 %collective-permute-done.6 = bf16[2,256,256]{1,2,0:T(8,128)(2,1)S(1)} collective-permute-done((bf16[2,256,256]{1,2,0:T(8,128)(2,1)S(1)}, bf16[2,256,256]{1,2,0:T(8,128)(2,1)S(1)}, u32[]{:S(2)}, u32[]{:S(2)}) %collective-permute-start.6) | collective-permute-done | bytes 262176 | tf_op jit(solution)/shard_map/ppermute | solution.py:10
  133.9 6.9 %collective-permute-done.7 = bf16[2,256,256]{1,2,0:T(8,128)(2,1)S(1)} collective-permute-done((bf16[2,256,256]{1,2,0:T(8,128)(2,1)S(1)}, bf16[2,256,256]{1,2,0:T(8,128)(2,1)S(1)}, u32[]{:S(2)}, u32[]{:S(2)}) %collective-permute-start.7) | collective-permute-done | bytes 262176 | tf_op jit(solution)/shard_map/ppermute | solution.py:10
  149.4 0.7 copy-done.17
  150.1 0.3 fusion.108
  150.4 0.3 fusion.106
  150.7 0.3 fusion.2
  151.1 0.3 fusion.1
  151.4 0.6 fusion.77
  152.0 0.5 copy.49
  152.6 0.8 scatter_fusion
  153.4 1.0 copy-done.18
  (222 shorter events, 29.5 us)
Async XLA Ops:
  0.0 1.2 copy-start
  1.2 1.2 copy-start.24
  3.1 1.0 copy-start.3
  4.1 1.0 copy-start.13
  4.6 8.6 %copy-start.2 = (bf16[2,2,512,512]{3,2,1,0:T(8,128)(2,1)S(1)}, bf16[2,2,512,512]{3,2,1,0:T(8,128)(2,1)}, u32[]{:S(2)}) copy-start(bf16[2,2,512,512]{3,2,1,0:T(8,128)(2,1)} %param.10) | copy-start | bytes 6291460
  5.1 0.7 copy-start.22
  5.8 46.4 %collective-permute-start = (bf16[2,256,256]{1,2,0:T(8,128)(2,1)}, bf16[2,256,256]{1,2,0:T(8,128)(2,1)}, u32[]{:S(2)}, u32[]{:S(2)}) collective-permute-start(bf16[2,256,256]{1,2,0:T(8,128)(2,1)} %maximum_bitcast_fusion), channel_id=1, source_target_pairs={{0,1},{1,0},{2,3},{3,2},{4,5},{5,4},{6,7},{7,6},{8,9},{9,8},{10,11... | collective-permute-start | bytes 786440 | tf_op jit(solution)/shard_map/ppermute | solution.py:10
  28.6 0.7 copy-start.35
  42.8 3.7 %copy-start.19 = (bf16[2,1,256,256]{3,2,1,0:T(8,128)(2,1)S(1)}, bf16[2,1,256,256]{3,2,1,0:T(8,128)(2,1)}, u32[]{:S(2)}) copy-start(bf16[2,1,256,256]{3,2,1,0:T(8,128)(2,1)} %param.14) | copy-start | bytes 786436
  42.8 3.7 %copy-start.27 = (f32[256,256]{1,0:T(8,128)S(1)}, f32[256,256]{1,0:T(8,128)}, u32[]{:S(2)}) copy-start(f32[256,256]{1,0:T(8,128)} %fusion.156) | copy-start | bytes 786436
  42.8 3.9 %copy-start.14 = (bf16[2,256,256]{2,1,0:T(8,128)(2,1)S(1)}, bf16[2,256,256]{2,1,0:T(8,128)(2,1)}, u32[]{:S(2)}) copy-start(bf16[2,256,256]{2,1,0:T(8,128)(2,1)} %copy-done.13) | copy-start | bytes 786436
  42.8 3.9 %copy-start.26 = (f32[256,256]{1,0:T(8,128)S(1)}, f32[256,256]{1,0:T(8,128)}, u32[]{:S(2)}) copy-start(f32[256,256]{1,0:T(8,128)} %fusion.154) | copy-start | bytes 786436
  42.8 4.1 %copy-start.25 = (f32[256,256]{1,0:T(8,128)S(1)}, f32[256,256]{1,0:T(8,128)}, u32[]{:S(2)}) copy-start(f32[256,256]{1,0:T(8,128)} %fusion.152) | copy-start | bytes 786436
  44.0 3.2 %copy-start.16 = (f32[2,256,512]{2,1,0:T(8,128)S(1)}, f32[2,256,512]{2,1,0:T(8,128)}, u32[]{:S(2)}) copy-start(f32[2,256,512]{2,1,0:T(8,128)} %fusion.81) | copy-start | bytes 3145732
  46.9 1.2 copy-start.15
  48.2 1.0 copy-start.5
  48.2 1.2 copy-start.9
  48.2 1.4 copy-start.10
  48.2 1.4 copy-start.30
  48.2 1.5 copy-start.31
  48.2 1.6 %copy-start.32 = (bf16[2,256,256]{1,2,0:T(8,128)(2,1)S(1)}, bf16[2,256,256]{1,2,0:T(8,128)(2,1)}, u32[]{:S(2)}) copy-start(bf16[2,256,256]{1,2,0:T(8,128)(2,1)} %copy.39) | copy-start | bytes 786436
  48.2 1.6 %copy-start.33 = (bf16[2,256,256]{1,2,0:T(8,128)(2,1)S(1)}, bf16[2,256,256]{1,2,0:T(8,128)(2,1)}, u32[]{:S(2)}) copy-start(bf16[2,256,256]{1,2,0:T(8,128)(2,1)} %copy.41) | copy-start | bytes 786436
  48.2 1.7 %copy-start.34 = (bf16[2,256,256]{1,2,0:T(8,128)(2,1)S(1)}, bf16[2,256,256]{1,2,0:T(8,128)(2,1)}, u32[]{:S(2)}) copy-start(bf16[2,256,256]{1,2,0:T(8,128)(2,1)} %copy.43) | copy-start | bytes 786436
  48.7 2.1 %copy-start.7 = (bf16[2,1,8,256,256]{4,3,2,1,0:T(8,128)(2,1)S(1)}, bf16[2,1,8,256,256]{4,3,2,1,0:T(8,128)(2,1)}, u32[]{:S(2)}) copy-start(bf16[2,1,8,256,256]{4,3,2,1,0:T(8,128)(2,1)} %param.16) | copy-start | bytes 6291460
  48.7 2.1 %copy-start.29 = (bf16[2,256,256]{1,2,0:T(8,128)(2,1)S(1)}, bf16[2,256,256]{1,2,0:T(8,128)(2,1)}, u32[]{:S(2)}) copy-start(bf16[2,256,256]{1,2,0:T(8,128)(2,1)} %copy.33) | copy-start | bytes 786436
  50.8 1.0 copy-start.28
  50.8 1.0 copy-start.36
  50.8 1.2 copy-start.11
  50.8 1.4 copy-start.12
  51.8 1.0 copy-start.23
  51.8 2.0 %copy-start.6 = (bf16[2,2,256,256]{3,2,1,0:T(8,128)(2,1)S(1)}, bf16[2,2,256,256]{3,2,1,0:T(8,128)(2,1)}, u32[]{:S(2)}) copy-start(bf16[2,2,256,256]{3,2,1,0:T(8,128)(2,1)} %get-tuple-element.11) | copy-start | bytes 1572868
  55.4 8.9 %collective-permute-start.1 = (bf16[2,256,256]{1,2,0:T(8,128)(2,1)S(1)}, bf16[2,256,256]{1,2,0:T(8,128)(2,1)S(1)}, u32[]{:S(2)}, u32[]{:S(2)}) collective-permute-start(bf16[2,256,256]{1,2,0:T(8,128)(2,1)S(1)} %fusion.90), channel_id=1, source_target_pairs={{0,2},{1,3},{2,0},{3,1},{4,6},{5,7},{6,4},{7,5},{8,10},{9,11},{10,... | collective-permute-start | bytes 786440 | tf_op jit(solution)/shard_map/ppermute | solution.py:10
  66.1 15.3 %collective-permute-start.2 = (bf16[2,256,256]{1,2,0:T(8,128)(2,1)S(1)}, bf16[2,256,256]{1,2,0:T(8,128)(2,1)S(1)}, u32[]{:S(2)}, u32[]{:S(2)}) collective-permute-start(bf16[2,256,256]{1,2,0:T(8,128)(2,1)S(1)} %fusion.92), channel_id=1, source_target_pairs={{0,4},{1,5},{2,6},{3,7},{4,0},{5,1},{6,2},{7,3},{8,12},{9,13},{10,... | collective-permute-start | bytes 786440 | tf_op jit(solution)/shard_map/ppermute | solution.py:10
  83.1 17.9 %collective-permute-start.3 = (bf16[2,256,256]{1,2,0:T(8,128)(2,1)S(1)}, bf16[2,256,256]{1,2,0:T(8,128)(2,1)S(1)}, u32[]{:S(2)}, u32[]{:S(2)}) collective-permute-start(bf16[2,256,256]{1,2,0:T(8,128)(2,1)S(1)} %fusion.94), channel_id=1, source_target_pairs={{0,8},{1,9},{2,10},{3,11},{4,12},{5,13},{6,14},{7,15},{8,0},{9,1},... | collective-permute-start | bytes 786440 | tf_op jit(solution)/shard_map/ppermute | solution.py:10
  102.8 7.8 %collective-permute-start.4 = (bf16[2,256,256]{1,2,0:T(8,128)(2,1)S(1)}, bf16[2,256,256]{1,2,0:T(8,128)(2,1)S(1)}, u32[]{:S(2)}, u32[]{:S(2)}) collective-permute-start(bf16[2,256,256]{1,2,0:T(8,128)(2,1)S(1)} %fusion.96), channel_id=1, source_target_pairs={{0,16},{16,0},{32,48},{48,32},{64,80},{80,64},{96,112},{112,96},{1... | collective-permute-start | bytes 786440 | tf_op jit(solution)/shard_map/ppermute | solution.py:10
  112.4 8.0 %collective-permute-start.5 = (bf16[2,256,256]{1,2,0:T(8,128)(2,1)S(1)}, bf16[2,256,256]{1,2,0:T(8,128)(2,1)S(1)}, u32[]{:S(2)}, u32[]{:S(2)}) collective-permute-start(bf16[2,256,256]{1,2,0:T(8,128)(2,1)S(1)} %fusion.98), channel_id=1, source_target_pairs={{0,32},{16,48},{32,0},{48,16},{64,96},{80,112},{96,64},{112,80},{1... | collective-permute-start | bytes 786440 | tf_op jit(solution)/shard_map/ppermute | solution.py:10
  122.2 8.9 %collective-permute-start.6 = (bf16[2,256,256]{1,2,0:T(8,128)(2,1)S(1)}, bf16[2,256,256]{1,2,0:T(8,128)(2,1)S(1)}, u32[]{:S(2)}, u32[]{:S(2)}) collective-permute-start(bf16[2,256,256]{1,2,0:T(8,128)(2,1)S(1)} %fusion.100), channel_id=1, source_target_pairs={{0,64},{16,80},{32,96},{48,112},{64,0},{80,16},{96,32},{112,48},{1... | collective-permute-start | bytes 786440 | tf_op jit(solution)/shard_map/ppermute | solution.py:10
  123.8 7.4 %copy-start.8 = (bf16[2,2,256,256]{3,2,1,0:T(8,128)(2,1)S(1)}, bf16[2,2,256,256]{3,2,1,0:T(8,128)(2,1)}, u32[]{:S(2)}) copy-start(bf16[2,2,256,256]{3,2,1,0:T(8,128)(2,1)} %get-tuple-element.12) | copy-start | bytes 1572868
  132.7 8.1 %copy-start.21 = (bf16[2,256,256]{2,1,0:T(8,128)(2,1)S(1)}, bf16[2,256,256]{2,1,0:T(8,128)(2,1)}, u32[]{:S(2)}) copy-start(bf16[2,256,256]{2,1,0:T(8,128)(2,1)} %bitcast_select_fusion.7) | copy-start | bytes 786436
  132.8 8.0 %collective-permute-start.7 = (bf16[2,256,256]{1,2,0:T(8,128)(2,1)S(1)}, bf16[2,256,256]{1,2,0:T(8,128)(2,1)S(1)}, u32[]{:S(2)}, u32[]{:S(2)}) collective-permute-start(bf16[2,256,256]{1,2,0:T(8,128)(2,1)S(1)} %fusion.102), channel_id=1, source_target_pairs={{0,128},{16,144},{32,160},{48,176},{64,192},{80,208},{96,224},{112... | collective-permute-start | bytes 786440 | tf_op jit(solution)/shard_map/ppermute | solution.py:10
  133.8 7.9 %copy-start.20 = (bf16[2,1,256,256]{3,2,1,0:T(8,128)(2,1)S(1)}, bf16[2,1,256,256]{3,2,1,0:T(8,128)(2,1)}, u32[]{:S(2)}) copy-start(bf16[2,1,256,256]{3,2,1,0:T(8,128)(2,1)} %get-tuple-element.44) | copy-start | bytes 786436
  147.0 1.0 copy-start.4
  148.8 1.2 copy-start.17
  152.0 2.4 %copy-start.1 = (bf16[2,1024,256]{2,1,0:T(8,128)(2,1)S(1)}, bf16[2,1024,256]{2,1,0:T(8,128)(2,1)}, u32[]{:S(2)}) copy-start(bf16[2,1024,256]{2,1,0:T(8,128)(2,1)} %param.9) | copy-start | bytes 3145732
  153.4 1.0 copy-start.18
where the time goes:
time: 155 us; the launch traced here: 154 us
  waiting for transfers between devices  50.1 us (32%)
  matrix products  45 us (29%)
  local copies, waits for them, and re-layouts  31.6 us (20%)
  starting transfers between devices  14.5 us (9%)
  other arithmetic  11.7 us (8%)
    ppermute x8, waiting for transfers between devices, swapped(): return lax.ppermute(value, axis, pairs)  50.1 us
    squeeze x9, local copies, waits for them, and re-layouts, shards(): cross_couple[:, 0, height]  17.2 us
    ppermute x8, starting transfers between devices, swapped(): return lax.ppermute(value, axis, pairs)  14.5 us
    dot_general x37, matrix products, complex_einsum(): jnp.einsum(pattern, first_arg[0], second_arg[0], preferred_element_type=j...  13 us
    dot_general x36, matrix products, complex_einsum(): jnp.einsum(pattern, first_arg[0], second_arg[1], preferred_element_type=j...  12.9 us
    dot_general x37, matrix products, complex_einsum(): jnp.einsum(pattern, first_arg[1], second_arg[1], preferred_element_type=j...  10.5 us
    dot_general x36, matrix products, complex_einsum(): jnp.einsum(pattern, first_arg[1], second_arg[0], preferred_element_type=j...  8.56 us
    unnamed x74, local copies, waits for them, and re-layouts  7.63 us
  transfers between devices with their start and end apart: 8, of which 7 were waited for; matrix products, arithmetic and copies ran while one was open for 34% of the time, Pallas kernels for 0%

commit v1 on v0

v1 whole, which is shorter than its diff:
```python
import jax
import jax.numpy as jnp
from jax import lax
from jax.experimental import pallas as pl
from jax.experimental.pallas import tpu as pltpu
from jax.sharding import PartitionSpec as P

BF = jnp.bfloat16
F32 = jnp.float32
NN = (((1,), (0,)), ((), ()))
NT = (((1,), (1,)), ((), ()))


def dot(a, b, dims=NN):
    return lax.dot_general(a, b, dims, preferred_element_type=F32)


def cmul(a, w_re, w_im, dims=NN):
    half = a.shape[0] // 2
    p = dot(a, w_re, dims)
    q = dot(a, w_im, dims)
    return jnp.concatenate([p[:half] - q[half:], p[half:] + q[:half]], axis=0)


def rows(ref, *at):
    return jnp.concatenate([ref[(0,) + at], ref[(1,) + at]], axis=0)


def put(ref, value, *at):
    half = value.shape[0] // 2
    ref[(0,) + at] = value[:half].astype(ref.dtype)
    ref[(1,) + at] = value[half:].astype(ref.dtype)


def lift(q, w, level, child):
    return cmul(q, w[0, level, child], w[1, level, child])


def lower(h, w, level, child):
    return cmul(h, w[0, level, child], w[1, level, child], NT)


def couple_left(q_right, b, level):
    return cmul(q_right, b[0, level], b[1, level], NT)


def couple_right(q_left, b, level):
    return cmul(q_left, b[0, level], b[1, level], NN)


def couple(q_other, b, level, child):
    return lax.cond(
        child == 0,
        lambda: couple_left(q_other, b, level),
        lambda: couple_right(q_other, b, level),
    )


def couple_both(q_own, q_other, b, level, child):
    q_left = jnp.where(child == 0, q_own, q_other)
    q_right = jnp.where(child == 0, q_other, q_own)
    left = couple_left(q_right, b, level)
    right = couple_right(q_left, b, level)
    return jnp.where(child == 0, left, right), jnp.where(child == 0, right, left)


def leaf_kernel(pos, order, x, u, wl, w, qleaf, q0, out, order_s, x_v, u_v, wl_v, w_v, sems):
    copies = [
        pltpu.make_async_copy(order, order_s, sems.at[0]),
        pltpu.make_async_copy(x.at[:], x_v.at[:], sems.at[1]),
        pltpu.make_async_copy(u.at[:, 0], u_v.at[:, 0], sems.at[2]),
        pltpu.make_async_copy(u.at[:, 1], u_v.at[:, 1], sems.at[3]),
        pltpu.make_async_copy(wl.at[:, 0], wl_v.at[:], sems.at[4]),
        pltpu.make_async_copy(w.at[:, 0], w_v.at[:], sems.at[5]),
    ]
    for copy in copies:
        copy.start()
    copies[0].wait()
    copies[1].wait()
    size = u.shape[2]
    for leaf in range(2):
        at = pl.ds(pl.multiple_of(order_s[0, leaf] * size, size), size)
        xt = jnp.concatenate([x_v[0, at].T, x_v[1, at].T], axis=0)
        copies[2 + leaf].wait()
        qleaf[leaf] = cmul(xt, u_v[0, leaf], u_v[1, leaf]).astype(BF)
    copies[4].wait()
    q = cmul(qleaf[0], wl_v[0, 0], wl_v[1, 0]) + cmul(qleaf[1], wl_v[0, 1], wl_v[1, 1])
    q = q.astype(BF)
    put(q0, q)
    copies[5].wait()
    bit = pos[0] & 1
    spread(out, cmul(q, w_v[0, bit], w_v[1, bit]).astype(BF))


def spread(out, value):
    blocks, _, part, _ = out.shape
    for i in range(blocks):
        for c in range(2):
            at = (c * blocks + i) * part
            out[i, c] = value[at : at + part]


def pick(got, i):
    return rows(got.at[i]).astype(F32)


def mid_kernel(pos, got, w, q_own, q_oth, q_up, out):
    digit = pos[0] & 3
    qa = (pick(got, digit) + pick(got, digit ^ 1)).astype(BF)
    qb = (pick(got, digit ^ 2) + pick(got, digit ^ 3)).astype(BF)
    put(q_own, qa)
    put(q_oth, qb)
    bit = digit >> 1
    up = (lift(qa, w, 1, bit) + lift(qb, w, 1, 1 - bit)).astype(BF)
    put(q_up, up)
    spread(out, lift(up, w, 2, (pos[0] >> 2) & 1).astype(BF))


def mid_last_kernel(pos, got, w, q_own, q_oth, out):
    digit = (pos[0] >> 2) & 3
    qa = (pick(got, digit) + pick(got, digit ^ 1)).astype(BF)
    qb = (pick(got, digit ^ 2) + pick(got, digit ^ 3)).astype(BF)
    put(q_own, qa)
    put(q_oth, qb)
    bit = digit >> 1
    part = (lift(qa, w, 3, bit) + lift(qb, w, 3, 1 - bit)).astype(BF)
    leaf = pos[0] >> 4
    put(out.at[leaf], part)
    for level in range(4):
        if level > 0:
            part = lift(part, w, 3 + level, (leaf >> (level - 1)) & 1).astype(BF)
        for flip in range(2**level, 2 ** (level + 1)):
            put(out.at[leaf ^ flip], part)


def store_both(out, digit, own, oth):
    for flip, value in enumerate((own, own, oth, oth)):
        put(out.at[digit ^ flip], value)


def top_kernel(pos, got, q_own3, q_oth3, w, b, out):
    def bit(level):
        return (pos[0] >> level) & 1

    leaf = pos[0] >> 4
    own3, oth3 = couple_both(rows(q_own3), rows(q_oth3), b, 3, bit(3))
    h = None
    for level in reversed(range(4)):
        q_sib = pick(got, leaf ^ 2**level)
        for flip in range(2**level + 1, 2 ** (level + 1)):
            q_sib = q_sib + pick(got, leaf ^ flip)
        c = couple(q_sib.astype(BF), b, 4 + level, bit(4 + level))
        h = c if h is None else c + lower(h.astype(BF), w, 4 + level, bit(4 + level))
    h = h.astype(BF)
    store_both(
        out,
        (pos[0] >> 2) & 3,
        (own3 + lower(h, w, 3, bit(3))).astype(BF),
        (oth3 + lower(h, w, 3, 1 - bit(3))).astype(BF),
    )


def gather(got):
    blocks = got.shape[0]
    return jnp.concatenate([got[i, c] for c in range(2) for i in range(blocks)], axis=0)


def down_kernel(pos, got, c2, c1_own, c1_oth, w, out):
    def bit(level):
        return (pos[0] >> level) & 1

    h = (rows(c2) + lower(gather(got), w, 2, bit(2))).astype(BF)
    store_both(
        out,
        pos[0] & 3,
        (rows(c1_own) + lower(h, w, 1, bit(1))).astype(BF),
        (rows(c1_oth) + lower(h, w, 1, 1 - bit(1))).astype(BF),
    )


def couple_kernel(pos, q_sib2, q_own1, q_oth1, b, c2, c1_own, c1_oth):
    put(c2, couple(rows(q_sib2), b, 2, (pos[0] >> 2) & 1))
    own, oth = couple_both(rows(q_own1), rows(q_oth1), b, 1, (pos[0] >> 1) & 1)
    put(c1_own, own)
    put(c1_oth, oth)


def low_couple_kernel(pos, q_sib0, qleaf, bl, b, c0, cleaf):
    put(c0, couple(rows(q_sib0), b, 0, pos[0] & 1))
    cleaf[0] = couple_left(qleaf[1], bl, 0)
    cleaf[1] = couple_right(qleaf[0], bl, 0)


def direct_kernel(order, x, d, out):
    size = d.shape[2]
    n = x.shape[2]
    tile = 128
    for leaf in range(2):
        start = pl.multiple_of(order[0, leaf] * size, size)
        xs = jnp.concatenate([x[0, pl.ds(start, size)], x[1, pl.ds(start, size)]], axis=1)

        def body(step, carry):
            at = pl.ds(pl.multiple_of(step * tile, tile), tile)
            to = pl.ds(pl.multiple_of(start + step * tile, tile), tile)
            p = dot(d[0, leaf, at], xs)
            q = dot(d[1, leaf, at], xs)
            out[0, to] = p[:, :n] - q[:, n:]
            out[1, to] = p[:, n:] + q[:, :n]
            return carry

        lax.fori_loop(0, size // tile, body, 0)


def last_kernel(pos, order, got, c0, cleaf, direct, w, wl, r, out):
    size = r.shape[2]
    n = out.shape[2]
    h = (rows(c0) + lower(gather(got), w, 0, pos[0] & 1)).astype(BF)
    tile = 256
    for leaf in range(2):
        hl = (cleaf[leaf] + lower(h, wl, 0, leaf)).astype(BF)
        start = pl.multiple_of(order[0, leaf] * size, size)
        for step in range(size // tile):
            at = pl.ds(step * tile, tile)
            to = pl.ds(pl.multiple_of(start + step * tile, tile), tile)
            p = dot(r[0, leaf, at], hl, NT)
            q = dot(r[1, leaf, at], hl, NT)
            out[0, to] = (direct[0, to] + (p[:, :n] - q[:, n:])).astype(BF)
            out[1, to] = (direct[1, to] + (p[:, n:] + q[:, :n])).astype(BF)


VMEM = pl.BlockSpec(memory_space=pltpu.VMEM)
SMEM = pl.BlockSpec(memory_space=pltpu.SMEM)
HBM = pl.BlockSpec(memory_space=pltpu.HBM)
GRANT = 20 * 2**20


def call(kernel, ins, outs, *args, scratch=(), flops=0, name=None):
    specs = {"s": SMEM, "v": VMEM, "a": HBM}
    moved = sum(a.size * a.dtype.itemsize for a in args)
    return pl.pallas_call(
        kernel,
        out_shape=[jax.ShapeDtypeStruct(shape, dtype) for shape, dtype in outs],
        in_specs=[specs[kind] for kind in ins],
        out_specs=[VMEM] * len(outs),
        scratch_shapes=list(scratch),
        compiler_params=pltpu.CompilerParams(vmem_limit_bytes=GRANT),
        cost_estimate=pl.CostEstimate(flops=flops, bytes_accessed=moved, transcendentals=0),
        name=name,
    )(*args)


def shards(rhs, diag, row_basis, col_basis, wl, bl, cross_w, cross_b, order):
    n = rhs.shape[2]
    rank = col_basis.shape[3]
    top = lax.axis_index("top")
    leaf = lax.axis_index("leaf")
    pos = (leaf * lax.axis_size("top") + top).astype(jnp.int32).reshape(1)
    w = cross_w[:, 0]
    b = cross_b[:, 0]

    def swap(value, flip):
        return lax.ppermute(value, "top", [(i, i ^ flip) for i in range(lax.axis_size("top"))])

    def exchange(value, axis, group):
        return lax.all_to_all(value, axis, 0, 0, axis_index_groups=group, tiled=True)

    near = [[4 * i + j for j in range(4)] for i in range(4)]
    far = [[i + 4 * j for j in range(4)] for i in range(4)]
    full, quarter, part = (2, n, rank), (2, n // 4, rank), (2, n // 16, rank)
    mac = 8 * rank * rank
    hbm = [pltpu.with_memory_space_constraint(a, pltpu.HBM) for a in (order, rhs, col_basis, wl, w)]
    qleaf, q0, out = call(
        leaf_kernel, "saaaaa",
        [((2, 2 * n, rank), BF), (full, BF), ((4,) + quarter, BF)],
        pos, *hbm,
        scratch=(
            pltpu.SMEM(order.shape, jnp.int32),
            pltpu.VMEM(rhs.shape, BF),
            pltpu.VMEM(col_basis.shape, BF),
            pltpu.VMEM((2, 2, rank, rank), BF),
            pltpu.VMEM((2, 2, rank, rank), BF),
            pltpu.SemaphoreType.DMA((6,)),
        ),
        flops=mac * n * 7, name="leaf_skeletons",
    )
    got = exchange(out, "top", near)
    q_sib0 = swap(q0, 1)
    q_own1, q_oth1, q2, out = call(
        mid_kernel, "svv",
        [(quarter, BF), (quarter, BF), (quarter, BF), ((4,) + part, BF)],
        pos, got, w, flops=mac * n, name="levels_0_1",
    )
    got = exchange(out, "top", far)
    q_sib2 = swap(q2, 4)
    q_own3, q_oth3, out = call(
        mid_last_kernel, "svv", [(part, BF), (part, BF), ((16,) + part, BF)],
        pos, got, w, flops=mac * n // 4, name="levels_2_5",
    )
    got = exchange(out, "leaf", None)
    (direct,) = call(
        direct_kernel, "svv", [(rhs.shape, F32)], order, rhs, diag,
        flops=mac * n * 8, name="direct",
    )
    c0, cleaf = call(
        low_couple_kernel, "svvvv", [(full, F32), (qleaf.shape, F32)],
        pos, q_sib0, qleaf, bl, b, flops=mac * n * 3, name="low_coupled",
    )
    c2, c1_own, c1_oth = call(
        couple_kernel, "svvvv", [(quarter, F32), (quarter, F32), (quarter, F32)],
        pos, q_sib2, q_own1, q_oth1, b, flops=mac * n, name="mid_coupled",
    )
    (out,) = call(
        top_kernel, "svvvvv", [((4,) + part, BF)],
        pos, got, q_own3, q_oth3, w, b, flops=mac * n // 2, name="top",
    )
    got = exchange(out, "top", far)
    (out,) = call(
        down_kernel, "svvvvv", [((4,) + quarter, BF)],
        pos, got, c2, c1_own, c1_oth, w, flops=mac * n, name="down",
    )
    got = exchange(out, "top", near)
    (out,) = call(
        last_kernel, "ssvvvvvvv", [(rhs.shape, BF)],
        pos, order, got, c0, cleaf, direct, w, wl, row_basis,
        flops=mac * n * 7, name="last",
    )
    return out


def solution(mesh):
    return jax.shard_map(
        shards,
        mesh=mesh,
        in_specs=(
            P(None, ("leaf", "top"), None),
            P(None, ("leaf", "top"), None, None),
            P(None, ("leaf", "top"), None, None),
            P(None, ("leaf", "top"), None, None),
            P(None, ("leaf", "top"), None, None, None),
            P(None, ("leaf", "top"), None, None),
            P(None, ("leaf", "top"), None, None, None, None),
            P(None, ("leaf", "top"), None, None, None),
            P(("leaf", "top"), None),
        ),
        out_specs=P(None, ("leaf", "top"), None),
        check_vma=False,
    )
```

time: 155 us -> 90.5 us (0.58)
  the two profiles are of different devices: /device:TPU:22 before, /device:TPU:1 now
where the time goes in v1:
time: 90.5 us; the launch traced here: 89.9 us
  blocking collectives  38 us (42%)
  local copies, waits for them, and re-layouts  18.5 us (20%)
  Pallas kernels  16 us (18%)
  starting transfers between devices  14.2 us (16%)
  waiting for transfers between devices  3.1 us (3%)
    all_to_all x3, blocking collectives, exchange(): lax.all_to_all(value, axis, 0, 0, axis_index_groups=group, tiled=True)  38 us
    unnamed x48, local copies, waits for them, and re-layouts  18.5 us
    pallas_call x9, Pallas kernels, call(): pl.pallas_call(kernel, out_shape=[jax.ShapeDtypeStruct(shape, dtype) for...  16 us
    all_to_all x2, starting transfers between devices, exchange(): lax.all_to_all(value, axis, 0, 0, axis_index_groups=group, tiled=True)  11.7 us
    ppermute x2, waiting for transfers between devices, swap(): lax.ppermute(value, 'top', [(i, i ^ flip) for i in range(lax.axis_size('t...  3.09 us
    ppermute x2, starting transfers between devices, swap(): lax.ppermute(value, 'top', [(i, i ^ flip) for i in range(lax.axis_size('t...  2.45 us
  transfers between devices with their start and end apart: 4, of which 1 were waited for; matrix products, arithmetic and copies ran while one was open for 0% of the time, Pallas kernels for 5%

profile of v1, /device:TPU:1, one launch (start us, length us, event | category | flops | bytes accessed | tf_op | source)
XLA Modules:
  0.0 89.9 jit_solution(13987095555053990822)
XLA Ops:
  0.0 0.0 copy-start
  0.0 4.0 %leaf_skeletons.1 = (bf16[2,512,256]{2,1,0:T(8,128)(2,1)S(1)}, bf16[2,256,256]{2,1,0:T(8,128)(2,1)S(1)}, bf16[4,2,64,256]{3,2,1,0:T(8,128)(2,1)S(1)}) custom-call(s32[1]{0:T(128)} %bitcast.pos, s32[1,2]{1,0:T(1,128)} %order.5, bf16[2,1024,256]{2,1,0:T(8,128)(2,1)} %x.3, bf16[2,2,512,256]{3,2,1,0:T(8,128)(2,1)} %u.1, bf16[2,1,2,256,256]{4,3,2,1,0:T(8,128)(2,1)} %wl.3, ...), custom_call_target="tpu_custom_call" | custom-call | flops 939524096 | bytes 6815756 | tf_op jit(solution)/shard_map/leaf_skeletons/pallas_call | solution.py:240
  4.0 0.0 copy-start.13
  4.0 0.8 copy-done.13
  4.8 0.0 copy-start.23
  4.8 10.6 %all_to_all.25.got = bf16[4,2,64,256]{3,2,1,0:T(8,128)(2,1)S(1)} all-to-all(bf16[4,2,64,256]{3,2,1,0:T(8,128)(2,1)S(1)} %get-tuple-element.20), channel_id=1, replica_groups={{0,1,2,3},{4,5,6,7},{8,9,10,11},{12,13,14,15},{16,17,18,19},{20,21,22,2..., dimensions={0} | all-to-all | bytes 524288 | tf_op jit(solution)/shard_map/all_to_all | solution.py:265
  15.4 0.0 copy-done
  15.4 0.4 levels_0_1.1
  15.9 0.0 copy-done.23
  15.9 13.2 %all_to_all.26.got = bf16[4,2,16,256]{3,2,1,0:T(8,128)(2,1)S(1)} all-to-all(bf16[4,2,16,256]{3,2,1,0:T(8,128)(2,1)S(1)} %get-tuple-element.21), channel_id=1, replica_groups={{0,4,8,12},{1,5,9,13},{2,6,10,14},{3,7,11,15},{16,20,24,28},{17,21,25,2..., dimensions={0} | all-to-all | bytes 131072 | tf_op jit(solution)/shard_map/all_to_all | solution.py:265
  29.1 0.0 copy-start.3
  29.1 0.7 levels_2_5.1
  29.8 14.1 %all_to_all.27.got = bf16[16,2,16,256]{3,2,1,0:T(8,128)(2,1)S(1)} all-to-all(bf16[16,2,16,256]{3,2,1,0:T(8,128)(2,1)S(1)} %get-tuple-element.22), channel_id=1, replica_groups=mesh['leaf'=16,'top'=16] {'leaf'}, dimensions={0} | all-to-all | bytes 524288 | tf_op jit(solution)/shard_map/all_to_all | solution.py:265
  44.0 0.0 copy-done.3
  44.0 2.4 %top.1 = bf16[4,2,16,256]{3,2,1,0:T(8,128)(2,1)} custom-call(s32[1]{0:T(128)} %bitcast.pos, bf16[16,2,16,256]{3,2,1,0:T(8,128)(2,1)S(1)} %all_to_all.27.got, bf16[2,16,256]{2,1,0:T(8,128)(2,1)S(1)} %get-tuple-element.23.q_own3, bf16[2,16,256]{2,1,0:T(8,128)(2,1)S(1)} %get-tuple-element.24.q_oth3, bf16[2,8,2,256,256]{4,3,2,1,0:T(8,128)(2,1)S(1)} %bitcast.6, ...), custom_call_target="tpu_custom_call" | custom-call | flops 67108864 | bytes 6586372 | tf_op jit(solution)/shard_map/top/pallas_call | solution.py:240
  46.4 3.3 %all-to-all-start.3 = ((bf16[4,2,16,256]{3,2,1,0:T(8,128)(2,1)}), bf16[4,2,16,256]{3,2,1,0:T(8,128)(2,1)S(1)}, u32[]{:S(2)}, u32[]{:S(2)}) async-start(bf16[4,2,16,256]{3,2,1,0:T(8,128)(2,1)} %top.1), calls=%async_computation.3 | async-start | bytes 131072 | tf_op jit(solution)/shard_map/all_to_all | solution.py:265
  49.7 2.3 %collective-permute-start = (bf16[2,64,256]{2,1,0:T(8,128)(2,1)S(1)}, bf16[2,64,256]{2,1,0:T(8,128)(2,1)S(1)}, u32[]{:S(2)}, u32[]{:S(2)}) collective-permute-start(bf16[2,64,256]{2,1,0:T(8,128)(2,1)S(1)} %get-tuple-element.25), channel_id=1, source_target_pairs={{0,4},{1,5},{2,6},{3,7},{4,0},{5,1},{6,2},{7,3},{8,12},{9,13},{10,... | collective-permute-start | bytes 196616 | tf_op jit(solution)/shard_map/ppermute | solution.py:262
  52.0 3.1 %collective-permute-done.q_sib2 = bf16[2,64,256]{2,1,0:T(8,128)(2,1)S(1)} collective-permute-done((bf16[2,64,256]{2,1,0:T(8,128)(2,1)S(1)}, bf16[2,64,256]{2,1,0:T(8,128)(2,1)S(1)}, u32[]{:S(2)}, u32[]{:S(2)}) %collective-permute-start) | collective-permute-done | bytes 65568 | tf_op jit(solution)/shard_map/ppermute | solution.py:262
  55.1 0.5 mid_coupled.1
  55.6 0.0 copy-start.16
  55.6 0.6 copy-done.16
  56.3 0.0 copy-start.18
  56.3 0.6 copy-done.18
  56.9 0.0 copy-start.20
  56.9 0.6 copy-done.20
  57.5 0.0 all-to-all-done.3.got
  57.5 0.0 copy-start.1
  57.5 2.2 %copy-done.1 = bf16[2,1,8,2,256,256]{5,4,3,2,1,0:T(8,128)(2,1)S(1)} copy-done((bf16[2,1,8,2,256,256]{5,4,3,2,1,0:T(8,128)(2,1)S(1)}, bf16[2,1,8,2,256,256]{5,4,3,2,1,0:T(8,128)(2,1)}, u32[]{:S(2)}) %copy-start.1) | copy-done | bytes 4194328
  59.7 0.0 copy-start.17
  59.7 0.9 %copy-done.17 = f32[2,64,256]{2,1,0:T(8,128)S(1)} copy-done((f32[2,64,256]{2,1,0:T(8,128)S(1)}, f32[2,64,256]{2,1,0:T(8,128)}, u32[]{:S(2)}) %copy-start.17) | copy-done | bytes 131096
  60.6 0.0 copy-start.19
  60.6 0.9 %copy-done.19 = f32[2,64,256]{2,1,0:T(8,128)S(1)} copy-done((f32[2,64,256]{2,1,0:T(8,128)S(1)}, f32[2,64,256]{2,1,0:T(8,128)}, u32[]{:S(2)}) %copy-start.19) | copy-done | bytes 131096
  61.5 0.0 copy-start.21
  61.5 0.9 %copy-done.21 = f32[2,64,256]{2,1,0:T(8,128)S(1)} copy-done((f32[2,64,256]{2,1,0:T(8,128)S(1)}, f32[2,64,256]{2,1,0:T(8,128)}, u32[]{:S(2)}) %copy-start.21) | copy-done | bytes 131096
  62.4 0.0 copy-start.6
  62.4 0.0 copy-start.22
  62.5 0.5 down.1
  62.9 0.0 copy-start.9
  62.9 0.7 copy-done.9
  63.7 8.4 %all-to-all-start.4 = ((bf16[4,2,64,256]{3,2,1,0:T(8,128)(2,1)}), bf16[4,2,64,256]{3,2,1,0:T(8,128)(2,1)S(1)}, u32[]{:S(2)}, u32[]{:S(2)}) async-start(bf16[4,2,64,256]{3,2,1,0:T(8,128)(2,1)} %copy-done.9), calls=%async_computation.4 | async-start | bytes 524288 | tf_op jit(solution)/shard_map/all_to_all | solution.py:265
  72.1 0.1 collective-permute-start.1
  72.2 0.0 copy-done.6
  72.2 0.0 copy-done.22
  72.2 0.0 copy-start.8
  72.2 1.6 %copy-done.8 = bf16[2,2,512,512]{3,2,1,0:T(8,128)(2,1)S(1)} copy-done((bf16[2,2,512,512]{3,2,1,0:T(8,128)(2,1)S(1)}, bf16[2,2,512,512]{3,2,1,0:T(8,128)(2,1)}, u32[]{:S(2)}) %copy-start.8) | copy-done | bytes 2097176
  73.8 0.0 copy-start.14
  73.8 0.0 copy-start.15
  73.8 3.1 %direct.1 = f32[2,1024,256]{2,1,0:T(8,128)S(1)} custom-call(s32[1,2]{1,0:T(1,128)S(1)} %copy-done.22, bf16[2,1024,256]{2,1,0:T(8,128)(2,1)S(1)} %copy-done.6, bf16[2,2,512,512]{3,2,1,0:T(8,128)(2,1)S(1)} %copy-done.8), custom_call_target="tpu_custom_call" | custom-call | flops 1073741824 | bytes 3145736 | tf_op jit(solution)/shard_map/direct/pallas_call | solution.py:240
  76.9 0.0 copy-start.4
  76.9 1.3 %copy-done.4 = f32[2,1024,256]{2,1,0:T(8,128)} copy-done((f32[2,1024,256]{2,1,0:T(8,128)}, f32[2,1024,256]{2,1,0:T(8,128)S(1)}, u32[]{:S(2)}) %copy-start.4) | copy-done | bytes 2097176
  78.2 0.0 copy-start.7
  78.2 0.0 collective-permute-done.1.q_sib0
  78.2 0.0 copy-done.14
  78.2 0.0 copy-done.15
  78.2 0.9 %low_coupled.1 = (f32[2,256,256]{2,1,0:T(8,128)S(1)}, f32[2,512,256]{2,1,0:T(8,128)S(1)}) custom-call(s32[1]{0:T(128)} %bitcast.pos, bf16[2,256,256]{2,1,0:T(8,128)(2,1)S(1)} %collective-permute-done.1.q_sib0, bf16[2,512,256]{2,1,0:T(8,128)(2,1)S(1)} %copy-done.14, bf16[2,1,256,256]{3,2,1,0:T(8,128)(2,1)S(1)} %copy-done.15, bf16[2,8,256,256]{3,2,1,0:T(8,128)(2,1)S(1)} %bitcast.11), custom_call_target="tpu_custom_call" | custom-call | flops 402653184 | bytes 3145732 | tf_op jit(solution)/shard_map/low_coupled/pallas_call | solution.py:240
  79.2 0.0 copy-start.11
  79.2 1.0 %copy-done.11 = f32[2,512,256]{2,1,0:T(8,128)} copy-done((f32[2,512,256]{2,1,0:T(8,128)}, f32[2,512,256]{2,1,0:T(8,128)S(1)}, u32[]{:S(2)}) %copy-start.11) | copy-done | bytes 1048600
  80.1 0.0 all-to-all-done.4.got
  80.1 0.0 copy-done.7
  80.1 2.2 %copy-done.2 = bf16[2,1,8,2,256,256]{5,4,3,2,1,0:T(8,128)(2,1)S(1)} copy-done((bf16[2,1,8,2,256,256]{5,4,3,2,1,0:T(8,128)(2,1)S(1)}, bf16[2,1,8,2,256,256]{5,4,3,2,1,0:T(8,128)(2,1)}, u32[]{:S(2)}) %copy-start.2) | copy-done | bytes 4194328
  82.3 1.6 %copy-done.5 = f32[2,1024,256]{2,1,0:T(8,128)S(1)} copy-done((f32[2,1024,256]{2,1,0:T(8,128)S(1)}, f32[2,1024,256]{2,1,0:T(8,128)}, u32[]{:S(2)}) %copy-start.5) | copy-done | bytes 2097176
  83.9 1.2 %copy-done.10 = bf16[2,2,512,256]{3,2,1,0:T(8,128)(2,1)S(1)} copy-done((bf16[2,2,512,256]{3,2,1,0:T(8,128)(2,1)S(1)}, bf16[2,2,512,256]{3,2,1,0:T(8,128)(2,1)}, u32[]{:S(2)}) %copy-start.10) | copy-done | bytes 1048600
  85.1 1.2 %copy-done.12 = f32[2,512,256]{2,1,0:T(8,128)S(1)} copy-done((f32[2,512,256]{2,1,0:T(8,128)S(1)}, f32[2,512,256]{2,1,0:T(8,128)}, u32[]{:S(2)}) %copy-start.12) | copy-done | bytes 1048600
  86.4 3.5 %last.1 = bf16[2,1024,256]{2,1,0:T(8,128)(2,1)} custom-call(s32[1]{0:T(128)} %bitcast.pos, s32[1,2]{1,0:T(1,128)S(1)} %copy-done.22, bf16[4,2,64,256]{3,2,1,0:T(8,128)(2,1)S(1)} %all-to-all-done.4.got, f32[2,256,256]{2,1,0:T(8,128)S(1)} %get-tuple-element.33.c0, f32[2,512,256]{2,1,0:T(8,128)S(1)} %copy-done.12, f32[2,1024,256]{2,1,0:T(8,128)S(1)} %copy-done.5, ...), custom_call_target="tpu_custom_call" | custom-call | flops 939524096 | bytes 9699340 | tf_op jit(solution)/shard_map/last/pallas_call | solution.py:240
  (4 shorter events, 0.0 us)
Async XLA Ops:
  0.0 15.4 %copy-start = (bf16[2,1,8,2,256,256]{5,4,3,2,1,0:T(8,128)(2,1)S(1)}, bf16[2,1,8,2,256,256]{5,4,3,2,1,0:T(8,128)(2,1)}, u32[]{:S(2)}) copy-start(bf16[2,1,8,2,256,256]{5,4,3,2,1,0:T(8,128)(2,1)} %param.15) | copy-start | bytes 12582916
  4.0 0.8 copy-start.13
  4.8 11.1 %copy-start.23 = (bf16[2,256,256]{2,1,0:T(8,128)(2,1)}, bf16[2,256,256]{2,1,0:T(8,128)(2,1)S(1)}, u32[]{:S(2)}) copy-start(bf16[2,256,256]{2,1,0:T(8,128)(2,1)S(1)} %get-tuple-element.31) | copy-start | bytes 786436
  29.1 14.9 %copy-start.3 = (bf16[2,1,8,256,256]{4,3,2,1,0:T(8,128)(2,1)S(1)}, bf16[2,1,8,256,256]{4,3,2,1,0:T(8,128)(2,1)}, u32[]{:S(2)}) copy-start(bf16[2,1,8,256,256]{4,3,2,1,0:T(8,128)(2,1)} %param.16) | copy-start | bytes 6291460
  46.4 11.2 %all-to-all-start.3 = ((bf16[4,2,16,256]{3,2,1,0:T(8,128)(2,1)}), bf16[4,2,16,256]{3,2,1,0:T(8,128)(2,1)S(1)}, u32[]{:S(2)}, u32[]{:S(2)}) async-start(bf16[4,2,16,256]{3,2,1,0:T(8,128)(2,1)} %top.1), calls=%async_computation.3 | async-start | bytes 131072 | tf_op jit(solution)/shard_map/all_to_all | solution.py:265
  49.7 5.4 %collective-permute-start = (bf16[2,64,256]{2,1,0:T(8,128)(2,1)S(1)}, bf16[2,64,256]{2,1,0:T(8,128)(2,1)S(1)}, u32[]{:S(2)}, u32[]{:S(2)}) collective-permute-start(bf16[2,64,256]{2,1,0:T(8,128)(2,1)S(1)} %get-tuple-element.25), channel_id=1, source_target_pairs={{0,4},{1,5},{2,6},{3,7},{4,0},{5,1},{6,2},{7,3},{8,12},{9,13},{10,... | collective-permute-start | bytes 196616 | tf_op jit(solution)/shard_map/ppermute | solution.py:262
  55.6 0.6 copy-start.16
  56.3 0.6 copy-start.18
  56.9 0.6 copy-start.20
  57.5 2.2 %copy-start.1 = (bf16[2,1,8,2,256,256]{5,4,3,2,1,0:T(8,128)(2,1)S(1)}, bf16[2,1,8,2,256,256]{5,4,3,2,1,0:T(8,128)(2,1)}, u32[]{:S(2)}) copy-start(bf16[2,1,8,2,256,256]{5,4,3,2,1,0:T(8,128)(2,1)} %param.15) | copy-start | bytes 12582916
  59.7 0.9 %copy-start.17 = (f32[2,64,256]{2,1,0:T(8,128)S(1)}, f32[2,64,256]{2,1,0:T(8,128)}, u32[]{:S(2)}) copy-start(f32[2,64,256]{2,1,0:T(8,128)} %copy-done.16) | copy-start | bytes 393220
  60.6 0.9 %copy-start.19 = (f32[2,64,256]{2,1,0:T(8,128)S(1)}, f32[2,64,256]{2,1,0:T(8,128)}, u32[]{:S(2)}) copy-start(f32[2,64,256]{2,1,0:T(8,128)} %copy-done.18) | copy-start | bytes 393220
  61.5 0.9 %copy-start.21 = (f32[2,64,256]{2,1,0:T(8,128)S(1)}, f32[2,64,256]{2,1,0:T(8,128)}, u32[]{:S(2)}) copy-start(f32[2,64,256]{2,1,0:T(8,128)} %copy-done.20) | copy-start | bytes 393220
  62.4 9.8 %copy-start.6 = (bf16[2,1024,256]{2,1,0:T(8,128)(2,1)S(1)}, bf16[2,1024,256]{2,1,0:T(8,128)(2,1)}, u32[]{:S(2)}) copy-start(bf16[2,1024,256]{2,1,0:T(8,128)(2,1)} %x.3) | copy-start | bytes 3145732
  62.4 9.8 %copy-start.22 = (s32[1,2]{1,0:T(1,128)S(1)}, s32[1,2]{1,0:T(1,128)}, u32[]{:S(2)}) copy-start(s32[1,2]{1,0:T(1,128)} %order.5) | copy-start | bytes 28
  62.9 0.7 copy-start.9
  63.7 16.5 %all-to-all-start.4 = ((bf16[4,2,64,256]{3,2,1,0:T(8,128)(2,1)}), bf16[4,2,64,256]{3,2,1,0:T(8,128)(2,1)S(1)}, u32[]{:S(2)}, u32[]{:S(2)}) async-start(bf16[4,2,64,256]{3,2,1,0:T(8,128)(2,1)} %copy-done.9), calls=%async_computation.4 | async-start | bytes 524288 | tf_op jit(solution)/shard_map/all_to_all | solution.py:265
  72.1 6.2 %collective-permute-start.1 = (bf16[2,256,256]{2,1,0:T(8,128)(2,1)}, bf16[2,256,256]{2,1,0:T(8,128)(2,1)S(1)}, u32[]{:S(2)}, u32[]{:S(2)}) collective-permute-start(bf16[2,256,256]{2,1,0:T(8,128)(2,1)} %copy-done.23), channel_id=1, source_target_pairs={{0,1},{1,0},{2,3},{3,2},{4,5},{5,4},{6,7},{7,6},{8,9},{9,8},{10,11... | collective-permute-start | bytes 786440 | tf_op jit(solution)/shard_map/ppermute | solution.py:262
  72.2 1.6 %copy-start.8 = (bf16[2,2,512,512]{3,2,1,0:T(8,128)(2,1)S(1)}, bf16[2,2,512,512]{3,2,1,0:T(8,128)(2,1)}, u32[]{:S(2)}) copy-start(bf16[2,2,512,512]{3,2,1,0:T(8,128)(2,1)} %d.1) | copy-start | bytes 6291460
  73.8 4.4 %copy-start.14 = (bf16[2,512,256]{2,1,0:T(8,128)(2,1)S(1)}, bf16[2,512,256]{2,1,0:T(8,128)(2,1)}, u32[]{:S(2)}) copy-start(bf16[2,512,256]{2,1,0:T(8,128)(2,1)} %copy-done.13) | copy-start | bytes 1572868
  73.8 4.4 %copy-start.15 = (bf16[2,1,256,256]{3,2,1,0:T(8,128)(2,1)S(1)}, bf16[2,1,256,256]{3,2,1,0:T(8,128)(2,1)}, u32[]{:S(2)}) copy-start(bf16[2,1,256,256]{3,2,1,0:T(8,128)(2,1)} %bl.1) | copy-start | bytes 786436
  76.9 1.4 %copy-start.4 = (f32[2,1024,256]{2,1,0:T(8,128)}, f32[2,1024,256]{2,1,0:T(8,128)S(1)}, u32[]{:S(2)}) copy-start(f32[2,1024,256]{2,1,0:T(8,128)S(1)} %direct.1) | copy-start | bytes 6291460
  78.2 1.9 %copy-start.7 = (bf16[2,1,2,256,256]{4,3,2,1,0:T(8,128)(2,1)S(1)}, bf16[2,1,2,256,256]{4,3,2,1,0:T(8,128)(2,1)}, u32[]{:S(2)}) copy-start(bf16[2,1,2,256,256]{4,3,2,1,0:T(8,128)(2,1)} %wl.3) | copy-start | bytes 1572868
  79.2 1.0 %copy-start.11 = (f32[2,512,256]{2,1,0:T(8,128)}, f32[2,512,256]{2,1,0:T(8,128)S(1)}, u32[]{:S(2)}) copy-start(f32[2,512,256]{2,1,0:T(8,128)S(1)} %get-tuple-element.34.cleaf) | copy-start | bytes 3145732
  80.1 2.2 %copy-start.2 = (bf16[2,1,8,2,256,256]{5,4,3,2,1,0:T(8,128)(2,1)S(1)}, bf16[2,1,8,2,256,256]{5,4,3,2,1,0:T(8,128)(2,1)}, u32[]{:S(2)}) copy-start(bf16[2,1,8,2,256,256]{5,4,3,2,1,0:T(8,128)(2,1)} %param.15) | copy-start | bytes 12582916
  82.3 1.6 %copy-start.5 = (f32[2,1024,256]{2,1,0:T(8,128)S(1)}, f32[2,1024,256]{2,1,0:T(8,128)}, u32[]{:S(2)}) copy-start(f32[2,1024,256]{2,1,0:T(8,128)} %copy-done.4) | copy-start | bytes 6291460
  83.9 1.2 %copy-start.10 = (bf16[2,2,512,256]{3,2,1,0:T(8,128)(2,1)S(1)}, bf16[2,2,512,256]{3,2,1,0:T(8,128)(2,1)}, u32[]{:S(2)}) copy-start(bf16[2,2,512,256]{3,2,1,0:T(8,128)(2,1)} %r.1) | copy-start | bytes 3145732
  85.1 1.2 %copy-start.12 = (f32[2,512,256]{2,1,0:T(8,128)S(1)}, f32[2,512,256]{2,1,0:T(8,128)}, u32[]{:S(2)}) copy-start(f32[2,512,256]{2,1,0:T(8,128)} %copy-done.11) | copy-start | bytes 3145732

commit v2 on v0

v2 whole, which is shorter than its diff:
```python
import jax
import jax.numpy as jnp
from jax import lax
from jax.experimental import pallas as pl
from jax.experimental.pallas import tpu as pltpu
from jax.sharding import PartitionSpec as P

BF = jnp.bfloat16
F32 = jnp.float32
NN = (((1,), (0,)), ((), ()))
NT = (((1,), (1,)), ((), ()))


def dot(a, b, dims=NN):
    return lax.dot_general(a, b, dims, preferred_element_type=F32)


def widen(a):
    half = a.shape[0] // 2
    re, im = a[:half], a[half:]
    return jnp.concatenate(
        [jnp.concatenate([re, -im], axis=1), jnp.concatenate([im, re], axis=1)], axis=0
    )


def times(a, w_re, w_im):
    return dot(widen(a), jnp.concatenate([w_re, w_im], axis=0))


def times_t(a, w_re, w_im):
    return dot(widen(a), jnp.concatenate([w_re, w_im], axis=1), NT)


def rows(ref):
    return jnp.concatenate([ref[0], ref[1]], axis=0)


def put(ref, value):
    half = value.shape[0] // 2
    ref[0] = value[:half].astype(ref.dtype)
    ref[1] = value[half:].astype(ref.dtype)


def bit(pos, level):
    return (pos[0] >> level) & 1


def lift(q, w, pos, level, flip=0):
    child = bit(pos, level) ^ flip
    return times(q, w[0, level, child], w[1, level, child])


def lower(h, w, pos, level, flip=0):
    child = bit(pos, level) ^ flip
    return times_t(h, w[0, level, child], w[1, level, child])


def couple(q, b, pos, level, flip=0):
    return lax.cond(
        (bit(pos, level) ^ flip) == 0,
        lambda: times_t(q, b[0, level], b[1, level]),
        lambda: times(q, b[0, level], b[1, level]),
    )


def split(value, side, keep, send):
    half = value.shape[0] // 2
    part = half // 2
    for c in range(2):
        low = value[c * half : c * half + part]
        high = value[c * half + part : (c + 1) * half]
        keep[c] = jnp.where(side == 0, low, high)
        send[c] = jnp.where(side == 0, high, low)


def join(own, got, side):
    parts = []
    for c in range(2):
        parts.append(jnp.where(side == 0, own[c], got[c]))
        parts.append(jnp.where(side == 0, got[c], own[c]))
    return jnp.concatenate(parts, axis=0)


def leaf_kernel(pos, order, x, u, wl, w, qleaf, keep, send, own, order_s, x_v, u_v, wl_v, w_v, sems):
    size = u.shape[2]
    copies = [
        pltpu.make_async_copy(order, order_s, sems.at[0]),
        pltpu.make_async_copy(x.at[:, pl.ds(0, size)], x_v.at[:, pl.ds(0, size)], sems.at[1]),
        pltpu.make_async_copy(u, u_v, sems.at[2]),
        pltpu.make_async_copy(x.at[:, pl.ds(size, size)], x_v.at[:, pl.ds(size, size)], sems.at[3]),
        pltpu.make_async_copy(wl.at[:, 0], wl_v, sems.at[4]),
        pltpu.make_async_copy(w.at[:, 0], w_v.at[:, 0], sems.at[5]),
    ]
    for copy in copies:
        copy.start()
    copies[0].wait()
    first = order_s[0, 0]
    for block in range(2):
        copies[1 + 2 * block].wait()
        at = pl.ds(block * size, size)
        xt = jnp.concatenate([x_v[0, at].T, x_v[1, at].T], axis=0)
        if block == 0:
            copies[2].wait()
        leaf = first ^ block
        qleaf[leaf] = times(xt, u_v[0, leaf], u_v[1, leaf]).astype(BF)
    copies[4].wait()
    q = times(qleaf[0], wl_v[0, 0], wl_v[1, 0]) + times(qleaf[1], wl_v[0, 1], wl_v[1, 1])
    split(q.astype(BF), bit(pos, 0), keep, send)
    copies[5].wait()
    put(own, lift(rows(keep), w_v, pos, 0))


def climb_kernel(level):
    def kernel(pos, got, own, w, *outs):
        q = (rows(own) + lift(rows(got), w, pos, level, 1)).astype(BF)
        if len(outs) == 2:
            split(q, bit(pos, level + 1), *outs)
        else:
            put(outs[0], q)

    return kernel


def direct(order, block, x, d, out):
    size = d.shape[2]
    leaf = order[0, 0] ^ block
    at = pl.ds(block * size, size)
    xs = jnp.concatenate([x[0, at], x[1, at]], axis=0)
    re, im = d[0, leaf], d[1, leaf]
    out[0] = dot(jnp.concatenate([re, -im], axis=1), xs)
    out[1] = dot(jnp.concatenate([im, re], axis=1), xs)


def shadow_1(pos, order, keep, w, x, d, own, part):
    put(own, lift(rows(keep), w, pos, 1))
    direct(order, 0, x, d, part)


def shadow_2(pos, order, keep, w, x, d, own, part):
    put(own, lift(rows(keep), w, pos, 2))
    direct(order, 1, x, d, part)


def shadow_3(pos, q3, w, b, bl, qleaf, keep0, got0, keep1, got1, keep2, got2, own, cleaf, *coupled):
    put(own, lift(rows(q3), w, pos, 3))
    cleaf[0] = times_t(qleaf[1], bl[0, 0], bl[1, 0]).astype(BF)
    cleaf[1] = times(qleaf[0], bl[0, 0], bl[1, 0]).astype(BF)
    for level, (keep, got) in enumerate(((keep0, got0), (keep1, got1), (keep2, got2))):
        put(coupled[2 * level], couple(rows(got), b, pos, level))
        put(coupled[2 * level + 1], couple(rows(keep), b, pos, level, 1))


def shadow_4(pos, order, q4, got3, w, b, r, cleaf, part_0, part_1, own, top, base):
    put(own, lift(rows(q4), w, pos, 4))
    put(top, couple(rows(got3), b, pos, 3))
    n = part_0.shape[2]
    size = r.shape[2]
    first = order[0, 0]
    for block, part in enumerate((part_0, part_1)):
        leaf = first ^ block
        add = dot(jnp.concatenate([r[0, leaf], r[1, leaf]], axis=1), widen(cleaf[leaf]), NT)
        for c in range(2):
            for half in range(2):
                lanes = slice(half * n // 2, (half + 1) * n // 2)
                base[half, c, pl.ds(block * size, size)] = (
                    part[c, :, lanes] + add[:, c * n + lanes.start : c * n + lanes.stop]
                )


def product(r, wl, leaf, out):
    put(out, times(jnp.concatenate([r[0, leaf], r[1, leaf]], axis=0), wl[0, 0, leaf], wl[1, 0, leaf]))


def shadow_5(pos, q5, got4, w, b, r, wl, top, own, top_out, path, rw):
    put(own, lift(rows(q5), w, pos, 5))
    c4 = couple(rows(got4), b, pos, 4).astype(BF)
    put(top_out, rows(top) + lower(c4, w, pos, 3))
    w3 = bit(pos, 3)
    put(path, lift(jnp.concatenate([w[0, 3, w3], w[1, 3, w3]], axis=0), w, pos, 4))
    product(r, wl, 0, rw)


def shadow_6(pos, q6, got5, w, b, r, wl, top, path, own, top_out, path_out, rw):
    put(own, lift(rows(q6), w, pos, 6))
    c5 = couple(rows(got5), b, pos, 5).astype(BF)
    put(top_out, rows(top) + times_t(c5, path[0], path[1]))
    put(path_out, lift(rows(path), w, pos, 5))
    product(r, wl, 1, rw)


def shadow_7(pos, got6, w, b, top, path, top_out, path_out):
    c6 = couple(rows(got6), b, pos, 6).astype(BF)
    put(top_out, rows(top) + times_t(c6, path[0], path[1]))
    longer = lift(rows(path), w, pos, 6).astype(BF)
    put(path_out, couple_path(longer, b, pos))


def couple_path(path, b, pos):
    return lax.cond(
        bit(pos, 7) == 0,
        lambda: times(path, b[0, 7], b[1, 7]),
        lambda: times_t(path, b[0, 7], b[1, 7]),
    )


def top_kernel(pos, got, top, path, c_own, c_oth, w, own, send):
    h = (rows(top) + times_t(rows(got), path[0], path[1])).astype(BF)
    put(own, rows(c_own) + lower(h, w, pos, 2))
    put(send, rows(c_oth) + lower(h, w, pos, 2, 1))


def down_kernel(level):
    def kernel(pos, mine, got, c_own, c_oth, w, own, send):
        h = join(mine, got, bit(pos, level + 1))
        put(own, rows(c_own) + lower(h, w, pos, level))
        put(send, rows(c_oth) + lower(h, w, pos, level, 1))

    return kernel


def finish(order, h, base, half, rws, emit):
    hw = widen(rows(h))
    n = h.shape[1]
    first = order[0, 0]
    for leaf, rw in enumerate(rws):
        size = rw.shape[1]
        at = pl.ds(pl.multiple_of((first ^ leaf) * size, size), size)
        add = dot(jnp.concatenate([rw[0], rw[1]], axis=1), hw, NT)
        for c in range(2):
            emit(c, at, (base[half, c, at] + add[:, c * n : (c + 1) * n]).astype(BF))


def own_kernel(pos, order, h, base, rw0, rw1, out):
    def emit(c, at, value):
        out[c, at] = value

    finish(order, h, base, bit(pos, 0), (rw0, rw1), emit)


def last_kernel(pos, order, h, base, rw0, rw1, done, out):
    side = bit(pos, 0)
    n = h.shape[1]
    at_own = pl.ds(pl.multiple_of(side * n, n), n)
    at_oth = pl.ds(pl.multiple_of((1 - side) * n, n), n)
    out[:, :, at_own] = done[...]

    def emit(c, at, value):
        out[c, at, at_oth] = value

    finish(order, h, base, 1 - side, (rw0, rw1), emit)


VMEM = pl.BlockSpec(memory_space=pltpu.VMEM)
SMEM = pl.BlockSpec(memory_space=pltpu.SMEM)
HBM = pl.BlockSpec(memory_space=pltpu.HBM)
GRANT = 20 * 2**20


def call(name, kernel, ins, outs, *args, scratch=(), flops=0):
    specs = {"s": SMEM, "v": VMEM, "h": HBM}
    moved = sum(a.size * a.dtype.itemsize for a in args)
    return pl.pallas_call(
        kernel,
        out_shape=[jax.ShapeDtypeStruct(shape, dtype) for shape, dtype in outs],
        in_specs=[specs[kind] for kind in ins],
        out_specs=[VMEM] * len(outs),
        scratch_shapes=list(scratch),
        compiler_params=pltpu.CompilerParams(vmem_limit_bytes=GRANT),
        cost_estimate=pl.CostEstimate(flops=flops, bytes_accessed=moved, transcendentals=0),
        name=name,
    )(*args)


def shards(rhs, diag, row_basis, col_basis, wl, bl, cross_w, cross_b, order):
    n = rhs.shape[2]
    rank = col_basis.shape[3]
    size = col_basis.shape[2]
    top_size = lax.axis_size("top")
    pos = (lax.axis_index("leaf") * top_size + lax.axis_index("top")).astype(jnp.int32).reshape(1)
    w = cross_w[:, 0]
    b = cross_b[:, 0]

    def swap(value, level):
        flip = 2**level
        axis, mask = ("top", flip) if flip < top_size else ("leaf", flip // top_size)
        return lax.ppermute(value, axis, [(i, i ^ mask) for i in range(lax.axis_size(axis))])

    def block(columns, dtype=BF):
        return ((2, columns, rank), dtype)

    mac = 8 * rank * rank
    hbm = [pltpu.with_memory_space_constraint(a, pltpu.HBM) for a in (order, rhs, col_basis, wl, w)]
    half, quarter, eighth = n // 2, n // 4, n // 8
    qleaf, keep0, send, own = call(
        "leaf_skeletons", leaf_kernel, "shhhhh",
        [((2, 2 * n, rank), BF), block(half), block(half), block(half, F32)], pos, *hbm,
        scratch=(
            pltpu.SMEM(order.shape, jnp.int32),
            pltpu.VMEM(rhs.shape, BF),
            pltpu.VMEM(col_basis.shape, BF),
            pltpu.VMEM((2, 2, rank, rank), BF),
            pltpu.VMEM((2, 1, 2, rank, rank), BF),
            pltpu.SemaphoreType.DMA((6,)),
        ),
        flops=mac * n * 6,
    )
    got0 = swap(send, 0)
    keep1, send = call(
        "climb_0", climb_kernel(0), "svvv", [block(quarter), block(quarter)],
        pos, got0, own, w, flops=mac * half,
    )
    got1 = swap(send, 1)
    own, part_0 = call(
        "shadow_1", shadow_1, "ssvvvv", [block(quarter, F32), ((2, size, n), F32)],
        pos, order, keep1, w, rhs, diag, flops=mac * n * 5,
    )
    keep2, send = call(
        "climb_1", climb_kernel(1), "svvv", [block(eighth), block(eighth)],
        pos, got1, own, w, flops=mac * quarter,
    )
    got2 = swap(send, 2)
    own, part_1 = call(
        "shadow_2", shadow_2, "ssvvvv", [block(eighth, F32), ((2, size, n), F32)],
        pos, order, keep2, w, rhs, diag, flops=mac * n * 5,
    )
    (q3,) = call("climb_2", climb_kernel(2), "svvv", [block(eighth)], pos, got2, own, w, flops=mac * eighth)
    got3 = swap(q3, 3)
    own, cleaf, c0, c0_oth, c1, c1_oth, c2, c2_oth = call(
        "shadow_3", shadow_3, "s" + "v" * 11,
        [block(eighth, F32), ((2, 2 * n, rank), BF)]
        + [block(half, F32)] * 2 + [block(quarter, F32)] * 2 + [block(eighth, F32)] * 2,
        pos, q3, w, b, bl, qleaf, keep0, got0, keep1, got1, keep2, got2, flops=mac * n * 4,
    )
    (q4,) = call("climb_3", climb_kernel(3), "svvv", [block(eighth)], pos, got3, own, w, flops=mac * eighth)
    got4 = swap(q4, 4)
    own, top, base = call(
        "shadow_4", shadow_4, "ss" + "v" * 8,
        [block(eighth, F32), block(eighth, F32), ((2, 2, 2 * size, half), F32)],
        pos, order, q4, got3, w, b, row_basis, cleaf, part_0, part_1, flops=mac * n * 4,
    )
    (q5,) = call("climb_4", climb_kernel(4), "svvv", [block(eighth)], pos, got4, own, w, flops=mac * eighth)
    got5 = swap(q5, 5)
    own, top, path, rw0 = call(
        "shadow_5", shadow_5, "s" + "v" * 7,
        [block(eighth, F32), block(eighth, F32), block(rank), block(size)],
        pos, q5, got4, w, b, row_basis, wl, top, flops=mac * n * 3,
    )
    (q6,) = call("climb_5", climb_kernel(5), "svvv", [block(eighth)], pos, got5, own, w, flops=mac * eighth)
    got6 = swap(q6, 6)
    own, top, path, rw1 = call(
        "shadow_6", shadow_6, "s" + "v" * 8,
        [block(eighth, F32), block(eighth, F32), block(rank), block(size)],
        pos, q6, got5, w, b, row_basis, wl, top, path, flops=mac * n * 3,
    )
    (q7,) = call("climb_6", climb_kernel(6), "svvv", [block(eighth)], pos, got6, own, w, flops=mac * eighth)
    got7 = swap(q7, 7)
    top, path = call(
        "shadow_7", shadow_7, "s" + "v" * 5, [block(eighth, F32), block(rank)],
        pos, got6, w, b, top, path, flops=mac * n * 2,
    )
    mine, send = call(
        "top", top_kernel, "s" + "v" * 6, [block(eighth), block(eighth)],
        pos, got7, top, path, c2, c2_oth, w, flops=mac * eighth * 3,
    )
    got = swap(send, 2)
    mine, send = call(
        "down_1", down_kernel(1), "s" + "v" * 5, [block(quarter), block(quarter)],
        pos, mine, got, c1, c1_oth, w, flops=mac * quarter * 2,
    )
    got = swap(send, 1)
    mine, send = call(
        "down_0", down_kernel(0), "s" + "v" * 5, [block(half), block(half)],
        pos, mine, got, c0, c0_oth, w, flops=mac * half * 2,
    )
    got = swap(send, 0)
    (done,) = call(
        "own_columns", own_kernel, "ss" + "v" * 4, [((2, 2 * size, half), BF)],
        pos, order, mine, base, rw0, rw1, flops=mac * n * 2,
    )
    (out,) = call(
        "other_columns", last_kernel, "ss" + "v" * 5, [(rhs.shape, BF)],
        pos, order, got, base, rw0, rw1, done, flops=mac * n * 2,
    )
    return out


def solution(mesh):
    return jax.shard_map(
        shards,
        mesh=mesh,
        in_specs=(
            P(None, ("leaf", "top"), None),
            P(None, ("leaf", "top"), None, None),
            P(None, ("leaf", "top"), None, None),
            P(None, ("leaf", "top"), None, None),
            P(None, ("leaf", "top"), None, None, None),
            P(None, ("leaf", "top"), None, None),
            P(None, ("leaf", "top"), None, None, None, None),
            P(None, ("leaf", "top"), None, None, None),
            P(("leaf", "top"), None),
        ),
        out_specs=P(None, ("leaf", "top"), None),
        check_vma=False,
    )
```

time: 155 us -> 60.3 us (0.39)
  the two profiles are of different devices: /device:TPU:22 before, /device:TPU:1 now
where the time goes in v2:
time: 60.3 us; the launch traced here: 60.1 us
  starting transfers between devices  31.8 us (53%)
  Pallas kernels  18.5 us (31%)
  waiting for transfers between devices  8.07 us (13%)
  local copies, waits for them, and re-layouts  1.6 us (3%)
    ppermute x11, starting transfers between devices, swap(): lax.ppermute(value, axis, [(i, i ^ mask) for i in range(lax.axis_size(axi...  31.8 us
    pallas_call x20, Pallas kernels, call(): pl.pallas_call(kernel, out_shape=[jax.ShapeDtypeStruct(shape, dtype) for...  18.5 us
    ppermute x11, waiting for transfers between devices, swap(): lax.ppermute(value, axis, [(i, i ^ mask) for i in range(lax.axis_size(axi...  8.07 us
    unnamed x16, local copies, waits for them, and re-layouts  1.6 us
  transfers between devices with their start and end apart: 11, of which 9 were waited for; matrix products, arithmetic and copies ran while one was open for 0% of the time, Pallas kernels for 17%

profile of v2, /device:TPU:1, one launch (start us, length us, event | category | flops | bytes accessed | tf_op | source)
XLA Modules:
  0.0 60.1 jit_solution(15608404230684274487)
XLA Ops:
  0.0 0.0 copy-start
  0.0 3.8 %leaf_skeletons.1 = (bf16[2,512,256]{2,1,0:T(8,128)(2,1)S(1)}, bf16[2,128,256]{2,1,0:T(8,128)(2,1)S(1)}, bf16[2,128,256]{2,1,0:T(8,128)(2,1)S(1)}, f32[2,128,256]{2,1,0:T(8,128)S(1)}) custom-call(s32[1]{0:T(128)} %bitcast.pos, s32[1,2]{1,0:T(1,128)} %order.11, bf16[2,1024,256]{2,1,0:T(8,128)(2,1)} %x.5, bf16[2,2,512,256]{3,2,1,0:T(8,128)(2,1)} %u.1, ...), custom_call_target="tpu_custom_call" | custom-call | flops 805306368 | bytes 6815756 | tf_op jit(solution)/shard_map/leaf_skeletons/pallas_call | solution.py:262
  3.8 3.3 %collective-permute-start = (bf16[2,128,256]{2,1,0:T(8,128)(2,1)S(1)}, bf16[2,128,256]{2,1,0:T(8,128)(2,1)S(1)}, u32[]{:S(2)}, u32[]{:S(2)}) collective-permute-start(bf16[2,128,256]{2,1,0:T(8,128)(2,1)S(1)} %get-tuple-element.44), channel_id=1, source_target_pairs={{0,1},{1,0},{2,3},{3,2},{4,5},{5,4},{6,7},{7,6},{8,9},{9,8},{10,11... | collective-permute-start | bytes 393224 | tf_op jit(solution)/shard_map/ppermute | solution.py:286
  7.1 1.0 %collective-permute-done.got.got0 = bf16[2,128,256]{2,1,0:T(8,128)(2,1)S(1)} collective-permute-done((bf16[2,128,256]{2,1,0:T(8,128)(2,1)S(1)}, bf16[2,128,256]{2,1,0:T(8,128)(2,1)S(1)}, u32[]{:S(2)}, u32[]{:S(2)}) %collective-permute-start) | collective-permute-done | bytes 131104 | tf_op jit(solution)/shard_map/ppermute | solution.py:286
  8.1 0.0 copy-done
  8.1 0.0 copy-start.2
  8.1 0.0 copy-start.4
  8.1 0.0 copy-start.7
  8.1 0.2 climb_0.1
  8.4 0.1 collective-permute-start.1
  8.5 0.9 %copy-done.2 = bf16[2,1024,256]{2,1,0:T(8,128)(2,1)S(1)} copy-done((bf16[2,1024,256]{2,1,0:T(8,128)(2,1)S(1)}, bf16[2,1024,256]{2,1,0:T(8,128)(2,1)}, u32[]{:S(2)}) %copy-start.2) | copy-done | bytes 1048600
  9.3 0.7 %copy-done.4 = bf16[2,2,512,512]{3,2,1,0:T(8,128)(2,1)S(1)} copy-done((bf16[2,2,512,512]{3,2,1,0:T(8,128)(2,1)S(1)}, bf16[2,2,512,512]{3,2,1,0:T(8,128)(2,1)}, u32[]{:S(2)}) %copy-start.4) | copy-done | bytes 2097176
  10.0 0.0 copy-done.7
  10.0 1.3 %shadow_1.1 = (f32[2,64,256]{2,1,0:T(8,128)S(1)}, f32[2,512,256]{2,1,0:T(8,128)S(1)}) custom-call(s32[1]{0:T(128)} %bitcast.pos, s32[1,2]{1,0:T(1,128)S(1)} %copy-done.7, bf16[2,64,256]{2,1,0:T(8,128)(2,1)S(1)} %get-tuple-element.47.keep.keep1, bf16[2,8,2,256,256]{4,3,2,1,0:T(8,128)(2,1)S(1)} %bitcast.5, bf16[2,1024,256]{2,1,0:T(8,128)(2,1)S(1)} %copy-done.2, ...), custom_call_target="tpu_custom_call" | custom-call | flops 671088640 | bytes 7405580 | tf_op jit(solution)/shard_map/shadow_1/pallas_call | solution.py:262
  11.3 0.2 collective-permute-done.1.got.got1
  11.6 0.2 climb_1.1
  11.8 1.9 %collective-permute-start.2 = (bf16[2,32,256]{2,1,0:T(8,128)(2,1)S(1)}, bf16[2,32,256]{2,1,0:T(8,128)(2,1)S(1)}, u32[]{:S(2)}, u32[]{:S(2)}) collective-permute-start(bf16[2,32,256]{2,1,0:T(8,128)(2,1)S(1)} %get-tuple-element.49), channel_id=1, source_target_pairs={{0,4},{1,5},{2,6},{3,7},{4,0},{5,1},{6,2},{7,3},{8,12},{9,13},{10,... | collective-permute-start | bytes 98312 | tf_op jit(solution)/shard_map/ppermute | solution.py:286
  13.7 1.3 %shadow_2.1 = (f32[2,32,256]{2,1,0:T(8,128)S(1)}, f32[2,512,256]{2,1,0:T(8,128)S(1)}) custom-call(s32[1]{0:T(128)} %bitcast.pos, s32[1,2]{1,0:T(1,128)S(1)} %copy-done.7, bf16[2,32,256]{2,1,0:T(8,128)(2,1)S(1)} %get-tuple-element.50.keep.keep2, bf16[2,8,2,256,256]{4,3,2,1,0:T(8,128)(2,1)S(1)} %bitcast.7, bf16[2,1024,256]{2,1,0:T(8,128)(2,1)S(1)} %copy-done.2, ...), custom_call_target="tpu_custom_call" | custom-call | flops 671088640 | bytes 7372812 | tf_op jit(solution)/shard_map/shadow_2/pallas_call | solution.py:262
  15.0 0.6 collective-permute-done.2.got.got2
  15.5 0.0 copy-start.1
  15.5 0.0 copy-start.6
  15.5 0.2 climb_2.1.q3
  15.7 5.3 %collective-permute-start.3 = (bf16[2,32,256]{2,1,0:T(8,128)(2,1)S(1)}, bf16[2,32,256]{2,1,0:T(8,128)(2,1)S(1)}, u32[]{:S(2)}, u32[]{:S(2)}) collective-permute-start(bf16[2,32,256]{2,1,0:T(8,128)(2,1)S(1)} %climb_2.1.q3), channel_id=1, source_target_pairs={{0,8},{1,9},{2,10},{3,11},{4,12},{5,13},{6,14},{7,15},{8,0},{9,1},... | collective-permute-start | bytes 98312 | tf_op jit(solution)/shard_map/ppermute | solution.py:286
  21.0 0.0 copy-done.1
  21.0 0.0 copy-done.6
  21.0 1.9 %shadow_3.1 = (f32[2,32,256]{2,1,0:T(8,128)S(1)}, bf16[2,512,256]{2,1,0:T(8,128)(2,1)S(1)}, f32[2,128,256]{2,1,0:T(8,128)S(1)}, f32[2,128,256]{2,1,0:T(8,128)S(1...) custom-call(s32[1]{0:T(128)} %bitcast.pos, ...), custom_call_target="tpu_custom_call" | custom-call | flops 536870912 | bytes 7569412 | tf_op jit(solution)/shard_map/shadow_3/pallas_call | solution.py:262
  22.8 0.0 collective-permute-done.3.got.got3
  22.8 0.0 copy-start.3
  22.8 0.2 climb_3.1.q4
  23.0 1.3 %collective-permute-start.4 = (bf16[2,32,256]{2,1,0:T(8,128)(2,1)S(1)}, bf16[2,32,256]{2,1,0:T(8,128)(2,1)S(1)}, u32[]{:S(2)}, u32[]{:S(2)}) collective-permute-start(bf16[2,32,256]{2,1,0:T(8,128)(2,1)S(1)} %climb_3.1.q4), channel_id=1, source_target_pairs={{0,16},{16,0},{32,48},{48,32},{64,80},{80,64},{96,112},{112,96},{1... | collective-permute-start | bytes 98312 | tf_op jit(solution)/shard_map/ppermute | solution.py:286
  24.3 0.0 copy-done.3
  24.3 1.7 %shadow_4.1 = (f32[2,32,256]{2,1,0:T(8,128)S(1)}, f32[2,32,256]{2,1,0:T(8,128)S(1)}, f32[2,2,1024,128]{3,2,1,0:T(8,128)S(1)}) custom-call(s32[1]{0:T(128)} %bitcast.pos, s32[1,2]{1,0:T(1,128)S(1)} %copy-done.7, bf16[2,32,256]{2,1,0:T(8,128)(2,1)S(1)} %climb_3.1.q4, bf16[2,32,256]{2,1,0:T(8,128)(2,1)S(1)} %collective-permute-done.3.got.got3, ...), custom_call_target="tpu_custom_call" | custom-call | flops 536870912 | bytes 10027020 | tf_op jit(solution)/shard_map/shadow_4/pallas_call | solution.py:262
  26.0 0.2 collective-permute-done.4.got.got4
  26.2 0.0 copy-start.5
  26.2 0.2 climb_4.1.q5
  26.3 2.5 %collective-permute-start.5 = (bf16[2,32,256]{2,1,0:T(8,128)(2,1)S(1)}, bf16[2,32,256]{2,1,0:T(8,128)(2,1)S(1)}, u32[]{:S(2)}, u32[]{:S(2)}) collective-permute-start(bf16[2,32,256]{2,1,0:T(8,128)(2,1)S(1)} %climb_4.1.q5), channel_id=1, source_target_pairs={{0,32},{16,48},{32,0},{48,16},{64,96},{80,112},{96,64},{112,80},{1... | collective-permute-start | bytes 98312 | tf_op jit(solution)/shard_map/ppermute | solution.py:286
  28.9 0.0 copy-done.5
  28.9 1.0 %shadow_5.1 = (f32[2,32,256]{2,1,0:T(8,128)S(1)}, f32[2,32,256]{2,1,0:T(8,128)S(1)}, bf16[2,256,256]{2,1,0:T(8,128)(2,1)S(1)}, bf16[2,512,256]{2,1,0:T(8,128)(2,1)S(1)}) custom-call(s32[1]{0:T(128)} %bitcast.pos, bf16[2,32,256]{2,1,0:T(8,128)(2,1)S(1)} %climb_4.1.q5, bf16[2,32,256]{2,1,0:T(8,128)(2,1)S(1)} %collective-permute-done.4.got.got4, ...), custom_call_target="tpu_custom_call" | custom-call | flops 402653184 | bytes 7995396 | tf_op jit(solution)/shard_map/shadow_5/pallas_call | solution.py:262
  29.9 0.8 %collective-permute-done.5.got.got5 = bf16[2,32,256]{2,1,0:T(8,128)(2,1)S(1)} collective-permute-done((bf16[2,32,256]{2,1,0:T(8,128)(2,1)S(1)}, bf16[2,32,256]{2,1,0:T(8,128)(2,1)S(1)}, u32[]{:S(2)}, u32[]{:S(2)}) %collective-permute-start.5) | collective-permute-done | bytes 32800 | tf_op jit(solution)/shard_map/ppermute | solution.py:286
  30.7 0.2 climb_5.1.q6
  30.9 1.2 %collective-permute-start.6 = (bf16[2,32,256]{2,1,0:T(8,128)(2,1)S(1)}, bf16[2,32,256]{2,1,0:T(8,128)(2,1)S(1)}, u32[]{:S(2)}, u32[]{:S(2)}) collective-permute-start(bf16[2,32,256]{2,1,0:T(8,128)(2,1)S(1)} %climb_5.1.q6), channel_id=1, source_target_pairs={{0,64},{16,80},{32,96},{48,112},{64,0},{80,16},{96,32},{112,48},{1... | collective-permute-start | bytes 98312 | tf_op jit(solution)/shard_map/ppermute | solution.py:286
  32.1 1.0 %shadow_6.1 = (f32[2,32,256]{2,1,0:T(8,128)S(1)}, f32[2,32,256]{2,1,0:T(8,128)S(1)}, bf16[2,256,256]{2,1,0:T(8,128)(2,1)S(1)}, bf16[2,512,256]{2,1,0:T(8,128)(2,1)S(1)}) custom-call(s32[1]{0:T(128)} %bitcast.pos, bf16[2,32,256]{2,1,0:T(8,128)(2,1)S(1)} %climb_5.1.q6, bf16[2,32,256]{2,1,0:T(8,128)(2,1)S(1)} %collective-permute-done.5.got.got5, ...), custom_call_target="tpu_custom_call" | custom-call | flops 402653184 | bytes 8257540 | tf_op jit(solution)/shard_map/shadow_6/pallas_call | solution.py:262
  33.1 0.6 collective-permute-done.6.got.got6
  33.7 0.2 climb_6.1
  33.9 2.9 %collective-permute-start.7 = (bf16[2,32,256]{2,1,0:T(8,128)(2,1)S(1)}, bf16[2,32,256]{2,1,0:T(8,128)(2,1)S(1)}, u32[]{:S(2)}, u32[]{:S(2)}) collective-permute-start(bf16[2,32,256]{2,1,0:T(8,128)(2,1)S(1)} %climb_6.1), channel_id=1, source_target_pairs={{0,128},{16,144},{32,160},{48,176},{64,192},{80,208},{96,224},{112... | collective-permute-start | bytes 98312 | tf_op jit(solution)/shard_map/ppermute | solution.py:286
  36.8 1.1 %shadow_7.1 = (f32[2,32,256]{2,1,0:T(8,128)S(1)}, bf16[2,256,256]{2,1,0:T(8,128)(2,1)S(1)}) custom-call(s32[1]{0:T(128)} %bitcast.pos, bf16[2,32,256]{2,1,0:T(8,128)(2,1)S(1)} %collective-permute-done.6.got.got6, bf16[2,8,2,256,256]{4,3,2,1,0:T(8,128)(2,1)S(1)} %bitcast.17, bf16[2,8,256,256]{3,2,1,0:T(8,128)(2,1)S(1)} %bitcast.25, ...), custom_call_target="tpu_custom_call" | custom-call | flops 268435456 | bytes 6651908 | tf_op jit(solution)/shard_map/shadow_7/pallas_call | solution.py:262
  37.9 0.3 collective-permute-done.7.got
  38.3 0.4 top.1
  38.7 1.9 %collective-permute-start.8 = (bf16[2,32,256]{2,1,0:T(8,128)(2,1)S(1)}, bf16[2,32,256]{2,1,0:T(8,128)(2,1)S(1)}, u32[]{:S(2)}, u32[]{:S(2)}) collective-permute-start(bf16[2,32,256]{2,1,0:T(8,128)(2,1)S(1)} %get-tuple-element.71), channel_id=1, source_target_pairs={{0,4},{1,5},{2,6},{3,7},{4,0},{5,1},{6,2},{7,3},{8,12},{9,13},{10,... | collective-permute-start | bytes 98312 | tf_op jit(solution)/shard_map/ppermute | solution.py:286
  40.5 1.9 %collective-permute-done.8.got = bf16[2,32,256]{2,1,0:T(8,128)(2,1)S(1)} collective-permute-done((bf16[2,32,256]{2,1,0:T(8,128)(2,1)S(1)}, bf16[2,32,256]{2,1,0:T(8,128)(2,1)S(1)}, u32[]{:S(2)}, u32[]{:S(2)}) %collective-permute-start.8) | collective-permute-done | bytes 32800 | tf_op jit(solution)/shard_map/ppermute | solution.py:286
  42.4 0.3 down_1.1
  42.7 0.7 %collective-permute-start.9 = (bf16[2,64,256]{2,1,0:T(8,128)(2,1)S(1)}, bf16[2,64,256]{2,1,0:T(8,128)(2,1)S(1)}, u32[]{:S(2)}, u32[]{:S(2)}) collective-permute-start(bf16[2,64,256]{2,1,0:T(8,128)(2,1)S(1)} %get-tuple-element.75), channel_id=1, source_target_pairs={{0,2},{1,3},{2,0},{3,1},{4,6},{5,7},{6,4},{7,5},{8,10},{9,11},{10,... | collective-permute-start | bytes 196616 | tf_op jit(solution)/shard_map/ppermute | solution.py:286
  43.4 2.5 %collective-permute-done.9.got = bf16[2,64,256]{2,1,0:T(8,128)(2,1)S(1)} collective-permute-done((bf16[2,64,256]{2,1,0:T(8,128)(2,1)S(1)}, bf16[2,64,256]{2,1,0:T(8,128)(2,1)S(1)}, u32[]{:S(2)}, u32[]{:S(2)}) %collective-permute-start.9) | collective-permute-done | bytes 65568 | tf_op jit(solution)/shard_map/ppermute | solution.py:286
  45.9 0.3 down_0.1
  46.3 10.7 %collective-permute-start.10 = (bf16[2,128,256]{2,1,0:T(8,128)(2,1)S(1)}, bf16[2,128,256]{2,1,0:T(8,128)(2,1)S(1)}, u32[]{:S(2)}, u32[]{:S(2)}) collective-permute-start(bf16[2,128,256]{2,1,0:T(8,128)(2,1)S(1)} %get-tuple-element.78), channel_id=1, source_target_pairs={{0,1},{1,0},{2,3},{3,2},{4,5},{5,4},{6,7},{7,6},{8,9},{9,8},{10,11... | collective-permute-start | bytes 393224 | tf_op jit(solution)/shard_map/ppermute | solution.py:286
  56.9 1.0 %own_columns.1.done = bf16[2,1024,128]{2,1,0:T(8,128)(2,1)S(1)} custom-call(s32[1]{0:T(128)} %bitcast.pos, s32[1,2]{1,0:T(1,128)S(1)} %copy-done.7, bf16[2,128,256]{2,1,0:T(8,128)(2,1)S(1)} %get-tuple-element.82.h, f32[2,2,1024,128]{3,2,1,0:T(8,128)S(1)} %get-tuple-element.79.base, bf16[2,512,256]{2,1,0:T(8,128)(2,1)S(1)} %get-tuple-element.80.rw0, ...), custom_call_target="tpu_custom_call" | custom-call | flops 268435456 | bytes 3276812 | tf_op jit(solution)/shard_map/own_columns/pallas_call | solution.py:262
  58.0 0.0 collective-permute-done.10.h
  58.0 2.1 %other_columns.1 = bf16[2,1024,256]{2,1,0:T(8,128)(2,1)} custom-call(s32[1]{0:T(128)} %bitcast.pos, s32[1,2]{1,0:T(1,128)S(1)} %copy-done.7, bf16[2,128,256]{2,1,0:T(8,128)(2,1)S(1)} %collective-permute-done.10.h, f32[2,2,1024,128]{3,2,1,0:T(8,128)S(1)} %get-tuple-element.79.base, bf16[2,512,256]{2,1,0:T(8,128)(2,1)S(1)} %get-tuple-element.80.rw0, ...), custom_call_target="tpu_custom_call" | custom-call | flops 268435456 | bytes 3801100 | tf_op jit(solution)/shard_map/other_columns/pallas_call | solution.py:262
Async XLA Ops:
  0.0 8.1 %copy-start = (bf16[2,1,8,2,256,256]{5,4,3,2,1,0:T(8,128)(2,1)S(1)}, bf16[2,1,8,2,256,256]{5,4,3,2,1,0:T(8,128)(2,1)}, u32[]{:S(2)}) copy-start(bf16[2,1,8,2,256,256]{5,4,3,2,1,0:T(8,128)(2,1)} %param.15) | copy-start | bytes 12582916
  3.8 4.3 %collective-permute-start = (bf16[2,128,256]{2,1,0:T(8,128)(2,1)S(1)}, bf16[2,128,256]{2,1,0:T(8,128)(2,1)S(1)}, u32[]{:S(2)}, u32[]{:S(2)}) collective-permute-start(bf16[2,128,256]{2,1,0:T(8,128)(2,1)S(1)} %get-tuple-element.44), channel_id=1, source_target_pairs={{0,1},{1,0},{2,3},{3,2},{4,5},{5,4},{6,7},{7,6},{8,9},{9,8},{10,11... | collective-permute-start | bytes 393224 | tf_op jit(solution)/shard_map/ppermute | solution.py:286
  8.1 1.2 %copy-start.2 = (bf16[2,1024,256]{2,1,0:T(8,128)(2,1)S(1)}, bf16[2,1024,256]{2,1,0:T(8,128)(2,1)}, u32[]{:S(2)}) copy-start(bf16[2,1024,256]{2,1,0:T(8,128)(2,1)} %x.5) | copy-start | bytes 3145732
  8.1 1.9 %copy-start.4 = (bf16[2,2,512,512]{3,2,1,0:T(8,128)(2,1)S(1)}, bf16[2,2,512,512]{3,2,1,0:T(8,128)(2,1)}, u32[]{:S(2)}) copy-start(bf16[2,2,512,512]{3,2,1,0:T(8,128)(2,1)} %d.3) | copy-start | bytes 6291460
  8.1 1.9 %copy-start.7 = (s32[1,2]{1,0:T(1,128)S(1)}, s32[1,2]{1,0:T(1,128)}, u32[]{:S(2)}) copy-start(s32[1,2]{1,0:T(1,128)} %order.11) | copy-start | bytes 28
  8.4 3.2 %collective-permute-start.1 = (bf16[2,64,256]{2,1,0:T(8,128)(2,1)S(1)}, bf16[2,64,256]{2,1,0:T(8,128)(2,1)S(1)}, u32[]{:S(2)}, u32[]{:S(2)}) collective-permute-start(bf16[2,64,256]{2,1,0:T(8,128)(2,1)S(1)} %get-tuple-element.46), channel_id=1, source_target_pairs={{0,2},{1,3},{2,0},{3,1},{4,6},{5,7},{6,4},{7,5},{8,10},{9,11},{10,... | collective-permute-start | bytes 196616 | tf_op jit(solution)/shard_map/ppermute | solution.py:286
  11.8 3.8 %collective-permute-start.2 = (bf16[2,32,256]{2,1,0:T(8,128)(2,1)S(1)}, bf16[2,32,256]{2,1,0:T(8,128)(2,1)S(1)}, u32[]{:S(2)}, u32[]{:S(2)}) collective-permute-start(bf16[2,32,256]{2,1,0:T(8,128)(2,1)S(1)} %get-tuple-element.49), channel_id=1, source_target_pairs={{0,4},{1,5},{2,6},{3,7},{4,0},{5,1},{6,2},{7,3},{8,12},{9,13},{10,... | collective-permute-start | bytes 98312 | tf_op jit(solution)/shard_map/ppermute | solution.py:286
  15.5 5.4 %copy-start.1 = (bf16[2,1,8,256,256]{4,3,2,1,0:T(8,128)(2,1)S(1)}, bf16[2,1,8,256,256]{4,3,2,1,0:T(8,128)(2,1)}, u32[]{:S(2)}) copy-start(bf16[2,1,8,256,256]{4,3,2,1,0:T(8,128)(2,1)} %param.16) | copy-start | bytes 6291460
  15.5 5.4 %copy-start.6 = (bf16[2,1,256,256]{3,2,1,0:T(8,128)(2,1)S(1)}, bf16[2,1,256,256]{3,2,1,0:T(8,128)(2,1)}, u32[]{:S(2)}) copy-start(bf16[2,1,256,256]{3,2,1,0:T(8,128)(2,1)} %bl.1) | copy-start | bytes 786436
  15.7 7.1 %collective-permute-start.3 = (bf16[2,32,256]{2,1,0:T(8,128)(2,1)S(1)}, bf16[2,32,256]{2,1,0:T(8,128)(2,1)S(1)}, u32[]{:S(2)}, u32[]{:S(2)}) collective-permute-start(bf16[2,32,256]{2,1,0:T(8,128)(2,1)S(1)} %climb_2.1.q3), channel_id=1, source_target_pairs={{0,8},{1,9},{2,10},{3,11},{4,12},{5,13},{6,14},{7,15},{8,0},{9,1},... | collective-permute-start | bytes 98312 | tf_op jit(solution)/shard_map/ppermute | solution.py:286
  22.8 1.5 %copy-start.3 = (bf16[2,2,512,256]{3,2,1,0:T(8,128)(2,1)S(1)}, bf16[2,2,512,256]{3,2,1,0:T(8,128)(2,1)}, u32[]{:S(2)}) copy-start(bf16[2,2,512,256]{3,2,1,0:T(8,128)(2,1)} %r.5) | copy-start | bytes 3145732
  23.0 3.1 %collective-permute-start.4 = (bf16[2,32,256]{2,1,0:T(8,128)(2,1)S(1)}, bf16[2,32,256]{2,1,0:T(8,128)(2,1)S(1)}, u32[]{:S(2)}, u32[]{:S(2)}) collective-permute-start(bf16[2,32,256]{2,1,0:T(8,128)(2,1)S(1)} %climb_3.1.q4), channel_id=1, source_target_pairs={{0,16},{16,0},{32,48},{48,32},{64,80},{80,64},{96,112},{112,96},{1... | collective-permute-start | bytes 98312 | tf_op jit(solution)/shard_map/ppermute | solution.py:286
  26.2 2.7 %copy-start.5 = (bf16[2,1,2,256,256]{4,3,2,1,0:T(8,128)(2,1)S(1)}, bf16[2,1,2,256,256]{4,3,2,1,0:T(8,128)(2,1)}, u32[]{:S(2)}) copy-start(bf16[2,1,2,256,256]{4,3,2,1,0:T(8,128)(2,1)} %wl.5) | copy-start | bytes 1572868
  26.3 4.4 %collective-permute-start.5 = (bf16[2,32,256]{2,1,0:T(8,128)(2,1)S(1)}, bf16[2,32,256]{2,1,0:T(8,128)(2,1)S(1)}, u32[]{:S(2)}, u32[]{:S(2)}) collective-permute-start(bf16[2,32,256]{2,1,0:T(8,128)(2,1)S(1)} %climb_4.1.q5), channel_id=1, source_target_pairs={{0,32},{16,48},{32,0},{48,16},{64,96},{80,112},{96,64},{112,80},{1... | collective-permute-start | bytes 98312 | tf_op jit(solution)/shard_map/ppermute | solution.py:286
  30.9 2.9 %collective-permute-start.6 = (bf16[2,32,256]{2,1,0:T(8,128)(2,1)S(1)}, bf16[2,32,256]{2,1,0:T(8,128)(2,1)S(1)}, u32[]{:S(2)}, u32[]{:S(2)}) collective-permute-start(bf16[2,32,256]{2,1,0:T(8,128)(2,1)S(1)} %climb_5.1.q6), channel_id=1, source_target_pairs={{0,64},{16,80},{32,96},{48,112},{64,0},{80,16},{96,32},{112,48},{1... | collective-permute-start | bytes 98312 | tf_op jit(solution)/shard_map/ppermute | solution.py:286
  33.9 4.4 %collective-permute-start.7 = (bf16[2,32,256]{2,1,0:T(8,128)(2,1)S(1)}, bf16[2,32,256]{2,1,0:T(8,128)(2,1)S(1)}, u32[]{:S(2)}, u32[]{:S(2)}) collective-permute-start(bf16[2,32,256]{2,1,0:T(8,128)(2,1)S(1)} %climb_6.1), channel_id=1, source_target_pairs={{0,128},{16,144},{32,160},{48,176},{64,192},{80,208},{96,224},{112... | collective-permute-start | bytes 98312 | tf_op jit(solution)/shard_map/ppermute | solution.py:286
  38.7 3.8 %collective-permute-start.8 = (bf16[2,32,256]{2,1,0:T(8,128)(2,1)S(1)}, bf16[2,32,256]{2,1,0:T(8,128)(2,1)S(1)}, u32[]{:S(2)}, u32[]{:S(2)}) collective-permute-start(bf16[2,32,256]{2,1,0:T(8,128)(2,1)S(1)} %get-tuple-element.71), channel_id=1, source_target_pairs={{0,4},{1,5},{2,6},{3,7},{4,0},{5,1},{6,2},{7,3},{8,12},{9,13},{10,... | collective-permute-start | bytes 98312 | tf_op jit(solution)/shard_map/ppermute | solution.py:286
  42.7 3.2 %collective-permute-start.9 = (bf16[2,64,256]{2,1,0:T(8,128)(2,1)S(1)}, bf16[2,64,256]{2,1,0:T(8,128)(2,1)S(1)}, u32[]{:S(2)}, u32[]{:S(2)}) collective-permute-start(bf16[2,64,256]{2,1,0:T(8,128)(2,1)S(1)} %get-tuple-element.75), channel_id=1, source_target_pairs={{0,2},{1,3},{2,0},{3,1},{4,6},{5,7},{6,4},{7,5},{8,10},{9,11},{10,... | collective-permute-start | bytes 196616 | tf_op jit(solution)/shard_map/ppermute | solution.py:286
  46.3 11.7 %collective-permute-start.10 = (bf16[2,128,256]{2,1,0:T(8,128)(2,1)S(1)}, bf16[2,128,256]{2,1,0:T(8,128)(2,1)S(1)}, u32[]{:S(2)}, u32[]{:S(2)}) collective-permute-start(bf16[2,128,256]{2,1,0:T(8,128)(2,1)S(1)} %get-tuple-element.78), channel_id=1, source_target_pairs={{0,1},{1,0},{2,3},{3,2},{4,5},{5,4},{6,7},{7,6},{8,9},{9,8},{10,11... | collective-permute-start | bytes 393224 | tf_op jit(solution)/shard_map/ppermute | solution.py:286

commit v3 on v2

v3 whole, which is shorter than its diff:
```python
import jax
import jax.numpy as jnp
from jax import lax
from jax.experimental import pallas as pl
from jax.experimental.pallas import tpu as pltpu
from jax.sharding import PartitionSpec as P

BF = jnp.bfloat16
F32 = jnp.float32
NN = (((1,), (0,)), ((), ()))
NT = (((1,), (1,)), ((), ()))


def dot(a, b, dims=NN):
    return lax.dot_general(a, b, dims, preferred_element_type=F32)


def widen(a):
    half = a.shape[0] // 2
    re, im = a[:half], a[half:]
    return jnp.concatenate(
        [jnp.concatenate([re, -im], axis=1), jnp.concatenate([im, re], axis=1)], axis=0
    )


def times(a, w_re, w_im):
    return dot(widen(a), jnp.concatenate([w_re, w_im], axis=0))


def times_t(a, w_re, w_im):
    return dot(widen(a), jnp.concatenate([w_re, w_im], axis=1), NT)


def rows(ref):
    return jnp.concatenate([ref[0], ref[1]], axis=0)


def put(ref, value):
    half = value.shape[0] // 2
    ref[0] = value[:half].astype(ref.dtype)
    ref[1] = value[half:].astype(ref.dtype)


def bit(pos, level):
    return (pos[0] >> level) & 1


def lift(q, w, pos, level, flip=0):
    child = bit(pos, level) ^ flip
    return times(q, w[0, level, child], w[1, level, child])


def lower(h, w, pos, level, flip=0):
    child = bit(pos, level) ^ flip
    return times_t(h, w[0, level, child], w[1, level, child])


def couple(q, b, pos, level, flip=0):
    return lax.cond(
        (bit(pos, level) ^ flip) == 0,
        lambda: times_t(q, b[0, level], b[1, level]),
        lambda: times(q, b[0, level], b[1, level]),
    )


def split(value, side, keep, send):
    half = value.shape[0] // 2
    part = half // 2
    for c in range(2):
        low = value[c * half : c * half + part]
        high = value[c * half + part : (c + 1) * half]
        keep[c] = jnp.where(side == 0, low, high)
        send[c] = jnp.where(side == 0, high, low)


def join(own, got, side):
    parts = []
    for c in range(2):
        parts.append(jnp.where(side == 0, own[c], got[c]))
        parts.append(jnp.where(side == 0, got[c], own[c]))
    return jnp.concatenate(parts, axis=0)


def leaf_kernel(pos, order, x, u, wl, w, qleaf, q0, w0, order_s, x_v, u_v, wl_v, sems):
    size = u.shape[2]
    copies = [
        pltpu.make_async_copy(order, order_s, sems.at[0]),
        pltpu.make_async_copy(x.at[:, pl.ds(0, size)], x_v.at[:, pl.ds(0, size)], sems.at[1]),
        pltpu.make_async_copy(u, u_v, sems.at[2]),
        pltpu.make_async_copy(x.at[:, pl.ds(size, size)], x_v.at[:, pl.ds(size, size)], sems.at[3]),
        pltpu.make_async_copy(wl.at[:, 0], wl_v, sems.at[4]),
        pltpu.make_async_copy(w.at[:, 0], w0.at[:, 0], sems.at[5]),
    ]
    for copy in copies:
        copy.start()
    copies[0].wait()
    first = order_s[0, 0]
    for block in range(2):
        copies[1 + 2 * block].wait()
        at = pl.ds(block * size, size)
        xt = jnp.concatenate([x_v[0, at].T, x_v[1, at].T], axis=0)
        if block == 0:
            copies[2].wait()
        leaf = first ^ block
        qleaf[leaf] = times(xt, u_v[0, leaf], u_v[1, leaf]).astype(BF)
    copies[4].wait()
    put(q0, times(qleaf[0], wl_v[0, 0], wl_v[1, 0]) + times(qleaf[1], wl_v[0, 1], wl_v[1, 1]))
    copies[5].wait()


def side(pos, level):
    return bit(pos, level) ^ bit(pos, level + 1) if level == 2 else bit(pos, level)


def climb_kernel(level):
    def kernel(pos, got, own, w, *outs):
        q = (rows(own) + lift(rows(got), w, pos, level, 1)).astype(BF)
        if len(outs) == 2:
            split(q, side(pos, level + 1), *outs)
        else:
            put(outs[0], q)

    return kernel


def direct(order, block, x, d, out):
    size = d.shape[2]
    leaf = order[0, 0] ^ block
    at = pl.ds(block * size, size)
    xs = jnp.concatenate([x[0, at], x[1, at]], axis=0)
    re, im = d[0, leaf], d[1, leaf]
    out[0] = dot(jnp.concatenate([re, -im], axis=1), xs)
    out[1] = dot(jnp.concatenate([im, re], axis=1), xs)


def shadow_0(pos, q0, w, own):
    put(own, lift(rows(q0), w, pos, 0))


def shadow_1(pos, order, keep, w, x, d, own, part):
    put(own, lift(rows(keep), w, pos, 1))
    direct(order, 0, x, d, part)


def shadow_2(pos, order, keep, w, x, d, own, part):
    put(own, lift(rows(keep), w, pos, 2))
    direct(order, 1, x, d, part)


def shadow_3(pos, q3, w, w0, b, bl, wl, qleaf, got0, keep2, got2, own, cleaf, c2, c2_oth):
    put(own, lift(rows(q3), w, pos, 3))
    c0 = couple(rows(got0), b, pos, 0).astype(BF)
    left = times_t(qleaf[1], bl[0, 0], bl[1, 0])
    right = times(qleaf[0], bl[0, 0], bl[1, 0])
    cleaf[0] = (left + times_t(c0, wl[0, 0, 0], wl[1, 0, 0])).astype(BF)
    cleaf[1] = (right + times_t(c0, wl[0, 0, 1], wl[1, 0, 1])).astype(BF)
    put(c2, couple(rows(got2), b, pos, 2))
    put(c2_oth, couple(rows(keep2), b, pos, 2, 1))


def shadow_4(pos, order, q4, got3, w, b, r, cleaf, part_0, part_1, own, top, base):
    put(own, lift(rows(q4), w, pos, 4))
    put(top, couple(rows(got3), b, pos, 3))
    n = part_0.shape[2]
    size = r.shape[2]
    first = order[0, 0]
    for block, part in enumerate((part_0, part_1)):
        leaf = first ^ block
        add = dot(jnp.concatenate([r[0, leaf], r[1, leaf]], axis=1), widen(cleaf[leaf]), NT)
        for c in range(2):
            for half in range(2):
                lanes = slice(half * n // 2, (half + 1) * n // 2)
                base[half, c, pl.ds(block * size, size)] = (
                    part[c, :, lanes] + add[:, c * n + lanes.start : c * n + lanes.stop]
                )


def product(r, wl, leaf, out):
    put(out, times(jnp.concatenate([r[0, leaf], r[1, leaf]], axis=0), wl[0, 0, leaf], wl[1, 0, leaf]))


def shadow_5(pos, q5, got4, w, b, r, wl, top, own, top_out, path, rw):
    put(own, lift(rows(q5), w, pos, 5))
    c4 = couple(rows(got4), b, pos, 4).astype(BF)
    put(top_out, rows(top) + lower(c4, w, pos, 3))
    w3 = bit(pos, 3)
    put(path, lift(jnp.concatenate([w[0, 3, w3], w[1, 3, w3]], axis=0), w, pos, 4))
    product(r, wl, 0, rw)


def shadow_6(pos, q6, got5, w, b, r, wl, top, path, own, top_out, path_out, rw):
    put(own, lift(rows(q6), w, pos, 6))
    c5 = couple(rows(got5), b, pos, 5).astype(BF)
    put(top_out, rows(top) + times_t(c5, path[0], path[1]))
    put(path_out, lift(rows(path), w, pos, 5))
    product(r, wl, 1, rw)


def shadow_7(pos, got6, w, b, top, path, top_out, path_out):
    c6 = couple(rows(got6), b, pos, 6).astype(BF)
    put(top_out, rows(top) + times_t(c6, path[0], path[1]))
    longer = lift(rows(path), w, pos, 6).astype(BF)
    put(path_out, couple_path(longer, b, pos))


def couple_path(path, b, pos):
    return lax.cond(
        bit(pos, 7) == 0,
        lambda: times(path, b[0, 7], b[1, 7]),
        lambda: times_t(path, b[0, 7], b[1, 7]),
    )


def top_kernel(pos, got, top, path, c_own, c_oth, w, own, send):
    h = (rows(top) + times_t(rows(got), path[0], path[1])).astype(BF)
    put(own, rows(c_own) + lower(h, w, pos, 2))
    put(send, rows(c_oth) + lower(h, w, pos, 2, 1))


def shadow_8(pos, mine, keep1, got1, b, w0, rw0, rw1, c1, c1_oth, g0, g1):
    put(c1, couple(rows(got1), b, pos, 1))
    put(c1_oth, couple(rows(keep1), b, pos, 1, 1))
    put(g0, lift(rows(rw0), w0, pos, 0))
    put(g1, lift(rows(rw1), w0, pos, 0))


def down_kernel(pos, mine, got, c_own, c_oth, w, own, send):
    h = join(mine, got, side(pos, 2))
    put(own, rows(c_own) + lower(h, w, pos, 1))
    put(send, rows(c_oth) + lower(h, w, pos, 1, 1))


def finish(pos, order, h_hub, h_other, base, gs, half, out, buf, sems):
    h = jnp.where(bit(pos, 0) == 1, rows(h_hub), rows(h_other))
    hw = widen(h)
    n = h_hub.shape[1]
    lanes = pl.ds(pl.multiple_of(half * n, n), n)
    copies = []
    for leaf, g in enumerate(gs):
        size = g.shape[1]
        at = pl.ds(pl.multiple_of((order[0, 0] ^ leaf) * size, size), size)
        add = dot(jnp.concatenate([g[0], g[1]], axis=1), hw, NT)
        for c in range(2):
            buf[leaf, c] = (base[half, c, at] + add[:, c * n : (c + 1) * n]).astype(BF)
            copies.append(
                pltpu.make_async_copy(buf.at[leaf, c], out.at[c, at, lanes], sems.at[leaf, c])
            )
            copies[-1].start()
    for copy in copies:
        copy.wait()


def own_kernel(pos, order, h_hub, h_other, base, g0, g1, out, buf, sems):
    finish(pos, order, h_hub, h_other, base, (g0, g1), bit(pos, 1), out, buf, sems)


def last_kernel(pos, order, h_hub, h_other, base, g0, g1, done, out, buf, sems):
    finish(pos, order, h_hub, h_other, base, (g0, g1), 1 - bit(pos, 1), out, buf, sems)


VMEM = pl.BlockSpec(memory_space=pltpu.VMEM)
SMEM = pl.BlockSpec(memory_space=pltpu.SMEM)
HBM = pl.BlockSpec(memory_space=pltpu.HBM)
GRANT = 20 * 2**20


def call(name, kernel, ins, outs, *args, scratch=(), flops=0, aliases=None, out_spec=VMEM):
    specs = {"s": SMEM, "v": VMEM, "h": HBM}
    moved = sum(a.size * a.dtype.itemsize for a in args)
    return pl.pallas_call(
        kernel,
        out_shape=[jax.ShapeDtypeStruct(shape, dtype) for shape, dtype in outs],
        in_specs=[specs[kind] for kind in ins],
        out_specs=[out_spec] * len(outs),
        scratch_shapes=list(scratch),
        input_output_aliases=aliases or {},
        compiler_params=pltpu.CompilerParams(vmem_limit_bytes=GRANT),
        cost_estimate=pl.CostEstimate(flops=flops, bytes_accessed=moved, transcendentals=0),
        name=name,
    )(*args)


def shards(rhs, diag, row_basis, col_basis, wl, bl, cross_w, cross_b, order):
    n = rhs.shape[2]
    rank = col_basis.shape[3]
    size = col_basis.shape[2]
    axes = ("leaf", "top")
    devices = lax.axis_size("leaf") * lax.axis_size("top")
    pos = lax.axis_index(axes).astype(jnp.int32).reshape(1)
    w = cross_w[:, 0]
    b = cross_b[:, 0]

    def hubs(value, flip):
        return lax.ppermute(value, axes, [(i, i ^ flip) for i in range(devices) if i & 1])

    def block(columns, dtype=BF):
        return ((2, columns, rank), dtype)

    mac = 8 * rank * rank
    hbm = [pltpu.with_memory_space_constraint(a, pltpu.HBM) for a in (order, rhs, col_basis, wl, w)]
    half, quarter = n // 2, n // 4
    qleaf, q0, w0 = call(
        "leaf_skeletons", leaf_kernel, "shhhhh",
        [((2, 2 * n, rank), BF), block(n), ((2, 1, 2, rank, rank), BF)], pos, *hbm,
        scratch=(
            pltpu.SMEM(order.shape, jnp.int32),
            pltpu.VMEM(rhs.shape, BF),
            pltpu.VMEM(col_basis.shape, BF),
            pltpu.VMEM((2, 2, rank, rank), BF),
            pltpu.SemaphoreType.DMA((6,)),
        ),
        flops=mac * n * 6,
    )
    got0 = lax.ppermute(q0, axes, [(i, i ^ 1) for i in range(devices)])
    (own,) = call("shadow_0", shadow_0, "svv", [block(n, F32)], pos, q0, w0, flops=mac * n)
    keep1, send = call(
        "climb_0", climb_kernel(0), "svvv", [block(half), block(half)],
        pos, got0, own, w0, flops=mac * n,
    )
    got1 = hubs(send, 2)
    own, part_0 = call(
        "shadow_1", shadow_1, "ssvvvv", [block(half, F32), ((2, size, n), F32)],
        pos, order, keep1, w, rhs, diag, flops=mac * n * 5,
    )
    keep2, send = call(
        "climb_1", climb_kernel(1), "svvv", [block(quarter), block(quarter)],
        pos, got1, own, w, flops=mac * half,
    )
    got2 = hubs(send, 4)
    own, part_1 = call(
        "shadow_2", shadow_2, "ssvvvv", [block(quarter, F32), ((2, size, n), F32)],
        pos, order, keep2, w, rhs, diag, flops=mac * n * 5,
    )
    (q3,) = call("climb_2", climb_kernel(2), "svvv", [block(quarter)], pos, got2, own, w, flops=mac * quarter)
    got3 = hubs(q3, 12)
    own, cleaf, c2, c2_oth = call(
        "shadow_3", shadow_3, "s" + "v" * 10,
        [block(quarter, F32), ((2, 2 * n, rank), BF), block(quarter, F32), block(quarter, F32)],
        pos, q3, w, w0, b, bl, wl, qleaf, got0, keep2, got2, flops=mac * n * 6,
    )
    (q4,) = call("climb_3", climb_kernel(3), "svvv", [block(quarter)], pos, got3, own, w, flops=mac * quarter)
    got4 = hubs(q4, 16)
    own, top, base = call(
        "shadow_4", shadow_4, "ss" + "v" * 8,
        [block(quarter, F32), block(quarter, F32), ((2, 2, 2 * size, half), F32)],
        pos, order, q4, got3, w, b, row_basis, cleaf, part_0, part_1, flops=mac * n * 4,
    )
    (q5,) = call("climb_4", climb_kernel(4), "svvv", [block(quarter)], pos, got4, own, w, flops=mac * quarter)
    got5 = hubs(q5, 48)
    own, top, path, rw0 = call(
        "shadow_5", shadow_5, "s" + "v" * 7,
        [block(quarter, F32), block(quarter, F32), block(rank), block(size)],
        pos, q5, got4, w, b, row_basis, wl, top, flops=mac * n * 3,
    )
    (q6,) = call("climb_5", climb_kernel(5), "svvv", [block(quarter)], pos, got5, own, w, flops=mac * quarter)
    got6 = hubs(q6, 64)
    own, top, path, rw1 = call(
        "shadow_6", shadow_6, "s" + "v" * 8,
        [block(quarter, F32), block(quarter, F32), block(rank), block(size)],
        pos, q6, got5, w, b, row_basis, wl, top, path, flops=mac * n * 3,
    )
    (q7,) = call("climb_6", climb_kernel(6), "svvv", [block(quarter)], pos, got6, own, w, flops=mac * quarter)
    got7 = hubs(q7, 192)
    top, path = call(
        "shadow_7", shadow_7, "s" + "v" * 5, [block(quarter, F32), block(rank)],
        pos, got6, w, b, top, path, flops=mac * n * 2,
    )
    mine, send = call(
        "top", top_kernel, "s" + "v" * 6, [block(quarter), block(quarter)],
        pos, got7, top, path, c2, c2_oth, w, flops=mac * quarter * 3,
    )
    got = hubs(send, 4)
    c1, c1_oth, g0, g1 = call(
        "shadow_8", shadow_8, "s" + "v" * 7,
        [block(half, F32), block(half, F32), block(size), block(size)],
        pos, mine, keep1, got1, b, w0, rw0, rw1, flops=mac * n * 5,
    )
    mine, send = call(
        "down", down_kernel, "s" + "v" * 5, [block(half), block(half)],
        pos, mine, got, c1, c1_oth, w, flops=mac * half * 2,
    )
    got = hubs(send, 2)

    def inward(value):
        return lax.ppermute(value, axes, [(i, i ^ 1) for i in range(devices) if i & 1])

    def output(name, kernel, h, *args, aliases=None):
        return call(
            name, kernel, "ss" + "v" * 5 + "h" * (len(args)), [(rhs.shape, BF)],
            pos, order, h, inward(h), base, g0, g1, *args,
            scratch=(
                pltpu.VMEM((2, 2, size, half), BF),
                pltpu.SemaphoreType.DMA((2, 2)),
            ),
            flops=mac * n * 2, aliases=aliases, out_spec=HBM,
        )[0]

    done = output("own_columns", own_kernel, mine)
    return output("other_columns", last_kernel, got, done, aliases={7: 0})


def solution(mesh):
    return jax.shard_map(
        shards,
        mesh=mesh,
        in_specs=(
            P(None, ("leaf", "top"), None),
            P(None, ("leaf", "top"), None, None),
            P(None, ("leaf", "top"), None, None),
            P(None, ("leaf", "top"), None, None),
            P(None, ("leaf", "top"), None, None, None),
            P(None, ("leaf", "top"), None, None),
            P(None, ("leaf", "top"), None, None, None, None),
            P(None, ("leaf", "top"), None, None, None),
            P(("leaf", "top"), None),
        ),
        out_specs=P(None, ("leaf", "top"), None),
        check_vma=False,
    )
```

time: 60.3 us -> 70.1 us (1.16)
  starting transfers between devices: 31.8 us -> 40.2 us
  Pallas kernels: 18.5 us -> 20.1 us
  local copies, waits for them, and re-layouts: 1.6 us -> 0.04 us
  waiting for transfers between devices: 8.07 us -> 8.98 us
    ppermute x11 -> x12, starting transfers between devices: 31.8 us -> 40.2 us  [the longest x9 34.3 us: hubs(): lax.ppermute(value, axes, [(i, i ^ flip) for i in range(devices) if i & 1])]
    pallas_call x20 -> x21, Pallas kernels: 18.5 us -> 20.1 us  [call(): pl.pallas_call(kernel, out_shape=[jax.ShapeDtypeStruct(shape, dtype) for...]
    unnamed x16, local copies, waits for them, and re-layouts: 1.6 us -> 0.04 us
    ppermute x11 -> x12, waiting for transfers between devices: 8.07 us -> 8.98 us  [the longest x9 8.12 us: hubs(): lax.ppermute(value, axes, [(i, i ^ flip) for i in range(devices) if i & 1])]
  transfers between devices with their start and end apart: 11 -> 12, of which waited for: 9 -> 9; matrix products, arithmetic and copies ran while one was open for 0% -> 0% of each run, Pallas kernels for 17% -> 18%
where the time goes in v3:
time: 70.1 us; the launch traced here: 69.7 us
  starting transfers between devices  40.2 us (57%)
  Pallas kernels  20.1 us (29%)
  waiting for transfers between devices  8.98 us (13%)
    ppermute x9, starting transfers between devices, hubs(): lax.ppermute(value, axes, [(i, i ^ flip) for i in range(devices) if i & 1])  34.3 us
    pallas_call x21, Pallas kernels, call(): pl.pallas_call(kernel, out_shape=[jax.ShapeDtypeStruct(shape, dtype) for...  20.1 us
    ppermute x9, waiting for transfers between devices, hubs(): lax.ppermute(value, axes, [(i, i ^ flip) for i in range(devices) if i & 1])  8.12 us
    ppermute x1, starting transfers between devices, shards(): got0 = lax.ppermute(q0, axes, [(i, i ^ 1) for i in range(devices)])  3.33 us
    ppermute x2, starting transfers between devices, inward(): lax.ppermute(value, axes, [(i, i ^ 1) for i in range(devices) if i & 1])  2.58 us
  transfers between devices with their start and end apart: 12, of which 9 were waited for; matrix products, arithmetic and copies ran while one was open for 0% of the time, Pallas kernels for 18%

profile of v3, /device:TPU:1, one launch (start us, length us, event | category | flops | bytes accessed | tf_op | source)
XLA Modules:
  0.0 69.7 jit_solution(5112015930484576537)
XLA Ops:
  0.0 0.0 copy-start
  0.0 0.0 copy-start.5
  0.0 3.4 %leaf_skeletons.1 = (bf16[2,512,256]{2,1,0:T(8,128)(2,1)S(1)}, bf16[2,256,256]{2,1,0:T(8,128)(2,1)S(1)}, bf16[2,1,2,256,256]{4,3,2,1,0:T(8,128)(2,1)S(1)}) custom-call(s32[1]{0:T(128)} %bitcast.pos, s32[1,2]{1,0:T(1,128)} %order.11, bf16[2,1024,256]{2,1,0:T(8,128)(2,1)} %x.5, bf16[2,2,512,256]{3,2,1,0:T(8,128)(2,1)} %u.1, bf16[2,1,2,256,256]{4,3,2,1,0:T(8,128)(2,1)} %wl.7, ...), custom_call_target="tpu_custom_call" | custom-call | flops 805306368 | bytes 6815756 | tf_op jit(solution)/shard_map/leaf_skeletons/pallas_call | solution.py:270
  3.4 0.0 copy-start.2
  3.5 0.0 copy-start.7
  3.5 3.3 %collective-permute-start = (bf16[2,256,256]{2,1,0:T(8,128)(2,1)S(1)}, bf16[2,256,256]{2,1,0:T(8,128)(2,1)S(1)}, u32[]{:S(2)}, u32[]{:S(2)}) collective-permute-start(bf16[2,256,256]{2,1,0:T(8,128)(2,1)S(1)} %get-tuple-element.41.q0), channel_id=1, source_target_pairs={{0,1},{1,0},{2,3},{3,2},{4,5},{5,4},{6,7},{7,6},{8,9},{9,8},{10,11... | collective-permute-start | bytes 786440 | tf_op jit(solution)/shard_map/ppermute | solution.py:314
  6.8 0.3 shadow_0.1.own
  7.1 0.9 %collective-permute-done.got.got0 = bf16[2,256,256]{2,1,0:T(8,128)(2,1)S(1)} collective-permute-done((bf16[2,256,256]{2,1,0:T(8,128)(2,1)S(1)}, bf16[2,256,256]{2,1,0:T(8,128)(2,1)S(1)}, u32[]{:S(2)}, u32[]{:S(2)}) %collective-permute-start) | collective-permute-done | bytes 262176 | tf_op jit(solution)/shard_map/ppermute | solution.py:314
  8.0 0.3 climb_0.1
  8.3 1.9 %collective-permute-start.1 = (bf16[2,128,256]{2,1,0:T(8,128)(2,1)S(1)}, bf16[2,128,256]{2,1,0:T(8,128)(2,1)S(1)}, u32[]{:S(2)}, u32[]{:S(2)}) collective-permute-start(bf16[2,128,256]{2,1,0:T(8,128)(2,1)S(1)} %get-tuple-element.43), channel_id=1, source_target_pairs={{1,3},{3,1},{5,7},{7,5},{9,11},{11,9},{13,15},{15,13},{17,19},{19,... | collective-permute-start | bytes 393224 | tf_op jit(solution)/shard_map/ppermute | solution.py:294
  10.2 0.0 copy-done
  10.2 0.0 copy-done.5
  10.2 0.0 copy-done.2
  10.2 0.0 copy-done.7
  10.2 1.3 %shadow_1.1 = (f32[2,128,256]{2,1,0:T(8,128)S(1)}, f32[2,512,256]{2,1,0:T(8,128)S(1)}) custom-call(s32[1]{0:T(128)} %bitcast.pos, s32[1,2]{1,0:T(1,128)S(1)} %copy-done.7, bf16[2,128,256]{2,1,0:T(8,128)(2,1)S(1)} %get-tuple-element.44.keep.keep1, bf16[2,8,2,256,256]{4,3,2,1,0:T(8,128)(2,1)S(1)} %bitcast.4, bf16[2,1024,256]{2,1,0:T(8,128)(2,1)S(1)} %copy-done.2, ...), custom_call_target="tpu_custom_call" | custom-call | flops 671088640 | bytes 7471116 | tf_op jit(solution)/shard_map/shadow_1/pallas_call | solution.py:270
  11.6 2.4 %collective-permute-done.1.got.got1 = bf16[2,128,256]{2,1,0:T(8,128)(2,1)S(1)} collective-permute-done((bf16[2,128,256]{2,1,0:T(8,128)(2,1)S(1)}, bf16[2,128,256]{2,1,0:T(8,128)(2,1)S(1)}, u32[]{:S(2)}, u32[]{:S(2)}) %collective-permute-start.1) | collective-permute-done | bytes 131104 | tf_op jit(solution)/shard_map/ppermute | solution.py:294
  14.0 0.2 climb_1.1
  14.2 3.3 %collective-permute-start.2 = (bf16[2,64,256]{2,1,0:T(8,128)(2,1)S(1)}, bf16[2,64,256]{2,1,0:T(8,128)(2,1)S(1)}, u32[]{:S(2)}, u32[]{:S(2)}) collective-permute-start(bf16[2,64,256]{2,1,0:T(8,128)(2,1)S(1)} %get-tuple-element.46), channel_id=1, source_target_pairs={{1,5},{3,7},{5,1},{7,3},{9,13},{11,15},{13,9},{15,11},{17,21},{19,... | collective-permute-start | bytes 196616 | tf_op jit(solution)/shard_map/ppermute | solution.py:294
  17.6 1.3 %shadow_2.1 = (f32[2,64,256]{2,1,0:T(8,128)S(1)}, f32[2,512,256]{2,1,0:T(8,128)S(1)}) custom-call(s32[1]{0:T(128)} %bitcast.pos, s32[1,2]{1,0:T(1,128)S(1)} %copy-done.7, bf16[2,64,256]{2,1,0:T(8,128)(2,1)S(1)} %get-tuple-element.47.keep.keep2, bf16[2,8,2,256,256]{4,3,2,1,0:T(8,128)(2,1)S(1)} %bitcast.6, bf16[2,1024,256]{2,1,0:T(8,128)(2,1)S(1)} %copy-done.2, ...), custom_call_target="tpu_custom_call" | custom-call | flops 671088640 | bytes 7405580 | tf_op jit(solution)/shard_map/shadow_2/pallas_call | solution.py:270
  18.9 2.0 %collective-permute-done.2.got.got2 = bf16[2,64,256]{2,1,0:T(8,128)(2,1)S(1)} collective-permute-done((bf16[2,64,256]{2,1,0:T(8,128)(2,1)S(1)}, bf16[2,64,256]{2,1,0:T(8,128)(2,1)S(1)}, u32[]{:S(2)}, u32[]{:S(2)}) %collective-permute-start.2) | collective-permute-done | bytes 65568 | tf_op jit(solution)/shard_map/ppermute | solution.py:294
  20.8 0.0 copy-start.1
  20.8 0.0 copy-start.4
  20.8 0.0 copy-start.6
  20.8 0.2 climb_2.1.q3
  21.0 5.7 %collective-permute-start.3 = (bf16[2,64,256]{2,1,0:T(8,128)(2,1)S(1)}, bf16[2,64,256]{2,1,0:T(8,128)(2,1)S(1)}, u32[]{:S(2)}, u32[]{:S(2)}) collective-permute-start(bf16[2,64,256]{2,1,0:T(8,128)(2,1)S(1)} %climb_2.1.q3), channel_id=1, source_target_pairs={{1,13},{3,15},{5,9},{7,11},{9,5},{11,7},{13,1},{15,3},{17,29},{19,... | collective-permute-start | bytes 196616 | tf_op jit(solution)/shard_map/ppermute | solution.py:294
  26.8 0.0 copy-done.1
  26.8 0.0 copy-done.4
  26.8 0.0 copy-done.6
  26.8 1.7 %shadow_3.1 = (f32[2,64,256]{2,1,0:T(8,128)S(1)}, bf16[2,512,256]{2,1,0:T(8,128)(2,1)S(1)}, f32[2,64,256]{2,1,0:T(8,128)S(1)}, f32[2,64,256]{2,1,0:T(8,128)S(1)}) custom-call(s32[1]{0:T(128)} %bitcast.pos, bf16[2,64,256]{2,1,0:T(8,128)(2,1)S(1)} %climb_2.1.q3, bf16[2,8,2,256,256]{4,3,2,1,0:T(8,128)(2,1)S(1)} %bitcast.8, ...), custom_call_target="tpu_custom_call" | custom-call | flops 805306368 | bytes 8585220 | tf_op jit(solution)/shard_map/shadow_3/pallas_call | solution.py:270
  28.5 0.0 collective-permute-done.3.got.got3
  28.6 0.0 copy-start.3
  28.6 0.2 climb_3.1.q4
  28.8 3.2 %collective-permute-start.4 = (bf16[2,64,256]{2,1,0:T(8,128)(2,1)S(1)}, bf16[2,64,256]{2,1,0:T(8,128)(2,1)S(1)}, u32[]{:S(2)}, u32[]{:S(2)}) collective-permute-start(bf16[2,64,256]{2,1,0:T(8,128)(2,1)S(1)} %climb_3.1.q4), channel_id=1, source_target_pairs={{1,17},{3,19},{5,21},{7,23},{9,25},{11,27},{13,29},{15,31},{17,1},... | collective-permute-start | bytes 196616 | tf_op jit(solution)/shard_map/ppermute | solution.py:294
  32.0 0.0 copy-done.3
  32.0 1.7 %shadow_4.1 = (f32[2,64,256]{2,1,0:T(8,128)S(1)}, f32[2,64,256]{2,1,0:T(8,128)S(1)}, f32[2,2,1024,128]{3,2,1,0:T(8,128)S(1)}) custom-call(s32[1]{0:T(128)} %bitcast.pos, s32[1,2]{1,0:T(1,128)S(1)} %copy-done.7, bf16[2,64,256]{2,1,0:T(8,128)(2,1)S(1)} %climb_3.1.q4, bf16[2,64,256]{2,1,0:T(8,128)(2,1)S(1)} %collective-permute-done.3.got.got3, ...), custom_call_target="tpu_custom_call" | custom-call | flops 536870912 | bytes 10092556 | tf_op jit(solution)/shard_map/shadow_4/pallas_call | solution.py:270
  33.8 0.2 collective-permute-done.4.got.got4
  33.9 0.2 climb_4.1.q5
  34.1 4.4 %collective-permute-start.5 = (bf16[2,64,256]{2,1,0:T(8,128)(2,1)S(1)}, bf16[2,64,256]{2,1,0:T(8,128)(2,1)S(1)}, u32[]{:S(2)}, u32[]{:S(2)}) collective-permute-start(bf16[2,64,256]{2,1,0:T(8,128)(2,1)S(1)} %climb_4.1.q5), channel_id=1, source_target_pairs={{1,49},{3,51},{5,53},{7,55},{9,57},{11,59},{13,61},{15,63},{17,33}... | collective-permute-start | bytes 196616 | tf_op jit(solution)/shard_map/ppermute | solution.py:294
  38.5 1.1 %shadow_5.1 = (f32[2,64,256]{2,1,0:T(8,128)S(1)}, f32[2,64,256]{2,1,0:T(8,128)S(1)}, bf16[2,256,256]{2,1,0:T(8,128)(2,1)S(1)}, bf16[2,512,256]{2,1,0:T(8,128)(2,1)S(1)}) custom-call(s32[1]{0:T(128)} %bitcast.pos, bf16[2,64,256]{2,1,0:T(8,128)(2,1)S(1)} %climb_4.1.q5, bf16[2,64,256]{2,1,0:T(8,128)(2,1)S(1)} %collective-permute-done.4.got.got4, ...), custom_call_target="tpu_custom_call" | custom-call | flops 402653184 | bytes 8126468 | tf_op jit(solution)/shard_map/shadow_5/pallas_call | solution.py:270
  39.6 0.8 %collective-permute-done.5.got.got5 = bf16[2,64,256]{2,1,0:T(8,128)(2,1)S(1)} collective-permute-done((bf16[2,64,256]{2,1,0:T(8,128)(2,1)S(1)}, bf16[2,64,256]{2,1,0:T(8,128)(2,1)S(1)}, u32[]{:S(2)}, u32[]{:S(2)}) %collective-permute-start.5) | collective-permute-done | bytes 65568 | tf_op jit(solution)/shard_map/ppermute | solution.py:294
  40.3 0.2 climb_5.1.q6
  40.5 3.2 %collective-permute-start.6 = (bf16[2,64,256]{2,1,0:T(8,128)(2,1)S(1)}, bf16[2,64,256]{2,1,0:T(8,128)(2,1)S(1)}, u32[]{:S(2)}, u32[]{:S(2)}) collective-permute-start(bf16[2,64,256]{2,1,0:T(8,128)(2,1)S(1)} %climb_5.1.q6), channel_id=1, source_target_pairs={{1,65},{3,67},{5,69},{7,71},{9,73},{11,75},{13,77},{15,79},{17,81}... | collective-permute-start | bytes 196616 | tf_op jit(solution)/shard_map/ppermute | solution.py:294
  43.7 1.1 %shadow_6.1 = (f32[2,64,256]{2,1,0:T(8,128)S(1)}, f32[2,64,256]{2,1,0:T(8,128)S(1)}, bf16[2,256,256]{2,1,0:T(8,128)(2,1)S(1)}, bf16[2,512,256]{2,1,0:T(8,128)(2,1)S(1)}) custom-call(s32[1]{0:T(128)} %bitcast.pos, bf16[2,64,256]{2,1,0:T(8,128)(2,1)S(1)} %climb_5.1.q6, bf16[2,64,256]{2,1,0:T(8,128)(2,1)S(1)} %collective-permute-done.5.got.got5, ...), custom_call_target="tpu_custom_call" | custom-call | flops 402653184 | bytes 8388612 | tf_op jit(solution)/shard_map/shadow_6/pallas_call | solution.py:270
  44.8 0.7 %collective-permute-done.6.got.got6 = bf16[2,64,256]{2,1,0:T(8,128)(2,1)S(1)} collective-permute-done((bf16[2,64,256]{2,1,0:T(8,128)(2,1)S(1)}, bf16[2,64,256]{2,1,0:T(8,128)(2,1)S(1)}, u32[]{:S(2)}, u32[]{:S(2)}) %collective-permute-start.6) | collective-permute-done | bytes 65568 | tf_op jit(solution)/shard_map/ppermute | solution.py:294
  45.5 0.2 climb_6.1
  45.7 4.6 %collective-permute-start.7 = (bf16[2,64,256]{2,1,0:T(8,128)(2,1)S(1)}, bf16[2,64,256]{2,1,0:T(8,128)(2,1)S(1)}, u32[]{:S(2)}, u32[]{:S(2)}) collective-permute-start(bf16[2,64,256]{2,1,0:T(8,128)(2,1)S(1)} %climb_6.1), channel_id=1, source_target_pairs={{1,193},{3,195},{5,197},{7,199},{9,201},{11,203},{13,205},{15,207}... | collective-permute-start | bytes 196616 | tf_op jit(solution)/shard_map/ppermute | solution.py:294
  50.4 1.0 %shadow_7.1 = (f32[2,64,256]{2,1,0:T(8,128)S(1)}, bf16[2,256,256]{2,1,0:T(8,128)(2,1)S(1)}) custom-call(s32[1]{0:T(128)} %bitcast.pos, bf16[2,64,256]{2,1,0:T(8,128)(2,1)S(1)} %collective-permute-done.6.got.got6, bf16[2,8,2,256,256]{4,3,2,1,0:T(8,128)(2,1)S(1)} %bitcast.16, bf16[2,8,256,256]{3,2,1,0:T(8,128)(2,1)S(1)} %bitcast.23, ...), custom_call_target="tpu_custom_call" | custom-call | flops 268435456 | bytes 6750212 | tf_op jit(solution)/shard_map/shadow_7/pallas_call | solution.py:270
  51.4 0.6 collective-permute-done.7.got
  52.0 0.4 top.1
  52.5 4.2 %collective-permute-start.8 = (bf16[2,64,256]{2,1,0:T(8,128)(2,1)S(1)}, bf16[2,64,256]{2,1,0:T(8,128)(2,1)S(1)}, u32[]{:S(2)}, u32[]{:S(2)}) collective-permute-start(bf16[2,64,256]{2,1,0:T(8,128)(2,1)S(1)} %get-tuple-element.67), channel_id=1, source_target_pairs={{1,5},{3,7},{5,1},{7,3},{9,13},{11,15},{13,9},{15,11},{17,21},{19,... | collective-permute-start | bytes 196616 | tf_op jit(solution)/shard_map/ppermute | solution.py:294
  56.7 1.3 %shadow_8.1 = (f32[2,128,256]{2,1,0:T(8,128)S(1)}, f32[2,128,256]{2,1,0:T(8,128)S(1)}, bf16[2,512,256]{2,1,0:T(8,128)(2,1)S(1)}, bf16[2,512,256]{2,1,0:T(8,128)(2,1)S(1)}) custom-call(s32[1]{0:T(128)} %bitcast.pos, bf16[2,64,256]{2,1,0:T(8,128)(2,1)S(1)} %get-tuple-element.66.mine, bf16[2,128,256]{2,1,0:T(8,128)(2,1)S(1)} %get-tuple-element.44.keep.keep1, ...), custom_call_target="tpu_custom_call" | custom-call | flops 671088640 | bytes 3997700 | tf_op jit(solution)/shard_map/shadow_8/pallas_call | solution.py:270
  58.0 0.4 collective-permute-done.8.got
  58.4 0.3 down.1
  58.7 3.6 %collective-permute-start.9 = (bf16[2,128,256]{2,1,0:T(8,128)(2,1)S(1)}, bf16[2,128,256]{2,1,0:T(8,128)(2,1)S(1)}, u32[]{:S(2)}, u32[]{:S(2)}) collective-permute-start(bf16[2,128,256]{2,1,0:T(8,128)(2,1)S(1)} %get-tuple-element.72), channel_id=1, source_target_pairs={{1,3},{3,1},{5,7},{7,5},{9,11},{11,9},{13,15},{15,13},{17,19},{19,... | collective-permute-start | bytes 393224 | tf_op jit(solution)/shard_map/ppermute | solution.py:294
  62.4 1.3 %collective-permute-start.11 = (bf16[2,128,256]{2,1,0:T(8,128)(2,1)S(1)}, bf16[2,128,256]{2,1,0:T(8,128)(2,1)S(1)}, u32[]{:S(2)}, u32[]{:S(2)}) collective-permute-start(bf16[2,128,256]{2,1,0:T(8,128)(2,1)S(1)} %get-tuple-element.76.h_hub), channel_id=1, source_target_pairs={{1,0},{3,2},{5,4},{7,6},{9,8},{11,10},{13,12},{15,14},{17,16},{19,... | collective-permute-start | bytes 393224 | tf_op jit(solution)/shard_map/ppermute | solution.py:385
  63.7 1.0 %collective-permute-done.9.h_hub = bf16[2,128,256]{2,1,0:T(8,128)(2,1)S(1)} collective-permute-done((bf16[2,128,256]{2,1,0:T(8,128)(2,1)S(1)}, bf16[2,128,256]{2,1,0:T(8,128)(2,1)S(1)}, u32[]{:S(2)}, u32[]{:S(2)}) %collective-permute-start.9) | collective-permute-done | bytes 131104 | tf_op jit(solution)/shard_map/ppermute | solution.py:294
  64.7 1.3 %collective-permute-start.10 = (bf16[2,128,256]{2,1,0:T(8,128)(2,1)S(1)}, bf16[2,128,256]{2,1,0:T(8,128)(2,1)S(1)}, u32[]{:S(2)}, u32[]{:S(2)}) collective-permute-start(bf16[2,128,256]{2,1,0:T(8,128)(2,1)S(1)} %collective-permute-done.9.h_hub), channel_id=1, source_target_pairs={{1,0},{3,2},{5,4},{7,6},{9,8},{11,10},{13,12},{15,14},{17,16},{19,... | collective-permute-start | bytes 393224 | tf_op jit(solution)/shard_map/ppermute | solution.py:385
  66.0 0.0 collective-permute-done.11.h_other
  66.0 1.8 %own_columns.1.done = bf16[2,1024,256]{2,1,0:T(8,128)(2,1)} custom-call(s32[1]{0:T(128)} %bitcast.pos, s32[1,2]{1,0:T(1,128)S(1)} %copy-done.7, bf16[2,128,256]{2,1,0:T(8,128)(2,1)S(1)} %get-tuple-element.76.h_hub, bf16[2,128,256]{2,1,0:T(8,128)(2,1)S(1)} %collective-permute-done.11.h_other, f32[2,2,1024,128]{3,2,1,0:T(8,128)S(1)} %get-tuple-element.73.base, ...), custom_call_target="tpu_custom_call" | custom-call | flops 268435456 | bytes 3407884 | tf_op jit(solution)/shard_map/own_columns/pallas_call | solution.py:270
  67.9 0.0 collective-permute-done.10.h_other
  67.9 1.8 %other_columns.1 = bf16[2,1024,256]{2,1,0:T(8,128)(2,1)} custom-call(s32[1]{0:T(128)} %bitcast.pos, s32[1,2]{1,0:T(1,128)S(1)} %copy-done.7, bf16[2,128,256]{2,1,0:T(8,128)(2,1)S(1)} %collective-permute-done.9.h_hub, bf16[2,128,256]{2,1,0:T(8,128)(2,1)S(1)} %collective-permute-done.10.h_other, ...), custom_call_target="tpu_custom_call", output_to_operand_aliasing={{}: (7, {})} | custom-call | flops 268435456 | bytes 4456460 | tf_op jit(solution)/shard_map/other_columns/pallas_call | solution.py:270
Async XLA Ops:
  0.0 10.2 %copy-start = (bf16[2,1,8,2,256,256]{5,4,3,2,1,0:T(8,128)(2,1)S(1)}, bf16[2,1,8,2,256,256]{5,4,3,2,1,0:T(8,128)(2,1)}, u32[]{:S(2)}) copy-start(bf16[2,1,8,2,256,256]{5,4,3,2,1,0:T(8,128)(2,1)} %param.15) | copy-start | bytes 12582916
  0.0 10.2 %copy-start.5 = (bf16[2,2,512,512]{3,2,1,0:T(8,128)(2,1)S(1)}, bf16[2,2,512,512]{3,2,1,0:T(8,128)(2,1)}, u32[]{:S(2)}) copy-start(bf16[2,2,512,512]{3,2,1,0:T(8,128)(2,1)} %d.3) | copy-start | bytes 6291460
  3.4 6.8 %copy-start.2 = (bf16[2,1024,256]{2,1,0:T(8,128)(2,1)S(1)}, bf16[2,1024,256]{2,1,0:T(8,128)(2,1)}, u32[]{:S(2)}) copy-start(bf16[2,1024,256]{2,1,0:T(8,128)(2,1)} %x.5) | copy-start | bytes 3145732
  3.5 6.8 %copy-start.7 = (s32[1,2]{1,0:T(1,128)S(1)}, s32[1,2]{1,0:T(1,128)}, u32[]{:S(2)}) copy-start(s32[1,2]{1,0:T(1,128)} %order.11) | copy-start | bytes 28
  3.5 4.5 %collective-permute-start = (bf16[2,256,256]{2,1,0:T(8,128)(2,1)S(1)}, bf16[2,256,256]{2,1,0:T(8,128)(2,1)S(1)}, u32[]{:S(2)}, u32[]{:S(2)}) collective-permute-start(bf16[2,256,256]{2,1,0:T(8,128)(2,1)S(1)} %get-tuple-element.41.q0), channel_id=1, source_target_pairs={{0,1},{1,0},{2,3},{3,2},{4,5},{5,4},{6,7},{7,6},{8,9},{9,8},{10,11... | collective-permute-start | bytes 786440 | tf_op jit(solution)/shard_map/ppermute | solution.py:314
  8.3 5.7 %collective-permute-start.1 = (bf16[2,128,256]{2,1,0:T(8,128)(2,1)S(1)}, bf16[2,128,256]{2,1,0:T(8,128)(2,1)S(1)}, u32[]{:S(2)}, u32[]{:S(2)}) collective-permute-start(bf16[2,128,256]{2,1,0:T(8,128)(2,1)S(1)} %get-tuple-element.43), channel_id=1, source_target_pairs={{1,3},{3,1},{5,7},{7,5},{9,11},{11,9},{13,15},{15,13},{17,19},{19,... | collective-permute-start | bytes 393224 | tf_op jit(solution)/shard_map/ppermute | solution.py:294
  14.2 6.6 %collective-permute-start.2 = (bf16[2,64,256]{2,1,0:T(8,128)(2,1)S(1)}, bf16[2,64,256]{2,1,0:T(8,128)(2,1)S(1)}, u32[]{:S(2)}, u32[]{:S(2)}) collective-permute-start(bf16[2,64,256]{2,1,0:T(8,128)(2,1)S(1)} %get-tuple-element.46), channel_id=1, source_target_pairs={{1,5},{3,7},{5,1},{7,3},{9,13},{11,15},{13,9},{15,11},{17,21},{19,... | collective-permute-start | bytes 196616 | tf_op jit(solution)/shard_map/ppermute | solution.py:294
  20.8 5.9 %copy-start.1 = (bf16[2,1,8,256,256]{4,3,2,1,0:T(8,128)(2,1)S(1)}, bf16[2,1,8,256,256]{4,3,2,1,0:T(8,128)(2,1)}, u32[]{:S(2)}) copy-start(bf16[2,1,8,256,256]{4,3,2,1,0:T(8,128)(2,1)} %param.16) | copy-start | bytes 6291460
  20.8 5.9 %copy-start.4 = (bf16[2,1,2,256,256]{4,3,2,1,0:T(8,128)(2,1)S(1)}, bf16[2,1,2,256,256]{4,3,2,1,0:T(8,128)(2,1)}, u32[]{:S(2)}) copy-start(bf16[2,1,2,256,256]{4,3,2,1,0:T(8,128)(2,1)} %wl.7) | copy-start | bytes 1572868
  20.8 5.9 %copy-start.6 = (bf16[2,1,256,256]{3,2,1,0:T(8,128)(2,1)S(1)}, bf16[2,1,256,256]{3,2,1,0:T(8,128)(2,1)}, u32[]{:S(2)}) copy-start(bf16[2,1,256,256]{3,2,1,0:T(8,128)(2,1)} %bl.1) | copy-start | bytes 786436
  21.0 7.5 %collective-permute-start.3 = (bf16[2,64,256]{2,1,0:T(8,128)(2,1)S(1)}, bf16[2,64,256]{2,1,0:T(8,128)(2,1)S(1)}, u32[]{:S(2)}, u32[]{:S(2)}) collective-permute-start(bf16[2,64,256]{2,1,0:T(8,128)(2,1)S(1)} %climb_2.1.q3), channel_id=1, source_target_pairs={{1,13},{3,15},{5,9},{7,11},{9,5},{11,7},{13,1},{15,3},{17,29},{19,... | collective-permute-start | bytes 196616 | tf_op jit(solution)/shard_map/ppermute | solution.py:294
  28.6 3.5 %copy-start.3 = (bf16[2,2,512,256]{3,2,1,0:T(8,128)(2,1)S(1)}, bf16[2,2,512,256]{3,2,1,0:T(8,128)(2,1)}, u32[]{:S(2)}) copy-start(bf16[2,2,512,256]{3,2,1,0:T(8,128)(2,1)} %r.5) | copy-start | bytes 3145732
  28.8 5.1 %collective-permute-start.4 = (bf16[2,64,256]{2,1,0:T(8,128)(2,1)S(1)}, bf16[2,64,256]{2,1,0:T(8,128)(2,1)S(1)}, u32[]{:S(2)}, u32[]{:S(2)}) collective-permute-start(bf16[2,64,256]{2,1,0:T(8,128)(2,1)S(1)} %climb_3.1.q4), channel_id=1, source_target_pairs={{1,17},{3,19},{5,21},{7,23},{9,25},{11,27},{13,29},{15,31},{17,1},... | collective-permute-start | bytes 196616 | tf_op jit(solution)/shard_map/ppermute | solution.py:294
  34.1 6.2 %collective-permute-start.5 = (bf16[2,64,256]{2,1,0:T(8,128)(2,1)S(1)}, bf16[2,64,256]{2,1,0:T(8,128)(2,1)S(1)}, u32[]{:S(2)}, u32[]{:S(2)}) collective-permute-start(bf16[2,64,256]{2,1,0:T(8,128)(2,1)S(1)} %climb_4.1.q5), channel_id=1, source_target_pairs={{1,49},{3,51},{5,53},{7,55},{9,57},{11,59},{13,61},{15,63},{17,33}... | collective-permute-start | bytes 196616 | tf_op jit(solution)/shard_map/ppermute | solution.py:294
  40.5 5.0 %collective-permute-start.6 = (bf16[2,64,256]{2,1,0:T(8,128)(2,1)S(1)}, bf16[2,64,256]{2,1,0:T(8,128)(2,1)S(1)}, u32[]{:S(2)}, u32[]{:S(2)}) collective-permute-start(bf16[2,64,256]{2,1,0:T(8,128)(2,1)S(1)} %climb_5.1.q6), channel_id=1, source_target_pairs={{1,65},{3,67},{5,69},{7,71},{9,73},{11,75},{13,77},{15,79},{17,81}... | collective-permute-start | bytes 196616 | tf_op jit(solution)/shard_map/ppermute | solution.py:294
  45.7 6.3 %collective-permute-start.7 = (bf16[2,64,256]{2,1,0:T(8,128)(2,1)S(1)}, bf16[2,64,256]{2,1,0:T(8,128)(2,1)S(1)}, u32[]{:S(2)}, u32[]{:S(2)}) collective-permute-start(bf16[2,64,256]{2,1,0:T(8,128)(2,1)S(1)} %climb_6.1), channel_id=1, source_target_pairs={{1,193},{3,195},{5,197},{7,199},{9,201},{11,203},{13,205},{15,207}... | collective-permute-start | bytes 196616 | tf_op jit(solution)/shard_map/ppermute | solution.py:294
  52.5 5.9 %collective-permute-start.8 = (bf16[2,64,256]{2,1,0:T(8,128)(2,1)S(1)}, bf16[2,64,256]{2,1,0:T(8,128)(2,1)S(1)}, u32[]{:S(2)}, u32[]{:S(2)}) collective-permute-start(bf16[2,64,256]{2,1,0:T(8,128)(2,1)S(1)} %get-tuple-element.67), channel_id=1, source_target_pairs={{1,5},{3,7},{5,1},{7,3},{9,13},{11,15},{13,9},{15,11},{17,21},{19,... | collective-permute-start | bytes 196616 | tf_op jit(solution)/shard_map/ppermute | solution.py:294
  58.7 6.0 %collective-permute-start.9 = (bf16[2,128,256]{2,1,0:T(8,128)(2,1)S(1)}, bf16[2,128,256]{2,1,0:T(8,128)(2,1)S(1)}, u32[]{:S(2)}, u32[]{:S(2)}) collective-permute-start(bf16[2,128,256]{2,1,0:T(8,128)(2,1)S(1)} %get-tuple-element.72), channel_id=1, source_target_pairs={{1,3},{3,1},{5,7},{7,5},{9,11},{11,9},{13,15},{15,13},{17,19},{19,... | collective-permute-start | bytes 393224 | tf_op jit(solution)/shard_map/ppermute | solution.py:294
  62.4 3.6 %collective-permute-start.11 = (bf16[2,128,256]{2,1,0:T(8,128)(2,1)S(1)}, bf16[2,128,256]{2,1,0:T(8,128)(2,1)S(1)}, u32[]{:S(2)}, u32[]{:S(2)}) collective-permute-start(bf16[2,128,256]{2,1,0:T(8,128)(2,1)S(1)} %get-tuple-element.76.h_hub), channel_id=1, source_target_pairs={{1,0},{3,2},{5,4},{7,6},{9,8},{11,10},{13,12},{15,14},{17,16},{19,... | collective-permute-start | bytes 393224 | tf_op jit(solution)/shard_map/ppermute | solution.py:385
  64.7 3.2 %collective-permute-start.10 = (bf16[2,128,256]{2,1,0:T(8,128)(2,1)S(1)}, bf16[2,128,256]{2,1,0:T(8,128)(2,1)S(1)}, u32[]{:S(2)}, u32[]{:S(2)}) collective-permute-start(bf16[2,128,256]{2,1,0:T(8,128)(2,1)S(1)} %collective-permute-done.9.h_hub), channel_id=1, source_target_pairs={{1,0},{3,2},{5,4},{7,6},{9,8},{11,10},{13,12},{15,14},{17,16},{19,... | collective-permute-start | bytes 393224 | tf_op jit(solution)/shard_map/ppermute | solution.py:385

commit v4 on v3

--- a/solution.py
+++ b/solution.py
@@ -291,7 +291,10 @@
     b = cross_b[:, 0]
 
     def hubs(value, flip):
-        return lax.ppermute(value, axes, [(i, i ^ flip) for i in range(devices) if i & 1])
+        return lax.ppermute(value, axes, [(i, i ^ flip if i & 1 else i) for i in range(devices)])
+
+    def swap(value):
+        return lax.ppermute(value, axes, [(i, i ^ 1) for i in range(devices)])
 
     def block(columns, dtype=BF):
         return ((2, columns, rank), dtype)
@@ -311,7 +314,7 @@
         ),
         flops=mac * n * 6,
     )
-    got0 = lax.ppermute(q0, axes, [(i, i ^ 1) for i in range(devices)])
+    got0 = swap(q0)
     (own,) = call("shadow_0", shadow_0, "svv", [block(n, F32)], pos, q0, w0, flops=mac * n)
     keep1, send = call(
         "climb_0", climb_kernel(0), "svvv", [block(half), block(half)],
@@ -381,13 +384,10 @@
     )
     got = hubs(send, 2)
 
-    def inward(value):
-        return lax.ppermute(value, axes, [(i, i ^ 1) for i in range(devices) if i & 1])
-
     def output(name, kernel, h, *args, aliases=None):
         return call(
             name, kernel, "ss" + "v" * 5 + "h" * (len(args)), [(rhs.shape, BF)],
-            pos, order, h, inward(h), base, g0, g1, *args,
+            pos, order, h, swap(h), base, g0, g1, *args,
             scratch=(
                 pltpu.VMEM((2, 2, size, half), BF),
                 pltpu.SemaphoreType.DMA((2, 2)),
@@ -396,6 +396,7 @@
         )[0]
 
     done = output("own_columns", own_kernel, mine)
+    got, done = lax.optimization_barrier((got, done))
     return output("other_columns", last_kernel, got, done, aliases={7: 0})
 
 

time: 70.1 us -> 68.3 us (0.974)
  starting transfers between devices: 40.2 us -> 37.7 us
  waiting for transfers between devices: 8.98 us -> 9.77 us
    ppermute x12, starting transfers between devices: 40.2 us -> 37.7 us  [the longest x9 34.3 us: hubs(): lax.ppermute(value, axes, [(i, i ^ flip if i & 1 else i) for i in range(d...]
    ppermute x12, waiting for transfers between devices: 8.98 us -> 9.77 us  [the longest x9 7.57 us: hubs(): lax.ppermute(value, axes, [(i, i ^ flip if i & 1 else i) for i in range(d...]
  transfers between devices with their start and end apart: 12 -> 12, of which waited for: 9 -> 10; matrix products, arithmetic and copies ran while one was open for 0% -> 0% of each run, Pallas kernels for 18% -> 18%
where the time goes in v4:
time: 68.3 us; the launch traced here: 68 us
  starting transfers between devices  37.7 us (55%)
  Pallas kernels  20.1 us (29%)
  waiting for transfers between devices  9.77 us (14%)
    ppermute x9, starting transfers between devices, hubs(): lax.ppermute(value, axes, [(i, i ^ flip if i & 1 else i) for i in range(d...  34.3 us
    pallas_call x21, Pallas kernels, call(): pl.pallas_call(kernel, out_shape=[jax.ShapeDtypeStruct(shape, dtype) for...  20.1 us
    ppermute x9, waiting for transfers between devices, hubs(): lax.ppermute(value, axes, [(i, i ^ flip if i & 1 else i) for i in range(d...  7.57 us
    ppermute x3, starting transfers between devices, swap(): return lax.ppermute(value, axes, [(i, i ^ 1) for i in range(devices)])  3.42 us
    ppermute x3, waiting for transfers between devices, swap(): return lax.ppermute(value, axes, [(i, i ^ 1) for i in range(devices)])  2.2 us
  transfers between devices with their start and end apart: 12, of which 10 were waited for; matrix products, arithmetic and copies ran while one was open for 0% of the time, Pallas kernels for 18%

profile of v4, /device:TPU:1, one launch (start us, length us, event | category | flops | bytes accessed | tf_op | source)
XLA Modules:
  0.0 68.0 jit_solution(1987626976876743800)
XLA Ops:
  0.0 0.0 copy-start
  0.0 0.0 copy-start.5
  0.0 3.4 %leaf_skeletons.1 = (bf16[2,512,256]{2,1,0:T(8,128)(2,1)S(1)}, bf16[2,256,256]{2,1,0:T(8,128)(2,1)S(1)}, bf16[2,1,2,256,256]{4,3,2,1,0:T(8,128)(2,1)S(1)}) custom-call(s32[1]{0:T(128)} %bitcast.pos, s32[1,2]{1,0:T(1,128)} %order.11, bf16[2,1024,256]{2,1,0:T(8,128)(2,1)} %x.5, bf16[2,2,512,256]{3,2,1,0:T(8,128)(2,1)} %u.1, bf16[2,1,2,256,256]{4,3,2,1,0:T(8,128)(2,1)} %wl.7, ...), custom_call_target="tpu_custom_call" | custom-call | flops 805306368 | bytes 6815756 | tf_op jit(solution)/shard_map/leaf_skeletons/pallas_call | solution.py:270
  3.4 0.0 copy-start.2
  3.5 0.0 copy-start.7
  3.5 3.3 %collective-permute-start = (bf16[2,256,256]{2,1,0:T(8,128)(2,1)S(1)}, bf16[2,256,256]{2,1,0:T(8,128)(2,1)S(1)}, u32[]{:S(2)}, u32[]{:S(2)}) collective-permute-start(bf16[2,256,256]{2,1,0:T(8,128)(2,1)S(1)} %get-tuple-element.43.q0), channel_id=1, source_target_pairs={{0,1},{1,0},{2,3},{3,2},{4,5},{5,4},{6,7},{7,6},{8,9},{9,8},{10,11... | collective-permute-start | bytes 786440 | tf_op jit(solution)/shard_map/ppermute | solution.py:297
  6.8 0.3 shadow_0.1.own
  7.1 0.9 %collective-permute-done.got.got0 = bf16[2,256,256]{2,1,0:T(8,128)(2,1)S(1)} collective-permute-done((bf16[2,256,256]{2,1,0:T(8,128)(2,1)S(1)}, bf16[2,256,256]{2,1,0:T(8,128)(2,1)S(1)}, u32[]{:S(2)}, u32[]{:S(2)}) %collective-permute-start) | collective-permute-done | bytes 262176 | tf_op jit(solution)/shard_map/ppermute | solution.py:297
  8.0 0.3 climb_0.1
  8.3 1.9 %collective-permute-start.1 = (bf16[2,128,256]{2,1,0:T(8,128)(2,1)S(1)}, bf16[2,128,256]{2,1,0:T(8,128)(2,1)S(1)}, u32[]{:S(2)}, u32[]{:S(2)}) collective-permute-start(bf16[2,128,256]{2,1,0:T(8,128)(2,1)S(1)} %get-tuple-element.45), channel_id=1, source_target_pairs={{0,0},{1,3},{2,2},{3,1},{4,4},{5,7},{6,6},{7,5},{8,8},{9,11},{10,1... | collective-permute-start | bytes 393224 | tf_op jit(solution)/shard_map/ppermute | solution.py:294
  10.2 0.0 copy-done
  10.2 0.0 copy-done.5
  10.2 0.0 copy-done.2
  10.2 0.0 copy-done.7
  10.2 1.3 %shadow_1.1 = (f32[2,128,256]{2,1,0:T(8,128)S(1)}, f32[2,512,256]{2,1,0:T(8,128)S(1)}) custom-call(s32[1]{0:T(128)} %bitcast.pos, s32[1,2]{1,0:T(1,128)S(1)} %copy-done.7, bf16[2,128,256]{2,1,0:T(8,128)(2,1)S(1)} %get-tuple-element.46.keep.keep1, bf16[2,8,2,256,256]{4,3,2,1,0:T(8,128)(2,1)S(1)} %bitcast.4, bf16[2,1024,256]{2,1,0:T(8,128)(2,1)S(1)} %copy-done.2, ...), custom_call_target="tpu_custom_call" | custom-call | flops 671088640 | bytes 7471116 | tf_op jit(solution)/shard_map/shadow_1/pallas_call | solution.py:270
  11.6 2.4 %collective-permute-done.1.got.got1 = bf16[2,128,256]{2,1,0:T(8,128)(2,1)S(1)} collective-permute-done((bf16[2,128,256]{2,1,0:T(8,128)(2,1)S(1)}, bf16[2,128,256]{2,1,0:T(8,128)(2,1)S(1)}, u32[]{:S(2)}, u32[]{:S(2)}) %collective-permute-start.1) | collective-permute-done | bytes 131104 | tf_op jit(solution)/shard_map/ppermute | solution.py:294
  14.0 0.2 climb_1.1
  14.2 3.3 %collective-permute-start.2 = (bf16[2,64,256]{2,1,0:T(8,128)(2,1)S(1)}, bf16[2,64,256]{2,1,0:T(8,128)(2,1)S(1)}, u32[]{:S(2)}, u32[]{:S(2)}) collective-permute-start(bf16[2,64,256]{2,1,0:T(8,128)(2,1)S(1)} %get-tuple-element.48), channel_id=1, source_target_pairs={{0,0},{1,5},{2,2},{3,7},{4,4},{5,1},{6,6},{7,3},{8,8},{9,13},{10,1... | collective-permute-start | bytes 196616 | tf_op jit(solution)/shard_map/ppermute | solution.py:294
  17.6 1.3 %shadow_2.1 = (f32[2,64,256]{2,1,0:T(8,128)S(1)}, f32[2,512,256]{2,1,0:T(8,128)S(1)}) custom-call(s32[1]{0:T(128)} %bitcast.pos, s32[1,2]{1,0:T(1,128)S(1)} %copy-done.7, bf16[2,64,256]{2,1,0:T(8,128)(2,1)S(1)} %get-tuple-element.49.keep.keep2, bf16[2,8,2,256,256]{4,3,2,1,0:T(8,128)(2,1)S(1)} %bitcast.6, bf16[2,1024,256]{2,1,0:T(8,128)(2,1)S(1)} %copy-done.2, ...), custom_call_target="tpu_custom_call" | custom-call | flops 671088640 | bytes 7405580 | tf_op jit(solution)/shard_map/shadow_2/pallas_call | solution.py:270
  18.9 2.0 %collective-permute-done.2.got.got2 = bf16[2,64,256]{2,1,0:T(8,128)(2,1)S(1)} collective-permute-done((bf16[2,64,256]{2,1,0:T(8,128)(2,1)S(1)}, bf16[2,64,256]{2,1,0:T(8,128)(2,1)S(1)}, u32[]{:S(2)}, u32[]{:S(2)}) %collective-permute-start.2) | collective-permute-done | bytes 65568 | tf_op jit(solution)/shard_map/ppermute | solution.py:294
  20.8 0.0 copy-start.1
  20.8 0.0 copy-start.4
  20.8 0.0 copy-start.6
  20.8 0.2 climb_2.1.q3
  21.0 5.7 %collective-permute-start.3 = (bf16[2,64,256]{2,1,0:T(8,128)(2,1)S(1)}, bf16[2,64,256]{2,1,0:T(8,128)(2,1)S(1)}, u32[]{:S(2)}, u32[]{:S(2)}) collective-permute-start(bf16[2,64,256]{2,1,0:T(8,128)(2,1)S(1)} %climb_2.1.q3), channel_id=1, source_target_pairs={{0,0},{1,13},{2,2},{3,15},{4,4},{5,9},{6,6},{7,11},{8,8},{9,5},{10... | collective-permute-start | bytes 196616 | tf_op jit(solution)/shard_map/ppermute | solution.py:294
  26.8 0.0 copy-done.1
  26.8 0.0 copy-done.4
  26.8 0.0 copy-done.6
  26.8 1.7 %shadow_3.1 = (f32[2,64,256]{2,1,0:T(8,128)S(1)}, bf16[2,512,256]{2,1,0:T(8,128)(2,1)S(1)}, f32[2,64,256]{2,1,0:T(8,128)S(1)}, f32[2,64,256]{2,1,0:T(8,128)S(1)}) custom-call(s32[1]{0:T(128)} %bitcast.pos, bf16[2,64,256]{2,1,0:T(8,128)(2,1)S(1)} %climb_2.1.q3, bf16[2,8,2,256,256]{4,3,2,1,0:T(8,128)(2,1)S(1)} %bitcast.8, ...), custom_call_target="tpu_custom_call" | custom-call | flops 805306368 | bytes 8585220 | tf_op jit(solution)/shard_map/shadow_3/pallas_call | solution.py:270
  28.5 0.0 collective-permute-done.3.got.got3
  28.6 0.0 copy-start.3
  28.6 0.2 climb_3.1.q4
  28.8 3.2 %collective-permute-start.4 = (bf16[2,64,256]{2,1,0:T(8,128)(2,1)S(1)}, bf16[2,64,256]{2,1,0:T(8,128)(2,1)S(1)}, u32[]{:S(2)}, u32[]{:S(2)}) collective-permute-start(bf16[2,64,256]{2,1,0:T(8,128)(2,1)S(1)} %climb_3.1.q4), channel_id=1, source_target_pairs={{0,0},{1,17},{2,2},{3,19},{4,4},{5,21},{6,6},{7,23},{8,8},{9,25},{... | collective-permute-start | bytes 196616 | tf_op jit(solution)/shard_map/ppermute | solution.py:294
  32.0 0.0 copy-done.3
  32.0 1.7 %shadow_4.1 = (f32[2,64,256]{2,1,0:T(8,128)S(1)}, f32[2,64,256]{2,1,0:T(8,128)S(1)}, f32[2,2,1024,128]{3,2,1,0:T(8,128)S(1)}) custom-call(s32[1]{0:T(128)} %bitcast.pos, s32[1,2]{1,0:T(1,128)S(1)} %copy-done.7, bf16[2,64,256]{2,1,0:T(8,128)(2,1)S(1)} %climb_3.1.q4, bf16[2,64,256]{2,1,0:T(8,128)(2,1)S(1)} %collective-permute-done.3.got.got3, ...), custom_call_target="tpu_custom_call" | custom-call | flops 536870912 | bytes 10092556 | tf_op jit(solution)/shard_map/shadow_4/pallas_call | solution.py:270
  33.8 0.2 collective-permute-done.4.got.got4
  33.9 0.2 climb_4.1.q5
  34.1 4.4 %collective-permute-start.5 = (bf16[2,64,256]{2,1,0:T(8,128)(2,1)S(1)}, bf16[2,64,256]{2,1,0:T(8,128)(2,1)S(1)}, u32[]{:S(2)}, u32[]{:S(2)}) collective-permute-start(bf16[2,64,256]{2,1,0:T(8,128)(2,1)S(1)} %climb_4.1.q5), channel_id=1, source_target_pairs={{0,0},{1,49},{2,2},{3,51},{4,4},{5,53},{6,6},{7,55},{8,8},{9,57},{... | collective-permute-start | bytes 196616 | tf_op jit(solution)/shard_map/ppermute | solution.py:294
  38.5 1.1 %shadow_5.1 = (f32[2,64,256]{2,1,0:T(8,128)S(1)}, f32[2,64,256]{2,1,0:T(8,128)S(1)}, bf16[2,256,256]{2,1,0:T(8,128)(2,1)S(1)}, bf16[2,512,256]{2,1,0:T(8,128)(2,1)S(1)}) custom-call(s32[1]{0:T(128)} %bitcast.pos, bf16[2,64,256]{2,1,0:T(8,128)(2,1)S(1)} %climb_4.1.q5, bf16[2,64,256]{2,1,0:T(8,128)(2,1)S(1)} %collective-permute-done.4.got.got4, ...), custom_call_target="tpu_custom_call" | custom-call | flops 402653184 | bytes 8126468 | tf_op jit(solution)/shard_map/shadow_5/pallas_call | solution.py:270
  39.6 0.8 %collective-permute-done.5.got.got5 = bf16[2,64,256]{2,1,0:T(8,128)(2,1)S(1)} collective-permute-done((bf16[2,64,256]{2,1,0:T(8,128)(2,1)S(1)}, bf16[2,64,256]{2,1,0:T(8,128)(2,1)S(1)}, u32[]{:S(2)}, u32[]{:S(2)}) %collective-permute-start.5) | collective-permute-done | bytes 65568 | tf_op jit(solution)/shard_map/ppermute | solution.py:294
  40.3 0.2 climb_5.1.q6
  40.5 3.2 %collective-permute-start.6 = (bf16[2,64,256]{2,1,0:T(8,128)(2,1)S(1)}, bf16[2,64,256]{2,1,0:T(8,128)(2,1)S(1)}, u32[]{:S(2)}, u32[]{:S(2)}) collective-permute-start(bf16[2,64,256]{2,1,0:T(8,128)(2,1)S(1)} %climb_5.1.q6), channel_id=1, source_target_pairs={{0,0},{1,65},{2,2},{3,67},{4,4},{5,69},{6,6},{7,71},{8,8},{9,73},{... | collective-permute-start | bytes 196616 | tf_op jit(solution)/shard_map/ppermute | solution.py:294
  43.7 1.1 %shadow_6.1 = (f32[2,64,256]{2,1,0:T(8,128)S(1)}, f32[2,64,256]{2,1,0:T(8,128)S(1)}, bf16[2,256,256]{2,1,0:T(8,128)(2,1)S(1)}, bf16[2,512,256]{2,1,0:T(8,128)(2,1)S(1)}) custom-call(s32[1]{0:T(128)} %bitcast.pos, bf16[2,64,256]{2,1,0:T(8,128)(2,1)S(1)} %climb_5.1.q6, bf16[2,64,256]{2,1,0:T(8,128)(2,1)S(1)} %collective-permute-done.5.got.got5, ...), custom_call_target="tpu_custom_call" | custom-call | flops 402653184 | bytes 8388612 | tf_op jit(solution)/shard_map/shadow_6/pallas_call | solution.py:270
  44.8 0.7 %collective-permute-done.6.got.got6 = bf16[2,64,256]{2,1,0:T(8,128)(2,1)S(1)} collective-permute-done((bf16[2,64,256]{2,1,0:T(8,128)(2,1)S(1)}, bf16[2,64,256]{2,1,0:T(8,128)(2,1)S(1)}, u32[]{:S(2)}, u32[]{:S(2)}) %collective-permute-start.6) | collective-permute-done | bytes 65568 | tf_op jit(solution)/shard_map/ppermute | solution.py:294
  45.5 0.2 climb_6.1
  45.7 4.6 %collective-permute-start.7 = (bf16[2,64,256]{2,1,0:T(8,128)(2,1)S(1)}, bf16[2,64,256]{2,1,0:T(8,128)(2,1)S(1)}, u32[]{:S(2)}, u32[]{:S(2)}) collective-permute-start(bf16[2,64,256]{2,1,0:T(8,128)(2,1)S(1)} %climb_6.1), channel_id=1, source_target_pairs={{0,0},{1,193},{2,2},{3,195},{4,4},{5,197},{6,6},{7,199},{8,8},{9,2... | collective-permute-start | bytes 196616 | tf_op jit(solution)/shard_map/ppermute | solution.py:294
  50.4 1.0 %shadow_7.1 = (f32[2,64,256]{2,1,0:T(8,128)S(1)}, bf16[2,256,256]{2,1,0:T(8,128)(2,1)S(1)}) custom-call(s32[1]{0:T(128)} %bitcast.pos, bf16[2,64,256]{2,1,0:T(8,128)(2,1)S(1)} %collective-permute-done.6.got.got6, bf16[2,8,2,256,256]{4,3,2,1,0:T(8,128)(2,1)S(1)} %bitcast.16, bf16[2,8,256,256]{3,2,1,0:T(8,128)(2,1)S(1)} %bitcast.23, ...), custom_call_target="tpu_custom_call" | custom-call | flops 268435456 | bytes 6750212 | tf_op jit(solution)/shard_map/shadow_7/pallas_call | solution.py:270
  51.4 0.6 collective-permute-done.7.got
  52.0 0.4 top.1
  52.5 4.2 %collective-permute-start.8 = (bf16[2,64,256]{2,1,0:T(8,128)(2,1)S(1)}, bf16[2,64,256]{2,1,0:T(8,128)(2,1)S(1)}, u32[]{:S(2)}, u32[]{:S(2)}) collective-permute-start(bf16[2,64,256]{2,1,0:T(8,128)(2,1)S(1)} %get-tuple-element.69), channel_id=1, source_target_pairs={{0,0},{1,5},{2,2},{3,7},{4,4},{5,1},{6,6},{7,3},{8,8},{9,13},{10,1... | collective-permute-start | bytes 196616 | tf_op jit(solution)/shard_map/ppermute | solution.py:294
  56.7 1.3 %shadow_8.1 = (f32[2,128,256]{2,1,0:T(8,128)S(1)}, f32[2,128,256]{2,1,0:T(8,128)S(1)}, bf16[2,512,256]{2,1,0:T(8,128)(2,1)S(1)}, bf16[2,512,256]{2,1,0:T(8,128)(2,1)S(1)}) custom-call(s32[1]{0:T(128)} %bitcast.pos, bf16[2,64,256]{2,1,0:T(8,128)(2,1)S(1)} %get-tuple-element.68.mine, bf16[2,128,256]{2,1,0:T(8,128)(2,1)S(1)} %get-tuple-element.46.keep.keep1, ...), custom_call_target="tpu_custom_call" | custom-call | flops 671088640 | bytes 3997700 | tf_op jit(solution)/shard_map/shadow_8/pallas_call | solution.py:270
  58.0 0.4 collective-permute-done.8.got
  58.4 0.3 down.1
  58.7 0.1 collective-permute-start.10
  58.8 3.6 %collective-permute-start.9 = (bf16[2,128,256]{2,1,0:T(8,128)(2,1)S(1)}, bf16[2,128,256]{2,1,0:T(8,128)(2,1)S(1)}, u32[]{:S(2)}, u32[]{:S(2)}) collective-permute-start(bf16[2,128,256]{2,1,0:T(8,128)(2,1)S(1)} %get-tuple-element.74), channel_id=1, source_target_pairs={{0,0},{1,3},{2,2},{3,1},{4,4},{5,7},{6,6},{7,5},{8,8},{9,11},{10,1... | collective-permute-start | bytes 393224 | tf_op jit(solution)/shard_map/ppermute | solution.py:294
  62.5 0.0 collective-permute-done.10.h_other
  62.5 1.8 %own_columns.1.done = bf16[2,1024,256]{2,1,0:T(8,128)(2,1)} custom-call(s32[1]{0:T(128)} %bitcast.pos, s32[1,2]{1,0:T(1,128)S(1)} %copy-done.7, bf16[2,128,256]{2,1,0:T(8,128)(2,1)S(1)} %get-tuple-element.75.h_hub, bf16[2,128,256]{2,1,0:T(8,128)(2,1)S(1)} %collective-permute-done.10.h_other, f32[2,2,1024,128]{3,2,1,0:T(8,128)S(1)} %get-tuple-element.76.base, ...), custom_call_target="tpu_custom_call" | custom-call | flops 268435456 | bytes 3407884 | tf_op jit(solution)/shard_map/own_columns/pallas_call | solution.py:270
  64.3 0.5 collective-permute-done.9.h_hub
  64.8 0.0 collective-permute-start.11
  64.8 1.3 %collective-permute-done.11.h_other = bf16[2,128,256]{2,1,0:T(8,128)(2,1)S(1)} collective-permute-done((bf16[2,128,256]{2,1,0:T(8,128)(2,1)S(1)}, bf16[2,128,256]{2,1,0:T(8,128)(2,1)S(1)}, u32[]{:S(2)}, u32[]{:S(2)}) %collective-permute-start.11) | collective-permute-done | bytes 131104 | tf_op jit(solution)/shard_map/ppermute | solution.py:297
  66.2 1.8 %other_columns.1 = bf16[2,1024,256]{2,1,0:T(8,128)(2,1)} custom-call(s32[1]{0:T(128)} %bitcast.pos, s32[1,2]{1,0:T(1,128)S(1)} %copy-done.7, bf16[2,128,256]{2,1,0:T(8,128)(2,1)S(1)} %collective-permute-done.9.h_hub, bf16[2,128,256]{2,1,0:T(8,128)(2,1)S(1)} %collective-permute-done.11.h_other, ...), custom_call_target="tpu_custom_call", output_to_operand_aliasing={{}: (7, {})} | custom-call | flops 268435456 | bytes 4456460 | tf_op jit(solution)/shard_map/other_columns/pallas_call | solution.py:270
Async XLA Ops:
  0.0 10.2 %copy-start = (bf16[2,1,8,2,256,256]{5,4,3,2,1,0:T(8,128)(2,1)S(1)}, bf16[2,1,8,2,256,256]{5,4,3,2,1,0:T(8,128)(2,1)}, u32[]{:S(2)}) copy-start(bf16[2,1,8,2,256,256]{5,4,3,2,1,0:T(8,128)(2,1)} %param.15) | copy-start | bytes 12582916
  0.0 10.2 %copy-start.5 = (bf16[2,2,512,512]{3,2,1,0:T(8,128)(2,1)S(1)}, bf16[2,2,512,512]{3,2,1,0:T(8,128)(2,1)}, u32[]{:S(2)}) copy-start(bf16[2,2,512,512]{3,2,1,0:T(8,128)(2,1)} %d.3) | copy-start | bytes 6291460
  3.4 6.8 %copy-start.2 = (bf16[2,1024,256]{2,1,0:T(8,128)(2,1)S(1)}, bf16[2,1024,256]{2,1,0:T(8,128)(2,1)}, u32[]{:S(2)}) copy-start(bf16[2,1024,256]{2,1,0:T(8,128)(2,1)} %x.5) | copy-start | bytes 3145732
  3.5 6.8 %copy-start.7 = (s32[1,2]{1,0:T(1,128)S(1)}, s32[1,2]{1,0:T(1,128)}, u32[]{:S(2)}) copy-start(s32[1,2]{1,0:T(1,128)} %order.11) | copy-start | bytes 28
  3.5 4.5 %collective-permute-start = (bf16[2,256,256]{2,1,0:T(8,128)(2,1)S(1)}, bf16[2,256,256]{2,1,0:T(8,128)(2,1)S(1)}, u32[]{:S(2)}, u32[]{:S(2)}) collective-permute-start(bf16[2,256,256]{2,1,0:T(8,128)(2,1)S(1)} %get-tuple-element.43.q0), channel_id=1, source_target_pairs={{0,1},{1,0},{2,3},{3,2},{4,5},{5,4},{6,7},{7,6},{8,9},{9,8},{10,11... | collective-permute-start | bytes 786440 | tf_op jit(solution)/shard_map/ppermute | solution.py:297
  8.3 5.7 %collective-permute-start.1 = (bf16[2,128,256]{2,1,0:T(8,128)(2,1)S(1)}, bf16[2,128,256]{2,1,0:T(8,128)(2,1)S(1)}, u32[]{:S(2)}, u32[]{:S(2)}) collective-permute-start(bf16[2,128,256]{2,1,0:T(8,128)(2,1)S(1)} %get-tuple-element.45), channel_id=1, source_target_pairs={{0,0},{1,3},{2,2},{3,1},{4,4},{5,7},{6,6},{7,5},{8,8},{9,11},{10,1... | collective-permute-start | bytes 393224 | tf_op jit(solution)/shard_map/ppermute | solution.py:294
  14.2 6.6 %collective-permute-start.2 = (bf16[2,64,256]{2,1,0:T(8,128)(2,1)S(1)}, bf16[2,64,256]{2,1,0:T(8,128)(2,1)S(1)}, u32[]{:S(2)}, u32[]{:S(2)}) collective-permute-start(bf16[2,64,256]{2,1,0:T(8,128)(2,1)S(1)} %get-tuple-element.48), channel_id=1, source_target_pairs={{0,0},{1,5},{2,2},{3,7},{4,4},{5,1},{6,6},{7,3},{8,8},{9,13},{10,1... | collective-permute-start | bytes 196616 | tf_op jit(solution)/shard_map/ppermute | solution.py:294
  20.8 5.9 %copy-start.1 = (bf16[2,1,8,256,256]{4,3,2,1,0:T(8,128)(2,1)S(1)}, bf16[2,1,8,256,256]{4,3,2,1,0:T(8,128)(2,1)}, u32[]{:S(2)}) copy-start(bf16[2,1,8,256,256]{4,3,2,1,0:T(8,128)(2,1)} %param.16) | copy-start | bytes 6291460
  20.8 5.9 %copy-start.4 = (bf16[2,1,2,256,256]{4,3,2,1,0:T(8,128)(2,1)S(1)}, bf16[2,1,2,256,256]{4,3,2,1,0:T(8,128)(2,1)}, u32[]{:S(2)}) copy-start(bf16[2,1,2,256,256]{4,3,2,1,0:T(8,128)(2,1)} %wl.7) | copy-start | bytes 1572868
  20.8 5.9 %copy-start.6 = (bf16[2,1,256,256]{3,2,1,0:T(8,128)(2,1)S(1)}, bf16[2,1,256,256]{3,2,1,0:T(8,128)(2,1)}, u32[]{:S(2)}) copy-start(bf16[2,1,256,256]{3,2,1,0:T(8,128)(2,1)} %bl.1) | copy-start | bytes 786436
  21.0 7.5 %collective-permute-start.3 = (bf16[2,64,256]{2,1,0:T(8,128)(2,1)S(1)}, bf16[2,64,256]{2,1,0:T(8,128)(2,1)S(1)}, u32[]{:S(2)}, u32[]{:S(2)}) collective-permute-start(bf16[2,64,256]{2,1,0:T(8,128)(2,1)S(1)} %climb_2.1.q3), channel_id=1, source_target_pairs={{0,0},{1,13},{2,2},{3,15},{4,4},{5,9},{6,6},{7,11},{8,8},{9,5},{10... | collective-permute-start | bytes 196616 | tf_op jit(solution)/shard_map/ppermute | solution.py:294
  28.6 3.5 %copy-start.3 = (bf16[2,2,512,256]{3,2,1,0:T(8,128)(2,1)S(1)}, bf16[2,2,512,256]{3,2,1,0:T(8,128)(2,1)}, u32[]{:S(2)}) copy-start(bf16[2,2,512,256]{3,2,1,0:T(8,128)(2,1)} %r.5) | copy-start | bytes 3145732
  28.8 5.1 %collective-permute-start.4 = (bf16[2,64,256]{2,1,0:T(8,128)(2,1)S(1)}, bf16[2,64,256]{2,1,0:T(8,128)(2,1)S(1)}, u32[]{:S(2)}, u32[]{:S(2)}) collective-permute-start(bf16[2,64,256]{2,1,0:T(8,128)(2,1)S(1)} %climb_3.1.q4), channel_id=1, source_target_pairs={{0,0},{1,17},{2,2},{3,19},{4,4},{5,21},{6,6},{7,23},{8,8},{9,25},{... | collective-permute-start | bytes 196616 | tf_op jit(solution)/shard_map/ppermute | solution.py:294
  34.1 6.2 %collective-permute-start.5 = (bf16[2,64,256]{2,1,0:T(8,128)(2,1)S(1)}, bf16[2,64,256]{2,1,0:T(8,128)(2,1)S(1)}, u32[]{:S(2)}, u32[]{:S(2)}) collective-permute-start(bf16[2,64,256]{2,1,0:T(8,128)(2,1)S(1)} %climb_4.1.q5), channel_id=1, source_target_pairs={{0,0},{1,49},{2,2},{3,51},{4,4},{5,53},{6,6},{7,55},{8,8},{9,57},{... | collective-permute-start | bytes 196616 | tf_op jit(solution)/shard_map/ppermute | solution.py:294
  40.5 5.0 %collective-permute-start.6 = (bf16[2,64,256]{2,1,0:T(8,128)(2,1)S(1)}, bf16[2,64,256]{2,1,0:T(8,128)(2,1)S(1)}, u32[]{:S(2)}, u32[]{:S(2)}) collective-permute-start(bf16[2,64,256]{2,1,0:T(8,128)(2,1)S(1)} %climb_5.1.q6), channel_id=1, source_target_pairs={{0,0},{1,65},{2,2},{3,67},{4,4},{5,69},{6,6},{7,71},{8,8},{9,73},{... | collective-permute-start | bytes 196616 | tf_op jit(solution)/shard_map/ppermute | solution.py:294
  45.7 6.3 %collective-permute-start.7 = (bf16[2,64,256]{2,1,0:T(8,128)(2,1)S(1)}, bf16[2,64,256]{2,1,0:T(8,128)(2,1)S(1)}, u32[]{:S(2)}, u32[]{:S(2)}) collective-permute-start(bf16[2,64,256]{2,1,0:T(8,128)(2,1)S(1)} %climb_6.1), channel_id=1, source_target_pairs={{0,0},{1,193},{2,2},{3,195},{4,4},{5,197},{6,6},{7,199},{8,8},{9,2... | collective-permute-start | bytes 196616 | tf_op jit(solution)/shard_map/ppermute | solution.py:294
  52.5 5.9 %collective-permute-start.8 = (bf16[2,64,256]{2,1,0:T(8,128)(2,1)S(1)}, bf16[2,64,256]{2,1,0:T(8,128)(2,1)S(1)}, u32[]{:S(2)}, u32[]{:S(2)}) collective-permute-start(bf16[2,64,256]{2,1,0:T(8,128)(2,1)S(1)} %get-tuple-element.69), channel_id=1, source_target_pairs={{0,0},{1,5},{2,2},{3,7},{4,4},{5,1},{6,6},{7,3},{8,8},{9,13},{10,1... | collective-permute-start | bytes 196616 | tf_op jit(solution)/shard_map/ppermute | solution.py:294
  58.7 3.7 %collective-permute-start.10 = (bf16[2,128,256]{2,1,0:T(8,128)(2,1)S(1)}, bf16[2,128,256]{2,1,0:T(8,128)(2,1)S(1)}, u32[]{:S(2)}, u32[]{:S(2)}) collective-permute-start(bf16[2,128,256]{2,1,0:T(8,128)(2,1)S(1)} %get-tuple-element.75.h_hub), channel_id=1, source_target_pairs={{0,1},{1,0},{2,3},{3,2},{4,5},{5,4},{6,7},{7,6},{8,9},{9,8},{10,11... | collective-permute-start | bytes 393224 | tf_op jit(solution)/shard_map/ppermute | solution.py:297
  58.8 6.0 %collective-permute-start.9 = (bf16[2,128,256]{2,1,0:T(8,128)(2,1)S(1)}, bf16[2,128,256]{2,1,0:T(8,128)(2,1)S(1)}, u32[]{:S(2)}, u32[]{:S(2)}) collective-permute-start(bf16[2,128,256]{2,1,0:T(8,128)(2,1)S(1)} %get-tuple-element.74), channel_id=1, source_target_pairs={{0,0},{1,3},{2,2},{3,1},{4,4},{5,7},{6,6},{7,5},{8,8},{9,11},{10,1... | collective-permute-start | bytes 393224 | tf_op jit(solution)/shard_map/ppermute | solution.py:294
  64.8 1.3 %collective-permute-start.11 = (bf16[2,128,256]{2,1,0:T(8,128)(2,1)S(1)}, bf16[2,128,256]{2,1,0:T(8,128)(2,1)S(1)}, u32[]{:S(2)}, u32[]{:S(2)}) collective-permute-start(bf16[2,128,256]{2,1,0:T(8,128)(2,1)S(1)} %collective-permute-done.9.h_hub), channel_id=1, source_target_pairs={{0,1},{1,0},{2,3},{3,2},{4,5},{5,4},{6,7},{7,6},{8,9},{9,8},{10,11... | collective-permute-start | bytes 393224 | tf_op jit(solution)/shard_map/ppermute | solution.py:297

commit v5 on v3

v5 whole, which is shorter than its diff:
```python
import jax
import jax.numpy as jnp
from jax import lax
from jax.experimental import pallas as pl
from jax.experimental.pallas import tpu as pltpu
from jax.sharding import PartitionSpec as P

BF = jnp.bfloat16
F32 = jnp.float32
NN = (((1,), (0,)), ((), ()))
NT = (((1,), (1,)), ((), ()))


def dot(a, b, dims=NN):
    return lax.dot_general(a, b, dims, preferred_element_type=F32)


def widen(a):
    half = a.shape[0] // 2
    re, im = a[:half], a[half:]
    return jnp.concatenate(
        [jnp.concatenate([re, -im], axis=1), jnp.concatenate([im, re], axis=1)], axis=0
    )


def times(a, w_re, w_im):
    return dot(widen(a), jnp.concatenate([w_re, w_im], axis=0))


def times_t(a, w_re, w_im):
    return dot(widen(a), jnp.concatenate([w_re, w_im], axis=1), NT)


def rows(ref):
    return jnp.concatenate([ref[0], ref[1]], axis=0)


def put(ref, value):
    half = value.shape[0] // 2
    ref[0] = value[:half].astype(ref.dtype)
    ref[1] = value[half:].astype(ref.dtype)


def bit(pos, level):
    return (pos[0] >> level) & 1


def lift(q, w, pos, level, flip=0):
    child = bit(pos, level) ^ flip
    return times(q, w[0, level, child], w[1, level, child])


def lower(h, w, pos, level, flip=0):
    child = bit(pos, level) ^ flip
    return times_t(h, w[0, level, child], w[1, level, child])


def couple(q, b, pos, level, flip=0):
    return lax.cond(
        (bit(pos, level) ^ flip) == 0,
        lambda: times_t(q, b[0, level], b[1, level]),
        lambda: times(q, b[0, level], b[1, level]),
    )


def split(value, side, keep, send):
    half = value.shape[0] // 2
    part = half // 2
    for c in range(2):
        low = value[c * half : c * half + part]
        high = value[c * half + part : (c + 1) * half]
        keep[c] = jnp.where(side == 0, low, high)
        send[c] = jnp.where(side == 0, high, low)


def join(own, got, side):
    parts = []
    for c in range(2):
        parts.append(jnp.where(side == 0, own[c], got[c]))
        parts.append(jnp.where(side == 0, got[c], own[c]))
    return jnp.concatenate(parts, axis=0)


def side(pos, level):
    if level == 0:
        return (pos[0] ^ (pos[0] >> 1) ^ (pos[0] >> 2) ^ (pos[0] >> 4) ^ (pos[0] >> 6)) & 1
    if level == 1:
        return bit(pos, 1)
    return bit(pos, 2) ^ bit(pos, 3)


def half_lanes(half, n):
    return pl.ds(pl.multiple_of(half * n, n), n)


def skeletons(first, half, x, u, wl, qleaf, ready):
    size = u.shape[2]
    lanes = half_lanes(half, x.shape[2] // 2)
    for block in range(2):
        ready(block)
        at = pl.ds(block * size, size)
        xt = jnp.concatenate([x[0, at, lanes].T, x[1, at, lanes].T], axis=0)
        leaf = first ^ block
        qleaf[leaf] = times(xt, u[0, leaf], u[1, leaf]).astype(BF)
    ready(2)
    q = times(qleaf[0], wl[0, 0, 0], wl[1, 0, 0]) + times(qleaf[1], wl[0, 0, 1], wl[1, 0, 1])
    return q.astype(BF)


def send_kernel(pos, order, x, u, wl, w, qleaf, send, x_v, u_v, wl_v, w0, order_s, sems):
    size = u.shape[2]
    copies = [
        pltpu.make_async_copy(order, order_s, sems.at[0]),
        pltpu.make_async_copy(x.at[:, pl.ds(0, size)], x_v.at[:, pl.ds(0, size)], sems.at[1]),
        pltpu.make_async_copy(u, u_v, sems.at[2]),
        pltpu.make_async_copy(x.at[:, pl.ds(size, size)], x_v.at[:, pl.ds(size, size)], sems.at[3]),
        pltpu.make_async_copy(wl, wl_v, sems.at[4]),
        pltpu.make_async_copy(w.at[:, 0], w0.at[:, 0], sems.at[5]),
    ]
    for copy in copies:
        copy.start()

    copies[0].wait()
    first = order_s[0, 0]

    def ready(step):
        for i in ((1, 2), (3,), (4,))[step]:
            copies[i].wait()

    put(send, skeletons(first, 1 - side(pos, 0), x_v, u_v, wl_v, qleaf, ready))
    copies[5].wait()


def keep_kernel(pos, order, x, u, wl, w0, qleaf, keep, own):
    q = skeletons(order[0, 0], side(pos, 0), x, u, wl, qleaf, lambda step: None)
    put(keep, q)
    put(own, lift(q, w0, pos, 0))


def climb_kernel(level):
    def kernel(pos, got, own, w, *outs):
        q = (rows(own) + lift(rows(got), w, pos, level, 1)).astype(BF)
        if len(outs) == 2:
            split(q, side(pos, level + 1), *outs)
        else:
            put(outs[0], q)

    return kernel


def direct(order, block, x, d, out):
    size = d.shape[2]
    leaf = order[0, 0] ^ block
    at = pl.ds(block * size, size)
    xs = jnp.concatenate([x[0, at], x[1, at]], axis=0)
    re, im = d[0, leaf], d[1, leaf]
    out[0] = dot(jnp.concatenate([re, -im], axis=1), xs)
    out[1] = dot(jnp.concatenate([im, re], axis=1), xs)


def shadow_1(pos, order, keep, w, x, d, own, part):
    put(own, lift(rows(keep), w, pos, 1))
    direct(order, 0, x, d, part)


def shadow_2(pos, order, keep, w, x, d, own, part):
    put(own, lift(rows(keep), w, pos, 2))
    direct(order, 1, x, d, part)


def shadow_3(
    pos, q3, w, b, bl, wl, q_mine, q_other, got0, got0_other, keep2, got2, own, cleaf, c2, c2_oth
):
    put(own, lift(rows(q3), w, pos, 3))
    for part, (q, got) in enumerate(((q_mine, got0), (q_other, got0_other))):
        c0 = couple(rows(got), b, pos, 0).astype(BF)
        left = times_t(q[1], bl[0, 0], bl[1, 0])
        right = times(q[0], bl[0, 0], bl[1, 0])
        cleaf[0, part] = (left + times_t(c0, wl[0, 0, 0], wl[1, 0, 0])).astype(BF)
        cleaf[1, part] = (right + times_t(c0, wl[0, 0, 1], wl[1, 0, 1])).astype(BF)
    put(c2, couple(rows(got2), b, pos, 2))
    put(c2_oth, couple(rows(keep2), b, pos, 2, 1))


def shadow_4(pos, order, q4, got3, w, b, r, cleaf, part_0, part_1, own, top, base):
    put(own, lift(rows(q4), w, pos, 4))
    put(top, couple(rows(got3), b, pos, 3))
    n = part_0.shape[2] // 2
    size = r.shape[2]
    first = order[0, 0]
    for block, direct_part in enumerate((part_0, part_1)):
        leaf = first ^ block
        basis = jnp.concatenate([r[0, leaf], r[1, leaf]], axis=1)
        for part in range(2):
            add = dot(basis, widen(cleaf[leaf, part]), NT)
            lanes = half_lanes(side(pos, 0) ^ part, n)
            for c in range(2):
                base[part, c, pl.ds(block * size, size)] = (
                    direct_part[c, :, lanes] + add[:, c * n : (c + 1) * n]
                )


def product(r, wl, leaf, out):
    put(out, times(jnp.concatenate([r[0, leaf], r[1, leaf]], axis=0), wl[0, 0, leaf], wl[1, 0, leaf]))


def shadow_5(pos, q5, got4, w, b, r, wl, top, own, top_out, path, rw):
    put(own, lift(rows(q5), w, pos, 5))
    c4 = couple(rows(got4), b, pos, 4).astype(BF)
    put(top_out, rows(top) + lower(c4, w, pos, 3))
    w3 = bit(pos, 3)
    put(path, lift(jnp.concatenate([w[0, 3, w3], w[1, 3, w3]], axis=0), w, pos, 4))
    product(r, wl, 0, rw)


def shadow_6(pos, q6, got5, w, b, r, wl, top, path, own, top_out, path_out, rw):
    put(own, lift(rows(q6), w, pos, 6))
    c5 = couple(rows(got5), b, pos, 5).astype(BF)
    put(top_out, rows(top) + times_t(c5, path[0], path[1]))
    put(path_out, lift(rows(path), w, pos, 5))
    product(r, wl, 1, rw)


def shadow_7(pos, got6, w, b, top, path, top_out, path_out):
    c6 = couple(rows(got6), b, pos, 6).astype(BF)
    put(top_out, rows(top) + times_t(c6, path[0], path[1]))
    longer = lift(rows(path), w, pos, 6).astype(BF)
    put(path_out, couple_path(longer, b, pos))


def couple_path(path, b, pos):
    return lax.cond(
        bit(pos, 7) == 0,
        lambda: times(path, b[0, 7], b[1, 7]),
        lambda: times_t(path, b[0, 7], b[1, 7]),
    )


def top_kernel(pos, got, top, path, c_own, c_oth, w, own, send):
    h = (rows(top) + times_t(rows(got), path[0], path[1])).astype(BF)
    put(own, rows(c_own) + lower(h, w, pos, 2))
    put(send, rows(c_oth) + lower(h, w, pos, 2, 1))


def shadow_8(pos, mine, keep1, got1, b, w0, rw0, rw1, c1, c1_oth, g0, g1):
    put(c1, couple(rows(got1), b, pos, 1))
    put(c1_oth, couple(rows(keep1), b, pos, 1, 1))
    put(g0, lift(rows(rw0), w0, pos, 0))
    put(g1, lift(rows(rw1), w0, pos, 0))


def down_kernel(pos, mine, got, c_own, c_oth, w, own, send):
    h = join(mine, got, side(pos, 2))
    put(own, rows(c_own) + lower(h, w, pos, 1))
    put(send, rows(c_oth) + lower(h, w, pos, 1, 1))


def finish(pos, order, mine, got, base, gs, part, out):
    hw = widen(join(mine, got, side(pos, 1)))
    n = base.shape[3]
    for leaf, g in enumerate(gs):
        size = g.shape[1]
        at = pl.ds(pl.multiple_of((order[0, 0] ^ leaf) * size, size), size)
        add = dot(jnp.concatenate([g[0], g[1]], axis=1), hw, NT)
        for c in range(2):
            out[leaf, c] = (base[part, c, at] + add[:, c * n : (c + 1) * n]).astype(BF)
        yield leaf, at


def own_kernel(pos, order, mine, got, base, g0, g1, out):
    for _ in finish(pos, order, mine, got, base, (g0, g1), 0, out):
        pass


def last_kernel(pos, order, mine, got, base, g0, g1, done, out, buf, sems):
    size = g0.shape[1]
    n = base.shape[3]
    copies = []

    def store(src, part, leaf, at):
        lanes = half_lanes(side(pos, 0) ^ part, n)
        copies.append(
            pltpu.make_async_copy(src.at[leaf], out.at[:, at, lanes], sems.at[part, leaf])
        )
        copies[-1].start()

    for leaf in range(2):
        at = pl.ds(pl.multiple_of((order[0, 0] ^ leaf) * size, size), size)
        store(done, 0, leaf, at)
    for leaf, at in finish(pos, order, mine, got, base, (g0, g1), 1, buf):
        store(buf, 1, leaf, at)
    for copy in copies:
        copy.wait()


VMEM = pl.BlockSpec(memory_space=pltpu.VMEM)
SMEM = pl.BlockSpec(memory_space=pltpu.SMEM)
HBM = pl.BlockSpec(memory_space=pltpu.HBM)
GRANT = 20 * 2**20


def call(name, kernel, ins, outs, *args, scratch=(), flops=0, out_spec=VMEM):
    specs = {"s": SMEM, "v": VMEM, "h": HBM}
    moved = sum(a.size * a.dtype.itemsize for a in args)
    return pl.pallas_call(
        kernel,
        out_shape=[jax.ShapeDtypeStruct(shape, dtype) for shape, dtype in outs],
        in_specs=[specs[kind] for kind in ins],
        out_specs=[out_spec] * len(outs),
        scratch_shapes=list(scratch),
        compiler_params=pltpu.CompilerParams(vmem_limit_bytes=GRANT),
        cost_estimate=pl.CostEstimate(flops=flops, bytes_accessed=moved, transcendentals=0),
        name=name,
    )(*args)


def shards(rhs, diag, row_basis, col_basis, wl, bl, cross_w, cross_b, order):
    n = rhs.shape[2]
    rank = col_basis.shape[3]
    size = col_basis.shape[2]
    axes = ("leaf", "top")
    devices = lax.axis_size("leaf") * lax.axis_size("top")
    pos = lax.axis_index(axes).astype(jnp.int32).reshape(1)
    w = cross_w[:, 0]
    b = cross_b[:, 0]

    def swap(value, flip):
        return lax.ppermute(value, axes, [(i, i ^ flip) for i in range(devices)])

    def block(columns, dtype=BF):
        return ((2, columns, rank), dtype)

    mac = 8 * rank * rank
    half, quarter, eighth = n // 2, n // 4, n // 8
    qleaf_shape = ((2, n, rank), BF)
    hbm = [pltpu.with_memory_space_constraint(a, pltpu.HBM) for a in (order, rhs, col_basis, wl, w)]
    q_other, send, x, u, wl, w0 = call(
        "send_half", send_kernel, "shhhhh",
        [qleaf_shape, block(half), (rhs.shape, BF), (col_basis.shape, BF), (wl.shape, BF),
         ((2, 1, 2, rank, rank), BF)],
        pos, *hbm,
        scratch=(pltpu.SMEM(order.shape, jnp.int32), pltpu.SemaphoreType.DMA((6,))),
        flops=mac * n * 3,
    )
    send, w, b, diag, row_basis = lax.optimization_barrier((send, w, b, diag, row_basis))
    got0 = swap(send, 1)
    q_mine, keep0, own = call(
        "keep_half", keep_kernel, "ssvvvv", [qleaf_shape, block(half), block(half, F32)],
        pos, order, x, u, wl, w0, flops=mac * n * 3,
    )
    got0_other = swap(keep0, 1)
    keep1, send = call(
        "climb_0", climb_kernel(0), "svvv", [block(quarter), block(quarter)],
        pos, got0, own, w0, flops=mac * half,
    )
    got1 = swap(send, 3)
    own, part_0 = call(
        "shadow_1", shadow_1, "ssvvvv", [block(quarter, F32), ((2, size, n), F32)],
        pos, order, keep1, w, x, diag, flops=mac * n * 5,
    )
    keep2, send = call(
        "climb_1", climb_kernel(1), "svvv", [block(eighth), block(eighth)],
        pos, got1, own, w, flops=mac * quarter,
    )
    got2 = swap(send, 5)
    own, part_1 = call(
        "shadow_2", shadow_2, "ssvvvv", [block(eighth, F32), ((2, size, n), F32)],
        pos, order, keep2, w, x, diag, flops=mac * n * 5,
    )
    (q3,) = call("climb_2", climb_kernel(2), "svvv", [block(eighth)], pos, got2, own, w, flops=mac * eighth)
    got3 = swap(q3, 13)
    own, cleaf, c2, c2_oth = call(
        "shadow_3", shadow_3, "s" + "v" * 11,
        [block(eighth, F32), ((2, 2, n, rank), BF), block(eighth, F32), block(eighth, F32)],
        pos, q3, w, b, bl, wl, q_mine, q_other, got0, got0_other, keep2, got2, flops=mac * n * 6,
    )
    (q4,) = call("climb_3", climb_kernel(3), "svvv", [block(eighth)], pos, got3, own, w, flops=mac * eighth)
    got4 = swap(q4, 17)
    own, top, base = call(
        "shadow_4", shadow_4, "ss" + "v" * 8,
        [block(eighth, F32), block(eighth, F32), ((2, 2, 2 * size, half), F32)],
        pos, order, q4, got3, w, b, row_basis, cleaf, part_0, part_1, flops=mac * n * 4,
    )
    (q5,) = call("climb_4", climb_kernel(4), "svvv", [block(eighth)], pos, got4, own, w, flops=mac * eighth)
    got5 = swap(q5, 49)
    own, top, path, rw0 = call(
        "shadow_5", shadow_5, "s" + "v" * 7,
        [block(eighth, F32), block(eighth, F32), block(rank), block(size)],
        pos, q5, got4, w, b, row_basis, wl, top, flops=mac * n * 3,
    )
    (q6,) = call("climb_5", climb_kernel(5), "svvv", [block(eighth)], pos, got5, own, w, flops=mac * eighth)
    got6 = swap(q6, 65)
    own, top, path, rw1 = call(
        "shadow_6", shadow_6, "s" + "v" * 8,
        [block(eighth, F32), block(eighth, F32), block(rank), block(size)],
        pos, q6, got5, w, b, row_basis, wl, top, path, flops=mac * n * 3,
    )
    (q7,) = call("climb_6", climb_kernel(6), "svvv", [block(eighth)], pos, got6, own, w, flops=mac * eighth)
    got7 = swap(q7, 193)
    top, path = call(
        "shadow_7", shadow_7, "s" + "v" * 5, [block(eighth, F32), block(rank)],
        pos, got6, w, b, top, path, flops=mac * n * 2,
    )
    mine, send = call(
        "top", top_kernel, "s" + "v" * 6, [block(eighth), block(eighth)],
        pos, got7, top, path, c2, c2_oth, w, flops=mac * eighth * 3,
    )
    got = swap(send, 5)
    c1, c1_oth, g0, g1 = call(
        "shadow_8", shadow_8, "s" + "v" * 7,
        [block(quarter, F32), block(quarter, F32), block(size), block(size)],
        pos, mine, keep1, got1, b, w0, rw0, rw1, flops=mac * n * 5,
    )
    mine, send = call(
        "down", down_kernel, "s" + "v" * 5, [block(quarter), block(quarter)],
        pos, mine, got, c1, c1_oth, w, flops=mac * quarter * 2,
    )
    got = swap(send, 3)
    mine_other = swap(mine, 1)
    got, mine_other = lax.optimization_barrier((got, mine_other))
    got_other = swap(got, 1)
    piece = (2, 2, size, half)
    (done,) = call(
        "own_columns", own_kernel, "ss" + "v" * 5, [(piece, BF)],
        pos, order, mine, got, base, g0, g1, flops=mac * n * 2,
    )
    (out,) = call(
        "other_columns", last_kernel, "ss" + "v" * 6, [(rhs.shape, BF)],
        pos, order, mine_other, got_other, base, g0, g1, done,
        scratch=(pltpu.VMEM(piece, BF), pltpu.SemaphoreType.DMA((2, 2))),
        flops=mac * n * 2, out_spec=HBM,
    )
    return out


def solution(mesh):
    return jax.shard_map(
        shards,
        mesh=mesh,
        in_specs=(
            P(None, ("leaf", "top"), None),
            P(None, ("leaf", "top"), None, None),
            P(None, ("leaf", "top"), None, None),
            P(None, ("leaf", "top"), None, None),
            P(None, ("leaf", "top"), None, None, None),
            P(None, ("leaf", "top"), None, None),
            P(None, ("leaf", "top"), None, None, None, None),
            P(None, ("leaf", "top"), None, None, None),
            P(("leaf", "top"), None),
        ),
        out_specs=P(None, ("leaf", "top"), None),
        check_vma=False,
    )
```

time: 70.1 us -> 53.1 us (0.76)
  starting transfers between devices: 40.2 us -> 23.4 us
    ppermute x12 -> x13, starting transfers between devices: 40.2 us -> 23.4 us  [swap(): return lax.ppermute(value, axes, [(i, i ^ flip) for i in range(devices)])]
    ppermute x12 -> x13, waiting for transfers between devices: 8.98 us -> 9.13 us  [swap(): return lax.ppermute(value, axes, [(i, i ^ flip) for i in range(devices)])]
  transfers between devices with their start and end apart: 12 -> 13, of which waited for: 9 -> 8; matrix products, arithmetic and copies ran while one was open for 0% -> 0% of each run, Pallas kernels for 18% -> 26%
where the time goes in v5:
time: 53.1 us; the launch traced here: 53 us
  starting transfers between devices  23.4 us (44%)
  Pallas kernels  20.1 us (38%)
  waiting for transfers between devices  9.13 us (17%)
    ppermute x13, starting transfers between devices, swap(): return lax.ppermute(value, axes, [(i, i ^ flip) for i in range(devices)])  23.4 us
    pallas_call x21, Pallas kernels, call(): pl.pallas_call(kernel, out_shape=[jax.ShapeDtypeStruct(shape, dtype) for...  20.1 us
    ppermute x13, waiting for transfers between devices, swap(): return lax.ppermute(value, axes, [(i, i ^ flip) for i in range(devices)])  9.13 us
  transfers between devices with their start and end apart: 13, of which 8 were waited for; matrix products, arithmetic and copies ran while one was open for 0% of the time, Pallas kernels for 26%

profile of v5, /device:TPU:1, one launch (start us, length us, event | category | flops | bytes accessed | tf_op | source)
XLA Modules:
  0.0 53.0 jit_solution(12277522542471626434)
XLA Ops:
  0.0 0.0 copy-start.5
  0.0 0.0 copy-start
  0.0 2.8 %send_half.1 = (bf16[2,256,256]{2,1,0:T(8,128)(2,1)S(1)}, bf16[2,128,256]{2,1,0:T(8,128)(2,1)S(1)}, bf16[2,1024,256]{2,1,0:T(8,128)(2,1)S(1)}, bf16[2,2,512,256]...) custom-call(s32[1]{0:T(128)} %bitcast.pos, s32[1,2]{1,0:T(1,128)} %order.13, ...), custom_call_target="tpu_custom_call" | custom-call | flops 402653184 | bytes 6815756 | tf_op jit(solution)/shard_map/send_half/pallas_call | solution.py:305
  2.8 0.0 copy-start.3
  2.8 3.3 %collective-permute-start = (bf16[2,128,256]{2,1,0:T(8,128)(2,1)S(1)}, bf16[2,128,256]{2,1,0:T(8,128)(2,1)S(1)}, u32[]{:S(2)}, u32[]{:S(2)}) collective-permute-start(bf16[2,128,256]{2,1,0:T(8,128)(2,1)S(1)} %get-tuple-element.55), channel_id=1, source_target_pairs={{0,1},{1,0},{2,3},{3,2},{4,5},{5,4},{6,7},{7,6},{8,9},{9,8},{10,11... | collective-permute-start | bytes 393224 | tf_op jit(solution)/shard_map/ppermute | solution.py:328
  6.2 0.0 copy-done.5
  6.2 1.6 %keep_half.1 = (bf16[2,256,256]{2,1,0:T(8,128)(2,1)S(1)}, bf16[2,128,256]{2,1,0:T(8,128)(2,1)S(1)}, f32[2,128,256]{2,1,0:T(8,128)S(1)}) custom-call(s32[1]{0:T(128)} %bitcast.pos, s32[1,2]{1,0:T(1,128)S(1)} %copy-done.5, bf16[2,1024,256]{2,1,0:T(8,128)(2,1)S(1)} %get-tuple-element.56.x, bf16[2,2,512,256]{3,2,1,0:T(8,128)(2,1)S(1)} %get-tuple-element.57.u, ...), custom_call_target="tpu_custom_call" | custom-call | flops 402653184 | bytes 3145740 | tf_op jit(solution)/shard_map/keep_half/pallas_call | solution.py:305
  7.8 0.0 collective-permute-done.got.got0
  7.8 0.2 climb_0.1
  8.1 0.1 collective-permute-start.1
  8.2 0.3 collective-permute-start.4
  8.4 0.0 copy-done
  8.4 0.0 copy-done.3
  8.4 1.3 %shadow_1.1 = (f32[2,64,256]{2,1,0:T(8,128)S(1)}, f32[2,512,256]{2,1,0:T(8,128)S(1)}) custom-call(s32[1]{0:T(128)} %bitcast.pos, s32[1,2]{1,0:T(1,128)S(1)} %copy-done.5, bf16[2,64,256]{2,1,0:T(8,128)(2,1)S(1)} %get-tuple-element.62.keep.keep1, bf16[2,8,2,256,256]{4,3,2,1,0:T(8,128)(2,1)S(1)} %bitcast.4, bf16[2,1024,256]{2,1,0:T(8,128)(2,1)S(1)} %get-tuple-element.56.x, ...), custom_call_target="tpu_custom_call" | custom-call | flops 671088640 | bytes 7405580 | tf_op jit(solution)/shard_map/shadow_1/pallas_call | solution.py:305
  9.7 2.2 %collective-permute-done.1.got.got1 = bf16[2,64,256]{2,1,0:T(8,128)(2,1)S(1)} collective-permute-done((bf16[2,64,256]{2,1,0:T(8,128)(2,1)S(1)}, bf16[2,64,256]{2,1,0:T(8,128)(2,1)S(1)}, u32[]{:S(2)}, u32[]{:S(2)}) %collective-permute-start.1) | collective-permute-done | bytes 65568 | tf_op jit(solution)/shard_map/ppermute | solution.py:328
  11.9 0.2 climb_1.1
  12.1 1.9 %collective-permute-start.2 = (bf16[2,32,256]{2,1,0:T(8,128)(2,1)S(1)}, bf16[2,32,256]{2,1,0:T(8,128)(2,1)S(1)}, u32[]{:S(2)}, u32[]{:S(2)}) collective-permute-start(bf16[2,32,256]{2,1,0:T(8,128)(2,1)S(1)} %get-tuple-element.66), channel_id=1, source_target_pairs={{0,5},{1,4},{2,7},{3,6},{4,1},{5,0},{6,3},{7,2},{8,13},{9,12},{10,... | collective-permute-start | bytes 98312 | tf_op jit(solution)/shard_map/ppermute | solution.py:328
  14.0 1.3 %shadow_2.1 = (f32[2,32,256]{2,1,0:T(8,128)S(1)}, f32[2,512,256]{2,1,0:T(8,128)S(1)}) custom-call(s32[1]{0:T(128)} %bitcast.pos, s32[1,2]{1,0:T(1,128)S(1)} %copy-done.5, bf16[2,32,256]{2,1,0:T(8,128)(2,1)S(1)} %get-tuple-element.67.keep.keep2, bf16[2,8,2,256,256]{4,3,2,1,0:T(8,128)(2,1)S(1)} %bitcast.6, bf16[2,1024,256]{2,1,0:T(8,128)(2,1)S(1)} %get-tuple-element.56.x, ...), custom_call_target="tpu_custom_call" | custom-call | flops 671088640 | bytes 7372812 | tf_op jit(solution)/shard_map/shadow_2/pallas_call | solution.py:305
  15.3 1.5 %collective-permute-done.2.got.got2 = bf16[2,32,256]{2,1,0:T(8,128)(2,1)S(1)} collective-permute-done((bf16[2,32,256]{2,1,0:T(8,128)(2,1)S(1)}, bf16[2,32,256]{2,1,0:T(8,128)(2,1)S(1)}, u32[]{:S(2)}, u32[]{:S(2)}) %collective-permute-start.2) | collective-permute-done | bytes 32800 | tf_op jit(solution)/shard_map/ppermute | solution.py:328
  16.8 0.0 copy-start.1
  16.8 0.0 copy-start.4
  16.8 0.2 climb_2.1.q3
  17.0 3.9 %collective-permute-start.3 = (bf16[2,32,256]{2,1,0:T(8,128)(2,1)S(1)}, bf16[2,32,256]{2,1,0:T(8,128)(2,1)S(1)}, u32[]{:S(2)}, u32[]{:S(2)}) collective-permute-start(bf16[2,32,256]{2,1,0:T(8,128)(2,1)S(1)} %climb_2.1.q3), channel_id=1, source_target_pairs={{0,13},{1,12},{2,15},{3,14},{4,9},{5,8},{6,11},{7,10},{8,5},{9,4},... | collective-permute-start | bytes 98312 | tf_op jit(solution)/shard_map/ppermute | solution.py:328
  20.9 0.0 collective-permute-done.4.got0_other
  20.9 0.0 copy-done.1
  20.9 0.0 copy-done.4
  20.9 2.0 %shadow_3.1 = (f32[2,32,256]{2,1,0:T(8,128)S(1)}, bf16[2,2,256,256]{3,2,1,0:T(8,128)(2,1)S(1)}, f32[2,32,256]{2,1,0:T(8,128)S(1)}, f32[2,32,256]{2,1,0:T(8,128)S(1)}) custom-call(s32[1]{0:T(128)} %bitcast.pos, bf16[2,32,256]{2,1,0:T(8,128)(2,1)S(1)} %climb_2.1.q3, bf16[2,8,2,256,256]{4,3,2,1,0:T(8,128)(2,1)S(1)} %bitcast.8, ...), custom_call_target="tpu_custom_call" | custom-call | flops 805306368 | bytes 7962628 | tf_op jit(solution)/shard_map/shadow_3/pallas_call | solution.py:305
  22.9 0.0 collective-permute-done.3.got.got3
  22.9 0.0 copy-start.2
  22.9 0.2 climb_3.1.q4
  23.1 1.7 %collective-permute-start.5 = (bf16[2,32,256]{2,1,0:T(8,128)(2,1)S(1)}, bf16[2,32,256]{2,1,0:T(8,128)(2,1)S(1)}, u32[]{:S(2)}, u32[]{:S(2)}) collective-permute-start(bf16[2,32,256]{2,1,0:T(8,128)(2,1)S(1)} %climb_3.1.q4), channel_id=1, source_target_pairs={{0,17},{1,16},{2,19},{3,18},{4,21},{5,20},{6,23},{7,22},{8,25},{9,... | collective-permute-start | bytes 98312 | tf_op jit(solution)/shard_map/ppermute | solution.py:328
  24.8 0.0 copy-done.2
  24.8 1.7 %shadow_4.1 = (f32[2,32,256]{2,1,0:T(8,128)S(1)}, f32[2,32,256]{2,1,0:T(8,128)S(1)}, f32[2,2,1024,128]{3,2,1,0:T(8,128)S(1)}) custom-call(s32[1]{0:T(128)} %bitcast.pos, s32[1,2]{1,0:T(1,128)S(1)} %copy-done.5, bf16[2,32,256]{2,1,0:T(8,128)(2,1)S(1)} %climb_3.1.q4, bf16[2,32,256]{2,1,0:T(8,128)(2,1)S(1)} %collective-permute-done.3.got.got3, ...), custom_call_target="tpu_custom_call" | custom-call | flops 536870912 | bytes 10027020 | tf_op jit(solution)/shard_map/shadow_4/pallas_call | solution.py:305
  26.4 0.3 collective-permute-done.5.got.got4
  26.8 0.2 climb_4.1.q5
  27.0 2.8 %collective-permute-start.6 = (bf16[2,32,256]{2,1,0:T(8,128)(2,1)S(1)}, bf16[2,32,256]{2,1,0:T(8,128)(2,1)S(1)}, u32[]{:S(2)}, u32[]{:S(2)}) collective-permute-start(bf16[2,32,256]{2,1,0:T(8,128)(2,1)S(1)} %climb_4.1.q5), channel_id=1, source_target_pairs={{0,49},{1,48},{2,51},{3,50},{4,53},{5,52},{6,55},{7,54},{8,57},{9,... | collective-permute-start | bytes 98312 | tf_op jit(solution)/shard_map/ppermute | solution.py:328
  29.8 1.0 %shadow_5.1 = (f32[2,32,256]{2,1,0:T(8,128)S(1)}, f32[2,32,256]{2,1,0:T(8,128)S(1)}, bf16[2,256,256]{2,1,0:T(8,128)(2,1)S(1)}, bf16[2,512,256]{2,1,0:T(8,128)(2,1)S(1)}) custom-call(s32[1]{0:T(128)} %bitcast.pos, bf16[2,32,256]{2,1,0:T(8,128)(2,1)S(1)} %climb_4.1.q5, bf16[2,32,256]{2,1,0:T(8,128)(2,1)S(1)} %collective-permute-done.5.got.got4, ...), custom_call_target="tpu_custom_call" | custom-call | flops 402653184 | bytes 7995396 | tf_op jit(solution)/shard_map/shadow_5/pallas_call | solution.py:305
  30.8 0.9 %collective-permute-done.6.got.got5 = bf16[2,32,256]{2,1,0:T(8,128)(2,1)S(1)} collective-permute-done((bf16[2,32,256]{2,1,0:T(8,128)(2,1)S(1)}, bf16[2,32,256]{2,1,0:T(8,128)(2,1)S(1)}, u32[]{:S(2)}, u32[]{:S(2)}) %collective-permute-start.6) | collective-permute-done | bytes 32800 | tf_op jit(solution)/shard_map/ppermute | solution.py:328
  31.6 0.2 climb_5.1.q6
  31.8 1.6 %collective-permute-start.7 = (bf16[2,32,256]{2,1,0:T(8,128)(2,1)S(1)}, bf16[2,32,256]{2,1,0:T(8,128)(2,1)S(1)}, u32[]{:S(2)}, u32[]{:S(2)}) collective-permute-start(bf16[2,32,256]{2,1,0:T(8,128)(2,1)S(1)} %climb_5.1.q6), channel_id=1, source_target_pairs={{0,65},{1,64},{2,67},{3,66},{4,69},{5,68},{6,71},{7,70},{8,73},{9,... | collective-permute-start | bytes 98312 | tf_op jit(solution)/shard_map/ppermute | solution.py:328
  33.5 1.0 %shadow_6.1 = (f32[2,32,256]{2,1,0:T(8,128)S(1)}, f32[2,32,256]{2,1,0:T(8,128)S(1)}, bf16[2,256,256]{2,1,0:T(8,128)(2,1)S(1)}, bf16[2,512,256]{2,1,0:T(8,128)(2,1)S(1)}) custom-call(s32[1]{0:T(128)} %bitcast.pos, bf16[2,32,256]{2,1,0:T(8,128)(2,1)S(1)} %climb_5.1.q6, bf16[2,32,256]{2,1,0:T(8,128)(2,1)S(1)} %collective-permute-done.6.got.got5, ...), custom_call_target="tpu_custom_call" | custom-call | flops 402653184 | bytes 8257540 | tf_op jit(solution)/shard_map/shadow_6/pallas_call | solution.py:305
  34.5 0.8 %collective-permute-done.7.got.got6 = bf16[2,32,256]{2,1,0:T(8,128)(2,1)S(1)} collective-permute-done((bf16[2,32,256]{2,1,0:T(8,128)(2,1)S(1)}, bf16[2,32,256]{2,1,0:T(8,128)(2,1)S(1)}, u32[]{:S(2)}, u32[]{:S(2)}) %collective-permute-start.7) | collective-permute-done | bytes 32800 | tf_op jit(solution)/shard_map/ppermute | solution.py:328
  35.3 0.2 climb_6.1
  35.5 3.1 %collective-permute-start.8 = (bf16[2,32,256]{2,1,0:T(8,128)(2,1)S(1)}, bf16[2,32,256]{2,1,0:T(8,128)(2,1)S(1)}, u32[]{:S(2)}, u32[]{:S(2)}) collective-permute-start(bf16[2,32,256]{2,1,0:T(8,128)(2,1)S(1)} %climb_6.1), channel_id=1, source_target_pairs={{0,193},{1,192},{2,195},{3,194},{4,197},{5,196},{6,199},{7,198},{8... | collective-permute-start | bytes 98312 | tf_op jit(solution)/shard_map/ppermute | solution.py:328
  38.5 1.1 %shadow_7.1 = (f32[2,32,256]{2,1,0:T(8,128)S(1)}, bf16[2,256,256]{2,1,0:T(8,128)(2,1)S(1)}) custom-call(s32[1]{0:T(128)} %bitcast.pos, bf16[2,32,256]{2,1,0:T(8,128)(2,1)S(1)} %collective-permute-done.7.got.got6, bf16[2,8,2,256,256]{4,3,2,1,0:T(8,128)(2,1)S(1)} %bitcast.16, bf16[2,8,256,256]{3,2,1,0:T(8,128)(2,1)S(1)} %bitcast.23, ...), custom_call_target="tpu_custom_call" | custom-call | flops 268435456 | bytes 6651908 | tf_op jit(solution)/shard_map/shadow_7/pallas_call | solution.py:305
  39.7 0.5 collective-permute-done.8.got
  40.2 0.4 top.1
  40.6 2.2 %collective-permute-start.9 = (bf16[2,32,256]{2,1,0:T(8,128)(2,1)S(1)}, bf16[2,32,256]{2,1,0:T(8,128)(2,1)S(1)}, u32[]{:S(2)}, u32[]{:S(2)}) collective-permute-start(bf16[2,32,256]{2,1,0:T(8,128)(2,1)S(1)} %get-tuple-element.91), channel_id=1, source_target_pairs={{0,5},{1,4},{2,7},{3,6},{4,1},{5,0},{6,3},{7,2},{8,13},{9,12},{10,... | collective-permute-start | bytes 98312 | tf_op jit(solution)/shard_map/ppermute | solution.py:328
  42.8 1.1 %shadow_8.1 = (f32[2,64,256]{2,1,0:T(8,128)S(1)}, f32[2,64,256]{2,1,0:T(8,128)S(1)}, bf16[2,512,256]{2,1,0:T(8,128)(2,1)S(1)}, bf16[2,512,256]{2,1,0:T(8,128)(2,1)S(1)}) custom-call(s32[1]{0:T(128)} %bitcast.pos, bf16[2,32,256]{2,1,0:T(8,128)(2,1)S(1)} %get-tuple-element.90.mine, bf16[2,64,256]{2,1,0:T(8,128)(2,1)S(1)} %get-tuple-element.62.keep.keep1, ...), custom_call_target="tpu_custom_call" | custom-call | flops 671088640 | bytes 3833860 | tf_op jit(solution)/shard_map/shadow_8/pallas_call | solution.py:305
  43.9 1.0 %collective-permute-done.9.got = bf16[2,32,256]{2,1,0:T(8,128)(2,1)S(1)} collective-permute-done((bf16[2,32,256]{2,1,0:T(8,128)(2,1)S(1)}, bf16[2,32,256]{2,1,0:T(8,128)(2,1)S(1)}, u32[]{:S(2)}, u32[]{:S(2)}) %collective-permute-start.9) | collective-permute-done | bytes 32800 | tf_op jit(solution)/shard_map/ppermute | solution.py:328
  44.9 0.3 down.1
  45.2 2.0 %collective-permute-start.10 = (bf16[2,64,256]{2,1,0:T(8,128)(2,1)S(1)}, bf16[2,64,256]{2,1,0:T(8,128)(2,1)S(1)}, u32[]{:S(2)}, u32[]{:S(2)}) collective-permute-start(bf16[2,64,256]{2,1,0:T(8,128)(2,1)S(1)} %get-tuple-element.96), channel_id=1, source_target_pairs={{0,3},{1,2},{2,1},{3,0},{4,7},{5,6},{6,5},{7,4},{8,11},{9,10},{10,... | collective-permute-start | bytes 196616 | tf_op jit(solution)/shard_map/ppermute | solution.py:328
  47.2 0.2 collective-permute-start.11
  47.4 2.0 %collective-permute-done.10.got = bf16[2,64,256]{2,1,0:T(8,128)(2,1)S(1)} collective-permute-done((bf16[2,64,256]{2,1,0:T(8,128)(2,1)S(1)}, bf16[2,64,256]{2,1,0:T(8,128)(2,1)S(1)}, u32[]{:S(2)}, u32[]{:S(2)}) %collective-permute-start.10) | collective-permute-done | bytes 65568 | tf_op jit(solution)/shard_map/ppermute | solution.py:328
  49.4 0.0 collective-permute-done.11.mine
  49.4 0.3 collective-permute-start.12
  49.6 1.0 %own_columns.1.done = bf16[2,2,512,128]{3,2,1,0:T(8,128)(2,1)S(1)} custom-call(s32[1]{0:T(128)} %bitcast.pos, s32[1,2]{1,0:T(1,128)S(1)} %copy-done.5, bf16[2,64,256]{2,1,0:T(8,128)(2,1)S(1)} %get-tuple-element.97.mine, bf16[2,64,256]{2,1,0:T(8,128)(2,1)S(1)} %collective-permute-done.10.got, f32[2,2,1024,128]{3,2,1,0:T(8,128)S(1)} %get-tuple-element.100.base, ...), custom_call_target="tpu_custom_call" | custom-call | flops 268435456 | bytes 3276812 | tf_op jit(solution)/shard_map/own_columns/pallas_call | solution.py:305
  50.6 0.0 collective-permute-done.12.got
  50.6 2.1 %other_columns.1 = bf16[2,1024,256]{2,1,0:T(8,128)(2,1)} custom-call(s32[1]{0:T(128)} %bitcast.pos, s32[1,2]{1,0:T(1,128)S(1)} %copy-done.5, bf16[2,64,256]{2,1,0:T(8,128)(2,1)S(1)} %collective-permute-done.11.mine, bf16[2,64,256]{2,1,0:T(8,128)(2,1)S(1)} %collective-permute-done.12.got, f32[2,2,1024,128]{3,2,1,0:T(8,128)S(1)} %get-tuple-element.100.base, ...), custom_call_target="tpu_custom_call" | custom-call | flops 268435456 | bytes 3801100 | tf_op jit(solution)/shard_map/other_columns/pallas_call | solution.py:305
Async XLA Ops:
  0.0 6.2 %copy-start.5 = (s32[1,2]{1,0:T(1,128)S(1)}, s32[1,2]{1,0:T(1,128)}, u32[]{:S(2)}) copy-start(s32[1,2]{1,0:T(1,128)} %order.13) | copy-start | bytes 28
  0.0 8.4 %copy-start = (bf16[2,1,8,2,256,256]{5,4,3,2,1,0:T(8,128)(2,1)S(1)}, bf16[2,1,8,2,256,256]{5,4,3,2,1,0:T(8,128)(2,1)}, u32[]{:S(2)}) copy-start(bf16[2,1,8,2,256,256]{5,4,3,2,1,0:T(8,128)(2,1)} %param.15) | copy-start | bytes 12582916
  2.8 5.6 %copy-start.3 = (bf16[2,2,512,512]{3,2,1,0:T(8,128)(2,1)S(1)}, bf16[2,2,512,512]{3,2,1,0:T(8,128)(2,1)}, u32[]{:S(2)}) copy-start(bf16[2,2,512,512]{3,2,1,0:T(8,128)(2,1)} %d.1) | copy-start | bytes 6291460
  2.8 5.0 %collective-permute-start = (bf16[2,128,256]{2,1,0:T(8,128)(2,1)S(1)}, bf16[2,128,256]{2,1,0:T(8,128)(2,1)S(1)}, u32[]{:S(2)}, u32[]{:S(2)}) collective-permute-start(bf16[2,128,256]{2,1,0:T(8,128)(2,1)S(1)} %get-tuple-element.55), channel_id=1, source_target_pairs={{0,1},{1,0},{2,3},{3,2},{4,5},{5,4},{6,7},{7,6},{8,9},{9,8},{10,11... | collective-permute-start | bytes 393224 | tf_op jit(solution)/shard_map/ppermute | solution.py:328
  8.1 3.8 %collective-permute-start.1 = (bf16[2,64,256]{2,1,0:T(8,128)(2,1)S(1)}, bf16[2,64,256]{2,1,0:T(8,128)(2,1)S(1)}, u32[]{:S(2)}, u32[]{:S(2)}) collective-permute-start(bf16[2,64,256]{2,1,0:T(8,128)(2,1)S(1)} %get-tuple-element.61), channel_id=1, source_target_pairs={{0,3},{1,2},{2,1},{3,0},{4,7},{5,6},{6,5},{7,4},{8,11},{9,10},{10,... | collective-permute-start | bytes 196616 | tf_op jit(solution)/shard_map/ppermute | solution.py:328
  8.2 12.8 %collective-permute-start.4 = (bf16[2,128,256]{2,1,0:T(8,128)(2,1)S(1)}, bf16[2,128,256]{2,1,0:T(8,128)(2,1)S(1)}, u32[]{:S(2)}, u32[]{:S(2)}) collective-permute-start(bf16[2,128,256]{2,1,0:T(8,128)(2,1)S(1)} %get-tuple-element.72), channel_id=1, source_target_pairs={{0,1},{1,0},{2,3},{3,2},{4,5},{5,4},{6,7},{7,6},{8,9},{9,8},{10,11... | collective-permute-start | bytes 393224 | tf_op jit(solution)/shard_map/ppermute | solution.py:328
  12.1 4.8 %collective-permute-start.2 = (bf16[2,32,256]{2,1,0:T(8,128)(2,1)S(1)}, bf16[2,32,256]{2,1,0:T(8,128)(2,1)S(1)}, u32[]{:S(2)}, u32[]{:S(2)}) collective-permute-start(bf16[2,32,256]{2,1,0:T(8,128)(2,1)S(1)} %get-tuple-element.66), channel_id=1, source_target_pairs={{0,5},{1,4},{2,7},{3,6},{4,1},{5,0},{6,3},{7,2},{8,13},{9,12},{10,... | collective-permute-start | bytes 98312 | tf_op jit(solution)/shard_map/ppermute | solution.py:328
  16.8 4.1 %copy-start.1 = (bf16[2,1,8,256,256]{4,3,2,1,0:T(8,128)(2,1)S(1)}, bf16[2,1,8,256,256]{4,3,2,1,0:T(8,128)(2,1)}, u32[]{:S(2)}) copy-start(bf16[2,1,8,256,256]{4,3,2,1,0:T(8,128)(2,1)} %param.16) | copy-start | bytes 6291460
  16.8 4.1 %copy-start.4 = (bf16[2,1,256,256]{3,2,1,0:T(8,128)(2,1)S(1)}, bf16[2,1,256,256]{3,2,1,0:T(8,128)(2,1)}, u32[]{:S(2)}) copy-start(bf16[2,1,256,256]{3,2,1,0:T(8,128)(2,1)} %bl.1) | copy-start | bytes 786436
  17.0 5.9 %collective-permute-start.3 = (bf16[2,32,256]{2,1,0:T(8,128)(2,1)S(1)}, bf16[2,32,256]{2,1,0:T(8,128)(2,1)S(1)}, u32[]{:S(2)}, u32[]{:S(2)}) collective-permute-start(bf16[2,32,256]{2,1,0:T(8,128)(2,1)S(1)} %climb_2.1.q3), channel_id=1, source_target_pairs={{0,13},{1,12},{2,15},{3,14},{4,9},{5,8},{6,11},{7,10},{8,5},{9,4},... | collective-permute-start | bytes 98312 | tf_op jit(solution)/shard_map/ppermute | solution.py:328
  22.9 1.9 %copy-start.2 = (bf16[2,2,512,256]{3,2,1,0:T(8,128)(2,1)S(1)}, bf16[2,2,512,256]{3,2,1,0:T(8,128)(2,1)}, u32[]{:S(2)}) copy-start(bf16[2,2,512,256]{3,2,1,0:T(8,128)(2,1)} %r.2) | copy-start | bytes 3145732
  23.1 3.7 %collective-permute-start.5 = (bf16[2,32,256]{2,1,0:T(8,128)(2,1)S(1)}, bf16[2,32,256]{2,1,0:T(8,128)(2,1)S(1)}, u32[]{:S(2)}, u32[]{:S(2)}) collective-permute-start(bf16[2,32,256]{2,1,0:T(8,128)(2,1)S(1)} %climb_3.1.q4), channel_id=1, source_target_pairs={{0,17},{1,16},{2,19},{3,18},{4,21},{5,20},{6,23},{7,22},{8,25},{9,... | collective-permute-start | bytes 98312 | tf_op jit(solution)/shard_map/ppermute | solution.py:328
  27.0 4.7 %collective-permute-start.6 = (bf16[2,32,256]{2,1,0:T(8,128)(2,1)S(1)}, bf16[2,32,256]{2,1,0:T(8,128)(2,1)S(1)}, u32[]{:S(2)}, u32[]{:S(2)}) collective-permute-start(bf16[2,32,256]{2,1,0:T(8,128)(2,1)S(1)} %climb_4.1.q5), channel_id=1, source_target_pairs={{0,49},{1,48},{2,51},{3,50},{4,53},{5,52},{6,55},{7,54},{8,57},{9,... | collective-permute-start | bytes 98312 | tf_op jit(solution)/shard_map/ppermute | solution.py:328
  31.8 3.5 %collective-permute-start.7 = (bf16[2,32,256]{2,1,0:T(8,128)(2,1)S(1)}, bf16[2,32,256]{2,1,0:T(8,128)(2,1)S(1)}, u32[]{:S(2)}, u32[]{:S(2)}) collective-permute-start(bf16[2,32,256]{2,1,0:T(8,128)(2,1)S(1)} %climb_5.1.q6), channel_id=1, source_target_pairs={{0,65},{1,64},{2,67},{3,66},{4,69},{5,68},{6,71},{7,70},{8,73},{9,... | collective-permute-start | bytes 98312 | tf_op jit(solution)/shard_map/ppermute | solution.py:328
  35.5 4.7 %collective-permute-start.8 = (bf16[2,32,256]{2,1,0:T(8,128)(2,1)S(1)}, bf16[2,32,256]{2,1,0:T(8,128)(2,1)S(1)}, u32[]{:S(2)}, u32[]{:S(2)}) collective-permute-start(bf16[2,32,256]{2,1,0:T(8,128)(2,1)S(1)} %climb_6.1), channel_id=1, source_target_pairs={{0,193},{1,192},{2,195},{3,194},{4,197},{5,196},{6,199},{7,198},{8... | collective-permute-start | bytes 98312 | tf_op jit(solution)/shard_map/ppermute | solution.py:328
  40.6 4.3 %collective-permute-start.9 = (bf16[2,32,256]{2,1,0:T(8,128)(2,1)S(1)}, bf16[2,32,256]{2,1,0:T(8,128)(2,1)S(1)}, u32[]{:S(2)}, u32[]{:S(2)}) collective-permute-start(bf16[2,32,256]{2,1,0:T(8,128)(2,1)S(1)} %get-tuple-element.91), channel_id=1, source_target_pairs={{0,5},{1,4},{2,7},{3,6},{4,1},{5,0},{6,3},{7,2},{8,13},{9,12},{10,... | collective-permute-start | bytes 98312 | tf_op jit(solution)/shard_map/ppermute | solution.py:328
  45.2 4.1 %collective-permute-start.10 = (bf16[2,64,256]{2,1,0:T(8,128)(2,1)S(1)}, bf16[2,64,256]{2,1,0:T(8,128)(2,1)S(1)}, u32[]{:S(2)}, u32[]{:S(2)}) collective-permute-start(bf16[2,64,256]{2,1,0:T(8,128)(2,1)S(1)} %get-tuple-element.96), channel_id=1, source_target_pairs={{0,3},{1,2},{2,1},{3,0},{4,7},{5,6},{6,5},{7,4},{8,11},{9,10},{10,... | collective-permute-start | bytes 196616 | tf_op jit(solution)/shard_map/ppermute | solution.py:328
  47.2 2.2 %collective-permute-start.11 = (bf16[2,64,256]{2,1,0:T(8,128)(2,1)S(1)}, bf16[2,64,256]{2,1,0:T(8,128)(2,1)S(1)}, u32[]{:S(2)}, u32[]{:S(2)}) collective-permute-start(bf16[2,64,256]{2,1,0:T(8,128)(2,1)S(1)} %get-tuple-element.97.mine), channel_id=1, source_target_pairs={{0,1},{1,0},{2,3},{3,2},{4,5},{5,4},{6,7},{7,6},{8,9},{9,8},{10,11... | collective-permute-start | bytes 196616 | tf_op jit(solution)/shard_map/ppermute | solution.py:328
  49.4 1.3 %collective-permute-start.12 = (bf16[2,64,256]{2,1,0:T(8,128)(2,1)S(1)}, bf16[2,64,256]{2,1,0:T(8,128)(2,1)S(1)}, u32[]{:S(2)}, u32[]{:S(2)}) collective-permute-start(bf16[2,64,256]{2,1,0:T(8,128)(2,1)S(1)} %collective-permute-done.10.got), channel_id=1, source_target_pairs={{0,1},{1,0},{2,3},{3,2},{4,5},{5,4},{6,7},{7,6},{8,9},{9,8},{10,11... | collective-permute-start | bytes 196616 | tf_op jit(solution)/shard_map/ppermute | solution.py:328

commit v6 on v5

v6 whole, which is shorter than its diff:
```python
import jax
import jax.numpy as jnp
from jax import lax
from jax.experimental import pallas as pl
from jax.experimental.pallas import tpu as pltpu
from jax.sharding import PartitionSpec as P

BF = jnp.bfloat16
F32 = jnp.float32
NN = (((1,), (0,)), ((), ()))
NT = (((1,), (1,)), ((), ()))


def dot(a, b, dims=NN):
    return lax.dot_general(a, b, dims, preferred_element_type=F32)


def widen(a):
    half = a.shape[0] // 2
    re, im = a[:half], a[half:]
    return jnp.concatenate(
        [jnp.concatenate([re, -im], axis=1), jnp.concatenate([im, re], axis=1)], axis=0
    )


def times(a, w_re, w_im):
    return dot(widen(a), jnp.concatenate([w_re, w_im], axis=0))


def times_t(a, w_re, w_im):
    return dot(widen(a), jnp.concatenate([w_re, w_im], axis=1), NT)


def rows(ref):
    return jnp.concatenate([ref[0], ref[1]], axis=0)


def put(ref, value):
    half = value.shape[0] // 2
    ref[0] = value[:half].astype(ref.dtype)
    ref[1] = value[half:].astype(ref.dtype)


def bit(pos, level):
    return (pos[0] >> level) & 1


def lift(q, w, pos, level, flip=0):
    child = bit(pos, level) ^ flip
    return times(q, w[0, level, child], w[1, level, child])


def lower(h, w, pos, level, flip=0):
    child = bit(pos, level) ^ flip
    return times_t(h, w[0, level, child], w[1, level, child])


def couple(q, b, pos, level, flip=0):
    return lax.cond(
        (bit(pos, level) ^ flip) == 0,
        lambda: times_t(q, b[0, level], b[1, level]),
        lambda: times(q, b[0, level], b[1, level]),
    )


def split(value, side, keep, send):
    half = value.shape[0] // 2
    part = half // 2
    for c in range(2):
        low = value[c * half : c * half + part]
        high = value[c * half + part : (c + 1) * half]
        keep[c] = jnp.where(side == 0, low, high)
        send[c] = jnp.where(side == 0, high, low)


def join(own, got, side):
    parts = []
    for c in range(2):
        parts.append(jnp.where(side == 0, own[c], got[c]))
        parts.append(jnp.where(side == 0, got[c], own[c]))
    return jnp.concatenate(parts, axis=0)


def side(pos, level):
    if level == 0:
        return (pos[0] ^ (pos[0] >> 1) ^ (pos[0] >> 2) ^ (pos[0] >> 4) ^ (pos[0] >> 6)) & 1
    if level == 1:
        return bit(pos, 1)
    return bit(pos, 2) ^ bit(pos, 3)


def half_lanes(half, n):
    return pl.ds(pl.multiple_of(half * n, n), n)


class Levels:
    def __init__(self, ref, start):
        self.ref, self.start = ref, start

    def __getitem__(self, key):
        c, level, child = key
        return self.ref[c, level - self.start, child]


def parent(qleaf, wl):
    q = times(qleaf[0], wl[0, 0, 0], wl[1, 0, 0]) + times(qleaf[1], wl[0, 0, 1], wl[1, 0, 1])
    return q.astype(BF)


def send_kernel(pos, order, x, u, wl, w, qleaf, send, xt, x_v, u_v, wl_v, w0, order_s, sems):
    size = u.shape[2]
    half = x.shape[2] // 2

    def x_copy(block):
        at = pl.ds(block * size, size)
        return pltpu.make_async_copy(x.at[:, at], x_v.at[:, at], sems.at[block])

    def u_copy(leaf):
        return pltpu.make_async_copy(u.at[:, leaf], u_v.at[:, leaf], sems.at[2 + leaf])

    order_copy = pltpu.make_async_copy(order, order_s, sems.at[4])
    wl_copy = pltpu.make_async_copy(wl, wl_v, sems.at[5])
    w_copy = pltpu.make_async_copy(w.at[:, 0], w0.at[:, 0], sems.at[6])
    order_copy.start()
    for i in range(2):
        x_copy(i).start()
        u_copy(i).start()
    wl_copy.start()
    w_copy.start()
    order_copy.wait()
    first = order_s[0, 0]

    def transposed(block, which):
        at = pl.ds(block * size, size)
        lanes = half_lanes(which, half)
        return jnp.concatenate([x_v[0, at, lanes].T, x_v[1, at, lanes].T], axis=0)

    keep = side(pos, 0)
    for block in range(2):
        x_copy(block).wait()
        xt[block] = transposed(block, keep)
        xs = transposed(block, 1 - keep)
        if block == 0:
            u_copy(0).wait()
            u_copy(1).wait()
        leaf = first ^ block
        qleaf[leaf] = times(xs, u_v[0, leaf], u_v[1, leaf]).astype(BF)
    wl_copy.wait()
    put(send, parent(qleaf, wl_v))
    w_copy.wait()


def keep_kernel(pos, order, xt, u, wl, w0, w, qleaf, keep, own, w_low, sem):
    copy = pltpu.make_async_copy(w.at[:, pl.ds(1, 3)], w_low, sem)
    copy.start()
    for block in range(2):
        leaf = order[0, 0] ^ block
        qleaf[leaf] = times(xt[block], u[0, leaf], u[1, leaf]).astype(BF)
    q = parent(qleaf, wl)
    put(keep, q)
    put(own, lift(q, w0, pos, 0))
    copy.wait()


def climb_kernel(level, start):
    def kernel(pos, got, own, w, *outs):
        q = (rows(own) + lift(rows(got), Levels(w, start), pos, level, 1)).astype(BF)
        if len(outs) == 2:
            split(q, side(pos, level + 1), *outs)
        else:
            put(outs[0], q)

    return kernel


def direct(order, block, x, d, out):
    size = d.shape[2]
    leaf = order[0, 0] ^ block
    at = pl.ds(block * size, size)
    xs = jnp.concatenate([x[0, at], x[1, at]], axis=0)
    re, im = d[0, leaf], d[1, leaf]
    out[0] = dot(jnp.concatenate([re, -im], axis=1), xs)
    out[1] = dot(jnp.concatenate([im, re], axis=1), xs)


def shadow_1(pos, order, keep, w, w_all, x, d, own, part, w_high, sem):
    copy = pltpu.make_async_copy(w_all.at[:, pl.ds(4, 4)], w_high, sem)
    copy.start()
    put(own, lift(rows(keep), Levels(w, 1), pos, 1))
    direct(order, 0, x, d, part)
    copy.wait()


def leaf_coupled(pos, q, got, b, bl, wl, cleaf):
    c0 = couple(rows(got), b, pos, 0).astype(BF)
    left = times_t(q[1], bl[0, 0], bl[1, 0])
    right = times(q[0], bl[0, 0], bl[1, 0])
    cleaf[0] = (left + times_t(c0, wl[0, 0, 0], wl[1, 0, 0])).astype(BF)
    cleaf[1] = (right + times_t(c0, wl[0, 0, 1], wl[1, 0, 1])).astype(BF)


def shadow_2(pos, order, keep, w, x, d, own, part):
    put(own, lift(rows(keep), Levels(w, 1), pos, 2))
    direct(order, 1, x, d, part)


def shadow_3(pos, q3, w, b, bl, wl, q_mine, got0, own, cleaf):
    put(own, lift(rows(q3), Levels(w, 1), pos, 3))
    leaf_coupled(pos, q_mine, got0, b, bl, wl, cleaf)


def set_base(pos, order, part, r, cleaf, parts, base):
    n = base.shape[2]
    size = r.shape[2]
    first = order[0, 0]
    lanes = half_lanes(side(pos, 0) ^ part, n)
    for block, direct_part in enumerate(parts):
        leaf = first ^ block
        add = dot(jnp.concatenate([r[0, leaf], r[1, leaf]], axis=1), widen(cleaf[leaf]), NT)
        for c in range(2):
            base[c, pl.ds(block * size, size)] = (
                direct_part[c, :, lanes] + add[:, c * n : (c + 1) * n]
            )


def shadow_4(pos, order, q4, got3, w, b, r, cleaf, part_0, part_1, own, top, base):
    put(own, lift(rows(q4), Levels(w, 4), pos, 4))
    put(top, couple(rows(got3), b, pos, 3))
    set_base(pos, order, 0, r, cleaf, (part_0, part_1), base)


def product(r, wl, leaf, out):
    put(out, times(jnp.concatenate([r[0, leaf], r[1, leaf]], axis=0), wl[0, 0, leaf], wl[1, 0, leaf]))


def shadow_5(pos, q5, got4, w_low, w_high, b, r, wl, top, own, top_out, path, rw):
    low, high = Levels(w_low, 1), Levels(w_high, 4)
    put(own, lift(rows(q5), high, pos, 5))
    c4 = couple(rows(got4), b, pos, 4).astype(BF)
    put(top_out, rows(top) + lower(c4, low, pos, 3))
    w3 = bit(pos, 3)
    put(path, lift(jnp.concatenate([low[0, 3, w3], low[1, 3, w3]], axis=0), high, pos, 4))
    product(r, wl, 0, rw)


def shadow_6(pos, q6, got5, w, b, r, wl, top, path, own, top_out, path_out, rw):
    high = Levels(w, 4)
    put(own, lift(rows(q6), high, pos, 6))
    c5 = couple(rows(got5), b, pos, 5).astype(BF)
    put(top_out, rows(top) + times_t(c5, path[0], path[1]))
    put(path_out, lift(rows(path), high, pos, 5))
    product(r, wl, 1, rw)


def shadow_7(pos, got6, w, b, top, path, keep2, got2, top_out, path_out, c2, c2_oth):
    c6 = couple(rows(got6), b, pos, 6).astype(BF)
    put(top_out, rows(top) + times_t(c6, path[0], path[1]))
    longer = lift(rows(path), Levels(w, 4), pos, 6).astype(BF)
    put(path_out, couple_path(longer, b, pos))
    put(c2, couple(rows(got2), b, pos, 2))
    put(c2_oth, couple(rows(keep2), b, pos, 2, 1))


def couple_path(path, b, pos):
    return lax.cond(
        bit(pos, 7) == 0,
        lambda: times(path, b[0, 7], b[1, 7]),
        lambda: times_t(path, b[0, 7], b[1, 7]),
    )


def top_kernel(pos, got, top, path, c_own, c_oth, w, own, send):
    h = (rows(top) + times_t(rows(got), path[0], path[1])).astype(BF)
    low = Levels(w, 1)
    put(own, rows(c_own) + lower(h, low, pos, 2))
    put(send, rows(c_oth) + lower(h, low, pos, 2, 1))


def shadow_8(pos, mine, keep1, got1, b, w0, rw0, rw1, c1, c1_oth, g0, g1):
    put(c1, couple(rows(got1), b, pos, 1))
    put(c1_oth, couple(rows(keep1), b, pos, 1, 1))
    put(g0, lift(rows(rw0), w0, pos, 0))
    put(g1, lift(rows(rw1), w0, pos, 0))


def down_kernel(pos, mine, got, c_own, c_oth, w, own, send):
    h = join(mine, got, side(pos, 2))
    low = Levels(w, 1)
    put(own, rows(c_own) + lower(h, low, pos, 1))
    put(send, rows(c_oth) + lower(h, low, pos, 1, 1))


def shadow_9(pos, order, mine, q_other, got0_other, b, bl, wl, r, part_0, part_1, base, cleaf):
    leaf_coupled(pos, q_other, got0_other, b, bl, wl, cleaf)
    set_base(pos, order, 1, r, cleaf, (part_0, part_1), base)


def finish(pos, order, mine, got, base, gs, out, tile):
    hw = widen(join(mine, got, side(pos, 1)))
    n = base.shape[2]
    for leaf, g in enumerate(gs):
        size = g.shape[1]
        for step in range(size // tile):
            here = pl.ds(step * tile, tile)
            start = (order[0, 0] ^ leaf) * size + step * tile
            at = pl.ds(pl.multiple_of(start, tile), tile)
            add = dot(jnp.concatenate([g[0, here], g[1, here]], axis=1), hw, NT)
            for c in range(2):
                out[leaf, c, here] = (base[c, at] + add[:, c * n : (c + 1) * n]).astype(BF)
            yield leaf, here, at


def own_kernel(pos, order, mine, got, base, g0, g1, out):
    for _ in finish(pos, order, mine, got, base, (g0, g1), out, g0.shape[1]):
        pass


def last_kernel(pos, order, mine, got, base, g0, g1, done, out, buf, sems):
    size = g0.shape[1]
    n = base.shape[2]
    copies = []

    def store(src, part, at):
        lanes = half_lanes(side(pos, 0) ^ part, n)
        sem = sems.at[len(copies)]
        copies.append(pltpu.make_async_copy(src, out.at[:, at, lanes], sem))
        copies[-1].start()

    for leaf in range(2):
        at = pl.ds(pl.multiple_of((order[0, 0] ^ leaf) * size, size), size)
        store(done.at[leaf], 0, at)
    for leaf, here, at in finish(pos, order, mine, got, base, (g0, g1), buf, size // 2):
        store(buf.at[leaf, :, here], 1, at)
    for copy in copies:
        copy.wait()


VMEM = pl.BlockSpec(memory_space=pltpu.VMEM)
SMEM = pl.BlockSpec(memory_space=pltpu.SMEM)
HBM = pl.BlockSpec(memory_space=pltpu.HBM)
GRANT = 20 * 2**20


def call(name, kernel, ins, outs, *args, scratch=(), flops=0, out_spec=VMEM):
    specs = {"s": SMEM, "v": VMEM, "h": HBM}
    moved = sum(a.size * a.dtype.itemsize for a in args)
    return pl.pallas_call(
        kernel,
        out_shape=[jax.ShapeDtypeStruct(shape, dtype) for shape, dtype in outs],
        in_specs=[specs[kind] for kind in ins],
        out_specs=[out_spec] * len(outs),
        scratch_shapes=list(scratch),
        compiler_params=pltpu.CompilerParams(vmem_limit_bytes=GRANT),
        cost_estimate=pl.CostEstimate(flops=flops, bytes_accessed=moved, transcendentals=0),
        name=name,
    )(*args)


def shards(rhs, diag, row_basis, col_basis, wl, bl, cross_w, cross_b, order):
    n = rhs.shape[2]
    rank = col_basis.shape[3]
    size = col_basis.shape[2]
    axes = ("leaf", "top")
    devices = lax.axis_size("leaf") * lax.axis_size("top")
    pos = lax.axis_index(axes).astype(jnp.int32).reshape(1)
    b = cross_b[:, 0]

    def swap(value, flip):
        return lax.ppermute(value, axes, [(i, i ^ flip) for i in range(devices)])

    def block(columns, dtype=BF):
        return ((2, columns, rank), dtype)

    mac = 8 * rank * rank
    half, quarter, eighth = n // 2, n // 4, n // 8
    qleaf_shape = ((2, n, rank), BF)
    hbm = [pltpu.with_memory_space_constraint(a, pltpu.HBM) for a in (order, rhs, col_basis, wl, cross_w[:, 0])]
    w_hbm = hbm[-1]
    q_other, send, xt, x, u, wl, w0 = call(
        "send_half", send_kernel, "shhhhh",
        [qleaf_shape, block(half), ((2, n, size), BF), (rhs.shape, BF), (col_basis.shape, BF),
         (wl.shape, BF), ((2, 1, 2, rank, rank), BF)],
        pos, *hbm,
        scratch=(pltpu.SMEM(order.shape, jnp.int32), pltpu.SemaphoreType.DMA((7,))),
        flops=mac * n * 3,
    )
    got0 = swap(send, 1)
    q_mine, keep0, own, w_low = call(
        "keep_half", keep_kernel, "ssvvvvh",
        [qleaf_shape, block(half), block(half, F32), ((2, 3, 2, rank, rank), BF)],
        pos, order, xt, u, wl, w0, w_hbm,
        scratch=(pltpu.SemaphoreType.DMA,), flops=mac * n * 3,
    )
    got0_other = swap(keep0, 1)
    keep1, send = call(
        "climb_0", climb_kernel(0, 0), "svvv", [block(quarter), block(quarter)],
        pos, got0, own, w0, flops=mac * half,
    )
    got1 = swap(send, 3)
    own, part_0, w_high = call(
        "shadow_1", shadow_1, "ssvvhvv",
        [block(quarter, F32), ((2, size, n), F32), ((2, 4, 2, rank, rank), BF)],
        pos, order, keep1, w_low, w_hbm, x, diag,
        scratch=(pltpu.SemaphoreType.DMA,), flops=mac * n * 5,
    )
    keep2, send = call(
        "climb_1", climb_kernel(1, 1), "svvv", [block(eighth), block(eighth)],
        pos, got1, own, w_low, flops=mac * quarter,
    )
    got2 = swap(send, 5)
    own, part_1 = call(
        "shadow_2", shadow_2, "ssvvvv", [block(eighth, F32), ((2, size, n), F32)],
        pos, order, keep2, w_low, x, diag, flops=mac * n * 5,
    )

    def climb(level, start, got, own, w):
        return call(
            "climb_%d" % level, climb_kernel(level, start), "svvv", [block(eighth)],
            pos, got, own, w, flops=mac * eighth,
        )[0]

    cleaf_shape = ((2, n, rank), BF)
    base_shape = ((2, 2 * size, half), F32)
    q3 = climb(2, 1, got2, own, w_low)
    got3 = swap(q3, 13)
    own, cleaf = call(
        "shadow_3", shadow_3, "s" + "v" * 7, [block(eighth, F32), cleaf_shape],
        pos, q3, w_low, b, bl, wl, q_mine, got0, flops=mac * n * 4,
    )
    q4 = climb(3, 1, got3, own, w_low)
    got4 = swap(q4, 17)
    own, top, base = call(
        "shadow_4", shadow_4, "ss" + "v" * 8,
        [block(eighth, F32), block(eighth, F32), base_shape],
        pos, order, q4, got3, w_high, b, row_basis, cleaf, part_0, part_1, flops=mac * n * 2,
    )
    q5 = climb(4, 4, got4, own, w_high)
    got5 = swap(q5, 49)
    own, top, path, rw0 = call(
        "shadow_5", shadow_5, "s" + "v" * 8,
        [block(eighth, F32), block(eighth, F32), block(rank), block(size)],
        pos, q5, got4, w_low, w_high, b, row_basis, wl, top, flops=mac * n * 3,
    )
    q6 = climb(5, 4, got5, own, w_high)
    got6 = swap(q6, 65)
    own, top, path, rw1 = call(
        "shadow_6", shadow_6, "s" + "v" * 8,
        [block(eighth, F32), block(eighth, F32), block(rank), block(size)],
        pos, q6, got5, w_high, b, row_basis, wl, top, path, flops=mac * n * 3,
    )
    q7 = climb(6, 4, got6, own, w_high)
    got7 = swap(q7, 193)
    top, path, c2, c2_oth = call(
        "shadow_7", shadow_7, "s" + "v" * 7,
        [block(eighth, F32), block(rank), block(eighth, F32), block(eighth, F32)],
        pos, got6, w_high, b, top, path, keep2, got2, flops=mac * n * 2,
    )
    mine, send = call(
        "top", top_kernel, "s" + "v" * 6, [block(eighth), block(eighth)],
        pos, got7, top, path, c2, c2_oth, w_low, flops=mac * eighth * 3,
    )
    got = swap(send, 5)
    c1, c1_oth, g0, g1 = call(
        "shadow_8", shadow_8, "s" + "v" * 7,
        [block(quarter, F32), block(quarter, F32), block(size), block(size)],
        pos, mine, keep1, got1, b, w0, rw0, rw1, flops=mac * n * 5,
    )
    mine, send = call(
        "down", down_kernel, "s" + "v" * 5, [block(quarter), block(quarter)],
        pos, mine, got, c1, c1_oth, w_low, flops=mac * quarter * 2,
    )
    got = swap(send, 3)
    mine_other = swap(mine, 1)
    (base_other,) = call(
        "shadow_9", shadow_9, "ss" + "v" * 9, [base_shape],
        pos, order, mine, q_other, got0_other, b, bl, wl, row_basis, part_0, part_1,
        scratch=(pltpu.VMEM(*cleaf_shape),), flops=mac * n * 4,
    )
    got, mine_other, base_other = lax.optimization_barrier((got, mine_other, base_other))
    got_other = swap(got, 1)
    piece = (2, 2, size, half)
    (done,) = call(
        "own_columns", own_kernel, "ss" + "v" * 5, [(piece, BF)],
        pos, order, mine, got, base, g0, g1, flops=mac * n * 2,
    )
    (out,) = call(
        "other_columns", last_kernel, "ss" + "v" * 6, [(rhs.shape, BF)],
        pos, order, mine_other, got_other, base_other, g0, g1, done,
        scratch=(pltpu.VMEM(piece, BF), pltpu.SemaphoreType.DMA((6,))),
        flops=mac * n * 2, out_spec=HBM,
    )
    return out


def solution(mesh):
    return jax.shard_map(
        shards,
        mesh=mesh,
        in_specs=(
            P(None, ("leaf", "top"), None),
            P(None, ("leaf", "top"), None, None),
            P(None, ("leaf", "top"), None, None),
            P(None, ("leaf", "top"), None, None),
            P(None, ("leaf", "top"), None, None, None),
            P(None, ("leaf", "top"), None, None),
            P(None, ("leaf", "top"), None, None, None, None),
            P(None, ("leaf", "top"), None, None, None),
            P(("leaf", "top"), None),
        ),
        out_specs=P(None, ("leaf", "top"), None),
        check_vma=False,
    )
```

time: 53.1 us -> 54.2 us (1.021)
  Pallas kernels: 20.1 us -> 22.4 us
  waiting for transfers between devices: 9.13 us -> 7.44 us
    pallas_call x21 -> x22, Pallas kernels: 20.1 us -> 22.4 us  [call(): pl.pallas_call(kernel, out_shape=[jax.ShapeDtypeStruct(shape, dtype) for...]
    ppermute x13, waiting for transfers between devices: 9.13 us -> 7.44 us  [swap(): return lax.ppermute(value, axes, [(i, i ^ flip) for i in range(devices)])]
  transfers between devices with their start and end apart: 13 -> 13, of which waited for: 8 -> 9; matrix products, arithmetic and copies ran while one was open for 0% -> 0% of each run, Pallas kernels for 26% -> 31%
where the time goes in v6:
time: 54.2 us; the launch traced here: 54 us
  starting transfers between devices  23.8 us (44%)
  Pallas kernels  22.4 us (41%)
  waiting for transfers between devices  7.44 us (14%)
    ppermute x13, starting transfers between devices, swap(): return lax.ppermute(value, axes, [(i, i ^ flip) for i in range(devices)])  23.8 us
    pallas_call x22, Pallas kernels, call(): pl.pallas_call(kernel, out_shape=[jax.ShapeDtypeStruct(shape, dtype) for...  22.4 us
    ppermute x13, waiting for transfers between devices, swap(): return lax.ppermute(value, axes, [(i, i ^ flip) for i in range(devices)])  7.44 us
  transfers between devices with their start and end apart: 13, of which 9 were waited for; matrix products, arithmetic and copies ran while one was open for 0% of the time, Pallas kernels for 31%

profile of v6, /device:TPU:1, one launch (start us, length us, event | category | flops | bytes accessed | tf_op | source)
XLA Modules:
  0.0 54.0 jit_solution(7676698060701806335)
XLA Ops:
  0.0 0.0 copy-start.4
  0.0 2.8 %send_half.1 = (bf16[2,256,256]{2,1,0:T(8,128)(2,1)S(1)}, bf16[2,128,256]{2,1,0:T(8,128)(2,1)S(1)}, bf16[2,256,512]{2,1,0:T(8,128)(2,1)S(1)}, bf16[2,1024,256]{2...) custom-call(s32[1]{0:T(128)} %bitcast.pos, ...), custom_call_target="tpu_custom_call" | custom-call | flops 402653184 | bytes 6815756 | tf_op jit(solution)/shard_map/send_half/pallas_call | solution.py:347
  2.8 3.3 %collective-permute-start = (bf16[2,128,256]{2,1,0:T(8,128)(2,1)S(1)}, bf16[2,128,256]{2,1,0:T(8,128)(2,1)S(1)}, u32[]{:S(2)}, u32[]{:S(2)}) collective-permute-start(bf16[2,128,256]{2,1,0:T(8,128)(2,1)S(1)} %get-tuple-element.53), channel_id=1, source_target_pairs={{0,1},{1,0},{2,3},{3,2},{4,5},{5,4},{6,7},{7,6},{8,9},{9,8},{10,11... | collective-permute-start | bytes 393224 | tf_op jit(solution)/shard_map/ppermute | solution.py:369
  6.1 0.0 copy-done.4
  6.1 0.0 copy-start.2
  6.1 2.3 %keep_half.1 = (bf16[2,256,256]{2,1,0:T(8,128)(2,1)S(1)}, bf16[2,128,256]{2,1,0:T(8,128)(2,1)S(1)}, f32[2,128,256]{2,1,0:T(8,128)S(1)}, bf16[2,3,2,256,256]{4,3,2,1,0:T(8,128)(2,1)S(1)}) custom-call(s32[1]{0:T(128)} %bitcast.pos, s32[1,2]{1,0:T(1,128)S(1)} %copy-done.4, bf16[2,256,512]{2,1,0:T(8,128)(2,1)S(1)} %get-tuple-element.54.xt, ...), custom_call_target="tpu_custom_call" | custom-call | flops 402653184 | bytes 6815756 | tf_op jit(solution)/shard_map/keep_half/pallas_call | solution.py:347
  8.5 0.0 collective-permute-done.got.got0
  8.5 0.2 climb_0.1
  8.7 0.1 collective-permute-start.1
  8.8 0.0 copy-done.2
  8.8 2.2 %shadow_1.1 = (f32[2,64,256]{2,1,0:T(8,128)S(1)}, f32[2,512,256]{2,1,0:T(8,128)S(1)}, bf16[2,4,2,256,256]{4,3,2,1,0:T(8,128)(2,1)S(1)}) custom-call(s32[1]{0:T(128)} %bitcast.pos, s32[1,2]{1,0:T(1,128)S(1)} %copy-done.4, bf16[2,64,256]{2,1,0:T(8,128)(2,1)S(1)} %get-tuple-element.60.keep.keep1, bf16[2,3,2,256,256]{4,3,2,1,0:T(8,128)(2,1)S(1)} %get-tuple-element.61.w.w_low, ...), custom_call_target="tpu_custom_call" | custom-call | flops 671088640 | bytes 8978444 | tf_op jit(solution)/shard_map/shadow_1/pallas_call | solution.py:347
  11.0 1.5 %collective-permute-done.1.got.got1 = bf16[2,64,256]{2,1,0:T(8,128)(2,1)S(1)} collective-permute-done((bf16[2,64,256]{2,1,0:T(8,128)(2,1)S(1)}, bf16[2,64,256]{2,1,0:T(8,128)(2,1)S(1)}, u32[]{:S(2)}, u32[]{:S(2)}) %collective-permute-start.1) | collective-permute-done | bytes 65568 | tf_op jit(solution)/shard_map/ppermute | solution.py:369
  12.5 0.2 climb_1.1
  12.7 1.9 %collective-permute-start.2 = (bf16[2,32,256]{2,1,0:T(8,128)(2,1)S(1)}, bf16[2,32,256]{2,1,0:T(8,128)(2,1)S(1)}, u32[]{:S(2)}, u32[]{:S(2)}) collective-permute-start(bf16[2,32,256]{2,1,0:T(8,128)(2,1)S(1)} %get-tuple-element.64), channel_id=1, source_target_pairs={{0,5},{1,4},{2,7},{3,6},{4,1},{5,0},{6,3},{7,2},{8,13},{9,12},{10,... | collective-permute-start | bytes 98312 | tf_op jit(solution)/shard_map/ppermute | solution.py:369
  14.6 0.0 copy-start
  14.6 0.0 copy-start.3
  14.6 1.3 %shadow_2.1 = (f32[2,32,256]{2,1,0:T(8,128)S(1)}, f32[2,512,256]{2,1,0:T(8,128)S(1)}) custom-call(s32[1]{0:T(128)} %bitcast.pos, s32[1,2]{1,0:T(1,128)S(1)} %copy-done.4, bf16[2,32,256]{2,1,0:T(8,128)(2,1)S(1)} %get-tuple-element.65.keep.keep2, bf16[2,3,2,256,256]{4,3,2,1,0:T(8,128)(2,1)S(1)} %get-tuple-element.61.w.w_low, ...), custom_call_target="tpu_custom_call" | custom-call | flops 671088640 | bytes 4751372 | tf_op jit(solution)/shard_map/shadow_2/pallas_call | solution.py:347
  15.9 1.6 %collective-permute-done.2.got.got2 = bf16[2,32,256]{2,1,0:T(8,128)(2,1)S(1)} collective-permute-done((bf16[2,32,256]{2,1,0:T(8,128)(2,1)S(1)}, bf16[2,32,256]{2,1,0:T(8,128)(2,1)S(1)}, u32[]{:S(2)}, u32[]{:S(2)}) %collective-permute-start.2) | collective-permute-done | bytes 32800 | tf_op jit(solution)/shard_map/ppermute | solution.py:369
  17.5 0.2 climb_2.1.q3
  17.7 3.9 %collective-permute-start.3 = (bf16[2,32,256]{2,1,0:T(8,128)(2,1)S(1)}, bf16[2,32,256]{2,1,0:T(8,128)(2,1)S(1)}, u32[]{:S(2)}, u32[]{:S(2)}) collective-permute-start(bf16[2,32,256]{2,1,0:T(8,128)(2,1)S(1)} %climb_2.1.q3), channel_id=1, source_target_pairs={{0,13},{1,12},{2,15},{3,14},{4,9},{5,8},{6,11},{7,10},{8,5},{9,4},... | collective-permute-start | bytes 98312 | tf_op jit(solution)/shard_map/ppermute | solution.py:369
  21.6 0.0 copy-done
  21.6 0.0 copy-done.3
  21.6 0.0 copy-start.1
  21.6 0.9 %shadow_3.1 = (f32[2,32,256]{2,1,0:T(8,128)S(1)}, bf16[2,256,256]{2,1,0:T(8,128)(2,1)S(1)}) custom-call(s32[1]{0:T(128)} %bitcast.pos, bf16[2,32,256]{2,1,0:T(8,128)(2,1)S(1)} %climb_2.1.q3, bf16[2,3,2,256,256]{4,3,2,1,0:T(8,128)(2,1)S(1)} %get-tuple-element.61.w.w_low, bf16[2,8,256,256]{3,2,1,0:T(8,128)(2,1)S(1)} %bitcast.3, ...), custom_call_target="tpu_custom_call" | custom-call | flops 536870912 | bytes 4882436 | tf_op jit(solution)/shard_map/shadow_3/pallas_call | solution.py:347
  22.5 0.9 %collective-permute-done.3.got.got3 = bf16[2,32,256]{2,1,0:T(8,128)(2,1)S(1)} collective-permute-done((bf16[2,32,256]{2,1,0:T(8,128)(2,1)S(1)}, bf16[2,32,256]{2,1,0:T(8,128)(2,1)S(1)}, u32[]{:S(2)}, u32[]{:S(2)}) %collective-permute-start.3) | collective-permute-done | bytes 32800 | tf_op jit(solution)/shard_map/ppermute | solution.py:369
  23.4 0.2 climb_3.1.q4
  23.5 1.6 %collective-permute-start.4 = (bf16[2,32,256]{2,1,0:T(8,128)(2,1)S(1)}, bf16[2,32,256]{2,1,0:T(8,128)(2,1)S(1)}, u32[]{:S(2)}, u32[]{:S(2)}) collective-permute-start(bf16[2,32,256]{2,1,0:T(8,128)(2,1)S(1)} %climb_3.1.q4), channel_id=1, source_target_pairs={{0,17},{1,16},{2,19},{3,18},{4,21},{5,20},{6,23},{7,22},{8,25},{9,... | collective-permute-start | bytes 98312 | tf_op jit(solution)/shard_map/ppermute | solution.py:369
  25.2 0.1 collective-permute-start.11
  25.2 0.0 copy-done.1
  25.3 1.4 %shadow_4.1 = (f32[2,32,256]{2,1,0:T(8,128)S(1)}, f32[2,32,256]{2,1,0:T(8,128)S(1)}, f32[2,1024,128]{2,1,0:T(8,128)S(1)}) custom-call(s32[1]{0:T(128)} %bitcast.pos, s32[1,2]{1,0:T(1,128)S(1)} %copy-done.4, bf16[2,32,256]{2,1,0:T(8,128)(2,1)S(1)} %climb_3.1.q4, bf16[2,32,256]{2,1,0:T(8,128)(2,1)S(1)} %collective-permute-done.3.got.got3, ...), custom_call_target="tpu_custom_call" | custom-call | flops 268435456 | bytes 7667724 | tf_op jit(solution)/shard_map/shadow_4/pallas_call | solution.py:347
  26.6 0.4 collective-permute-done.4.got.got4
  27.0 0.2 climb_4.1.q5
  27.2 2.9 %collective-permute-start.5 = (bf16[2,32,256]{2,1,0:T(8,128)(2,1)S(1)}, bf16[2,32,256]{2,1,0:T(8,128)(2,1)S(1)}, u32[]{:S(2)}, u32[]{:S(2)}) collective-permute-start(bf16[2,32,256]{2,1,0:T(8,128)(2,1)S(1)} %climb_4.1.q5), channel_id=1, source_target_pairs={{0,49},{1,48},{2,51},{3,50},{4,53},{5,52},{6,55},{7,54},{8,57},{9,... | collective-permute-start | bytes 98312 | tf_op jit(solution)/shard_map/ppermute | solution.py:369
  30.1 1.0 %shadow_5.1 = (f32[2,32,256]{2,1,0:T(8,128)S(1)}, f32[2,32,256]{2,1,0:T(8,128)S(1)}, bf16[2,256,256]{2,1,0:T(8,128)(2,1)S(1)}, bf16[2,512,256]{2,1,0:T(8,128)(2,1)S(1)}) custom-call(s32[1]{0:T(128)} %bitcast.pos, bf16[2,32,256]{2,1,0:T(8,128)(2,1)S(1)} %climb_4.1.q5, bf16[2,32,256]{2,1,0:T(8,128)(2,1)S(1)} %collective-permute-done.4.got.got4, ...), custom_call_target="tpu_custom_call" | custom-call | flops 402653184 | bytes 7471108 | tf_op jit(solution)/shard_map/shadow_5/pallas_call | solution.py:347
  31.1 0.8 %collective-permute-done.5.got.got5 = bf16[2,32,256]{2,1,0:T(8,128)(2,1)S(1)} collective-permute-done((bf16[2,32,256]{2,1,0:T(8,128)(2,1)S(1)}, bf16[2,32,256]{2,1,0:T(8,128)(2,1)S(1)}, u32[]{:S(2)}, u32[]{:S(2)}) %collective-permute-start.5) | collective-permute-done | bytes 32800 | tf_op jit(solution)/shard_map/ppermute | solution.py:369
  31.9 0.2 climb_5.1.q6
  32.1 1.7 %collective-permute-start.6 = (bf16[2,32,256]{2,1,0:T(8,128)(2,1)S(1)}, bf16[2,32,256]{2,1,0:T(8,128)(2,1)S(1)}, u32[]{:S(2)}, u32[]{:S(2)}) collective-permute-start(bf16[2,32,256]{2,1,0:T(8,128)(2,1)S(1)} %climb_5.1.q6), channel_id=1, source_target_pairs={{0,65},{1,64},{2,67},{3,66},{4,69},{5,68},{6,71},{7,70},{8,73},{9,... | collective-permute-start | bytes 98312 | tf_op jit(solution)/shard_map/ppermute | solution.py:369
  33.8 1.0 %shadow_6.1 = (f32[2,32,256]{2,1,0:T(8,128)S(1)}, f32[2,32,256]{2,1,0:T(8,128)S(1)}, bf16[2,256,256]{2,1,0:T(8,128)(2,1)S(1)}, bf16[2,512,256]{2,1,0:T(8,128)(2,1)S(1)}) custom-call(s32[1]{0:T(128)} %bitcast.pos, bf16[2,32,256]{2,1,0:T(8,128)(2,1)S(1)} %climb_5.1.q6, bf16[2,32,256]{2,1,0:T(8,128)(2,1)S(1)} %collective-permute-done.5.got.got5, ...), custom_call_target="tpu_custom_call" | custom-call | flops 402653184 | bytes 6160388 | tf_op jit(solution)/shard_map/shadow_6/pallas_call | solution.py:347
  34.8 0.7 %collective-permute-done.6.got.got6 = bf16[2,32,256]{2,1,0:T(8,128)(2,1)S(1)} collective-permute-done((bf16[2,32,256]{2,1,0:T(8,128)(2,1)S(1)}, bf16[2,32,256]{2,1,0:T(8,128)(2,1)S(1)}, u32[]{:S(2)}, u32[]{:S(2)}) %collective-permute-start.6) | collective-permute-done | bytes 32800 | tf_op jit(solution)/shard_map/ppermute | solution.py:369
  35.5 0.2 climb_6.1
  35.7 3.2 %collective-permute-start.7 = (bf16[2,32,256]{2,1,0:T(8,128)(2,1)S(1)}, bf16[2,32,256]{2,1,0:T(8,128)(2,1)S(1)}, u32[]{:S(2)}, u32[]{:S(2)}) collective-permute-start(bf16[2,32,256]{2,1,0:T(8,128)(2,1)S(1)} %climb_6.1), channel_id=1, source_target_pairs={{0,193},{1,192},{2,195},{3,194},{4,197},{5,196},{6,199},{7,198},{8... | collective-permute-start | bytes 98312 | tf_op jit(solution)/shard_map/ppermute | solution.py:369
  38.9 1.3 %shadow_7.1 = (f32[2,32,256]{2,1,0:T(8,128)S(1)}, bf16[2,256,256]{2,1,0:T(8,128)(2,1)S(1)}, f32[2,32,256]{2,1,0:T(8,128)S(1)}, f32[2,32,256]{2,1,0:T(8,128)S(1)}) custom-call(s32[1]{0:T(128)} %bitcast.pos, bf16[2,32,256]{2,1,0:T(8,128)(2,1)S(1)} %collective-permute-done.6.got.got6, bf16[2,4,2,256,256]{4,3,2,1,0:T(8,128)(2,1)S(1)} %get-tuple-element.69.w.w_high, ...), custom_call_target="tpu_custom_call" | custom-call | flops 268435456 | bytes 4620292 | tf_op jit(solution)/shard_map/shadow_7/pallas_call | solution.py:347
  40.2 0.2 collective-permute-done.7.got
  40.5 0.4 top.1
  40.9 2.3 %collective-permute-start.8 = (bf16[2,32,256]{2,1,0:T(8,128)(2,1)S(1)}, bf16[2,32,256]{2,1,0:T(8,128)(2,1)S(1)}, u32[]{:S(2)}, u32[]{:S(2)}) collective-permute-start(bf16[2,32,256]{2,1,0:T(8,128)(2,1)S(1)} %get-tuple-element.86), channel_id=1, source_target_pairs={{0,5},{1,4},{2,7},{3,6},{4,1},{5,0},{6,3},{7,2},{8,13},{9,12},{10,... | collective-permute-start | bytes 98312 | tf_op jit(solution)/shard_map/ppermute | solution.py:369
  43.2 1.1 %shadow_8.1 = (f32[2,64,256]{2,1,0:T(8,128)S(1)}, f32[2,64,256]{2,1,0:T(8,128)S(1)}, bf16[2,512,256]{2,1,0:T(8,128)(2,1)S(1)}, bf16[2,512,256]{2,1,0:T(8,128)(2,1)S(1)}) custom-call(s32[1]{0:T(128)} %bitcast.pos, bf16[2,32,256]{2,1,0:T(8,128)(2,1)S(1)} %get-tuple-element.85.mine, bf16[2,64,256]{2,1,0:T(8,128)(2,1)S(1)} %get-tuple-element.60.keep.keep1, ...), custom_call_target="tpu_custom_call" | custom-call | flops 671088640 | bytes 3833860 | tf_op jit(solution)/shard_map/shadow_8/pallas_call | solution.py:347
  44.4 1.0 %collective-permute-done.8.got = bf16[2,32,256]{2,1,0:T(8,128)(2,1)S(1)} collective-permute-done((bf16[2,32,256]{2,1,0:T(8,128)(2,1)S(1)}, bf16[2,32,256]{2,1,0:T(8,128)(2,1)S(1)}, u32[]{:S(2)}, u32[]{:S(2)}) %collective-permute-start.8) | collective-permute-done | bytes 32800 | tf_op jit(solution)/shard_map/ppermute | solution.py:369
  45.4 0.3 down.1
  45.7 2.4 %collective-permute-start.9 = (bf16[2,64,256]{2,1,0:T(8,128)(2,1)S(1)}, bf16[2,64,256]{2,1,0:T(8,128)(2,1)S(1)}, u32[]{:S(2)}, u32[]{:S(2)}) collective-permute-start(bf16[2,64,256]{2,1,0:T(8,128)(2,1)S(1)} %get-tuple-element.91), channel_id=1, source_target_pairs={{0,3},{1,2},{2,1},{3,0},{4,7},{5,6},{6,5},{7,4},{8,11},{9,10},{10,... | collective-permute-start | bytes 196616 | tf_op jit(solution)/shard_map/ppermute | solution.py:369
  48.1 0.2 collective-permute-start.10
  48.3 0.0 collective-permute-done.11.got0_other
  48.3 1.7 %shadow_9.1.base = f32[2,1024,128]{2,1,0:T(8,128)S(1)} custom-call(s32[1]{0:T(128)} %bitcast.pos, s32[1,2]{1,0:T(1,128)S(1)} %copy-done.4, bf16[2,64,256]{2,1,0:T(8,128)(2,1)S(1)} %get-tuple-element.92.mine, bf16[2,256,256]{2,1,0:T(8,128)(2,1)S(1)} %get-tuple-element.93.q_other, bf16[2,128,256]{2,1,0:T(8,128)(2,1)S(1)} %collective-permute-done.11.got0_other, ...), custom_call_target="tpu_custom_call" | custom-call | flops 536870912 | bytes 6488076 | tf_op jit(solution)/shard_map/shadow_9/pallas_call | solution.py:347
  50.0 0.2 collective-permute-done.9.got
  50.2 0.0 collective-permute-done.10.mine
  50.2 0.3 collective-permute-start.12
  50.5 1.0 %own_columns.1.done = bf16[2,2,512,128]{3,2,1,0:T(8,128)(2,1)S(1)} custom-call(s32[1]{0:T(128)} %bitcast.pos, s32[1,2]{1,0:T(1,128)S(1)} %copy-done.4, bf16[2,64,256]{2,1,0:T(8,128)(2,1)S(1)} %get-tuple-element.92.mine, bf16[2,64,256]{2,1,0:T(8,128)(2,1)S(1)} %collective-permute-done.9.got, f32[2,1024,128]{2,1,0:T(8,128)S(1)} %get-tuple-element.100.base, ...), custom_call_target="tpu_custom_call" | custom-call | flops 268435456 | bytes 2228236 | tf_op jit(solution)/shard_map/own_columns/pallas_call | solution.py:347
  51.5 0.0 collective-permute-done.12.got
  51.5 2.3 %other_columns.1 = bf16[2,1024,256]{2,1,0:T(8,128)(2,1)} custom-call(s32[1]{0:T(128)} %bitcast.pos, s32[1,2]{1,0:T(1,128)S(1)} %copy-done.4, bf16[2,64,256]{2,1,0:T(8,128)(2,1)S(1)} %collective-permute-done.10.mine, bf16[2,64,256]{2,1,0:T(8,128)(2,1)S(1)} %collective-permute-done.12.got, f32[2,1024,128]{2,1,0:T(8,128)S(1)} %shadow_9.1.base, ...), custom_call_target="tpu_custom_call" | custom-call | flops 268435456 | bytes 2752524 | tf_op jit(solution)/shard_map/other_columns/pallas_call | solution.py:347
Async XLA Ops:
  0.0 6.1 %copy-start.4 = (s32[1,2]{1,0:T(1,128)S(1)}, s32[1,2]{1,0:T(1,128)}, u32[]{:S(2)}) copy-start(s32[1,2]{1,0:T(1,128)} %order.15) | copy-start | bytes 28
  2.8 5.7 %collective-permute-start = (bf16[2,128,256]{2,1,0:T(8,128)(2,1)S(1)}, bf16[2,128,256]{2,1,0:T(8,128)(2,1)S(1)}, u32[]{:S(2)}, u32[]{:S(2)}) collective-permute-start(bf16[2,128,256]{2,1,0:T(8,128)(2,1)S(1)} %get-tuple-element.53), channel_id=1, source_target_pairs={{0,1},{1,0},{2,3},{3,2},{4,5},{5,4},{6,7},{7,6},{8,9},{9,8},{10,11... | collective-permute-start | bytes 393224 | tf_op jit(solution)/shard_map/ppermute | solution.py:369
  6.1 2.7 %copy-start.2 = (bf16[2,2,512,512]{3,2,1,0:T(8,128)(2,1)S(1)}, bf16[2,2,512,512]{3,2,1,0:T(8,128)(2,1)}, u32[]{:S(2)}) copy-start(bf16[2,2,512,512]{3,2,1,0:T(8,128)(2,1)} %d.3) | copy-start | bytes 6291460
  8.7 3.8 %collective-permute-start.1 = (bf16[2,64,256]{2,1,0:T(8,128)(2,1)S(1)}, bf16[2,64,256]{2,1,0:T(8,128)(2,1)S(1)}, u32[]{:S(2)}, u32[]{:S(2)}) collective-permute-start(bf16[2,64,256]{2,1,0:T(8,128)(2,1)S(1)} %get-tuple-element.59), channel_id=1, source_target_pairs={{0,3},{1,2},{2,1},{3,0},{4,7},{5,6},{6,5},{7,4},{8,11},{9,10},{10,... | collective-permute-start | bytes 196616 | tf_op jit(solution)/shard_map/ppermute | solution.py:369
  12.7 4.8 %collective-permute-start.2 = (bf16[2,32,256]{2,1,0:T(8,128)(2,1)S(1)}, bf16[2,32,256]{2,1,0:T(8,128)(2,1)S(1)}, u32[]{:S(2)}, u32[]{:S(2)}) collective-permute-start(bf16[2,32,256]{2,1,0:T(8,128)(2,1)S(1)} %get-tuple-element.64), channel_id=1, source_target_pairs={{0,5},{1,4},{2,7},{3,6},{4,1},{5,0},{6,3},{7,2},{8,13},{9,12},{10,... | collective-permute-start | bytes 98312 | tf_op jit(solution)/shard_map/ppermute | solution.py:369
  14.6 7.0 %copy-start = (bf16[2,1,8,256,256]{4,3,2,1,0:T(8,128)(2,1)S(1)}, bf16[2,1,8,256,256]{4,3,2,1,0:T(8,128)(2,1)}, u32[]{:S(2)}) copy-start(bf16[2,1,8,256,256]{4,3,2,1,0:T(8,128)(2,1)} %param.16) | copy-start | bytes 6291460
  14.6 7.0 %copy-start.3 = (bf16[2,1,256,256]{3,2,1,0:T(8,128)(2,1)S(1)}, bf16[2,1,256,256]{3,2,1,0:T(8,128)(2,1)}, u32[]{:S(2)}) copy-start(bf16[2,1,256,256]{3,2,1,0:T(8,128)(2,1)} %bl.3) | copy-start | bytes 786436
  17.7 5.7 %collective-permute-start.3 = (bf16[2,32,256]{2,1,0:T(8,128)(2,1)S(1)}, bf16[2,32,256]{2,1,0:T(8,128)(2,1)S(1)}, u32[]{:S(2)}, u32[]{:S(2)}) collective-permute-start(bf16[2,32,256]{2,1,0:T(8,128)(2,1)S(1)} %climb_2.1.q3), channel_id=1, source_target_pairs={{0,13},{1,12},{2,15},{3,14},{4,9},{5,8},{6,11},{7,10},{8,5},{9,4},... | collective-permute-start | bytes 98312 | tf_op jit(solution)/shard_map/ppermute | solution.py:369
  21.6 3.7 %copy-start.1 = (bf16[2,2,512,256]{3,2,1,0:T(8,128)(2,1)S(1)}, bf16[2,2,512,256]{3,2,1,0:T(8,128)(2,1)}, u32[]{:S(2)}) copy-start(bf16[2,2,512,256]{3,2,1,0:T(8,128)(2,1)} %r.7) | copy-start | bytes 3145732
  23.5 3.5 %collective-permute-start.4 = (bf16[2,32,256]{2,1,0:T(8,128)(2,1)S(1)}, bf16[2,32,256]{2,1,0:T(8,128)(2,1)S(1)}, u32[]{:S(2)}, u32[]{:S(2)}) collective-permute-start(bf16[2,32,256]{2,1,0:T(8,128)(2,1)S(1)} %climb_3.1.q4), channel_id=1, source_target_pairs={{0,17},{1,16},{2,19},{3,18},{4,21},{5,20},{6,23},{7,22},{8,25},{9,... | collective-permute-start | bytes 98312 | tf_op jit(solution)/shard_map/ppermute | solution.py:369
  25.2 23.1 %collective-permute-start.11 = (bf16[2,128,256]{2,1,0:T(8,128)(2,1)S(1)}, bf16[2,128,256]{2,1,0:T(8,128)(2,1)S(1)}, u32[]{:S(2)}, u32[]{:S(2)}) collective-permute-start(bf16[2,128,256]{2,1,0:T(8,128)(2,1)S(1)} %get-tuple-element.94), channel_id=1, source_target_pairs={{0,1},{1,0},{2,3},{3,2},{4,5},{5,4},{6,7},{7,6},{8,9},{9,8},{10,11... | collective-permute-start | bytes 393224 | tf_op jit(solution)/shard_map/ppermute | solution.py:369
  27.2 4.7 %collective-permute-start.5 = (bf16[2,32,256]{2,1,0:T(8,128)(2,1)S(1)}, bf16[2,32,256]{2,1,0:T(8,128)(2,1)S(1)}, u32[]{:S(2)}, u32[]{:S(2)}) collective-permute-start(bf16[2,32,256]{2,1,0:T(8,128)(2,1)S(1)} %climb_4.1.q5), channel_id=1, source_target_pairs={{0,49},{1,48},{2,51},{3,50},{4,53},{5,52},{6,55},{7,54},{8,57},{9,... | collective-permute-start | bytes 98312 | tf_op jit(solution)/shard_map/ppermute | solution.py:369
  32.1 3.5 %collective-permute-start.6 = (bf16[2,32,256]{2,1,0:T(8,128)(2,1)S(1)}, bf16[2,32,256]{2,1,0:T(8,128)(2,1)S(1)}, u32[]{:S(2)}, u32[]{:S(2)}) collective-permute-start(bf16[2,32,256]{2,1,0:T(8,128)(2,1)S(1)} %climb_5.1.q6), channel_id=1, source_target_pairs={{0,65},{1,64},{2,67},{3,66},{4,69},{5,68},{6,71},{7,70},{8,73},{9,... | collective-permute-start | bytes 98312 | tf_op jit(solution)/shard_map/ppermute | solution.py:369
  35.7 4.8 %collective-permute-start.7 = (bf16[2,32,256]{2,1,0:T(8,128)(2,1)S(1)}, bf16[2,32,256]{2,1,0:T(8,128)(2,1)S(1)}, u32[]{:S(2)}, u32[]{:S(2)}) collective-permute-start(bf16[2,32,256]{2,1,0:T(8,128)(2,1)S(1)} %climb_6.1), channel_id=1, source_target_pairs={{0,193},{1,192},{2,195},{3,194},{4,197},{5,196},{6,199},{7,198},{8... | collective-permute-start | bytes 98312 | tf_op jit(solution)/shard_map/ppermute | solution.py:369
  40.9 4.5 %collective-permute-start.8 = (bf16[2,32,256]{2,1,0:T(8,128)(2,1)S(1)}, bf16[2,32,256]{2,1,0:T(8,128)(2,1)S(1)}, u32[]{:S(2)}, u32[]{:S(2)}) collective-permute-start(bf16[2,32,256]{2,1,0:T(8,128)(2,1)S(1)} %get-tuple-element.86), channel_id=1, source_target_pairs={{0,5},{1,4},{2,7},{3,6},{4,1},{5,0},{6,3},{7,2},{8,13},{9,12},{10,... | collective-permute-start | bytes 98312 | tf_op jit(solution)/shard_map/ppermute | solution.py:369
  45.7 4.5 %collective-permute-start.9 = (bf16[2,64,256]{2,1,0:T(8,128)(2,1)S(1)}, bf16[2,64,256]{2,1,0:T(8,128)(2,1)S(1)}, u32[]{:S(2)}, u32[]{:S(2)}) collective-permute-start(bf16[2,64,256]{2,1,0:T(8,128)(2,1)S(1)} %get-tuple-element.91), channel_id=1, source_target_pairs={{0,3},{1,2},{2,1},{3,0},{4,7},{5,6},{6,5},{7,4},{8,11},{9,10},{10,... | collective-permute-start | bytes 196616 | tf_op jit(solution)/shard_map/ppermute | solution.py:369
  48.1 2.1 %collective-permute-start.10 = (bf16[2,64,256]{2,1,0:T(8,128)(2,1)S(1)}, bf16[2,64,256]{2,1,0:T(8,128)(2,1)S(1)}, u32[]{:S(2)}, u32[]{:S(2)}) collective-permute-start(bf16[2,64,256]{2,1,0:T(8,128)(2,1)S(1)} %get-tuple-element.92.mine), channel_id=1, source_target_pairs={{0,1},{1,0},{2,3},{3,2},{4,5},{5,4},{6,7},{7,6},{8,9},{9,8},{10,11... | collective-permute-start | bytes 196616 | tf_op jit(solution)/shard_map/ppermute | solution.py:369
  50.2 1.3 %collective-permute-start.12 = (bf16[2,64,256]{2,1,0:T(8,128)(2,1)S(1)}, bf16[2,64,256]{2,1,0:T(8,128)(2,1)S(1)}, u32[]{:S(2)}, u32[]{:S(2)}) collective-permute-start(bf16[2,64,256]{2,1,0:T(8,128)(2,1)S(1)} %collective-permute-done.9.got), channel_id=1, source_target_pairs={{0,1},{1,0},{2,3},{3,2},{4,5},{5,4},{6,7},{7,6},{8,9},{9,8},{10,11... | collective-permute-start | bytes 196616 | tf_op jit(solution)/shard_map/ppermute | solution.py:369

commit v7 on v6

--- a/solution.py
+++ b/solution.py
@@ -93,21 +93,12 @@
     return pl.ds(pl.multiple_of(half * n, n), n)
 
 
-class Levels:
-    def __init__(self, ref, start):
-        self.ref, self.start = ref, start
-
-    def __getitem__(self, key):
-        c, level, child = key
-        return self.ref[c, level - self.start, child]
-
-
 def parent(qleaf, wl):
     q = times(qleaf[0], wl[0, 0, 0], wl[1, 0, 0]) + times(qleaf[1], wl[0, 0, 1], wl[1, 0, 1])
     return q.astype(BF)
 
 
-def send_kernel(pos, order, x, u, wl, w, qleaf, send, xt, x_v, u_v, wl_v, w0, order_s, sems):
+def send_kernel(pos, order, x, u, wl, w, qleaf, send, xt, x_v, u_v, wl_v, w0, order_s, xs, sems):
     size = u.shape[2]
     half = x.shape[2] // 2
 
@@ -115,56 +106,46 @@
         at = pl.ds(block * size, size)
         return pltpu.make_async_copy(x.at[:, at], x_v.at[:, at], sems.at[block])
 
-    def u_copy(leaf):
-        return pltpu.make_async_copy(u.at[:, leaf], u_v.at[:, leaf], sems.at[2 + leaf])
-
-    order_copy = pltpu.make_async_copy(order, order_s, sems.at[4])
-    wl_copy = pltpu.make_async_copy(wl, wl_v, sems.at[5])
-    w_copy = pltpu.make_async_copy(w.at[:, 0], w0.at[:, 0], sems.at[6])
+    order_copy = pltpu.make_async_copy(order, order_s, sems.at[2])
+    u_copy = pltpu.make_async_copy(u, u_v, sems.at[3])
+    wl_copy = pltpu.make_async_copy(wl, wl_v, sems.at[4])
+    w_copy = pltpu.make_async_copy(w.at[:, 0], w0.at[:, 0], sems.at[5])
+    x_copy(0).start()
+    x_copy(1).start()
     order_copy.start()
-    for i in range(2):
-        x_copy(i).start()
-        u_copy(i).start()
+    u_copy.start()
     wl_copy.start()
     w_copy.start()
-    order_copy.wait()
-    first = order_s[0, 0]
-
-    def transposed(block, which):
-        at = pl.ds(block * size, size)
-        lanes = half_lanes(which, half)
-        return jnp.concatenate([x_v[0, at, lanes].T, x_v[1, at, lanes].T], axis=0)
-
     keep = side(pos, 0)
     for block in range(2):
         x_copy(block).wait()
-        xt[block] = transposed(block, keep)
-        xs = transposed(block, 1 - keep)
-        if block == 0:
-            u_copy(0).wait()
-            u_copy(1).wait()
-        leaf = first ^ block
-        qleaf[leaf] = times(xs, u_v[0, leaf], u_v[1, leaf]).astype(BF)
+        at = pl.ds(block * size, size)
+        for out, which in ((xs, 1 - keep), (xt, keep)):
+            lanes = half_lanes(which, half)
+            out[block, :half] = x_v[0, at, lanes].T
+            out[block, half:] = x_v[1, at, lanes].T
+    order_copy.wait()
+    u_copy.wait()
+    for block in range(2):
+        leaf = order_s[0, 0] ^ block
+        qleaf[leaf] = times(xs[block], u_v[0, leaf], u_v[1, leaf]).astype(BF)
     wl_copy.wait()
     put(send, parent(qleaf, wl_v))
     w_copy.wait()
 
 
-def keep_kernel(pos, order, xt, u, wl, w0, w, qleaf, keep, own, w_low, sem):
-    copy = pltpu.make_async_copy(w.at[:, pl.ds(1, 3)], w_low, sem)
-    copy.start()
+def keep_kernel(pos, order, xt, u, wl, w0, qleaf, keep, own):
     for block in range(2):
         leaf = order[0, 0] ^ block
         qleaf[leaf] = times(xt[block], u[0, leaf], u[1, leaf]).astype(BF)
     q = parent(qleaf, wl)
     put(keep, q)
     put(own, lift(q, w0, pos, 0))
-    copy.wait()
-
-
-def climb_kernel(level, start):
+
+
+def climb_kernel(level):
     def kernel(pos, got, own, w, *outs):
-        q = (rows(own) + lift(rows(got), Levels(w, start), pos, level, 1)).astype(BF)
+        q = (rows(own) + lift(rows(got), w, pos, level, 1)).astype(BF)
         if len(outs) == 2:
             split(q, side(pos, level + 1), *outs)
         else:
@@ -183,12 +164,9 @@
     out[1] = dot(jnp.concatenate([im, re], axis=1), xs)
 
 
-def shadow_1(pos, order, keep, w, w_all, x, d, own, part, w_high, sem):
-    copy = pltpu.make_async_copy(w_all.at[:, pl.ds(4, 4)], w_high, sem)
-    copy.start()
-    put(own, lift(rows(keep), Levels(w, 1), pos, 1))
+def shadow_1(pos, order, keep, w, x, d, own, part):
+    put(own, lift(rows(keep), w, pos, 1))
     direct(order, 0, x, d, part)
-    copy.wait()
 
 
 def leaf_coupled(pos, q, got, b, bl, wl, cleaf):
@@ -199,14 +177,15 @@
     cleaf[1] = (right + times_t(c0, wl[0, 0, 1], wl[1, 0, 1])).astype(BF)
 
 
-def shadow_2(pos, order, keep, w, x, d, own, part):
-    put(own, lift(rows(keep), Levels(w, 1), pos, 2))
+def shadow_2(pos, order, keep, w, x, d, b, bl, wl, q_mine, got0, own, part, cleaf):
+    put(own, lift(rows(keep), w, pos, 2))
     direct(order, 1, x, d, part)
-
-
-def shadow_3(pos, q3, w, b, bl, wl, q_mine, got0, own, cleaf):
-    put(own, lift(rows(q3), Levels(w, 1), pos, 3))
     leaf_coupled(pos, q_mine, got0, b, bl, wl, cleaf)
+
+
+def shadow_3(pos, q3, w, b, bl, wl, q_other, got0_other, own, cleaf):
+    put(own, lift(rows(q3), w, pos, 3))
+    leaf_coupled(pos, q_other, got0_other, b, bl, wl, cleaf)
 
 
 def set_base(pos, order, part, r, cleaf, parts, base):
@@ -224,7 +203,7 @@
 
 
 def shadow_4(pos, order, q4, got3, w, b, r, cleaf, part_0, part_1, own, top, base):
-    put(own, lift(rows(q4), Levels(w, 4), pos, 4))
+    put(own, lift(rows(q4), w, pos, 4))
     put(top, couple(rows(got3), b, pos, 3))
     set_base(pos, order, 0, r, cleaf, (part_0, part_1), base)
 
@@ -233,29 +212,27 @@
     put(out, times(jnp.concatenate([r[0, leaf], r[1, leaf]], axis=0), wl[0, 0, leaf], wl[1, 0, leaf]))
 
 
-def shadow_5(pos, q5, got4, w_low, w_high, b, r, wl, top, own, top_out, path, rw):
-    low, high = Levels(w_low, 1), Levels(w_high, 4)
-    put(own, lift(rows(q5), high, pos, 5))
+def shadow_5(pos, q5, got4, w, b, r, wl, top, own, top_out, path, rw):
+    put(own, lift(rows(q5), w, pos, 5))
     c4 = couple(rows(got4), b, pos, 4).astype(BF)
-    put(top_out, rows(top) + lower(c4, low, pos, 3))
+    put(top_out, rows(top) + lower(c4, w, pos, 3))
     w3 = bit(pos, 3)
-    put(path, lift(jnp.concatenate([low[0, 3, w3], low[1, 3, w3]], axis=0), high, pos, 4))
+    put(path, lift(jnp.concatenate([w[0, 3, w3], w[1, 3, w3]], axis=0), w, pos, 4))
     product(r, wl, 0, rw)
 
 
 def shadow_6(pos, q6, got5, w, b, r, wl, top, path, own, top_out, path_out, rw):
-    high = Levels(w, 4)
-    put(own, lift(rows(q6), high, pos, 6))
+    put(own, lift(rows(q6), w, pos, 6))
     c5 = couple(rows(got5), b, pos, 5).astype(BF)
     put(top_out, rows(top) + times_t(c5, path[0], path[1]))
-    put(path_out, lift(rows(path), high, pos, 5))
+    put(path_out, lift(rows(path), w, pos, 5))
     product(r, wl, 1, rw)
 
 
 def shadow_7(pos, got6, w, b, top, path, keep2, got2, top_out, path_out, c2, c2_oth):
     c6 = couple(rows(got6), b, pos, 6).astype(BF)
     put(top_out, rows(top) + times_t(c6, path[0], path[1]))
-    longer = lift(rows(path), Levels(w, 4), pos, 6).astype(BF)
+    longer = lift(rows(path), w, pos, 6).astype(BF)
     put(path_out, couple_path(longer, b, pos))
     put(c2, couple(rows(got2), b, pos, 2))
     put(c2_oth, couple(rows(keep2), b, pos, 2, 1))
@@ -271,9 +248,8 @@
 
 def top_kernel(pos, got, top, path, c_own, c_oth, w, own, send):
     h = (rows(top) + times_t(rows(got), path[0], path[1])).astype(BF)
-    low = Levels(w, 1)
-    put(own, rows(c_own) + lower(h, low, pos, 2))
-    put(send, rows(c_oth) + lower(h, low, pos, 2, 1))
+    put(own, rows(c_own) + lower(h, w, pos, 2))
+    put(send, rows(c_oth) + lower(h, w, pos, 2, 1))
 
 
 def shadow_8(pos, mine, keep1, got1, b, w0, rw0, rw1, c1, c1_oth, g0, g1):
@@ -285,13 +261,11 @@
 
 def down_kernel(pos, mine, got, c_own, c_oth, w, own, send):
     h = join(mine, got, side(pos, 2))
-    low = Levels(w, 1)
-    put(own, rows(c_own) + lower(h, low, pos, 1))
-    put(send, rows(c_oth) + lower(h, low, pos, 1, 1))
-
-
-def shadow_9(pos, order, mine, q_other, got0_other, b, bl, wl, r, part_0, part_1, base, cleaf):
-    leaf_coupled(pos, q_other, got0_other, b, bl, wl, cleaf)
+    put(own, rows(c_own) + lower(h, w, pos, 1))
+    put(send, rows(c_oth) + lower(h, w, pos, 1, 1))
+
+
+def shadow_9(pos, order, mine, r, cleaf, part_0, part_1, base):
     set_base(pos, order, 1, r, cleaf, (part_0, part_1), base)
 
 
@@ -329,7 +303,7 @@
     for leaf in range(2):
         at = pl.ds(pl.multiple_of((order[0, 0] ^ leaf) * size, size), size)
         store(done.at[leaf], 0, at)
-    for leaf, here, at in finish(pos, order, mine, got, base, (g0, g1), buf, size // 2):
+    for leaf, here, at in finish(pos, order, mine, got, base, (g0, g1), buf, size):
         store(buf.at[leaf, :, here], 1, at)
     for copy in copies:
         copy.wait()
@@ -363,6 +337,7 @@
     axes = ("leaf", "top")
     devices = lax.axis_size("leaf") * lax.axis_size("top")
     pos = lax.axis_index(axes).astype(jnp.int32).reshape(1)
+    w = cross_w[:, 0]
     b = cross_b[:, 0]
 
     def swap(value, flip):
@@ -374,90 +349,90 @@
     mac = 8 * rank * rank
     half, quarter, eighth = n // 2, n // 4, n // 8
     qleaf_shape = ((2, n, rank), BF)
-    hbm = [pltpu.with_memory_space_constraint(a, pltpu.HBM) for a in (order, rhs, col_basis, wl, cross_w[:, 0])]
-    w_hbm = hbm[-1]
+    hbm = [pltpu.with_memory_space_constraint(a, pltpu.HBM) for a in (order, rhs, col_basis, wl, w)]
     q_other, send, xt, x, u, wl, w0 = call(
         "send_half", send_kernel, "shhhhh",
         [qleaf_shape, block(half), ((2, n, size), BF), (rhs.shape, BF), (col_basis.shape, BF),
          (wl.shape, BF), ((2, 1, 2, rank, rank), BF)],
         pos, *hbm,
-        scratch=(pltpu.SMEM(order.shape, jnp.int32), pltpu.SemaphoreType.DMA((7,))),
+        scratch=(
+            pltpu.SMEM(order.shape, jnp.int32),
+            pltpu.VMEM((2, n, size), BF),
+            pltpu.SemaphoreType.DMA((6,)),
+        ),
         flops=mac * n * 3,
     )
     got0 = swap(send, 1)
-    q_mine, keep0, own, w_low = call(
-        "keep_half", keep_kernel, "ssvvvvh",
-        [qleaf_shape, block(half), block(half, F32), ((2, 3, 2, rank, rank), BF)],
-        pos, order, xt, u, wl, w0, w_hbm,
-        scratch=(pltpu.SemaphoreType.DMA,), flops=mac * n * 3,
+    q_mine, keep0, own = call(
+        "keep_half", keep_kernel, "ssvvvv", [qleaf_shape, block(half), block(half, F32)],
+        pos, order, xt, u, wl, w0, flops=mac * n * 3,
     )
     got0_other = swap(keep0, 1)
     keep1, send = call(
-        "climb_0", climb_kernel(0, 0), "svvv", [block(quarter), block(quarter)],
+        "climb_0", climb_kernel(0), "svvv", [block(quarter), block(quarter)],
         pos, got0, own, w0, flops=mac * half,
     )
     got1 = swap(send, 3)
-    own, part_0, w_high = call(
-        "shadow_1", shadow_1, "ssvvhvv",
-        [block(quarter, F32), ((2, size, n), F32), ((2, 4, 2, rank, rank), BF)],
-        pos, order, keep1, w_low, w_hbm, x, diag,
-        scratch=(pltpu.SemaphoreType.DMA,), flops=mac * n * 5,
+    own, part_0 = call(
+        "shadow_1", shadow_1, "ssvvvv", [block(quarter, F32), ((2, size, n), F32)],
+        pos, order, keep1, w, x, diag, flops=mac * n * 5,
     )
     keep2, send = call(
-        "climb_1", climb_kernel(1, 1), "svvv", [block(eighth), block(eighth)],
-        pos, got1, own, w_low, flops=mac * quarter,
+        "climb_1", climb_kernel(1), "svvv", [block(eighth), block(eighth)],
+        pos, got1, own, w, flops=mac * quarter,
     )
     got2 = swap(send, 5)
-    own, part_1 = call(
-        "shadow_2", shadow_2, "ssvvvv", [block(eighth, F32), ((2, size, n), F32)],
-        pos, order, keep2, w_low, x, diag, flops=mac * n * 5,
-    )
-
-    def climb(level, start, got, own, w):
+    cleaf_shape = ((2, n, rank), BF)
+    own, part_1, cleaf = call(
+        "shadow_2", shadow_2, "ss" + "v" * 9,
+        [block(eighth, F32), ((2, size, n), F32), cleaf_shape],
+        pos, order, keep2, w, x, diag, b, bl, wl, q_mine, got0, flops=mac * n * 8,
+    )
+
+    def climb(level, got, own):
         return call(
-            "climb_%d" % level, climb_kernel(level, start), "svvv", [block(eighth)],
+            "climb_%d" % level, climb_kernel(level), "svvv", [block(eighth)],
             pos, got, own, w, flops=mac * eighth,
         )[0]
 
-    cleaf_shape = ((2, n, rank), BF)
     base_shape = ((2, 2 * size, half), F32)
-    q3 = climb(2, 1, got2, own, w_low)
+    q3 = climb(2, got2, own)
     got3 = swap(q3, 13)
-    own, cleaf = call(
+    own, cleaf_other = call(
         "shadow_3", shadow_3, "s" + "v" * 7, [block(eighth, F32), cleaf_shape],
-        pos, q3, w_low, b, bl, wl, q_mine, got0, flops=mac * n * 4,
-    )
-    q4 = climb(3, 1, got3, own, w_low)
+        pos, q3, w, b, bl, wl, q_other, got0_other, flops=mac * n * 4,
+    )
+    q4 = climb(3, got3, own)
     got4 = swap(q4, 17)
     own, top, base = call(
         "shadow_4", shadow_4, "ss" + "v" * 8,
         [block(eighth, F32), block(eighth, F32), base_shape],
-        pos, order, q4, got3, w_high, b, row_basis, cleaf, part_0, part_1, flops=mac * n * 2,
-    )
-    q5 = climb(4, 4, got4, own, w_high)
+        pos, order, q4, got3, w, b, row_basis, cleaf, part_0, part_1, flops=mac * n * 2,
+    )
+    q5 = climb(4, got4, own)
     got5 = swap(q5, 49)
     own, top, path, rw0 = call(
-        "shadow_5", shadow_5, "s" + "v" * 8,
+        "shadow_5", shadow_5, "s" + "v" * 7,
         [block(eighth, F32), block(eighth, F32), block(rank), block(size)],
-        pos, q5, got4, w_low, w_high, b, row_basis, wl, top, flops=mac * n * 3,
-    )
-    q6 = climb(5, 4, got5, own, w_high)
+        pos, q5, got4, w, b, row_basis, wl, top, flops=mac * n * 3,
+    )
+    q6 = climb(5, got5, own)
     got6 = swap(q6, 65)
     own, top, path, rw1 = call(
         "shadow_6", shadow_6, "s" + "v" * 8,
         [block(eighth, F32), block(eighth, F32), block(rank), block(size)],
-        pos, q6, got5, w_high, b, row_basis, wl, top, path, flops=mac * n * 3,
-    )
-    q7 = climb(6, 4, got6, own, w_high)
+        pos, q6, got5, w, b, row_basis, wl, top, path, flops=mac * n * 3,
+    )
+    q7 = climb(6, got6, own)
     got7 = swap(q7, 193)
     top, path, c2, c2_oth = call(
         "shadow_7", shadow_7, "s" + "v" * 7,
         [block(eighth, F32), block(rank), block(eighth, F32), block(eighth, F32)],
-        pos, got6, w_high, b, top, path, keep2, got2, flops=mac * n * 2,
+        pos, got6, w, b, top, path, keep2, got2, flops=mac * n * 2,
     )
     mine, send = call(
         "top", top_kernel, "s" + "v" * 6, [block(eighth), block(eighth)],
-        pos, got7, top, path, c2, c2_oth, w_low, flops=mac * eighth * 3,
+        pos, got7, top, path, c2, c2_oth, w, flops=mac * eighth * 3,
     )
     got = swap(send, 5)
     c1, c1_oth, g0, g1 = call(
@@ -467,14 +442,13 @@
     )
     mine, send = call(
         "down", down_kernel, "s" + "v" * 5, [block(quarter), block(quarter)],
-        pos, mine, got, c1, c1_oth, w_low, flops=mac * quarter * 2,
+        pos, mine, got, c1, c1_oth, w, flops=mac * quarter * 2,
     )
     got = swap(send, 3)
     mine_other = swap(mine, 1)
     (base_other,) = call(
-        "shadow_9", shadow_9, "ss" + "v" * 9, [base_shape],
-        pos, order, mine, q_other, got0_other, b, bl, wl, row_basis, part_0, part_1,
-        scratch=(pltpu.VMEM(*cleaf_shape),), flops=mac * n * 4,
+        "shadow_9", shadow_9, "ss" + "v" * 5, [base_shape],
+        pos, order, mine, row_basis, cleaf_other, part_0, part_1, flops=mac * n * 2,
     )
     got, mine_other, base_other = lax.optimization_barrier((got, mine_other, base_other))
     got_other = swap(got, 1)

time: 54.2 us -> 53.1 us (0.980)
  Pallas kernels: 22.4 us -> 20.8 us
    pallas_call x22, Pallas kernels: 22.4 us -> 20.8 us  [call(): pl.pallas_call(kernel, out_shape=[jax.ShapeDtypeStruct(shape, dtype) for...]
  transfers between devices with their start and end apart: 13 -> 13, of which waited for: 9 -> 9; matrix products, arithmetic and copies ran while one was open for 0% -> 0% of each run, Pallas kernels for 31% -> 27%
where the time goes in v7:
time: 53.1 us; the launch traced here: 52.9 us
  starting transfers between devices  23.9 us (45%)
  Pallas kernels  20.8 us (39%)
  waiting for transfers between devices  7.91 us (15%)
    ppermute x13, starting transfers between devices, swap(): return lax.ppermute(value, axes, [(i, i ^ flip) for i in range(devices)])  23.9 us
    pallas_call x22, Pallas kernels, call(): pl.pallas_call(kernel, out_shape=[jax.ShapeDtypeStruct(shape, dtype) for...  20.8 us
    ppermute x13, waiting for transfers between devices, swap(): return lax.ppermute(value, axes, [(i, i ^ flip) for i in range(devices)])  7.91 us
  transfers between devices with their start and end apart: 13, of which 9 were waited for; matrix products, arithmetic and copies ran while one was open for 0% of the time, Pallas kernels for 27%

profile of v7, /device:TPU:1, one launch (start us, length us, event | category | flops | bytes accessed | tf_op | source)
XLA Modules:
  0.0 52.9 jit_solution(11214610527248275853)
XLA Ops:
  0.0 0.0 copy-start.5
  0.0 0.0 copy-start
  0.0 2.7 %send_half.1 = (bf16[2,256,256]{2,1,0:T(8,128)(2,1)S(1)}, bf16[2,128,256]{2,1,0:T(8,128)(2,1)S(1)}, bf16[2,256,512]{2,1,0:T(8,128)(2,1)S(1)}, bf16[2,1024,256]{2...) custom-call(s32[1]{0:T(128)} %bitcast.pos, ...), custom_call_target="tpu_custom_call" | custom-call | flops 402653184 | bytes 6815756 | tf_op jit(solution)/shard_map/send_half/pallas_call | solution.py:321
  2.8 0.0 copy-start.3
  2.8 3.3 %collective-permute-start = (bf16[2,128,256]{2,1,0:T(8,128)(2,1)S(1)}, bf16[2,128,256]{2,1,0:T(8,128)(2,1)S(1)}, u32[]{:S(2)}, u32[]{:S(2)}) collective-permute-start(bf16[2,128,256]{2,1,0:T(8,128)(2,1)S(1)} %get-tuple-element.52), channel_id=1, source_target_pairs={{0,1},{1,0},{2,3},{3,2},{4,5},{5,4},{6,7},{7,6},{8,9},{9,8},{10,11... | collective-permute-start | bytes 393224 | tf_op jit(solution)/shard_map/ppermute | solution.py:344
  6.1 0.0 copy-done.5
  6.1 1.6 %keep_half.1 = (bf16[2,256,256]{2,1,0:T(8,128)(2,1)S(1)}, bf16[2,128,256]{2,1,0:T(8,128)(2,1)S(1)}, f32[2,128,256]{2,1,0:T(8,128)S(1)}) custom-call(s32[1]{0:T(128)} %bitcast.pos, s32[1,2]{1,0:T(1,128)S(1)} %copy-done.5, bf16[2,256,512]{2,1,0:T(8,128)(2,1)S(1)} %get-tuple-element.53.xt, bf16[2,2,512,256]{3,2,1,0:T(8,128)(2,1)S(1)} %get-tuple-element.54.u, ...), custom_call_target="tpu_custom_call" | custom-call | flops 402653184 | bytes 2621452 | tf_op jit(solution)/shard_map/keep_half/pallas_call | solution.py:321
  7.7 0.0 collective-permute-done.got.got0
  7.7 0.2 climb_0.1
  8.0 0.1 collective-permute-start.1
  8.1 0.3 collective-permute-start.4
  8.4 0.0 copy-done
  8.4 0.0 copy-done.3
  8.4 1.3 %shadow_1.1 = (f32[2,64,256]{2,1,0:T(8,128)S(1)}, f32[2,512,256]{2,1,0:T(8,128)S(1)}) custom-call(s32[1]{0:T(128)} %bitcast.pos, s32[1,2]{1,0:T(1,128)S(1)} %copy-done.5, bf16[2,64,256]{2,1,0:T(8,128)(2,1)S(1)} %get-tuple-element.59.keep.keep1, bf16[2,8,2,256,256]{4,3,2,1,0:T(8,128)(2,1)S(1)} %bitcast.4, bf16[2,1024,256]{2,1,0:T(8,128)(2,1)S(1)} %get-tuple-element.60.x, ...), custom_call_target="tpu_custom_call" | custom-call | flops 671088640 | bytes 7405580 | tf_op jit(solution)/shard_map/shadow_1/pallas_call | solution.py:321
  9.7 2.1 %collective-permute-done.1.got.got1 = bf16[2,64,256]{2,1,0:T(8,128)(2,1)S(1)} collective-permute-done((bf16[2,64,256]{2,1,0:T(8,128)(2,1)S(1)}, bf16[2,64,256]{2,1,0:T(8,128)(2,1)S(1)}, u32[]{:S(2)}, u32[]{:S(2)}) %collective-permute-start.1) | collective-permute-done | bytes 65568 | tf_op jit(solution)/shard_map/ppermute | solution.py:344
  11.8 0.0 copy-start.1
  11.8 0.0 copy-start.4
  11.8 0.2 climb_1.1
  12.0 1.9 %collective-permute-start.2 = (bf16[2,32,256]{2,1,0:T(8,128)(2,1)S(1)}, bf16[2,32,256]{2,1,0:T(8,128)(2,1)S(1)}, u32[]{:S(2)}, u32[]{:S(2)}) collective-permute-start(bf16[2,32,256]{2,1,0:T(8,128)(2,1)S(1)} %get-tuple-element.62), channel_id=1, source_target_pairs={{0,5},{1,4},{2,7},{3,6},{4,1},{5,0},{6,3},{7,2},{8,13},{9,12},{10,... | collective-permute-start | bytes 98312 | tf_op jit(solution)/shard_map/ppermute | solution.py:344
  13.9 0.0 copy-done.1
  13.9 0.0 copy-done.4
  13.9 2.0 %shadow_2.1 = (f32[2,32,256]{2,1,0:T(8,128)S(1)}, f32[2,512,256]{2,1,0:T(8,128)S(1)}, bf16[2,256,256]{2,1,0:T(8,128)(2,1)S(1)}) custom-call(s32[1]{0:T(128)} %bitcast.pos, s32[1,2]{1,0:T(1,128)S(1)} %copy-done.5, bf16[2,32,256]{2,1,0:T(8,128)(2,1)S(1)} %get-tuple-element.63.keep.keep2, bf16[2,8,2,256,256]{4,3,2,1,0:T(8,128)(2,1)S(1)} %bitcast.6, ...), custom_call_target="tpu_custom_call" | custom-call | flops 1073741824 | bytes 10649612 | tf_op jit(solution)/shard_map/shadow_2/pallas_call | solution.py:321
  15.9 0.9 %collective-permute-done.2.got.got2 = bf16[2,32,256]{2,1,0:T(8,128)(2,1)S(1)} collective-permute-done((bf16[2,32,256]{2,1,0:T(8,128)(2,1)S(1)}, bf16[2,32,256]{2,1,0:T(8,128)(2,1)S(1)}, u32[]{:S(2)}, u32[]{:S(2)}) %collective-permute-start.2) | collective-permute-done | bytes 32800 | tf_op jit(solution)/shard_map/ppermute | solution.py:344
  16.8 0.2 climb_2.1.q3
  16.9 3.9 %collective-permute-start.3 = (bf16[2,32,256]{2,1,0:T(8,128)(2,1)S(1)}, bf16[2,32,256]{2,1,0:T(8,128)(2,1)S(1)}, u32[]{:S(2)}, u32[]{:S(2)}) collective-permute-start(bf16[2,32,256]{2,1,0:T(8,128)(2,1)S(1)} %climb_2.1.q3), channel_id=1, source_target_pairs={{0,13},{1,12},{2,15},{3,14},{4,9},{5,8},{6,11},{7,10},{8,5},{9,4},... | collective-permute-start | bytes 98312 | tf_op jit(solution)/shard_map/ppermute | solution.py:344
  20.8 0.0 collective-permute-done.4.got0_other
  20.8 0.9 %shadow_3.1 = (f32[2,32,256]{2,1,0:T(8,128)S(1)}, bf16[2,256,256]{2,1,0:T(8,128)(2,1)S(1)}) custom-call(s32[1]{0:T(128)} %bitcast.pos, bf16[2,32,256]{2,1,0:T(8,128)(2,1)S(1)} %climb_2.1.q3, bf16[2,8,2,256,256]{4,3,2,1,0:T(8,128)(2,1)S(1)} %bitcast.8, bf16[2,8,256,256]{3,2,1,0:T(8,128)(2,1)S(1)} %bitcast.20, bf16[2,1,256,256]{3,2,1,0:T(8,128)(2,1)S(1)} %copy-done.4, ...), custom_call_target="tpu_custom_call" | custom-call | flops 536870912 | bytes 7503876 | tf_op jit(solution)/shard_map/shadow_3/pallas_call | solution.py:321
  21.7 0.9 %collective-permute-done.3.got.got3 = bf16[2,32,256]{2,1,0:T(8,128)(2,1)S(1)} collective-permute-done((bf16[2,32,256]{2,1,0:T(8,128)(2,1)S(1)}, bf16[2,32,256]{2,1,0:T(8,128)(2,1)S(1)}, u32[]{:S(2)}, u32[]{:S(2)}) %collective-permute-start.3) | collective-permute-done | bytes 32800 | tf_op jit(solution)/shard_map/ppermute | solution.py:344
  22.6 0.0 copy-start.2
  22.6 0.2 climb_3.1.q4
  22.8 1.6 %collective-permute-start.5 = (bf16[2,32,256]{2,1,0:T(8,128)(2,1)S(1)}, bf16[2,32,256]{2,1,0:T(8,128)(2,1)S(1)}, u32[]{:S(2)}, u32[]{:S(2)}) collective-permute-start(bf16[2,32,256]{2,1,0:T(8,128)(2,1)S(1)} %climb_3.1.q4), channel_id=1, source_target_pairs={{0,17},{1,16},{2,19},{3,18},{4,21},{5,20},{6,23},{7,22},{8,25},{9,... | collective-permute-start | bytes 98312 | tf_op jit(solution)/shard_map/ppermute | solution.py:344
  24.4 0.0 copy-done.2
  24.4 1.4 %shadow_4.1 = (f32[2,32,256]{2,1,0:T(8,128)S(1)}, f32[2,32,256]{2,1,0:T(8,128)S(1)}, f32[2,1024,128]{2,1,0:T(8,128)S(1)}) custom-call(s32[1]{0:T(128)} %bitcast.pos, s32[1,2]{1,0:T(1,128)S(1)} %copy-done.5, bf16[2,32,256]{2,1,0:T(8,128)(2,1)S(1)} %climb_3.1.q4, bf16[2,32,256]{2,1,0:T(8,128)(2,1)S(1)} %collective-permute-done.3.got.got3, ...), custom_call_target="tpu_custom_call" | custom-call | flops 268435456 | bytes 9764876 | tf_op jit(solution)/shard_map/shadow_4/pallas_call | solution.py:321
  25.8 0.5 collective-permute-done.5.got.got4
  26.3 0.2 climb_4.1.q5
  26.5 2.9 %collective-permute-start.6 = (bf16[2,32,256]{2,1,0:T(8,128)(2,1)S(1)}, bf16[2,32,256]{2,1,0:T(8,128)(2,1)S(1)}, u32[]{:S(2)}, u32[]{:S(2)}) collective-permute-start(bf16[2,32,256]{2,1,0:T(8,128)(2,1)S(1)} %climb_4.1.q5), channel_id=1, source_target_pairs={{0,49},{1,48},{2,51},{3,50},{4,53},{5,52},{6,55},{7,54},{8,57},{9,... | collective-permute-start | bytes 98312 | tf_op jit(solution)/shard_map/ppermute | solution.py:344
  29.4 1.0 %shadow_5.1 = (f32[2,32,256]{2,1,0:T(8,128)S(1)}, f32[2,32,256]{2,1,0:T(8,128)S(1)}, bf16[2,256,256]{2,1,0:T(8,128)(2,1)S(1)}, bf16[2,512,256]{2,1,0:T(8,128)(2,1)S(1)}) custom-call(s32[1]{0:T(128)} %bitcast.pos, bf16[2,32,256]{2,1,0:T(8,128)(2,1)S(1)} %climb_4.1.q5, bf16[2,32,256]{2,1,0:T(8,128)(2,1)S(1)} %collective-permute-done.5.got.got4, ...), custom_call_target="tpu_custom_call" | custom-call | flops 402653184 | bytes 7995396 | tf_op jit(solution)/shard_map/shadow_5/pallas_call | solution.py:321
  30.4 0.8 %collective-permute-done.6.got.got5 = bf16[2,32,256]{2,1,0:T(8,128)(2,1)S(1)} collective-permute-done((bf16[2,32,256]{2,1,0:T(8,128)(2,1)S(1)}, bf16[2,32,256]{2,1,0:T(8,128)(2,1)S(1)}, u32[]{:S(2)}, u32[]{:S(2)}) %collective-permute-start.6) | collective-permute-done | bytes 32800 | tf_op jit(solution)/shard_map/ppermute | solution.py:344
  31.1 0.2 climb_5.1.q6
  31.3 1.7 %collective-permute-start.7 = (bf16[2,32,256]{2,1,0:T(8,128)(2,1)S(1)}, bf16[2,32,256]{2,1,0:T(8,128)(2,1)S(1)}, u32[]{:S(2)}, u32[]{:S(2)}) collective-permute-start(bf16[2,32,256]{2,1,0:T(8,128)(2,1)S(1)} %climb_5.1.q6), channel_id=1, source_target_pairs={{0,65},{1,64},{2,67},{3,66},{4,69},{5,68},{6,71},{7,70},{8,73},{9,... | collective-permute-start | bytes 98312 | tf_op jit(solution)/shard_map/ppermute | solution.py:344
  33.1 1.0 %shadow_6.1 = (f32[2,32,256]{2,1,0:T(8,128)S(1)}, f32[2,32,256]{2,1,0:T(8,128)S(1)}, bf16[2,256,256]{2,1,0:T(8,128)(2,1)S(1)}, bf16[2,512,256]{2,1,0:T(8,128)(2,1)S(1)}) custom-call(s32[1]{0:T(128)} %bitcast.pos, bf16[2,32,256]{2,1,0:T(8,128)(2,1)S(1)} %climb_5.1.q6, bf16[2,32,256]{2,1,0:T(8,128)(2,1)S(1)} %collective-permute-done.6.got.got5, ...), custom_call_target="tpu_custom_call" | custom-call | flops 402653184 | bytes 8257540 | tf_op jit(solution)/shard_map/shadow_6/pallas_call | solution.py:321
  34.1 0.7 %collective-permute-done.7.got.got6 = bf16[2,32,256]{2,1,0:T(8,128)(2,1)S(1)} collective-permute-done((bf16[2,32,256]{2,1,0:T(8,128)(2,1)S(1)}, bf16[2,32,256]{2,1,0:T(8,128)(2,1)S(1)}, u32[]{:S(2)}, u32[]{:S(2)}) %collective-permute-start.7) | collective-permute-done | bytes 32800 | tf_op jit(solution)/shard_map/ppermute | solution.py:344
  34.8 0.2 climb_6.1
  35.0 3.2 %collective-permute-start.8 = (bf16[2,32,256]{2,1,0:T(8,128)(2,1)S(1)}, bf16[2,32,256]{2,1,0:T(8,128)(2,1)S(1)}, u32[]{:S(2)}, u32[]{:S(2)}) collective-permute-start(bf16[2,32,256]{2,1,0:T(8,128)(2,1)S(1)} %climb_6.1), channel_id=1, source_target_pairs={{0,193},{1,192},{2,195},{3,194},{4,197},{5,196},{6,199},{7,198},{8... | collective-permute-start | bytes 98312 | tf_op jit(solution)/shard_map/ppermute | solution.py:344
  38.1 1.5 %shadow_7.1 = (f32[2,32,256]{2,1,0:T(8,128)S(1)}, bf16[2,256,256]{2,1,0:T(8,128)(2,1)S(1)}, f32[2,32,256]{2,1,0:T(8,128)S(1)}, f32[2,32,256]{2,1,0:T(8,128)S(1)}) custom-call(s32[1]{0:T(128)} %bitcast.pos, bf16[2,32,256]{2,1,0:T(8,128)(2,1)S(1)} %collective-permute-done.7.got.got6, bf16[2,8,2,256,256]{4,3,2,1,0:T(8,128)(2,1)S(1)} %bitcast.16, ...), custom_call_target="tpu_custom_call" | custom-call | flops 268435456 | bytes 6717444 | tf_op jit(solution)/shard_map/shadow_7/pallas_call | solution.py:321
  39.7 0.1 collective-permute-done.8.got
  39.7 0.4 top.1
  40.1 2.2 %collective-permute-start.9 = (bf16[2,32,256]{2,1,0:T(8,128)(2,1)S(1)}, bf16[2,32,256]{2,1,0:T(8,128)(2,1)S(1)}, u32[]{:S(2)}, u32[]{:S(2)}) collective-permute-start(bf16[2,32,256]{2,1,0:T(8,128)(2,1)S(1)} %get-tuple-element.85), channel_id=1, source_target_pairs={{0,5},{1,4},{2,7},{3,6},{4,1},{5,0},{6,3},{7,2},{8,13},{9,12},{10,... | collective-permute-start | bytes 98312 | tf_op jit(solution)/shard_map/ppermute | solution.py:344
  42.3 1.1 %shadow_8.1 = (f32[2,64,256]{2,1,0:T(8,128)S(1)}, f32[2,64,256]{2,1,0:T(8,128)S(1)}, bf16[2,512,256]{2,1,0:T(8,128)(2,1)S(1)}, bf16[2,512,256]{2,1,0:T(8,128)(2,1)S(1)}) custom-call(s32[1]{0:T(128)} %bitcast.pos, bf16[2,32,256]{2,1,0:T(8,128)(2,1)S(1)} %get-tuple-element.84.mine, bf16[2,64,256]{2,1,0:T(8,128)(2,1)S(1)} %get-tuple-element.59.keep.keep1, ...), custom_call_target="tpu_custom_call" | custom-call | flops 671088640 | bytes 3833860 | tf_op jit(solution)/shard_map/shadow_8/pallas_call | solution.py:321
  43.4 1.0 %collective-permute-done.9.got = bf16[2,32,256]{2,1,0:T(8,128)(2,1)S(1)} collective-permute-done((bf16[2,32,256]{2,1,0:T(8,128)(2,1)S(1)}, bf16[2,32,256]{2,1,0:T(8,128)(2,1)S(1)}, u32[]{:S(2)}, u32[]{:S(2)}) %collective-permute-start.9) | collective-permute-done | bytes 32800 | tf_op jit(solution)/shard_map/ppermute | solution.py:344
  44.5 0.3 down.1
  44.8 2.4 %collective-permute-start.10 = (bf16[2,64,256]{2,1,0:T(8,128)(2,1)S(1)}, bf16[2,64,256]{2,1,0:T(8,128)(2,1)S(1)}, u32[]{:S(2)}, u32[]{:S(2)}) collective-permute-start(bf16[2,64,256]{2,1,0:T(8,128)(2,1)S(1)} %get-tuple-element.90), channel_id=1, source_target_pairs={{0,3},{1,2},{2,1},{3,0},{4,7},{5,6},{6,5},{7,4},{8,11},{9,10},{10,... | collective-permute-start | bytes 196616 | tf_op jit(solution)/shard_map/ppermute | solution.py:344
  47.1 0.2 collective-permute-start.11
  47.3 1.0 %shadow_9.1.base = f32[2,1024,128]{2,1,0:T(8,128)S(1)} custom-call(s32[1]{0:T(128)} %bitcast.pos, s32[1,2]{1,0:T(1,128)S(1)} %copy-done.5, bf16[2,64,256]{2,1,0:T(8,128)(2,1)S(1)} %get-tuple-element.91.mine, bf16[2,2,512,256]{3,2,1,0:T(8,128)(2,1)S(1)} %copy-done.2, bf16[2,256,256]{2,1,0:T(8,128)(2,1)S(1)} %get-tuple-element.92.cleaf, ...), custom_call_target="tpu_custom_call" | custom-call | flops 268435456 | bytes 3473420 | tf_op jit(solution)/shard_map/shadow_9/pallas_call | solution.py:321
  48.4 0.9 %collective-permute-done.10.got = bf16[2,64,256]{2,1,0:T(8,128)(2,1)S(1)} collective-permute-done((bf16[2,64,256]{2,1,0:T(8,128)(2,1)S(1)}, bf16[2,64,256]{2,1,0:T(8,128)(2,1)S(1)}, u32[]{:S(2)}, u32[]{:S(2)}) %collective-permute-start.10) | collective-permute-done | bytes 65568 | tf_op jit(solution)/shard_map/ppermute | solution.py:344
  49.3 0.0 collective-permute-done.11.mine
  49.3 0.3 collective-permute-start.12
  49.6 1.0 %own_columns.1.done = bf16[2,2,512,128]{3,2,1,0:T(8,128)(2,1)S(1)} custom-call(s32[1]{0:T(128)} %bitcast.pos, s32[1,2]{1,0:T(1,128)S(1)} %copy-done.5, bf16[2,64,256]{2,1,0:T(8,128)(2,1)S(1)} %get-tuple-element.91.mine, bf16[2,64,256]{2,1,0:T(8,128)(2,1)S(1)} %collective-permute-done.10.got, f32[2,1024,128]{2,1,0:T(8,128)S(1)} %get-tuple-element.98.base, ...), custom_call_target="tpu_custom_call" | custom-call | flops 268435456 | bytes 2228236 | tf_op jit(solution)/shard_map/own_columns/pallas_call | solution.py:321
  50.6 0.0 collective-permute-done.12.got
  50.6 2.2 %other_columns.1 = bf16[2,1024,256]{2,1,0:T(8,128)(2,1)} custom-call(s32[1]{0:T(128)} %bitcast.pos, s32[1,2]{1,0:T(1,128)S(1)} %copy-done.5, bf16[2,64,256]{2,1,0:T(8,128)(2,1)S(1)} %collective-permute-done.11.mine, bf16[2,64,256]{2,1,0:T(8,128)(2,1)S(1)} %collective-permute-done.12.got, f32[2,1024,128]{2,1,0:T(8,128)S(1)} %shadow_9.1.base, ...), custom_call_target="tpu_custom_call" | custom-call | flops 268435456 | bytes 2752524 | tf_op jit(solution)/shard_map/other_columns/pallas_call | solution.py:321
Async XLA Ops:
  0.0 6.1 %copy-start.5 = (s32[1,2]{1,0:T(1,128)S(1)}, s32[1,2]{1,0:T(1,128)}, u32[]{:S(2)}) copy-start(s32[1,2]{1,0:T(1,128)} %order.15) | copy-start | bytes 28
  0.0 8.4 %copy-start = (bf16[2,1,8,2,256,256]{5,4,3,2,1,0:T(8,128)(2,1)S(1)}, bf16[2,1,8,2,256,256]{5,4,3,2,1,0:T(8,128)(2,1)}, u32[]{:S(2)}) copy-start(bf16[2,1,8,2,256,256]{5,4,3,2,1,0:T(8,128)(2,1)} %param.15) | copy-start | bytes 12582916
  2.8 5.6 %copy-start.3 = (bf16[2,2,512,512]{3,2,1,0:T(8,128)(2,1)S(1)}, bf16[2,2,512,512]{3,2,1,0:T(8,128)(2,1)}, u32[]{:S(2)}) copy-start(bf16[2,2,512,512]{3,2,1,0:T(8,128)(2,1)} %d.3) | copy-start | bytes 6291460
  2.8 5.0 %collective-permute-start = (bf16[2,128,256]{2,1,0:T(8,128)(2,1)S(1)}, bf16[2,128,256]{2,1,0:T(8,128)(2,1)S(1)}, u32[]{:S(2)}, u32[]{:S(2)}) collective-permute-start(bf16[2,128,256]{2,1,0:T(8,128)(2,1)S(1)} %get-tuple-element.52), channel_id=1, source_target_pairs={{0,1},{1,0},{2,3},{3,2},{4,5},{5,4},{6,7},{7,6},{8,9},{9,8},{10,11... | collective-permute-start | bytes 393224 | tf_op jit(solution)/shard_map/ppermute | solution.py:344
  8.0 3.8 %collective-permute-start.1 = (bf16[2,64,256]{2,1,0:T(8,128)(2,1)S(1)}, bf16[2,64,256]{2,1,0:T(8,128)(2,1)S(1)}, u32[]{:S(2)}, u32[]{:S(2)}) collective-permute-start(bf16[2,64,256]{2,1,0:T(8,128)(2,1)S(1)} %get-tuple-element.58), channel_id=1, source_target_pairs={{0,3},{1,2},{2,1},{3,0},{4,7},{5,6},{6,5},{7,4},{8,11},{9,10},{10,... | collective-permute-start | bytes 196616 | tf_op jit(solution)/shard_map/ppermute | solution.py:344
  8.1 12.8 %collective-permute-start.4 = (bf16[2,128,256]{2,1,0:T(8,128)(2,1)S(1)}, bf16[2,128,256]{2,1,0:T(8,128)(2,1)S(1)}, u32[]{:S(2)}, u32[]{:S(2)}) collective-permute-start(bf16[2,128,256]{2,1,0:T(8,128)(2,1)S(1)} %get-tuple-element.67), channel_id=1, source_target_pairs={{0,1},{1,0},{2,3},{3,2},{4,5},{5,4},{6,7},{7,6},{8,9},{9,8},{10,11... | collective-permute-start | bytes 393224 | tf_op jit(solution)/shard_map/ppermute | solution.py:344
  11.8 2.1 %copy-start.1 = (bf16[2,1,8,256,256]{4,3,2,1,0:T(8,128)(2,1)S(1)}, bf16[2,1,8,256,256]{4,3,2,1,0:T(8,128)(2,1)}, u32[]{:S(2)}) copy-start(bf16[2,1,8,256,256]{4,3,2,1,0:T(8,128)(2,1)} %param.16) | copy-start | bytes 6291460
  11.8 2.1 %copy-start.4 = (bf16[2,1,256,256]{3,2,1,0:T(8,128)(2,1)S(1)}, bf16[2,1,256,256]{3,2,1,0:T(8,128)(2,1)}, u32[]{:S(2)}) copy-start(bf16[2,1,256,256]{3,2,1,0:T(8,128)(2,1)} %bl.3) | copy-start | bytes 786436
  12.0 4.8 %collective-permute-start.2 = (bf16[2,32,256]{2,1,0:T(8,128)(2,1)S(1)}, bf16[2,32,256]{2,1,0:T(8,128)(2,1)S(1)}, u32[]{:S(2)}, u32[]{:S(2)}) collective-permute-start(bf16[2,32,256]{2,1,0:T(8,128)(2,1)S(1)} %get-tuple-element.62), channel_id=1, source_target_pairs={{0,5},{1,4},{2,7},{3,6},{4,1},{5,0},{6,3},{7,2},{8,13},{9,12},{10,... | collective-permute-start | bytes 98312 | tf_op jit(solution)/shard_map/ppermute | solution.py:344
  16.9 5.7 %collective-permute-start.3 = (bf16[2,32,256]{2,1,0:T(8,128)(2,1)S(1)}, bf16[2,32,256]{2,1,0:T(8,128)(2,1)S(1)}, u32[]{:S(2)}, u32[]{:S(2)}) collective-permute-start(bf16[2,32,256]{2,1,0:T(8,128)(2,1)S(1)} %climb_2.1.q3), channel_id=1, source_target_pairs={{0,13},{1,12},{2,15},{3,14},{4,9},{5,8},{6,11},{7,10},{8,5},{9,4},... | collective-permute-start | bytes 98312 | tf_op jit(solution)/shard_map/ppermute | solution.py:344
  22.6 1.8 %copy-start.2 = (bf16[2,2,512,256]{3,2,1,0:T(8,128)(2,1)S(1)}, bf16[2,2,512,256]{3,2,1,0:T(8,128)(2,1)}, u32[]{:S(2)}) copy-start(bf16[2,2,512,256]{3,2,1,0:T(8,128)(2,1)} %r.7) | copy-start | bytes 3145732
  22.8 3.5 %collective-permute-start.5 = (bf16[2,32,256]{2,1,0:T(8,128)(2,1)S(1)}, bf16[2,32,256]{2,1,0:T(8,128)(2,1)S(1)}, u32[]{:S(2)}, u32[]{:S(2)}) collective-permute-start(bf16[2,32,256]{2,1,0:T(8,128)(2,1)S(1)} %climb_3.1.q4), channel_id=1, source_target_pairs={{0,17},{1,16},{2,19},{3,18},{4,21},{5,20},{6,23},{7,22},{8,25},{9,... | collective-permute-start | bytes 98312 | tf_op jit(solution)/shard_map/ppermute | solution.py:344
  26.5 4.7 %collective-permute-start.6 = (bf16[2,32,256]{2,1,0:T(8,128)(2,1)S(1)}, bf16[2,32,256]{2,1,0:T(8,128)(2,1)S(1)}, u32[]{:S(2)}, u32[]{:S(2)}) collective-permute-start(bf16[2,32,256]{2,1,0:T(8,128)(2,1)S(1)} %climb_4.1.q5), channel_id=1, source_target_pairs={{0,49},{1,48},{2,51},{3,50},{4,53},{5,52},{6,55},{7,54},{8,57},{9,... | collective-permute-start | bytes 98312 | tf_op jit(solution)/shard_map/ppermute | solution.py:344
  31.3 3.5 %collective-permute-start.7 = (bf16[2,32,256]{2,1,0:T(8,128)(2,1)S(1)}, bf16[2,32,256]{2,1,0:T(8,128)(2,1)S(1)}, u32[]{:S(2)}, u32[]{:S(2)}) collective-permute-start(bf16[2,32,256]{2,1,0:T(8,128)(2,1)S(1)} %climb_5.1.q6), channel_id=1, source_target_pairs={{0,65},{1,64},{2,67},{3,66},{4,69},{5,68},{6,71},{7,70},{8,73},{9,... | collective-permute-start | bytes 98312 | tf_op jit(solution)/shard_map/ppermute | solution.py:344
  35.0 4.8 %collective-permute-start.8 = (bf16[2,32,256]{2,1,0:T(8,128)(2,1)S(1)}, bf16[2,32,256]{2,1,0:T(8,128)(2,1)S(1)}, u32[]{:S(2)}, u32[]{:S(2)}) collective-permute-start(bf16[2,32,256]{2,1,0:T(8,128)(2,1)S(1)} %climb_6.1), channel_id=1, source_target_pairs={{0,193},{1,192},{2,195},{3,194},{4,197},{5,196},{6,199},{7,198},{8... | collective-permute-start | bytes 98312 | tf_op jit(solution)/shard_map/ppermute | solution.py:344
  40.1 4.3 %collective-permute-start.9 = (bf16[2,32,256]{2,1,0:T(8,128)(2,1)S(1)}, bf16[2,32,256]{2,1,0:T(8,128)(2,1)S(1)}, u32[]{:S(2)}, u32[]{:S(2)}) collective-permute-start(bf16[2,32,256]{2,1,0:T(8,128)(2,1)S(1)} %get-tuple-element.85), channel_id=1, source_target_pairs={{0,5},{1,4},{2,7},{3,6},{4,1},{5,0},{6,3},{7,2},{8,13},{9,12},{10,... | collective-permute-start | bytes 98312 | tf_op jit(solution)/shard_map/ppermute | solution.py:344
  44.8 4.5 %collective-permute-start.10 = (bf16[2,64,256]{2,1,0:T(8,128)(2,1)S(1)}, bf16[2,64,256]{2,1,0:T(8,128)(2,1)S(1)}, u32[]{:S(2)}, u32[]{:S(2)}) collective-permute-start(bf16[2,64,256]{2,1,0:T(8,128)(2,1)S(1)} %get-tuple-element.90), channel_id=1, source_target_pairs={{0,3},{1,2},{2,1},{3,0},{4,7},{5,6},{6,5},{7,4},{8,11},{9,10},{10,... | collective-permute-start | bytes 196616 | tf_op jit(solution)/shard_map/ppermute | solution.py:344
  47.1 2.2 %collective-permute-start.11 = (bf16[2,64,256]{2,1,0:T(8,128)(2,1)S(1)}, bf16[2,64,256]{2,1,0:T(8,128)(2,1)S(1)}, u32[]{:S(2)}, u32[]{:S(2)}) collective-permute-start(bf16[2,64,256]{2,1,0:T(8,128)(2,1)S(1)} %get-tuple-element.91.mine), channel_id=1, source_target_pairs={{0,1},{1,0},{2,3},{3,2},{4,5},{5,4},{6,7},{7,6},{8,9},{9,8},{10,11... | collective-permute-start | bytes 196616 | tf_op jit(solution)/shard_map/ppermute | solution.py:344
  49.3 1.3 %collective-permute-start.12 = (bf16[2,64,256]{2,1,0:T(8,128)(2,1)S(1)}, bf16[2,64,256]{2,1,0:T(8,128)(2,1)S(1)}, u32[]{:S(2)}, u32[]{:S(2)}) collective-permute-start(bf16[2,64,256]{2,1,0:T(8,128)(2,1)S(1)} %collective-permute-done.10.got), channel_id=1, source_target_pairs={{0,1},{1,0},{2,3},{3,2},{4,5},{5,4},{6,7},{7,6},{8,9},{9,8},{10,11... | collective-permute-start | bytes 196616 | tf_op jit(solution)/shard_map/ppermute | solution.py:344

commit v8 on v7

v8 whole, which is shorter than its diff:
```python
import jax
import jax.numpy as jnp
from jax import lax
from jax.experimental import pallas as pl
from jax.experimental.pallas import tpu as pltpu
from jax.sharding import PartitionSpec as P

BF = jnp.bfloat16
F32 = jnp.float32
NN = (((1,), (0,)), ((), ()))
NT = (((1,), (1,)), ((), ()))


def dot(a, b, dims=NN):
    return lax.dot_general(a, b, dims, preferred_element_type=F32)


def widen(a):
    half = a.shape[0] // 2
    re, im = a[:half], a[half:]
    return jnp.concatenate(
        [jnp.concatenate([re, -im], axis=1), jnp.concatenate([im, re], axis=1)], axis=0
    )


def times(a, w_re, w_im):
    return dot(widen(a), jnp.concatenate([w_re, w_im], axis=0))


def times_t(a, w_re, w_im):
    return dot(widen(a), jnp.concatenate([w_re, w_im], axis=1), NT)


def rows(ref):
    return jnp.concatenate([ref[0], ref[1]], axis=0)


def put(ref, value):
    half = value.shape[0] // 2
    ref[0] = value[:half].astype(ref.dtype)
    ref[1] = value[half:].astype(ref.dtype)


def bit(pos, level):
    return (pos[0] >> level) & 1


def lift(q, w, pos, level, flip=0):
    child = bit(pos, level) ^ flip
    return times(q, w[0, level, child], w[1, level, child])


def lower(h, w, pos, level, flip=0):
    child = bit(pos, level) ^ flip
    return times_t(h, w[0, level, child], w[1, level, child])


def couple(q, b, pos, level, flip=0):
    return lax.cond(
        (bit(pos, level) ^ flip) == 0,
        lambda: times_t(q, b[0, level], b[1, level]),
        lambda: times(q, b[0, level], b[1, level]),
    )


def split(value, side, keep, send):
    half = value.shape[0] // 2
    part = half // 2
    for c in range(2):
        low = value[c * half : c * half + part]
        high = value[c * half + part : (c + 1) * half]
        keep[c] = jnp.where(side == 0, low, high)
        send[c] = jnp.where(side == 0, high, low)


def join(own, got, side):
    parts = []
    for c in range(2):
        parts.append(jnp.where(side == 0, own[c], got[c]))
        parts.append(jnp.where(side == 0, got[c], own[c]))
    return jnp.concatenate(parts, axis=0)


def side(pos, level):
    if level == 0:
        return (pos[0] ^ (pos[0] >> 1) ^ (pos[0] >> 2) ^ (pos[0] >> 4) ^ (pos[0] >> 6)) & 1
    if level == 1:
        return bit(pos, 1)
    return bit(pos, 2) ^ bit(pos, 3)


def half_lanes(half, n):
    return pl.ds(pl.multiple_of(half * n, n), n)


def parent(qleaf, wl):
    q = times(qleaf[0], wl[0, 0, 0], wl[1, 0, 0]) + times(qleaf[1], wl[0, 0, 1], wl[1, 0, 1])
    return q.astype(BF)


def send_kernel(pos, order, x, u, wl, w, qleaf, send, xt, x_v, u_v, wl_v, w0, order_s, sems):
    size = u.shape[2]
    part = x.shape[2] // 4

    def x_copy(block):
        at = pl.ds(block * size, size)
        return pltpu.make_async_copy(x.at[:, at], x_v.at[:, at], sems.at[block])

    order_copy = pltpu.make_async_copy(order, order_s, sems.at[2])
    u_copy = pltpu.make_async_copy(u, u_v, sems.at[3])
    wl_copy = pltpu.make_async_copy(wl, wl_v, sems.at[4])
    w_copy = pltpu.make_async_copy(w.at[:, 0], w0.at[:, 0], sems.at[5])
    x_copy(0).start()
    x_copy(1).start()
    order_copy.start()
    u_copy.start()
    wl_copy.start()
    w_copy.start()
    for block in range(2):
        x_copy(block).wait()
        at = pl.ds(block * size, size)
        for c in range(2):
            turned = x_v[c, at].T
            for s1 in range(2):
                for s0 in range(2):
                    here = (2 * s1 + s0) * part
                    to = (2 * c + s1) * part
                    xt[s0, block, to : to + part] = turned[here : here + part]
    order_copy.wait()
    u_copy.wait()
    share = 1 - side(pos, 0)
    for block in range(2):
        leaf = order_s[0, 0] ^ block
        qleaf[leaf] = times(xt[share, block], u_v[0, leaf], u_v[1, leaf]).astype(BF)
    wl_copy.wait()
    put(send, parent(qleaf, wl_v))
    w_copy.wait()


def keep_kernel(pos, order, xt, u, wl, w0, qleaf, keep, own):
    share = side(pos, 0)
    for block in range(2):
        leaf = order[0, 0] ^ block
        qleaf[leaf] = times(xt[share, block], u[0, leaf], u[1, leaf]).astype(BF)
    q = parent(qleaf, wl)
    put(keep, q)
    put(own, lift(q, w0, pos, 0))


def climb_kernel(level):
    def kernel(pos, got, own, w, *outs):
        q = (rows(own) + lift(rows(got), w, pos, level, 1)).astype(BF)
        if len(outs) == 2:
            split(q, side(pos, level + 1), *outs)
        else:
            put(outs[0], q)

    return kernel


def direct(order, block, x, d, out):
    size = d.shape[2]
    leaf = order[0, 0] ^ block
    at = pl.ds(block * size, size)
    xs = jnp.concatenate([x[0, at], x[1, at]], axis=0)
    re, im = d[0, leaf], d[1, leaf]
    out[0] = dot(jnp.concatenate([re, -im], axis=1), xs)
    out[1] = dot(jnp.concatenate([im, re], axis=1), xs)


def stack(w, level, child):
    return jnp.concatenate([w[0, level, child], w[1, level, child]], axis=0)


def shadow_1(pos, order, keep, w, w0, wl, x, d, own, part, paths):
    put(own, lift(rows(keep), w, pos, 1))
    two = lift(stack(w0, 0, bit(pos, 0)), w, pos, 1).astype(BF)
    half = two.shape[0] // 2
    for leaf in range(2):
        put(paths.at[leaf], times(stack(wl, 0, leaf), two[:half], two[half:]))
    direct(order, 0, x, d, part)


def product(r, paths, leaf, out):
    put(out, times(rows(r.at[:, leaf]), paths[leaf, 0], paths[leaf, 1]))


def shadow_2(pos, order, keep, w, x, d, r, paths, own, part, g):
    put(own, lift(rows(keep), w, pos, 2))
    direct(order, 1, x, d, part)
    product(r, paths, 0, g)


def shadow_3(pos, q3, w, b, r, paths, keep2, got2, own, c2, c2_oth, g):
    put(own, lift(rows(q3), w, pos, 3))
    put(c2, couple(rows(got2), b, pos, 2))
    put(c2_oth, couple(rows(keep2), b, pos, 2, 1))
    product(r, paths, 1, g)


def leaf_coupled(pos, q, got0, got1, got1_far, b, bl, w0, wl, cleaf):
    c1 = couple(join(got1, got1_far, bit(pos, 1)), b, pos, 1).astype(BF)
    c0 = (couple(rows(got0), b, pos, 0) + lower(c1, w0, pos, 0)).astype(BF)
    left = times_t(q[1], bl[0, 0], bl[1, 0])
    right = times(q[0], bl[0, 0], bl[1, 0])
    put(cleaf.at[0], left + times_t(c0, wl[0, 0, 0], wl[1, 0, 0]))
    put(cleaf.at[1], right + times_t(c0, wl[0, 0, 1], wl[1, 0, 1]))


def shares(pos, mine, other):
    a = side(pos, 0)
    half = mine.shape[0] // 2
    low = jnp.where(a == 0, mine, other)
    high = jnp.where(a == 0, other, mine)
    return jnp.concatenate([low[:half], high[:half], low[half:], high[half:]], axis=0)


def set_base(pos, order, tile, r, cleaf, cleaf_other, parts, base):
    n = base.shape[2]
    size = r.shape[2]
    part = n // 2
    at = pl.ds(pl.multiple_of(tile * part, part), part)
    lanes = half_lanes(tile, n)
    for block, direct_part in enumerate(parts):
        leaf = order[0, 0] ^ block
        h = [jnp.concatenate([c[leaf, 0, at], c[leaf, 1, at]], axis=0) for c in (cleaf, cleaf_other)]
        basis = jnp.concatenate([r[0, leaf], r[1, leaf]], axis=1)
        add = dot(basis, widen(shares(pos, *h)), NT)
        for c in range(2):
            base[c, pl.ds(block * size, size)] = (
                direct_part[c, :, lanes] + add[:, c * n : (c + 1) * n]
            )


def shadow_4(pos, q4, got3, w, b, own, top):
    put(own, lift(rows(q4), w, pos, 4))
    put(top, couple(rows(got3), b, pos, 3))


def shadow_5(pos, q5, got4, w, b, top, own, top_out, path_5, path_6):
    put(own, lift(rows(q5), w, pos, 5))
    c4 = couple(rows(got4), b, pos, 4).astype(BF)
    put(top_out, rows(top) + lower(c4, w, pos, 3))
    path = lift(stack(w, 3, bit(pos, 3)), w, pos, 4).astype(BF)
    put(path_5, path)
    put(path_6, lift(path, w, pos, 5))


def shadow_6(pos, q6, got5, w, b, top, path, q, got0, got1, got1_far, bl, w0, wl, own, top_out, cleaf):
    put(own, lift(rows(q6), w, pos, 6))
    c5 = couple(rows(got5), b, pos, 5).astype(BF)
    put(top_out, rows(top) + times_t(c5, path[0], path[1]))
    leaf_coupled(pos, q, got0, got1, got1_far, b, bl, w0, wl, cleaf)


def shadow_7(pos, got6, w, b, top, path, q, got0, got1, got1_far, bl, w0, wl, top_out, path_out, cleaf):
    c6 = couple(rows(got6), b, pos, 6).astype(BF)
    put(top_out, rows(top) + times_t(c6, path[0], path[1]))
    longer = lift(rows(path), w, pos, 6).astype(BF)
    put(path_out, couple_path(longer, b, pos))
    leaf_coupled(pos, q, got0, got1, got1_far, b, bl, w0, wl, cleaf)


def couple_path(path, b, pos):
    return lax.cond(
        bit(pos, 7) == 0,
        lambda: times(path, b[0, 7], b[1, 7]),
        lambda: times_t(path, b[0, 7], b[1, 7]),
    )


def top_kernel(pos, got, top, path, c_oth, w, send, h_out):
    h = (rows(top) + times_t(rows(got), path[0], path[1])).astype(BF)
    put(h_out, h)
    put(send, rows(c_oth) + lower(h, w, pos, 2, 1))


def own_kernel(pos, h, send, c_own, w, own):
    put(own, rows(c_own) + lower(rows(h), w, pos, 2))


def shadow_8(pos, order, send, r, cleaf, cleaf_other, part_0, part_1, base):
    set_base(pos, order, bit(pos, 1), r, cleaf, cleaf_other, (part_0, part_1), base)


def shadow_9(pos, order, got, far, far_other, r, cleaf, cleaf_other, part_0, part_1, base):
    set_base(pos, order, 1 - bit(pos, 1), r, cleaf, cleaf_other, (part_0, part_1), base)


def finish(pos, order, h_mine, h_other, base, gs, out):
    f = side(pos, 2)
    hw = widen(shares(pos, join(*h_mine, f), join(*h_other, f)))
    n = base.shape[2]
    for leaf, g in enumerate(gs):
        size = g.shape[1]
        at = pl.ds(pl.multiple_of((order[0, 0] ^ leaf) * size, size), size)
        add = dot(jnp.concatenate([g[0], g[1]], axis=1), hw, NT)
        for c in range(2):
            out[leaf, c] = (base[c, at] + add[:, c * n : (c + 1) * n]).astype(BF)
        yield leaf, at


def near_kernel(pos, order, mine, got, mine_other, got_other, base, g0, g1, out):
    for _ in finish(pos, order, (mine, got), (mine_other, got_other), base, (g0, g1), out):
        pass


def last_kernel(pos, order, mine, got, mine_other, got_other, base, g0, g1, done, out, buf, sems):
    size = g0.shape[1]
    n = base.shape[2]
    near = bit(pos, 1)
    copies = []

    def store(src, tile, leaf, at):
        sem = sems.at[len(copies)]
        copies.append(pltpu.make_async_copy(src.at[leaf], out.at[:, at, half_lanes(tile, n)], sem))
        copies[-1].start()

    for leaf in range(2):
        at = pl.ds(pl.multiple_of((order[0, 0] ^ leaf) * size, size), size)
        store(done, near, leaf, at)
    for leaf, at in finish(pos, order, (mine, got), (mine_other, got_other), base, (g0, g1), buf):
        store(buf, 1 - near, leaf, at)
    for copy in copies:
        copy.wait()


VMEM = pl.BlockSpec(memory_space=pltpu.VMEM)
SMEM = pl.BlockSpec(memory_space=pltpu.SMEM)
HBM = pl.BlockSpec(memory_space=pltpu.HBM)
GRANT = 20 * 2**20


def call(name, kernel, ins, outs, *args, scratch=(), flops=0, out_spec=VMEM):
    specs = {"s": SMEM, "v": VMEM, "h": HBM}
    moved = sum(a.size * a.dtype.itemsize for a in args)
    return pl.pallas_call(
        kernel,
        out_shape=[jax.ShapeDtypeStruct(shape, dtype) for shape, dtype in outs],
        in_specs=[specs[kind] for kind in ins],
        out_specs=[out_spec] * len(outs),
        scratch_shapes=list(scratch),
        compiler_params=pltpu.CompilerParams(vmem_limit_bytes=GRANT),
        cost_estimate=pl.CostEstimate(flops=flops, bytes_accessed=moved, transcendentals=0),
        name=name,
    )(*args)


def shards(rhs, diag, row_basis, col_basis, wl, bl, cross_w, cross_b, order):
    n = rhs.shape[2]
    rank = col_basis.shape[3]
    size = col_basis.shape[2]
    axes = ("leaf", "top")
    devices = lax.axis_size("leaf") * lax.axis_size("top")
    pos = lax.axis_index(axes).astype(jnp.int32).reshape(1)
    w = cross_w[:, 0]
    b = cross_b[:, 0]

    def swap(value, flip):
        return lax.ppermute(value, axes, [(i, i ^ flip) for i in range(devices)])

    def block(columns, dtype=BF):
        return ((2, columns, rank), dtype)

    mac = 8 * rank * rank
    half, quarter, eighth = n // 2, n // 4, n // 8
    qleaf_shape = ((2, n, rank), BF)
    hbm = [pltpu.with_memory_space_constraint(a, pltpu.HBM) for a in (order, rhs, col_basis, wl, w)]
    q_other, send, xt, x, u, wl, w0 = call(
        "send_half", send_kernel, "shhhhh",
        [qleaf_shape, block(half), ((2, 2, n, size), BF), (rhs.shape, BF), (col_basis.shape, BF),
         (wl.shape, BF), ((2, 1, 2, rank, rank), BF)],
        pos, *hbm,
        scratch=(pltpu.SMEM(order.shape, jnp.int32), pltpu.SemaphoreType.DMA((6,))),
        flops=mac * n * 3,
    )
    got0 = swap(send, 1)
    q_mine, keep0, own = call(
        "keep_half", keep_kernel, "ssvvvv", [qleaf_shape, block(half), block(half, F32)],
        pos, order, xt, u, wl, w0, flops=mac * n * 3,
    )
    got0_other = swap(keep0, 1)
    keep1, send = call(
        "climb_0", climb_kernel(0), "svvv", [block(quarter), block(quarter)],
        pos, got0, own, w0, flops=mac * half,
    )
    got1 = swap(send, 3)
    own, part_0, paths = call(
        "shadow_1", shadow_1, "ss" + "v" * 6,
        [block(quarter, F32), ((2, size, n), F32), ((2, 2, rank, rank), BF)],
        pos, order, keep1, w, w0, wl, x, diag, flops=mac * n * 8,
    )
    keep2, send = call(
        "climb_1", climb_kernel(1), "svvv", [block(eighth), block(eighth)],
        pos, got1, own, w, flops=mac * quarter,
    )
    got2 = swap(send, 5)
    own, part_1, g0 = call(
        "shadow_2", shadow_2, "ss" + "v" * 6,
        [block(eighth, F32), ((2, size, n), F32), block(size)],
        pos, order, keep2, w, x, diag, row_basis, paths, flops=mac * n * 7,
    )

    def climb(level, got, own):
        return call(
            "climb_%d" % level, climb_kernel(level), "svvv", [block(eighth)],
            pos, got, own, w, flops=mac * eighth,
        )[0]

    top_shape = block(eighth, F32)
    cleaf_shape = ((2, 2, half, rank), BF)
    base_shape = ((2, 2 * size, half), F32)
    q3 = climb(2, got2, own)
    got3 = swap(q3, 13)
    own, c2, c2_oth, g1 = call(
        "shadow_3", shadow_3, "s" + "v" * 7, [top_shape, top_shape, top_shape, block(size)],
        pos, q3, w, b, row_basis, paths, keep2, got2, flops=mac * n * 3,
    )
    q4 = climb(3, got3, own)
    q4, keep1 = lax.optimization_barrier((q4, keep1))
    got4 = swap(q4, 17)
    own, top = call(
        "shadow_4", shadow_4, "s" + "v" * 4, [top_shape, top_shape],
        pos, q4, got3, w, b, flops=mac * half,
    )
    got1_far, got1_far_other = swap(keep1, 3), swap(keep1, 2)
    got1_other = swap(got1, 1)
    q5 = climb(4, got4, own)
    got5 = swap(q5, 49)
    own, top, path_5, path_6 = call(
        "shadow_5", shadow_5, "s" + "v" * 5, [top_shape, top_shape, block(rank), block(rank)],
        pos, q5, got4, w, b, top, flops=mac * n * 2,
    )
    q6 = climb(5, got5, own)
    got6 = swap(q6, 65)
    own, top, cleaf = call(
        "shadow_6", shadow_6, "s" + "v" * 13, [top_shape, top_shape, cleaf_shape],
        pos, q6, got5, w, b, top, path_5, q_mine, got0, got1, got1_far, bl, w0, wl,
        flops=mac * n * 3,
    )
    q7 = climb(6, got6, own)
    got7 = swap(q7, 193)
    top, path, cleaf_other = call(
        "shadow_7", shadow_7, "s" + "v" * 12, [top_shape, block(rank), cleaf_shape],
        pos, got6, w, b, top, path_6, q_other, got0_other, got1_other, got1_far_other, bl, w0, wl,
        flops=mac * n * 4,
    )
    send, h = call(
        "top", top_kernel, "s" + "v" * 5, [block(eighth), block(eighth)],
        pos, got7, top, path, c2_oth, w, flops=mac * eighth * 2,
    )
    got = swap(send, 5)
    (mine,) = call(
        "own_h", own_kernel, "s" + "v" * 4, [block(eighth)],
        pos, h, send, c2, w, flops=mac * eighth,
    )
    far, far_other, mine_other = swap(mine, 3), swap(mine, 2), swap(mine, 1)
    (base_near,) = call(
        "shadow_8", shadow_8, "ss" + "v" * 6, [base_shape],
        pos, order, send, row_basis, cleaf, cleaf_other, part_0, part_1, flops=mac * n * 2,
    )
    got, base_near = lax.optimization_barrier((got, base_near))
    far_got, far_got_other = swap(got, 3), swap(got, 2)
    (base_far,) = call(
        "shadow_9", shadow_9, "ss" + "v" * 8, [base_shape],
        pos, order, got, far, far_other, row_basis, cleaf, cleaf_other, part_0, part_1, flops=mac * n * 2,
    )
    got_other = swap(got, 1)
    piece = (2, 2, size, half)
    (done,) = call(
        "near_columns", near_kernel, "ss" + "v" * 7, [(piece, BF)],
        pos, order, mine, got, mine_other, got_other, base_near, g0, g1, flops=mac * n * 2,
    )
    (out,) = call(
        "far_columns", last_kernel, "ss" + "v" * 8, [(rhs.shape, BF)],
        pos, order, far, far_got, far_other, far_got_other, base_far, g0, g1, done,
        scratch=(pltpu.VMEM(piece, BF), pltpu.SemaphoreType.DMA((4,))),
        flops=mac * n * 2, out_spec=HBM,
    )
    return out


def solution(mesh):
    return jax.shard_map(
        shards,
        mesh=mesh,
        in_specs=(
            P(None, ("leaf", "top"), None),
            P(None, ("leaf", "top"), None, None),
            P(None, ("leaf", "top"), None, None),
            P(None, ("leaf", "top"), None, None),
            P(None, ("leaf", "top"), None, None, None),
            P(None, ("leaf", "top"), None, None),
            P(None, ("leaf", "top"), None, None, None, None),
            P(None, ("leaf", "top"), None, None, None),
            P(("leaf", "top"), None),
        ),
        out_specs=P(None, ("leaf", "top"), None),
        check_vma=False,
    )
```

time: 53.1 us -> 54.6 us (1.028)
  starting transfers between devices: 23.9 us -> 26.1 us
  waiting for transfers between devices: 7.91 us -> 6.69 us
  Pallas kernels: 20.8 us -> 21.4 us
    ppermute x13 -> x19, starting transfers between devices: 23.9 us -> 26.1 us  [swap(): return lax.ppermute(value, axes, [(i, i ^ flip) for i in range(devices)])]
    ppermute x13 -> x19, waiting for transfers between devices: 7.91 us -> 6.69 us  [swap(): return lax.ppermute(value, axes, [(i, i ^ flip) for i in range(devices)])]
    pallas_call x22, Pallas kernels: 20.8 us -> 21.4 us  [call(): pl.pallas_call(kernel, out_shape=[jax.ShapeDtypeStruct(shape, dtype) for...]
  transfers between devices with their start and end apart: 13 -> 19, of which waited for: 9 -> 4; matrix products, arithmetic and copies ran while one was open for 0% -> 0% of each run, Pallas kernels for 27% -> 29%
where the time goes in v8:
time: 54.6 us; the launch traced here: 54.5 us
  starting transfers between devices  26.1 us (48%)
  Pallas kernels  21.4 us (39%)
  waiting for transfers between devices  6.69 us (12%)
    ppermute x19, starting transfers between devices, swap(): return lax.ppermute(value, axes, [(i, i ^ flip) for i in range(devices)])  26.1 us
    pallas_call x22, Pallas kernels, call(): pl.pallas_call(kernel, out_shape=[jax.ShapeDtypeStruct(shape, dtype) for...  21.4 us
    ppermute x19, waiting for transfers between devices, swap(): return lax.ppermute(value, axes, [(i, i ^ flip) for i in range(devices)])  6.69 us
  transfers between devices with their start and end apart: 19, of which 4 were waited for; matrix products, arithmetic and copies ran while one was open for 0% of the time, Pallas kernels for 29%

profile of v8, /device:TPU:1, one launch (start us, length us, event | category | flops | bytes accessed | tf_op | source)
XLA Modules:
  0.0 54.5 jit_solution(13140034418653902522)
XLA Ops:
  0.0 2.7 %send_half.1 = (bf16[2,256,256]{2,1,0:T(8,128)(2,1)S(1)}, bf16[2,128,256]{2,1,0:T(8,128)(2,1)S(1)}, bf16[2,2,256,512]{3,2,1,0:T(8,128)(2,1)S(1)}, bf16[2,1024,25...) custom-call(s32[1]{0:T(128)} %bitcast.pos, ...), custom_call_target="tpu_custom_call" | custom-call | flops 402653184 | bytes 6815756 | tf_op jit(solution)/shard_map/send_half/pallas_call | solution.py:337
  2.8 0.0 copy-start.3
  2.8 3.3 %collective-permute-start = (bf16[2,128,256]{2,1,0:T(8,128)(2,1)S(1)}, bf16[2,128,256]{2,1,0:T(8,128)(2,1)S(1)}, u32[]{:S(2)}, u32[]{:S(2)}) collective-permute-start(bf16[2,128,256]{2,1,0:T(8,128)(2,1)S(1)} %get-tuple-element.47), channel_id=1, source_target_pairs={{0,1},{1,0},{2,3},{3,2},{4,5},{5,4},{6,7},{7,6},{8,9},{9,8},{10,11... | collective-permute-start | bytes 393224 | tf_op jit(solution)/shard_map/ppermute | solution.py:360
  6.1 0.0 copy-done.5
  6.1 1.6 %keep_half.1 = (bf16[2,256,256]{2,1,0:T(8,128)(2,1)S(1)}, bf16[2,128,256]{2,1,0:T(8,128)(2,1)S(1)}, f32[2,128,256]{2,1,0:T(8,128)S(1)}) custom-call(s32[1]{0:T(128)} %bitcast.pos, s32[1,2]{1,0:T(1,128)S(1)} %copy-done.5, bf16[2,2,256,512]{3,2,1,0:T(8,128)(2,1)S(1)} %get-tuple-element.48.xt, bf16[2,2,512,256]{3,2,1,0:T(8,128)(2,1)S(1)} %get-tuple-element.49.u, ...), custom_call_target="tpu_custom_call" | custom-call | flops 402653184 | bytes 3145740 | tf_op jit(solution)/shard_map/keep_half/pallas_call | solution.py:337
  7.7 0.1 collective-permute-start.9
  7.8 0.0 collective-permute-done.got.got0
  7.8 0.2 climb_0.1
  8.1 0.4 collective-permute-start.1
  8.4 0.0 copy-done.3
  8.4 1.8 %shadow_1.1 = (f32[2,64,256]{2,1,0:T(8,128)S(1)}, f32[2,512,256]{2,1,0:T(8,128)S(1)}, bf16[2,2,256,256]{3,2,1,0:T(8,128)(2,1)S(1)}) custom-call(s32[1]{0:T(128)} %bitcast.pos, s32[1,2]{1,0:T(1,128)S(1)} %copy-done.5, bf16[2,64,256]{2,1,0:T(8,128)(2,1)S(1)} %get-tuple-element.69.keep, bf16[2,8,2,256,256]{4,3,2,1,0:T(8,128)(2,1)S(1)} %bitcast.4, ...), custom_call_target="tpu_custom_call" | custom-call | flops 1073741824 | bytes 8454156 | tf_op jit(solution)/shard_map/shadow_1/pallas_call | solution.py:337
  10.2 2.2 %collective-permute-done.1.got.got1 = bf16[2,64,256]{2,1,0:T(8,128)(2,1)S(1)} collective-permute-done((bf16[2,64,256]{2,1,0:T(8,128)(2,1)S(1)}, bf16[2,64,256]{2,1,0:T(8,128)(2,1)S(1)}, u32[]{:S(2)}, u32[]{:S(2)}) %collective-permute-start.1) | collective-permute-done | bytes 65568 | tf_op jit(solution)/shard_map/ppermute | solution.py:360
  12.4 0.2 climb_1.1
  12.6 1.4 %collective-permute-start.2 = (bf16[2,32,256]{2,1,0:T(8,128)(2,1)S(1)}, bf16[2,32,256]{2,1,0:T(8,128)(2,1)S(1)}, u32[]{:S(2)}, u32[]{:S(2)}) collective-permute-start(bf16[2,32,256]{2,1,0:T(8,128)(2,1)S(1)} %get-tuple-element.57), channel_id=1, source_target_pairs={{0,5},{1,4},{2,7},{3,6},{4,1},{5,0},{6,3},{7,2},{8,13},{9,12},{10,... | collective-permute-start | bytes 98312 | tf_op jit(solution)/shard_map/ppermute | solution.py:360
  14.1 1.6 %shadow_2.1 = (f32[2,32,256]{2,1,0:T(8,128)S(1)}, f32[2,512,256]{2,1,0:T(8,128)S(1)}, bf16[2,512,256]{2,1,0:T(8,128)(2,1)S(1)}) custom-call(s32[1]{0:T(128)} %bitcast.pos, s32[1,2]{1,0:T(1,128)S(1)} %copy-done.5, bf16[2,32,256]{2,1,0:T(8,128)(2,1)S(1)} %get-tuple-element.58.keep.keep2, bf16[2,8,2,256,256]{4,3,2,1,0:T(8,128)(2,1)S(1)} %bitcast.6, ...), custom_call_target="tpu_custom_call" | custom-call | flops 939524096 | bytes 8945676 | tf_op jit(solution)/shard_map/shadow_2/pallas_call | solution.py:337
  15.6 2.3 %collective-permute-done.2.got.got2 = bf16[2,32,256]{2,1,0:T(8,128)(2,1)S(1)} collective-permute-done((bf16[2,32,256]{2,1,0:T(8,128)(2,1)S(1)}, bf16[2,32,256]{2,1,0:T(8,128)(2,1)S(1)}, u32[]{:S(2)}, u32[]{:S(2)}) %collective-permute-start.2) | collective-permute-done | bytes 32800 | tf_op jit(solution)/shard_map/ppermute | solution.py:360
  18.0 0.2 climb_2.1.q3
  18.1 3.8 %collective-permute-start.3 = (bf16[2,32,256]{2,1,0:T(8,128)(2,1)S(1)}, bf16[2,32,256]{2,1,0:T(8,128)(2,1)S(1)}, u32[]{:S(2)}, u32[]{:S(2)}) collective-permute-start(bf16[2,32,256]{2,1,0:T(8,128)(2,1)S(1)} %climb_2.1.q3), channel_id=1, source_target_pairs={{0,13},{1,12},{2,15},{3,14},{4,9},{5,8},{6,11},{7,10},{8,5},{9,4},... | collective-permute-start | bytes 98312 | tf_op jit(solution)/shard_map/ppermute | solution.py:360
  21.9 1.0 %shadow_3.1 = (f32[2,32,256]{2,1,0:T(8,128)S(1)}, f32[2,32,256]{2,1,0:T(8,128)S(1)}, f32[2,32,256]{2,1,0:T(8,128)S(1)}, bf16[2,512,256]{2,1,0:T(8,128)(2,1)S(1)}) custom-call(s32[1]{0:T(128)} %bitcast.pos, bf16[2,32,256]{2,1,0:T(8,128)(2,1)S(1)} %climb_2.1.q3, bf16[2,8,2,256,256]{4,3,2,1,0:T(8,128)(2,1)S(1)} %bitcast.8, ...), custom_call_target="tpu_custom_call" | custom-call | flops 402653184 | bytes 7962628 | tf_op jit(solution)/shard_map/shadow_3/pallas_call | solution.py:337
  22.9 0.9 %collective-permute-done.3.got.got3 = bf16[2,32,256]{2,1,0:T(8,128)(2,1)S(1)} collective-permute-done((bf16[2,32,256]{2,1,0:T(8,128)(2,1)S(1)}, bf16[2,32,256]{2,1,0:T(8,128)(2,1)S(1)}, u32[]{:S(2)}, u32[]{:S(2)}) %collective-permute-start.3) | collective-permute-done | bytes 32800 | tf_op jit(solution)/shard_map/ppermute | solution.py:360
  23.8 0.2 climb_3.1.q4
  24.0 1.3 %collective-permute-start.4 = (bf16[2,32,256]{2,1,0:T(8,128)(2,1)S(1)}, bf16[2,32,256]{2,1,0:T(8,128)(2,1)S(1)}, u32[]{:S(2)}, u32[]{:S(2)}) collective-permute-start(bf16[2,32,256]{2,1,0:T(8,128)(2,1)S(1)} %climb_3.1.q4), channel_id=1, source_target_pairs={{0,17},{1,16},{2,19},{3,18},{4,21},{5,20},{6,23},{7,22},{8,25},{9,... | collective-permute-start | bytes 98312 | tf_op jit(solution)/shard_map/ppermute | solution.py:360
  25.3 2.0 %collective-permute-start.7 = (bf16[2,64,256]{2,1,0:T(8,128)(2,1)S(1)}, bf16[2,64,256]{2,1,0:T(8,128)(2,1)S(1)}, u32[]{:S(2)}, u32[]{:S(2)}) collective-permute-start(bf16[2,64,256]{2,1,0:T(8,128)(2,1)S(1)} %get-tuple-element.69.keep), channel_id=1, source_target_pairs={{0,3},{1,2},{2,1},{3,0},{4,7},{5,6},{6,5},{7,4},{8,11},{9,10},{10,... | collective-permute-start | bytes 196616 | tf_op jit(solution)/shard_map/ppermute | solution.py:360
  27.2 0.4 shadow_4.1
  27.6 0.0 collective-permute-done.4.got.got4
  27.6 0.2 climb_4.1.q5
  27.8 2.4 %collective-permute-start.5 = (bf16[2,32,256]{2,1,0:T(8,128)(2,1)S(1)}, bf16[2,32,256]{2,1,0:T(8,128)(2,1)S(1)}, u32[]{:S(2)}, u32[]{:S(2)}) collective-permute-start(bf16[2,32,256]{2,1,0:T(8,128)(2,1)S(1)} %climb_4.1.q5), channel_id=1, source_target_pairs={{0,49},{1,48},{2,51},{3,50},{4,53},{5,52},{6,55},{7,54},{8,57},{9,... | collective-permute-start | bytes 98312 | tf_op jit(solution)/shard_map/ppermute | solution.py:360
  30.2 0.1 collective-permute-start.10
  30.3 2.3 %collective-permute-start.11 = (bf16[2,64,256]{2,1,0:T(8,128)(2,1)S(1)}, bf16[2,64,256]{2,1,0:T(8,128)(2,1)S(1)}, u32[]{:S(2)}, u32[]{:S(2)}) collective-permute-start(bf16[2,64,256]{2,1,0:T(8,128)(2,1)S(1)} %get-tuple-element.69.keep), channel_id=1, source_target_pairs={{0,2},{1,3},{2,0},{3,1},{4,6},{5,7},{6,4},{7,5},{8,10},{9,11},{10,... | collective-permute-start | bytes 196616 | tf_op jit(solution)/shard_map/ppermute | solution.py:360
  32.6 1.1 %shadow_5.1 = (f32[2,32,256]{2,1,0:T(8,128)S(1)}, f32[2,32,256]{2,1,0:T(8,128)S(1)}, bf16[2,256,256]{2,1,0:T(8,128)(2,1)S(1)}, bf16[2,256,256]{2,1,0:T(8,128)(2,1)S(1)}) custom-call(s32[1]{0:T(128)} %bitcast.pos, bf16[2,32,256]{2,1,0:T(8,128)(2,1)S(1)} %climb_4.1.q5, bf16[2,32,256]{2,1,0:T(8,128)(2,1)S(1)} %collective-permute-done.4.got.got4, ...), custom_call_target="tpu_custom_call" | custom-call | flops 268435456 | bytes 6422532 | tf_op jit(solution)/shard_map/shadow_5/pallas_call | solution.py:337
  33.8 0.0 collective-permute-done.5.got.got5
  33.8 0.0 copy-start.4
  33.8 0.2 climb_5.1.q6
  34.0 1.6 %collective-permute-start.6 = (bf16[2,32,256]{2,1,0:T(8,128)(2,1)S(1)}, bf16[2,32,256]{2,1,0:T(8,128)(2,1)S(1)}, u32[]{:S(2)}, u32[]{:S(2)}) collective-permute-start(bf16[2,32,256]{2,1,0:T(8,128)(2,1)S(1)} %climb_5.1.q6), channel_id=1, source_target_pairs={{0,65},{1,64},{2,67},{3,66},{4,69},{5,68},{6,71},{7,70},{8,73},{9,... | collective-permute-start | bytes 98312 | tf_op jit(solution)/shard_map/ppermute | solution.py:360
  35.6 0.0 collective-permute-done.7.got1_far
  35.6 1.9 %shadow_6.1 = (f32[2,32,256]{2,1,0:T(8,128)S(1)}, f32[2,32,256]{2,1,0:T(8,128)S(1)}, bf16[2,2,128,256]{3,2,1,0:T(8,128)(2,1)S(1)}) custom-call(s32[1]{0:T(128)} %bitcast.pos, bf16[2,32,256]{2,1,0:T(8,128)(2,1)S(1)} %climb_5.1.q6, bf16[2,32,256]{2,1,0:T(8,128)(2,1)S(1)} %collective-permute-done.5.got.got5, bf16[2,8,2,256,256]{4,3,2,1,0:T(8,128)(2,1)S(1)} %bitcast.14, ...), custom_call_target="tpu_custom_call" | custom-call | flops 402653184 | bytes 8519684 | tf_op jit(solution)/shard_map/shadow_6/pallas_call | solution.py:337
  37.5 0.0 collective-permute-done.6.got.got6
  37.5 0.2 climb_6.1
  37.7 3.0 %collective-permute-start.8 = (bf16[2,32,256]{2,1,0:T(8,128)(2,1)S(1)}, bf16[2,32,256]{2,1,0:T(8,128)(2,1)S(1)}, u32[]{:S(2)}, u32[]{:S(2)}) collective-permute-start(bf16[2,32,256]{2,1,0:T(8,128)(2,1)S(1)} %climb_6.1), channel_id=1, source_target_pairs={{0,193},{1,192},{2,195},{3,194},{4,197},{5,196},{6,199},{7,198},{8... | collective-permute-start | bytes 98312 | tf_op jit(solution)/shard_map/ppermute | solution.py:360
  40.6 0.0 collective-permute-done.9.got0
  40.6 0.0 collective-permute-done.10.got1
  40.6 0.0 collective-permute-done.11.got1_far
  40.6 2.1 %shadow_7.1 = (f32[2,32,256]{2,1,0:T(8,128)S(1)}, bf16[2,256,256]{2,1,0:T(8,128)(2,1)S(1)}, bf16[2,2,128,256]{3,2,1,0:T(8,128)(2,1)S(1)}) custom-call(s32[1]{0:T(128)} %bitcast.pos, bf16[2,32,256]{2,1,0:T(8,128)(2,1)S(1)} %collective-permute-done.6.got.got6, bf16[2,8,2,256,256]{4,3,2,1,0:T(8,128)(2,1)S(1)} %bitcast.16, ...), custom_call_target="tpu_custom_call" | custom-call | flops 536870912 | bytes 8486916 | tf_op jit(solution)/shard_map/shadow_7/pallas_call | solution.py:337
  42.8 0.0 collective-permute-done.8.got
  42.8 0.5 top.1
  43.2 0.6 %collective-permute-start.13 = (bf16[2,32,256]{2,1,0:T(8,128)(2,1)S(1)}, bf16[2,32,256]{2,1,0:T(8,128)(2,1)S(1)}, u32[]{:S(2)}, u32[]{:S(2)}) collective-permute-start(bf16[2,32,256]{2,1,0:T(8,128)(2,1)S(1)} %get-tuple-element.79.send), channel_id=1, source_target_pairs={{0,5},{1,4},{2,7},{3,6},{4,1},{5,0},{6,3},{7,2},{8,13},{9,12},{10,... | collective-permute-start | bytes 98312 | tf_op jit(solution)/shard_map/ppermute | solution.py:360
  43.8 0.2 own_h.1.mine
  44.1 0.4 collective-permute-start.17
  44.5 1.1 %collective-permute-start.12 = (bf16[2,32,256]{2,1,0:T(8,128)(2,1)S(1)}, bf16[2,32,256]{2,1,0:T(8,128)(2,1)S(1)}, u32[]{:S(2)}, u32[]{:S(2)}) collective-permute-start(bf16[2,32,256]{2,1,0:T(8,128)(2,1)S(1)} %own_h.1.mine), channel_id=1, source_target_pairs={{0,3},{1,2},{2,1},{3,0},{4,7},{5,6},{6,5},{7,4},{8,11},{9,10},{10,... | collective-permute-start | bytes 98312 | tf_op jit(solution)/shard_map/ppermute | solution.py:360
  45.6 0.4 collective-permute-start.15
  46.0 1.0 %shadow_8.1.base = f32[2,1024,128]{2,1,0:T(8,128)S(1)} custom-call(s32[1]{0:T(128)} %bitcast.pos, s32[1,2]{1,0:T(1,128)S(1)} %copy-done.5, bf16[2,32,256]{2,1,0:T(8,128)(2,1)S(1)} %get-tuple-element.79.send, bf16[2,2,512,256]{3,2,1,0:T(8,128)(2,1)S(1)} %copy-done.2, bf16[2,2,128,256]{3,2,1,0:T(8,128)(2,1)S(1)} %get-tuple-element.81.cleaf, ...), custom_call_target="tpu_custom_call" | custom-call | flops 268435456 | bytes 3702796 | tf_op jit(solution)/shard_map/shadow_8/pallas_call | solution.py:337
  47.0 1.2 %collective-permute-done.13.got = bf16[2,32,256]{2,1,0:T(8,128)(2,1)S(1)} collective-permute-done((bf16[2,32,256]{2,1,0:T(8,128)(2,1)S(1)}, bf16[2,32,256]{2,1,0:T(8,128)(2,1)S(1)}, u32[]{:S(2)}, u32[]{:S(2)}) %collective-permute-start.13) | collective-permute-done | bytes 32800 | tf_op jit(solution)/shard_map/ppermute | solution.py:360
  48.2 0.4 collective-permute-start.18
  48.7 0.1 collective-permute-start.14
  48.8 0.0 collective-permute-done.12.far.mine
  48.8 1.3 %collective-permute-start.16 = (bf16[2,32,256]{2,1,0:T(8,128)(2,1)S(1)}, bf16[2,32,256]{2,1,0:T(8,128)(2,1)S(1)}, u32[]{:S(2)}, u32[]{:S(2)}) collective-permute-start(bf16[2,32,256]{2,1,0:T(8,128)(2,1)S(1)} %collective-permute-done.13.got), channel_id=1, source_target_pairs={{0,2},{1,3},{2,0},{3,1},{4,6},{5,7},{6,4},{7,5},{8,10},{9,11},{10,... | collective-permute-start | bytes 98312 | tf_op jit(solution)/shard_map/ppermute | solution.py:360
  50.1 0.0 collective-permute-done.15.far_other.mine_other
  50.1 1.0 %shadow_9.1.base = f32[2,1024,128]{2,1,0:T(8,128)S(1)} custom-call(s32[1]{0:T(128)} %bitcast.pos, s32[1,2]{1,0:T(1,128)S(1)} %copy-done.5, bf16[2,32,256]{2,1,0:T(8,128)(2,1)S(1)} %collective-permute-done.13.got, bf16[2,32,256]{2,1,0:T(8,128)(2,1)S(1)} %collective-permute-done.12.far.mine, ...), custom_call_target="tpu_custom_call" | custom-call | flops 268435456 | bytes 3768332 | tf_op jit(solution)/shard_map/shadow_9/pallas_call | solution.py:337
  51.1 0.0 collective-permute-done.17.mine_other
  51.1 0.0 collective-permute-done.18.got_other
  51.2 1.0 %near_columns.1.done = bf16[2,2,512,128]{3,2,1,0:T(8,128)(2,1)S(1)} custom-call(s32[1]{0:T(128)} %bitcast.pos, s32[1,2]{1,0:T(1,128)S(1)} %copy-done.5, bf16[2,32,256]{2,1,0:T(8,128)(2,1)S(1)} %own_h.1.mine, bf16[2,32,256]{2,1,0:T(8,128)(2,1)S(1)} %collective-permute-done.13.got, bf16[2,32,256]{2,1,0:T(8,128)(2,1)S(1)} %collective-permute-done.17.mine_other, ...), custom_call_target="tpu_custom_call" | custom-call | flops 268435456 | bytes 2228236 | tf_op jit(solution)/shard_map/near_columns/pallas_call | solution.py:337
  52.2 0.0 collective-permute-done.14.got
  52.2 0.0 collective-permute-done.16.got_other
  52.2 2.1 %far_columns.1 = bf16[2,1024,256]{2,1,0:T(8,128)(2,1)} custom-call(s32[1]{0:T(128)} %bitcast.pos, s32[1,2]{1,0:T(1,128)S(1)} %copy-done.5, bf16[2,32,256]{2,1,0:T(8,128)(2,1)S(1)} %collective-permute-done.12.far.mine, bf16[2,32,256]{2,1,0:T(8,128)(2,1)S(1)} %collective-permute-done.14.got, ...), custom_call_target="tpu_custom_call" | custom-call | flops 268435456 | bytes 2752524 | tf_op jit(solution)/shard_map/far_columns/pallas_call | solution.py:337
  (8 shorter events, 0.0 us)
Async XLA Ops:
  0.0 6.1 %copy-start.5 = (s32[1,2]{1,0:T(1,128)S(1)}, s32[1,2]{1,0:T(1,128)}, u32[]{:S(2)}) copy-start(s32[1,2]{1,0:T(1,128)} %order.15) | copy-start | bytes 28
  0.0 8.4 %copy-start = (bf16[2,1,8,2,256,256]{5,4,3,2,1,0:T(8,128)(2,1)S(1)}, bf16[2,1,8,2,256,256]{5,4,3,2,1,0:T(8,128)(2,1)}, u32[]{:S(2)}) copy-start(bf16[2,1,8,2,256,256]{5,4,3,2,1,0:T(8,128)(2,1)} %param.15) | copy-start | bytes 12582916
  2.8 5.7 %copy-start.3 = (bf16[2,2,512,512]{3,2,1,0:T(8,128)(2,1)S(1)}, bf16[2,2,512,512]{3,2,1,0:T(8,128)(2,1)}, u32[]{:S(2)}) copy-start(bf16[2,2,512,512]{3,2,1,0:T(8,128)(2,1)} %d.3) | copy-start | bytes 6291460
  2.8 5.1 %collective-permute-start = (bf16[2,128,256]{2,1,0:T(8,128)(2,1)S(1)}, bf16[2,128,256]{2,1,0:T(8,128)(2,1)S(1)}, u32[]{:S(2)}, u32[]{:S(2)}) collective-permute-start(bf16[2,128,256]{2,1,0:T(8,128)(2,1)S(1)} %get-tuple-element.47), channel_id=1, source_target_pairs={{0,1},{1,0},{2,3},{3,2},{4,5},{5,4},{6,7},{7,6},{8,9},{9,8},{10,11... | collective-permute-start | bytes 393224 | tf_op jit(solution)/shard_map/ppermute | solution.py:360
  7.7 32.9 %collective-permute-start.9 = (bf16[2,128,256]{2,1,0:T(8,128)(2,1)S(1)}, bf16[2,128,256]{2,1,0:T(8,128)(2,1)S(1)}, u32[]{:S(2)}, u32[]{:S(2)}) collective-permute-start(bf16[2,128,256]{2,1,0:T(8,128)(2,1)S(1)} %get-tuple-element.74), channel_id=1, source_target_pairs={{0,1},{1,0},{2,3},{3,2},{4,5},{5,4},{6,7},{7,6},{8,9},{9,8},{10,11... | collective-permute-start | bytes 393224 | tf_op jit(solution)/shard_map/ppermute | solution.py:360
  8.1 4.4 %collective-permute-start.1 = (bf16[2,64,256]{2,1,0:T(8,128)(2,1)S(1)}, bf16[2,64,256]{2,1,0:T(8,128)(2,1)S(1)}, u32[]{:S(2)}, u32[]{:S(2)}) collective-permute-start(bf16[2,64,256]{2,1,0:T(8,128)(2,1)S(1)} %get-tuple-element.53), channel_id=1, source_target_pairs={{0,3},{1,2},{2,1},{3,0},{4,7},{5,6},{6,5},{7,4},{8,11},{9,10},{10,... | collective-permute-start | bytes 196616 | tf_op jit(solution)/shard_map/ppermute | solution.py:360
  12.4 1.6 %copy-start.2 = (bf16[2,2,512,256]{3,2,1,0:T(8,128)(2,1)S(1)}, bf16[2,2,512,256]{3,2,1,0:T(8,128)(2,1)}, u32[]{:S(2)}) copy-start(bf16[2,2,512,256]{3,2,1,0:T(8,128)(2,1)} %r.7) | copy-start | bytes 3145732
  12.6 5.3 %collective-permute-start.2 = (bf16[2,32,256]{2,1,0:T(8,128)(2,1)S(1)}, bf16[2,32,256]{2,1,0:T(8,128)(2,1)S(1)}, u32[]{:S(2)}, u32[]{:S(2)}) collective-permute-start(bf16[2,32,256]{2,1,0:T(8,128)(2,1)S(1)} %get-tuple-element.57), channel_id=1, source_target_pairs={{0,5},{1,4},{2,7},{3,6},{4,1},{5,0},{6,3},{7,2},{8,13},{9,12},{10,... | collective-permute-start | bytes 98312 | tf_op jit(solution)/shard_map/ppermute | solution.py:360
  18.0 4.0 %copy-start.1 = (bf16[2,1,8,256,256]{4,3,2,1,0:T(8,128)(2,1)S(1)}, bf16[2,1,8,256,256]{4,3,2,1,0:T(8,128)(2,1)}, u32[]{:S(2)}) copy-start(bf16[2,1,8,256,256]{4,3,2,1,0:T(8,128)(2,1)} %param.16) | copy-start | bytes 6291460
  18.1 5.7 %collective-permute-start.3 = (bf16[2,32,256]{2,1,0:T(8,128)(2,1)S(1)}, bf16[2,32,256]{2,1,0:T(8,128)(2,1)S(1)}, u32[]{:S(2)}, u32[]{:S(2)}) collective-permute-start(bf16[2,32,256]{2,1,0:T(8,128)(2,1)S(1)} %climb_2.1.q3), channel_id=1, source_target_pairs={{0,13},{1,12},{2,15},{3,14},{4,9},{5,8},{6,11},{7,10},{8,5},{9,4},... | collective-permute-start | bytes 98312 | tf_op jit(solution)/shard_map/ppermute | solution.py:360
  24.0 3.6 %collective-permute-start.4 = (bf16[2,32,256]{2,1,0:T(8,128)(2,1)S(1)}, bf16[2,32,256]{2,1,0:T(8,128)(2,1)S(1)}, u32[]{:S(2)}, u32[]{:S(2)}) collective-permute-start(bf16[2,32,256]{2,1,0:T(8,128)(2,1)S(1)} %climb_3.1.q4), channel_id=1, source_target_pairs={{0,17},{1,16},{2,19},{3,18},{4,21},{5,20},{6,23},{7,22},{8,25},{9,... | collective-permute-start | bytes 98312 | tf_op jit(solution)/shard_map/ppermute | solution.py:360
  25.3 10.3 %collective-permute-start.7 = (bf16[2,64,256]{2,1,0:T(8,128)(2,1)S(1)}, bf16[2,64,256]{2,1,0:T(8,128)(2,1)S(1)}, u32[]{:S(2)}, u32[]{:S(2)}) collective-permute-start(bf16[2,64,256]{2,1,0:T(8,128)(2,1)S(1)} %get-tuple-element.69.keep), channel_id=1, source_target_pairs={{0,3},{1,2},{2,1},{3,0},{4,7},{5,6},{6,5},{7,4},{8,11},{9,10},{10,... | collective-permute-start | bytes 196616 | tf_op jit(solution)/shard_map/ppermute | solution.py:360
  27.8 6.0 %collective-permute-start.5 = (bf16[2,32,256]{2,1,0:T(8,128)(2,1)S(1)}, bf16[2,32,256]{2,1,0:T(8,128)(2,1)S(1)}, u32[]{:S(2)}, u32[]{:S(2)}) collective-permute-start(bf16[2,32,256]{2,1,0:T(8,128)(2,1)S(1)} %climb_4.1.q5), channel_id=1, source_target_pairs={{0,49},{1,48},{2,51},{3,50},{4,53},{5,52},{6,55},{7,54},{8,57},{9,... | collective-permute-start | bytes 98312 | tf_op jit(solution)/shard_map/ppermute | solution.py:360
  30.2 10.4 %collective-permute-start.10 = (bf16[2,64,256]{2,1,0:T(8,128)(2,1)S(1)}, bf16[2,64,256]{2,1,0:T(8,128)(2,1)S(1)}, u32[]{:S(2)}, u32[]{:S(2)}) collective-permute-start(bf16[2,64,256]{2,1,0:T(8,128)(2,1)S(1)} %collective-permute-done.1.got.got1), channel_id=1, source_target_pairs={{0,1},{1,0},{2,3},{3,2},{4,5},{5,4},{6,7},{7,6},{8,9},{9,8},{10,11... | collective-permute-start | bytes 196616 | tf_op jit(solution)/shard_map/ppermute | solution.py:360
  30.3 10.3 %collective-permute-start.11 = (bf16[2,64,256]{2,1,0:T(8,128)(2,1)S(1)}, bf16[2,64,256]{2,1,0:T(8,128)(2,1)S(1)}, u32[]{:S(2)}, u32[]{:S(2)}) collective-permute-start(bf16[2,64,256]{2,1,0:T(8,128)(2,1)S(1)} %get-tuple-element.69.keep), channel_id=1, source_target_pairs={{0,2},{1,3},{2,0},{3,1},{4,6},{5,7},{6,4},{7,5},{8,10},{9,11},{10,... | collective-permute-start | bytes 196616 | tf_op jit(solution)/shard_map/ppermute | solution.py:360
  33.8 1.8 %copy-start.4 = (bf16[2,1,256,256]{3,2,1,0:T(8,128)(2,1)S(1)}, bf16[2,1,256,256]{3,2,1,0:T(8,128)(2,1)}, u32[]{:S(2)}) copy-start(bf16[2,1,256,256]{3,2,1,0:T(8,128)(2,1)} %bl.3) | copy-start | bytes 786436
  34.0 3.5 %collective-permute-start.6 = (bf16[2,32,256]{2,1,0:T(8,128)(2,1)S(1)}, bf16[2,32,256]{2,1,0:T(8,128)(2,1)S(1)}, u32[]{:S(2)}, u32[]{:S(2)}) collective-permute-start(bf16[2,32,256]{2,1,0:T(8,128)(2,1)S(1)} %climb_5.1.q6), channel_id=1, source_target_pairs={{0,65},{1,64},{2,67},{3,66},{4,69},{5,68},{6,71},{7,70},{8,73},{9,... | collective-permute-start | bytes 98312 | tf_op jit(solution)/shard_map/ppermute | solution.py:360
  37.7 5.1 %collective-permute-start.8 = (bf16[2,32,256]{2,1,0:T(8,128)(2,1)S(1)}, bf16[2,32,256]{2,1,0:T(8,128)(2,1)S(1)}, u32[]{:S(2)}, u32[]{:S(2)}) collective-permute-start(bf16[2,32,256]{2,1,0:T(8,128)(2,1)S(1)} %climb_6.1), channel_id=1, source_target_pairs={{0,193},{1,192},{2,195},{3,194},{4,197},{5,196},{6,199},{7,198},{8... | collective-permute-start | bytes 98312 | tf_op jit(solution)/shard_map/ppermute | solution.py:360
  43.2 5.0 %collective-permute-start.13 = (bf16[2,32,256]{2,1,0:T(8,128)(2,1)S(1)}, bf16[2,32,256]{2,1,0:T(8,128)(2,1)S(1)}, u32[]{:S(2)}, u32[]{:S(2)}) collective-permute-start(bf16[2,32,256]{2,1,0:T(8,128)(2,1)S(1)} %get-tuple-element.79.send), channel_id=1, source_target_pairs={{0,5},{1,4},{2,7},{3,6},{4,1},{5,0},{6,3},{7,2},{8,13},{9,12},{10,... | collective-permute-start | bytes 98312 | tf_op jit(solution)/shard_map/ppermute | solution.py:360
  44.1 7.1 %collective-permute-start.17 = (bf16[2,32,256]{2,1,0:T(8,128)(2,1)S(1)}, bf16[2,32,256]{2,1,0:T(8,128)(2,1)S(1)}, u32[]{:S(2)}, u32[]{:S(2)}) collective-permute-start(bf16[2,32,256]{2,1,0:T(8,128)(2,1)S(1)} %own_h.1.mine), channel_id=1, source_target_pairs={{0,1},{1,0},{2,3},{3,2},{4,5},{5,4},{6,7},{7,6},{8,9},{9,8},{10,11... | collective-permute-start | bytes 98312 | tf_op jit(solution)/shard_map/ppermute | solution.py:360
  44.5 4.3 %collective-permute-start.12 = (bf16[2,32,256]{2,1,0:T(8,128)(2,1)S(1)}, bf16[2,32,256]{2,1,0:T(8,128)(2,1)S(1)}, u32[]{:S(2)}, u32[]{:S(2)}) collective-permute-start(bf16[2,32,256]{2,1,0:T(8,128)(2,1)S(1)} %own_h.1.mine), channel_id=1, source_target_pairs={{0,3},{1,2},{2,1},{3,0},{4,7},{5,6},{6,5},{7,4},{8,11},{9,10},{10,... | collective-permute-start | bytes 98312 | tf_op jit(solution)/shard_map/ppermute | solution.py:360
  45.6 4.5 %collective-permute-start.15 = (bf16[2,32,256]{2,1,0:T(8,128)(2,1)S(1)}, bf16[2,32,256]{2,1,0:T(8,128)(2,1)S(1)}, u32[]{:S(2)}, u32[]{:S(2)}) collective-permute-start(bf16[2,32,256]{2,1,0:T(8,128)(2,1)S(1)} %own_h.1.mine), channel_id=1, source_target_pairs={{0,2},{1,3},{2,0},{3,1},{4,6},{5,7},{6,4},{7,5},{8,10},{9,11},{10,... | collective-permute-start | bytes 98312 | tf_op jit(solution)/shard_map/ppermute | solution.py:360
  48.2 2.9 %collective-permute-start.18 = (bf16[2,32,256]{2,1,0:T(8,128)(2,1)S(1)}, bf16[2,32,256]{2,1,0:T(8,128)(2,1)S(1)}, u32[]{:S(2)}, u32[]{:S(2)}) collective-permute-start(bf16[2,32,256]{2,1,0:T(8,128)(2,1)S(1)} %collective-permute-done.13.got), channel_id=1, source_target_pairs={{0,1},{1,0},{2,3},{3,2},{4,5},{5,4},{6,7},{7,6},{8,9},{9,8},{10,11... | collective-permute-start | bytes 98312 | tf_op jit(solution)/shard_map/ppermute | solution.py:360
  48.7 3.5 %collective-permute-start.14 = (bf16[2,32,256]{2,1,0:T(8,128)(2,1)S(1)}, bf16[2,32,256]{2,1,0:T(8,128)(2,1)S(1)}, u32[]{:S(2)}, u32[]{:S(2)}) collective-permute-start(bf16[2,32,256]{2,1,0:T(8,128)(2,1)S(1)} %collective-permute-done.13.got), channel_id=1, source_target_pairs={{0,3},{1,2},{2,1},{3,0},{4,7},{5,6},{6,5},{7,4},{8,11},{9,10},{10,... | collective-permute-start | bytes 98312 | tf_op jit(solution)/shard_map/ppermute | solution.py:360
  48.8 3.4 %collective-permute-start.16 = (bf16[2,32,256]{2,1,0:T(8,128)(2,1)S(1)}, bf16[2,32,256]{2,1,0:T(8,128)(2,1)S(1)}, u32[]{:S(2)}, u32[]{:S(2)}) collective-permute-start(bf16[2,32,256]{2,1,0:T(8,128)(2,1)S(1)} %collective-permute-done.13.got), channel_id=1, source_target_pairs={{0,2},{1,3},{2,0},{3,1},{4,6},{5,7},{6,4},{7,5},{8,10},{9,11},{10,... | collective-permute-start | bytes 98312 | tf_op jit(solution)/shard_map/ppermute | solution.py:360

commit v9 on v8

--- a/solution.py
+++ b/solution.py
@@ -174,10 +174,8 @@
 
 def shadow_1(pos, order, keep, w, w0, wl, x, d, own, part, paths):
     put(own, lift(rows(keep), w, pos, 1))
-    two = lift(stack(w0, 0, bit(pos, 0)), w, pos, 1).astype(BF)
-    half = two.shape[0] // 2
     for leaf in range(2):
-        put(paths.at[leaf], times(stack(wl, 0, leaf), two[:half], two[half:]))
+        put(paths.at[leaf], lift(stack(wl, 0, leaf), w0, pos, 0))
     direct(order, 0, x, d, part)
 
 
@@ -185,26 +183,25 @@
     put(out, times(rows(r.at[:, leaf]), paths[leaf, 0], paths[leaf, 1]))
 
 
-def shadow_2(pos, order, keep, w, x, d, r, paths, own, part, g):
-    put(own, lift(rows(keep), w, pos, 2))
-    direct(order, 1, x, d, part)
-    product(r, paths, 0, g)
-
-
-def shadow_3(pos, q3, w, b, r, paths, keep2, got2, own, c2, c2_oth, g):
-    put(own, lift(rows(q3), w, pos, 3))
-    put(c2, couple(rows(got2), b, pos, 2))
-    put(c2_oth, couple(rows(keep2), b, pos, 2, 1))
-    product(r, paths, 1, g)
-
-
-def leaf_coupled(pos, q, got0, got1, got1_far, b, bl, w0, wl, cleaf):
-    c1 = couple(join(got1, got1_far, bit(pos, 1)), b, pos, 1).astype(BF)
-    c0 = (couple(rows(got0), b, pos, 0) + lower(c1, w0, pos, 0)).astype(BF)
+def leaf_coupled(pos, q, got, b, bl, wl, cleaf):
+    c0 = couple(rows(got), b, pos, 0).astype(BF)
     left = times_t(q[1], bl[0, 0], bl[1, 0])
     right = times(q[0], bl[0, 0], bl[1, 0])
     put(cleaf.at[0], left + times_t(c0, wl[0, 0, 0], wl[1, 0, 0]))
     put(cleaf.at[1], right + times_t(c0, wl[0, 0, 1], wl[1, 0, 1]))
+
+
+def shadow_2(pos, order, keep, w, x, d, r, paths, b, bl, wl, q, got0, own, part, g, cleaf):
+    put(own, lift(rows(keep), w, pos, 2))
+    direct(order, 1, x, d, part)
+    product(r, paths, 0, g)
+    leaf_coupled(pos, q, got0, b, bl, wl, cleaf)
+
+
+def shadow_3(pos, q3, w, r, paths, b, bl, wl, q, got0, own, g, cleaf):
+    put(own, lift(rows(q3), w, pos, 3))
+    product(r, paths, 1, g)
+    leaf_coupled(pos, q, got0, b, bl, wl, cleaf)
 
 
 def shares(pos, mine, other):
@@ -232,33 +229,41 @@
             )
 
 
-def shadow_4(pos, q4, got3, w, b, own, top):
+def shadow_4(pos, order, q4, got3, w, b, r, cleaf, cleaf_other, part_0, part_1, own, top, base):
     put(own, lift(rows(q4), w, pos, 4))
     put(top, couple(rows(got3), b, pos, 3))
-
-
-def shadow_5(pos, q5, got4, w, b, top, own, top_out, path_5, path_6):
+    set_base(pos, order, bit(pos, 1), r, cleaf, cleaf_other, (part_0, part_1), base)
+
+
+def shadow_5(
+    pos, order, q5, got4, w, b, top, r, cleaf, cleaf_other, part_0, part_1, own, top_out, path, base
+):
     put(own, lift(rows(q5), w, pos, 5))
     c4 = couple(rows(got4), b, pos, 4).astype(BF)
     put(top_out, rows(top) + lower(c4, w, pos, 3))
-    path = lift(stack(w, 3, bit(pos, 3)), w, pos, 4).astype(BF)
-    put(path_5, path)
-    put(path_6, lift(path, w, pos, 5))
-
-
-def shadow_6(pos, q6, got5, w, b, top, path, q, got0, got1, got1_far, bl, w0, wl, own, top_out, cleaf):
+    put(path, lift(stack(w, 3, bit(pos, 3)), w, pos, 4))
+    set_base(pos, order, 1 - bit(pos, 1), r, cleaf, cleaf_other, (part_0, part_1), base)
+
+
+def shadow_6(
+    pos, q6, got5, w, b, top, path, keep2, got2, keep1, got1,
+    own, top_out, path_out, c2, c2_oth, c1, c1_oth,
+):
     put(own, lift(rows(q6), w, pos, 6))
     c5 = couple(rows(got5), b, pos, 5).astype(BF)
     put(top_out, rows(top) + times_t(c5, path[0], path[1]))
-    leaf_coupled(pos, q, got0, got1, got1_far, b, bl, w0, wl, cleaf)
-
-
-def shadow_7(pos, got6, w, b, top, path, q, got0, got1, got1_far, bl, w0, wl, top_out, path_out, cleaf):
+    put(path_out, lift(rows(path), w, pos, 5))
+    put(c2, couple(rows(got2), b, pos, 2))
+    put(c2_oth, couple(rows(keep2), b, pos, 2, 1))
+    put(c1, couple(rows(got1), b, pos, 1))
+    put(c1_oth, couple(rows(keep1), b, pos, 1, 1))
+
+
+def shadow_7(pos, got6, w, b, top, path, top_out, path_out):
     c6 = couple(rows(got6), b, pos, 6).astype(BF)
     put(top_out, rows(top) + times_t(c6, path[0], path[1]))
     longer = lift(rows(path), w, pos, 6).astype(BF)
     put(path_out, couple_path(longer, b, pos))
-    leaf_coupled(pos, q, got0, got1, got1_far, b, bl, w0, wl, cleaf)
 
 
 def couple_path(path, b, pos):
@@ -269,22 +274,23 @@
     )
 
 
-def top_kernel(pos, got, top, path, c_oth, w, send, h_out):
+def top_kernel(pos, got, top, path, c_own, c_oth, w, own, send):
     h = (rows(top) + times_t(rows(got), path[0], path[1])).astype(BF)
-    put(h_out, h)
     put(send, rows(c_oth) + lower(h, w, pos, 2, 1))
-
-
-def own_kernel(pos, h, send, c_own, w, own):
-    put(own, rows(c_own) + lower(rows(h), w, pos, 2))
-
-
-def shadow_8(pos, order, send, r, cleaf, cleaf_other, part_0, part_1, base):
-    set_base(pos, order, bit(pos, 1), r, cleaf, cleaf_other, (part_0, part_1), base)
-
-
-def shadow_9(pos, order, got, far, far_other, r, cleaf, cleaf_other, part_0, part_1, base):
-    set_base(pos, order, 1 - bit(pos, 1), r, cleaf, cleaf_other, (part_0, part_1), base)
+    put(own, rows(c_own) + lower(h, w, pos, 2))
+
+
+def piece_kernel(other):
+    def kernel(pos, h, c_own, c_oth, w, own, send):
+        n = h.shape[1]
+        at = pl.ds(pl.multiple_of((side(pos, 2) ^ other) * n, n), n)
+        values = rows(h)
+        const = jnp.concatenate([c_oth[0, at], c_oth[1, at]], axis=0)
+        put(send, const + lower(values, w, pos, 1, 1))
+        const = jnp.concatenate([c_own[0, at], c_own[1, at]], axis=0)
+        put(own, const + lower(values, w, pos, 1))
+
+    return kernel
 
 
 def finish(pos, order, h_mine, h_other, base, gs, out):
@@ -300,29 +306,24 @@
         yield leaf, at
 
 
-def near_kernel(pos, order, mine, got, mine_other, got_other, base, g0, g1, out):
-    for _ in finish(pos, order, (mine, got), (mine_other, got_other), base, (g0, g1), out):
-        pass
-
-
-def last_kernel(pos, order, mine, got, mine_other, got_other, base, g0, g1, done, out, buf, sems):
-    size = g0.shape[1]
-    n = base.shape[2]
-    near = bit(pos, 1)
+def write(pos, order, tile, h_mine, h_other, base, gs, out, buf, sems):
+    lanes = half_lanes(tile, base.shape[2])
     copies = []
-
-    def store(src, tile, leaf, at):
-        sem = sems.at[len(copies)]
-        copies.append(pltpu.make_async_copy(src.at[leaf], out.at[:, at, half_lanes(tile, n)], sem))
+    for leaf, at in finish(pos, order, h_mine, h_other, base, gs, buf):
+        copies.append(pltpu.make_async_copy(buf.at[leaf], out.at[:, at, lanes], sems.at[leaf]))
         copies[-1].start()
-
-    for leaf in range(2):
-        at = pl.ds(pl.multiple_of((order[0, 0] ^ leaf) * size, size), size)
-        store(done, near, leaf, at)
-    for leaf, at in finish(pos, order, (mine, got), (mine_other, got_other), base, (g0, g1), buf):
-        store(buf, 1 - near, leaf, at)
     for copy in copies:
         copy.wait()
+
+
+def near_kernel(pos, order, mine, got, mine_other, got_other, base, g0, g1, far, far_other, out, buf, sems):
+    tile = bit(pos, 1)
+    write(pos, order, tile, (mine, got), (mine_other, got_other), base, (g0, g1), out, buf, sems)
+
+
+def far_kernel(pos, order, mine, got, mine_other, got_other, base, g0, g1, done, out, buf, sems):
+    tile = 1 - bit(pos, 1)
+    write(pos, order, tile, (mine, got), (mine_other, got_other), base, (g0, g1), out, buf, sems)
 
 
 VMEM = pl.BlockSpec(memory_space=pltpu.VMEM)
@@ -331,7 +332,7 @@
 GRANT = 20 * 2**20
 
 
-def call(name, kernel, ins, outs, *args, scratch=(), flops=0, out_spec=VMEM):
+def call(name, kernel, ins, outs, *args, scratch=(), flops=0, out_spec=VMEM, aliases=None):
     specs = {"s": SMEM, "v": VMEM, "h": HBM}
     moved = sum(a.size * a.dtype.itemsize for a in args)
     return pl.pallas_call(
@@ -340,6 +341,7 @@
         in_specs=[specs[kind] for kind in ins],
         out_specs=[out_spec] * len(outs),
         scratch_shapes=list(scratch),
+        input_output_aliases=aliases or {},
         compiler_params=pltpu.CompilerParams(vmem_limit_bytes=GRANT),
         cost_estimate=pl.CostEstimate(flops=flops, bytes_accessed=moved, transcendentals=0),
         name=name,
@@ -395,10 +397,12 @@
         pos, got1, own, w, flops=mac * quarter,
     )
     got2 = swap(send, 5)
-    own, part_1, g0 = call(
-        "shadow_2", shadow_2, "ss" + "v" * 6,
-        [block(eighth, F32), ((2, size, n), F32), block(size)],
-        pos, order, keep2, w, x, diag, row_basis, paths, flops=mac * n * 7,
+    cleaf_shape = ((2, 2, half, rank), BF)
+    own, part_1, g0, cleaf = call(
+        "shadow_2", shadow_2, "ss" + "v" * 11,
+        [block(eighth, F32), ((2, size, n), F32), block(size), cleaf_shape],
+        pos, order, keep2, w, x, diag, row_basis, paths, b, bl, wl, q_mine, got0,
+        flops=mac * n * 9,
     )
 
     def climb(level, got, own):
@@ -408,74 +412,65 @@
         )[0]
 
     top_shape = block(eighth, F32)
-    cleaf_shape = ((2, 2, half, rank), BF)
     base_shape = ((2, 2 * size, half), F32)
     q3 = climb(2, got2, own)
     got3 = swap(q3, 13)
-    own, c2, c2_oth, g1 = call(
-        "shadow_3", shadow_3, "s" + "v" * 7, [top_shape, top_shape, top_shape, block(size)],
-        pos, q3, w, b, row_basis, paths, keep2, got2, flops=mac * n * 3,
+    own, g1, cleaf_other = call(
+        "shadow_3", shadow_3, "s" + "v" * 9, [top_shape, block(size), cleaf_shape],
+        pos, q3, w, row_basis, paths, b, bl, wl, q_other, got0_other, flops=mac * n * 5,
     )
     q4 = climb(3, got3, own)
-    q4, keep1 = lax.optimization_barrier((q4, keep1))
     got4 = swap(q4, 17)
-    own, top = call(
-        "shadow_4", shadow_4, "s" + "v" * 4, [top_shape, top_shape],
-        pos, q4, got3, w, b, flops=mac * half,
-    )
-    got1_far, got1_far_other = swap(keep1, 3), swap(keep1, 2)
-    got1_other = swap(got1, 1)
+    own, top, base_near = call(
+        "shadow_4", shadow_4, "ss" + "v" * 9, [top_shape, top_shape, base_shape],
+        pos, order, q4, got3, w, b, row_basis, cleaf, cleaf_other, part_0, part_1,
+        flops=mac * n * 2,
+    )
     q5 = climb(4, got4, own)
     got5 = swap(q5, 49)
-    own, top, path_5, path_6 = call(
-        "shadow_5", shadow_5, "s" + "v" * 5, [top_shape, top_shape, block(rank), block(rank)],
-        pos, q5, got4, w, b, top, flops=mac * n * 2,
+    own, top, path, base_far = call(
+        "shadow_5", shadow_5, "ss" + "v" * 10, [top_shape, top_shape, block(rank), base_shape],
+        pos, order, q5, got4, w, b, top, row_basis, cleaf, cleaf_other, part_0, part_1,
+        flops=mac * n * 3,
     )
     q6 = climb(5, got5, own)
     got6 = swap(q6, 65)
-    own, top, cleaf = call(
-        "shadow_6", shadow_6, "s" + "v" * 13, [top_shape, top_shape, cleaf_shape],
-        pos, q6, got5, w, b, top, path_5, q_mine, got0, got1, got1_far, bl, w0, wl,
-        flops=mac * n * 3,
+    own, top, path, c2, c2_oth, c1, c1_oth = call(
+        "shadow_6", shadow_6, "s" + "v" * 10,
+        [top_shape, top_shape, block(rank), top_shape, top_shape, block(quarter, F32), block(quarter, F32)],
+        pos, q6, got5, w, b, top, path, keep2, got2, keep1, got1, flops=mac * n * 2,
     )
     q7 = climb(6, got6, own)
     got7 = swap(q7, 193)
-    top, path, cleaf_other = call(
-        "shadow_7", shadow_7, "s" + "v" * 12, [top_shape, block(rank), cleaf_shape],
-        pos, got6, w, b, top, path_6, q_other, got0_other, got1_other, got1_far_other, bl, w0, wl,
-        flops=mac * n * 4,
-    )
-    send, h = call(
-        "top", top_kernel, "s" + "v" * 5, [block(eighth), block(eighth)],
-        pos, got7, top, path, c2_oth, w, flops=mac * eighth * 2,
+    top, path = call(
+        "shadow_7", shadow_7, "s" + "v" * 5, [top_shape, block(rank)],
+        pos, got6, w, b, top, path, flops=mac * n * 2,
+    )
+    mine, send = call(
+        "top", top_kernel, "s" + "v" * 6, [block(eighth), block(eighth)],
+        pos, got7, top, path, c2, c2_oth, w, flops=mac * eighth * 3,
     )
     got = swap(send, 5)
-    (mine,) = call(
-        "own_h", own_kernel, "s" + "v" * 4, [block(eighth)],
-        pos, h, send, c2, w, flops=mac * eighth,
-    )
-    far, far_other, mine_other = swap(mine, 3), swap(mine, 2), swap(mine, 1)
-    (base_near,) = call(
-        "shadow_8", shadow_8, "ss" + "v" * 6, [base_shape],
-        pos, order, send, row_basis, cleaf, cleaf_other, part_0, part_1, flops=mac * n * 2,
-    )
-    got, base_near = lax.optimization_barrier((got, base_near))
-    far_got, far_got_other = swap(got, 3), swap(got, 2)
-    (base_far,) = call(
-        "shadow_9", shadow_9, "ss" + "v" * 8, [base_shape],
-        pos, order, got, far, far_other, row_basis, cleaf, cleaf_other, part_0, part_1, flops=mac * n * 2,
-    )
-    got_other = swap(got, 1)
-    piece = (2, 2, size, half)
+
+    def piece(name, other, h):
+        own, send = call(
+            name, piece_kernel(other), "s" + "v" * 4, [block(eighth), block(eighth)],
+            pos, h, c1, c1_oth, w, flops=mac * eighth * 2,
+        )
+        return own, swap(send, 3), swap(send, 2), swap(own, 1)
+
+    near_a, far_a, far_a_other, near_a_other = piece("first_piece", 0, mine)
+    near_b, far_b, far_b_other, near_b_other = piece("second_piece", 1, got)
+    scratch = (pltpu.VMEM((2, 2, size, half), BF), pltpu.SemaphoreType.DMA((2,)))
     (done,) = call(
-        "near_columns", near_kernel, "ss" + "v" * 7, [(piece, BF)],
-        pos, order, mine, got, mine_other, got_other, base_near, g0, g1, flops=mac * n * 2,
+        "near_columns", near_kernel, "ss" + "v" * 9, [(rhs.shape, BF)],
+        pos, order, near_a, near_b, near_a_other, near_b_other, base_near, g0, g1, far_a, far_a_other,
+        scratch=scratch, flops=mac * n * 2, out_spec=HBM,
     )
     (out,) = call(
-        "far_columns", last_kernel, "ss" + "v" * 8, [(rhs.shape, BF)],
-        pos, order, far, far_got, far_other, far_got_other, base_far, g0, g1, done,
-        scratch=(pltpu.VMEM(piece, BF), pltpu.SemaphoreType.DMA((4,))),
-        flops=mac * n * 2, out_spec=HBM,
+        "far_columns", far_kernel, "ss" + "v" * 7 + "h", [(rhs.shape, BF)],
+        pos, order, far_a, far_b, far_a_other, far_b_other, base_far, g0, g1, done,
+        scratch=scratch, flops=mac * n * 2, out_spec=HBM, aliases={9: 0},
     )
     return out
 

time: 54.6 us -> 54.8 us (level)
  starting transfers between devices: 26.1 us -> 23.8 us
  waiting for transfers between devices: 6.69 us -> 8.97 us
    ppermute x19 -> x16, waiting for transfers between devices: 6.69 us -> 8.97 us  [swap(): return lax.ppermute(value, axes, [(i, i ^ flip) for i in range(devices)])]
    ppermute x19 -> x16, starting transfers between devices: 26.1 us -> 23.8 us  [swap(): return lax.ppermute(value, axes, [(i, i ^ flip) for i in range(devices)])]
    pallas_call x22 -> x21, Pallas kernels: 21.4 us -> 21.3 us  [call(): pl.pallas_call(kernel, out_shape=[jax.ShapeDtypeStruct(shape, dtype) for...]
  transfers between devices with their start and end apart: 19 -> 16, of which waited for: 4 -> 9; matrix products, arithmetic and copies ran while one was open for 0% -> 0% of each run, Pallas kernels for 29% -> 28%
where the time goes in v9:
time: 54.8 us; the launch traced here: 54.7 us
  starting transfers between devices  23.8 us (43%)
  Pallas kernels  21.3 us (39%)
  waiting for transfers between devices  8.97 us (16%)
    ppermute x16, starting transfers between devices, swap(): return lax.ppermute(value, axes, [(i, i ^ flip) for i in range(devices)])  23.8 us
    pallas_call x21, Pallas kernels, call(): pl.pallas_call(kernel, out_shape=[jax.ShapeDtypeStruct(shape, dtype) for...  21.3 us
    ppermute x16, waiting for transfers between devices, swap(): return lax.ppermute(value, axes, [(i, i ^ flip) for i in range(devices)])  8.97 us
  transfers between devices with their start and end apart: 16, of which 9 were waited for; matrix products, arithmetic and copies ran while one was open for 0% of the time, Pallas kernels for 28%

profile of v9, /device:TPU:1, one launch (start us, length us, event | category | flops | bytes accessed | tf_op | source)
XLA Modules:
  0.0 54.7 jit_solution(11903325530529937212)
XLA Ops:
  0.0 0.0 copy-start.5
  0.0 0.0 copy-start
  0.0 2.7 %send_half.1 = (bf16[2,256,256]{2,1,0:T(8,128)(2,1)S(1)}, bf16[2,128,256]{2,1,0:T(8,128)(2,1)S(1)}, bf16[2,2,256,512]{3,2,1,0:T(8,128)(2,1)S(1)}, bf16[2,1024,25...) custom-call(s32[1]{0:T(128)} %bitcast.pos, ...), custom_call_target="tpu_custom_call" | custom-call | flops 402653184 | bytes 6815756 | tf_op jit(solution)/shard_map/send_half/pallas_call | solution.py:338
  2.8 0.0 copy-start.3
  2.8 3.3 %collective-permute-start = (bf16[2,128,256]{2,1,0:T(8,128)(2,1)S(1)}, bf16[2,128,256]{2,1,0:T(8,128)(2,1)S(1)}, u32[]{:S(2)}, u32[]{:S(2)}) collective-permute-start(bf16[2,128,256]{2,1,0:T(8,128)(2,1)S(1)} %get-tuple-element.51), channel_id=1, source_target_pairs={{0,1},{1,0},{2,3},{3,2},{4,5},{5,4},{6,7},{7,6},{8,9},{9,8},{10,11... | collective-permute-start | bytes 393224 | tf_op jit(solution)/shard_map/ppermute | solution.py:362
  6.1 0.0 copy-done.5
  6.1 1.6 %keep_half.1 = (bf16[2,256,256]{2,1,0:T(8,128)(2,1)S(1)}, bf16[2,128,256]{2,1,0:T(8,128)(2,1)S(1)}, f32[2,128,256]{2,1,0:T(8,128)S(1)}) custom-call(s32[1]{0:T(128)} %bitcast.pos, s32[1,2]{1,0:T(1,128)S(1)} %copy-done.5, bf16[2,2,256,512]{3,2,1,0:T(8,128)(2,1)S(1)} %get-tuple-element.52.xt, bf16[2,2,512,256]{3,2,1,0:T(8,128)(2,1)S(1)} %get-tuple-element.53.u, ...), custom_call_target="tpu_custom_call" | custom-call | flops 402653184 | bytes 3145740 | tf_op jit(solution)/shard_map/keep_half/pallas_call | solution.py:338
  7.7 0.1 collective-permute-start.4
  7.8 0.0 collective-permute-done.got.got0
  7.8 0.2 climb_0.1
  8.1 0.4 collective-permute-start.1
  8.4 0.0 copy-done
  8.4 0.0 copy-done.3
  8.4 1.6 %shadow_1.1 = (f32[2,64,256]{2,1,0:T(8,128)S(1)}, f32[2,512,256]{2,1,0:T(8,128)S(1)}, bf16[2,2,256,256]{3,2,1,0:T(8,128)(2,1)S(1)}) custom-call(s32[1]{0:T(128)} %bitcast.pos, s32[1,2]{1,0:T(1,128)S(1)} %copy-done.5, bf16[2,64,256]{2,1,0:T(8,128)(2,1)S(1)} %get-tuple-element.58.keep.keep1, bf16[2,8,2,256,256]{4,3,2,1,0:T(8,128)(2,1)S(1)} %bitcast.4, ...), custom_call_target="tpu_custom_call" | custom-call | flops 1073741824 | bytes 8454156 | tf_op jit(solution)/shard_map/shadow_1/pallas_call | solution.py:338
  10.0 2.4 %collective-permute-done.1.got.got1 = bf16[2,64,256]{2,1,0:T(8,128)(2,1)S(1)} collective-permute-done((bf16[2,64,256]{2,1,0:T(8,128)(2,1)S(1)}, bf16[2,64,256]{2,1,0:T(8,128)(2,1)S(1)}, u32[]{:S(2)}, u32[]{:S(2)}) %collective-permute-start.1) | collective-permute-done | bytes 65568 | tf_op jit(solution)/shard_map/ppermute | solution.py:362
  12.4 0.0 copy-start.1
  12.4 0.0 copy-start.2
  12.4 0.2 climb_1.1
  12.6 1.5 %collective-permute-start.2 = (bf16[2,32,256]{2,1,0:T(8,128)(2,1)S(1)}, bf16[2,32,256]{2,1,0:T(8,128)(2,1)S(1)}, u32[]{:S(2)}, u32[]{:S(2)}) collective-permute-start(bf16[2,32,256]{2,1,0:T(8,128)(2,1)S(1)} %get-tuple-element.61), channel_id=1, source_target_pairs={{0,5},{1,4},{2,7},{3,6},{4,1},{5,0},{6,3},{7,2},{8,13},{9,12},{10,... | collective-permute-start | bytes 98312 | tf_op jit(solution)/shard_map/ppermute | solution.py:362
  14.1 0.0 copy-done.1
  14.1 0.2 copy-done.2
  14.3 0.0 copy-done.4
  14.3 2.3 %shadow_2.1 = (f32[2,32,256]{2,1,0:T(8,128)S(1)}, f32[2,512,256]{2,1,0:T(8,128)S(1)}, bf16[2,512,256]{2,1,0:T(8,128)(2,1)S(1)}, bf16[2,2,128,256]{3,2,1,0:T(8,128)(2,1)S(1)}) custom-call(s32[1]{0:T(128)} %bitcast.pos, s32[1,2]{1,0:T(1,128)S(1)} %copy-done.5, bf16[2,32,256]{2,1,0:T(8,128)(2,1)S(1)} %get-tuple-element.62.keep.keep2, ...), custom_call_target="tpu_custom_call" | custom-call | flops 1207959552 | bytes 12222476 | tf_op jit(solution)/shard_map/shadow_2/pallas_call | solution.py:338
  16.6 1.4 %collective-permute-done.2.got.got2 = bf16[2,32,256]{2,1,0:T(8,128)(2,1)S(1)} collective-permute-done((bf16[2,32,256]{2,1,0:T(8,128)(2,1)S(1)}, bf16[2,32,256]{2,1,0:T(8,128)(2,1)S(1)}, u32[]{:S(2)}, u32[]{:S(2)}) %collective-permute-start.2) | collective-permute-done | bytes 32800 | tf_op jit(solution)/shard_map/ppermute | solution.py:362
  18.0 0.2 climb_2.1.q3
  18.1 3.8 %collective-permute-start.3 = (bf16[2,32,256]{2,1,0:T(8,128)(2,1)S(1)}, bf16[2,32,256]{2,1,0:T(8,128)(2,1)S(1)}, u32[]{:S(2)}, u32[]{:S(2)}) collective-permute-start(bf16[2,32,256]{2,1,0:T(8,128)(2,1)S(1)} %climb_2.1.q3), channel_id=1, source_target_pairs={{0,13},{1,12},{2,15},{3,14},{4,9},{5,8},{6,11},{7,10},{8,5},{9,4},... | collective-permute-start | bytes 98312 | tf_op jit(solution)/shard_map/ppermute | solution.py:362
  22.0 0.0 collective-permute-done.4.got0
  22.0 1.2 %shadow_3.1 = (f32[2,32,256]{2,1,0:T(8,128)S(1)}, bf16[2,512,256]{2,1,0:T(8,128)(2,1)S(1)}, bf16[2,2,128,256]{3,2,1,0:T(8,128)(2,1)S(1)}) custom-call(s32[1]{0:T(128)} %bitcast.pos, bf16[2,32,256]{2,1,0:T(8,128)(2,1)S(1)} %climb_2.1.q3, bf16[2,8,2,256,256]{4,3,2,1,0:T(8,128)(2,1)S(1)} %bitcast.8, bf16[2,2,512,256]{3,2,1,0:T(8,128)(2,1)S(1)} %copy-done.2, ...), custom_call_target="tpu_custom_call" | custom-call | flops 671088640 | bytes 9076740 | tf_op jit(solution)/shard_map/shadow_3/pallas_call | solution.py:338
  23.2 0.7 %collective-permute-done.3.got.got3 = bf16[2,32,256]{2,1,0:T(8,128)(2,1)S(1)} collective-permute-done((bf16[2,32,256]{2,1,0:T(8,128)(2,1)S(1)}, bf16[2,32,256]{2,1,0:T(8,128)(2,1)S(1)}, u32[]{:S(2)}, u32[]{:S(2)}) %collective-permute-start.3) | collective-permute-done | bytes 32800 | tf_op jit(solution)/shard_map/ppermute | solution.py:362
  23.8 0.2 climb_3.1.q4
  24.0 1.3 %collective-permute-start.5 = (bf16[2,32,256]{2,1,0:T(8,128)(2,1)S(1)}, bf16[2,32,256]{2,1,0:T(8,128)(2,1)S(1)}, u32[]{:S(2)}, u32[]{:S(2)}) collective-permute-start(bf16[2,32,256]{2,1,0:T(8,128)(2,1)S(1)} %climb_3.1.q4), channel_id=1, source_target_pairs={{0,17},{1,16},{2,19},{3,18},{4,21},{5,20},{6,23},{7,22},{8,25},{9,... | collective-permute-start | bytes 98312 | tf_op jit(solution)/shard_map/ppermute | solution.py:362
  25.3 1.4 %shadow_4.1 = (f32[2,32,256]{2,1,0:T(8,128)S(1)}, f32[2,32,256]{2,1,0:T(8,128)S(1)}, f32[2,1024,128]{2,1,0:T(8,128)S(1)}) custom-call(s32[1]{0:T(128)} %bitcast.pos, s32[1,2]{1,0:T(1,128)S(1)} %copy-done.5, bf16[2,32,256]{2,1,0:T(8,128)(2,1)S(1)} %climb_3.1.q4, bf16[2,32,256]{2,1,0:T(8,128)(2,1)S(1)} %collective-permute-done.3.got.got3, ...), custom_call_target="tpu_custom_call" | custom-call | flops 268435456 | bytes 10027020 | tf_op jit(solution)/shard_map/shadow_4/pallas_call | solution.py:338
  26.7 0.8 %collective-permute-done.5.got.got4 = bf16[2,32,256]{2,1,0:T(8,128)(2,1)S(1)} collective-permute-done((bf16[2,32,256]{2,1,0:T(8,128)(2,1)S(1)}, bf16[2,32,256]{2,1,0:T(8,128)(2,1)S(1)}, u32[]{:S(2)}, u32[]{:S(2)}) %collective-permute-start.5) | collective-permute-done | bytes 32800 | tf_op jit(solution)/shard_map/ppermute | solution.py:362
  27.5 0.2 climb_4.1.q5
  27.7 2.6 %collective-permute-start.6 = (bf16[2,32,256]{2,1,0:T(8,128)(2,1)S(1)}, bf16[2,32,256]{2,1,0:T(8,128)(2,1)S(1)}, u32[]{:S(2)}, u32[]{:S(2)}) collective-permute-start(bf16[2,32,256]{2,1,0:T(8,128)(2,1)S(1)} %climb_4.1.q5), channel_id=1, source_target_pairs={{0,49},{1,48},{2,51},{3,50},{4,53},{5,52},{6,55},{7,54},{8,57},{9,... | collective-permute-start | bytes 98312 | tf_op jit(solution)/shard_map/ppermute | solution.py:362
  30.2 1.6 %shadow_5.1 = (f32[2,32,256]{2,1,0:T(8,128)S(1)}, f32[2,32,256]{2,1,0:T(8,128)S(1)}, bf16[2,256,256]{2,1,0:T(8,128)(2,1)S(1)}, f32[2,1024,128]{2,1,0:T(8,128)S(1)}) custom-call(s32[1]{0:T(128)} %bitcast.pos, s32[1,2]{1,0:T(1,128)S(1)} %copy-done.5, bf16[2,32,256]{2,1,0:T(8,128)(2,1)S(1)} %climb_4.1.q5, ...), custom_call_target="tpu_custom_call" | custom-call | flops 402653184 | bytes 10092556 | tf_op jit(solution)/shard_map/shadow_5/pallas_call | solution.py:338
  31.8 0.6 %collective-permute-done.6.got.got5 = bf16[2,32,256]{2,1,0:T(8,128)(2,1)S(1)} collective-permute-done((bf16[2,32,256]{2,1,0:T(8,128)(2,1)S(1)}, bf16[2,32,256]{2,1,0:T(8,128)(2,1)S(1)}, u32[]{:S(2)}, u32[]{:S(2)}) %collective-permute-start.6) | collective-permute-done | bytes 32800 | tf_op jit(solution)/shard_map/ppermute | solution.py:362
  32.3 0.2 climb_5.1.q6
  32.5 1.4 %collective-permute-start.7 = (bf16[2,32,256]{2,1,0:T(8,128)(2,1)S(1)}, bf16[2,32,256]{2,1,0:T(8,128)(2,1)S(1)}, u32[]{:S(2)}, u32[]{:S(2)}) collective-permute-start(bf16[2,32,256]{2,1,0:T(8,128)(2,1)S(1)} %climb_5.1.q6), channel_id=1, source_target_pairs={{0,65},{1,64},{2,67},{3,66},{4,69},{5,68},{6,71},{7,70},{8,73},{9,... | collective-permute-start | bytes 98312 | tf_op jit(solution)/shard_map/ppermute | solution.py:362
  33.9 1.6 %shadow_6.1 = (f32[2,32,256]{2,1,0:T(8,128)S(1)}, f32[2,32,256]{2,1,0:T(8,128)S(1)}, bf16[2,256,256]{2,1,0:T(8,128)(2,1)S(1)}, f32[2,32,256]{2,1,0:T(8,128)S(1)}...) custom-call(s32[1]{0:T(128)} %bitcast.pos, bf16[2,32,256]{2,1,0:T(8,128)(2,1)S(1)} %climb_5.1.q6, ...), custom_call_target="tpu_custom_call" | custom-call | flops 268435456 | bytes 6881284 | tf_op jit(solution)/shard_map/shadow_6/pallas_call | solution.py:338
  35.4 0.5 collective-permute-done.7.got.got6
  36.0 0.2 climb_6.1
  36.2 3.0 %collective-permute-start.8 = (bf16[2,32,256]{2,1,0:T(8,128)(2,1)S(1)}, bf16[2,32,256]{2,1,0:T(8,128)(2,1)S(1)}, u32[]{:S(2)}, u32[]{:S(2)}) collective-permute-start(bf16[2,32,256]{2,1,0:T(8,128)(2,1)S(1)} %climb_6.1), channel_id=1, source_target_pairs={{0,193},{1,192},{2,195},{3,194},{4,197},{5,196},{6,199},{7,198},{8... | collective-permute-start | bytes 98312 | tf_op jit(solution)/shard_map/ppermute | solution.py:362
  39.1 1.0 %shadow_7.1 = (f32[2,32,256]{2,1,0:T(8,128)S(1)}, bf16[2,256,256]{2,1,0:T(8,128)(2,1)S(1)}) custom-call(s32[1]{0:T(128)} %bitcast.pos, bf16[2,32,256]{2,1,0:T(8,128)(2,1)S(1)} %collective-permute-done.7.got.got6, bf16[2,8,2,256,256]{4,3,2,1,0:T(8,128)(2,1)S(1)} %bitcast.16, bf16[2,8,256,256]{3,2,1,0:T(8,128)(2,1)S(1)} %bitcast.25, ...), custom_call_target="tpu_custom_call" | custom-call | flops 268435456 | bytes 6651908 | tf_op jit(solution)/shard_map/shadow_7/pallas_call | solution.py:338
  40.1 0.9 %collective-permute-done.8.got = bf16[2,32,256]{2,1,0:T(8,128)(2,1)S(1)} collective-permute-done((bf16[2,32,256]{2,1,0:T(8,128)(2,1)S(1)}, bf16[2,32,256]{2,1,0:T(8,128)(2,1)S(1)}, u32[]{:S(2)}, u32[]{:S(2)}) %collective-permute-start.8) | collective-permute-done | bytes 32800 | tf_op jit(solution)/shard_map/ppermute | solution.py:362
  41.0 0.4 top.1
  41.4 1.9 %collective-permute-start.10 = (bf16[2,32,256]{2,1,0:T(8,128)(2,1)S(1)}, bf16[2,32,256]{2,1,0:T(8,128)(2,1)S(1)}, u32[]{:S(2)}, u32[]{:S(2)}) collective-permute-start(bf16[2,32,256]{2,1,0:T(8,128)(2,1)S(1)} %get-tuple-element.89), channel_id=1, source_target_pairs={{0,5},{1,4},{2,7},{3,6},{4,1},{5,0},{6,3},{7,2},{8,13},{9,12},{10,... | collective-permute-start | bytes 98312 | tf_op jit(solution)/shard_map/ppermute | solution.py:362
  43.4 0.3 first_piece.1
  43.6 0.6 %collective-permute-start.12 = (bf16[2,32,256]{2,1,0:T(8,128)(2,1)S(1)}, bf16[2,32,256]{2,1,0:T(8,128)(2,1)S(1)}, u32[]{:S(2)}, u32[]{:S(2)}) collective-permute-start(bf16[2,32,256]{2,1,0:T(8,128)(2,1)S(1)} %get-tuple-element.88), channel_id=1, source_target_pairs={{0,2},{1,3},{2,0},{3,1},{4,6},{5,7},{6,4},{7,5},{8,10},{9,11},{10,... | collective-permute-start | bytes 98312 | tf_op jit(solution)/shard_map/ppermute | solution.py:362
  44.2 1.3 %collective-permute-start.9 = (bf16[2,32,256]{2,1,0:T(8,128)(2,1)S(1)}, bf16[2,32,256]{2,1,0:T(8,128)(2,1)S(1)}, u32[]{:S(2)}, u32[]{:S(2)}) collective-permute-start(bf16[2,32,256]{2,1,0:T(8,128)(2,1)S(1)} %get-tuple-element.88), channel_id=1, source_target_pairs={{0,3},{1,2},{2,1},{3,0},{4,7},{5,6},{6,5},{7,4},{8,11},{9,10},{10,... | collective-permute-start | bytes 98312 | tf_op jit(solution)/shard_map/ppermute | solution.py:362
  45.5 0.1 collective-permute-start.14
  45.6 0.2 collective-permute-done.10.h
  45.8 0.3 second_piece.1
  46.1 0.5 collective-permute-start.15
  46.5 1.9 %collective-permute-start.13 = (bf16[2,32,256]{2,1,0:T(8,128)(2,1)S(1)}, bf16[2,32,256]{2,1,0:T(8,128)(2,1)S(1)}, u32[]{:S(2)}, u32[]{:S(2)}) collective-permute-start(bf16[2,32,256]{2,1,0:T(8,128)(2,1)S(1)} %get-tuple-element.90), channel_id=1, source_target_pairs={{0,2},{1,3},{2,0},{3,1},{4,6},{5,7},{6,4},{7,5},{8,10},{9,11},{10,... | collective-permute-start | bytes 98312 | tf_op jit(solution)/shard_map/ppermute | solution.py:362
  48.4 0.0 collective-permute-done.12.far_other.mine_other
  48.4 0.3 collective-permute-start.11
  48.8 0.0 collective-permute-done.9.far.mine
  48.8 0.0 collective-permute-done.14.mine_other
  48.8 0.0 collective-permute-done.15.got_other
  48.8 2.1 %near_columns.1.done = bf16[2,1024,256]{2,1,0:T(8,128)(2,1)} custom-call(s32[1]{0:T(128)} %bitcast.pos, s32[1,2]{1,0:T(1,128)S(1)} %copy-done.5, bf16[2,32,256]{2,1,0:T(8,128)(2,1)S(1)} %get-tuple-element.94.mine, bf16[2,32,256]{2,1,0:T(8,128)(2,1)S(1)} %get-tuple-element.95.got, bf16[2,32,256]{2,1,0:T(8,128)(2,1)S(1)} %collective-permute-done.14.mine_other, ...), custom_call_target="tpu_custom_call" | custom-call | flops 268435456 | bytes 2293772 | tf_op jit(solution)/shard_map/near_columns/pallas_call | solution.py:338
  50.9 0.0 collective-permute-done.13.got_other
  50.9 1.5 %collective-permute-done.11.got = bf16[2,32,256]{2,1,0:T(8,128)(2,1)S(1)} collective-permute-done((bf16[2,32,256]{2,1,0:T(8,128)(2,1)S(1)}, bf16[2,32,256]{2,1,0:T(8,128)(2,1)S(1)}, u32[]{:S(2)}, u32[]{:S(2)}) %collective-permute-start.11) | collective-permute-done | bytes 32800 | tf_op jit(solution)/shard_map/ppermute | solution.py:362
  52.4 2.1 %far_columns.1 = bf16[2,1024,256]{2,1,0:T(8,128)(2,1)} custom-call(s32[1]{0:T(128)} %bitcast.pos, s32[1,2]{1,0:T(1,128)S(1)} %copy-done.5, bf16[2,32,256]{2,1,0:T(8,128)(2,1)S(1)} %collective-permute-done.9.far.mine, bf16[2,32,256]{2,1,0:T(8,128)(2,1)S(1)} %collective-permute-done.11.got, ...), custom_call_target="tpu_custom_call", output_to_operand_aliasing={{}: (9, {})} | custom-call | flops 268435456 | bytes 3276812 | tf_op jit(solution)/shard_map/far_columns/pallas_call | solution.py:338
  (1 shorter events, 0.0 us)
Async XLA Ops:
  0.0 6.1 %copy-start.5 = (s32[1,2]{1,0:T(1,128)S(1)}, s32[1,2]{1,0:T(1,128)}, u32[]{:S(2)}) copy-start(s32[1,2]{1,0:T(1,128)} %order.15) | copy-start | bytes 28
  0.0 8.4 %copy-start = (bf16[2,1,8,2,256,256]{5,4,3,2,1,0:T(8,128)(2,1)S(1)}, bf16[2,1,8,2,256,256]{5,4,3,2,1,0:T(8,128)(2,1)}, u32[]{:S(2)}) copy-start(bf16[2,1,8,2,256,256]{5,4,3,2,1,0:T(8,128)(2,1)} %param.15) | copy-start | bytes 12582916
  2.8 5.7 %copy-start.3 = (bf16[2,2,512,512]{3,2,1,0:T(8,128)(2,1)S(1)}, bf16[2,2,512,512]{3,2,1,0:T(8,128)(2,1)}, u32[]{:S(2)}) copy-start(bf16[2,2,512,512]{3,2,1,0:T(8,128)(2,1)} %d.3) | copy-start | bytes 6291460
  2.8 5.1 %collective-permute-start = (bf16[2,128,256]{2,1,0:T(8,128)(2,1)S(1)}, bf16[2,128,256]{2,1,0:T(8,128)(2,1)S(1)}, u32[]{:S(2)}, u32[]{:S(2)}) collective-permute-start(bf16[2,128,256]{2,1,0:T(8,128)(2,1)S(1)} %get-tuple-element.51), channel_id=1, source_target_pairs={{0,1},{1,0},{2,3},{3,2},{4,5},{5,4},{6,7},{7,6},{8,9},{9,8},{10,11... | collective-permute-start | bytes 393224 | tf_op jit(solution)/shard_map/ppermute | solution.py:362
  7.7 14.2 %collective-permute-start.4 = (bf16[2,128,256]{2,1,0:T(8,128)(2,1)S(1)}, bf16[2,128,256]{2,1,0:T(8,128)(2,1)S(1)}, u32[]{:S(2)}, u32[]{:S(2)}) collective-permute-start(bf16[2,128,256]{2,1,0:T(8,128)(2,1)S(1)} %get-tuple-element.67), channel_id=1, source_target_pairs={{0,1},{1,0},{2,3},{3,2},{4,5},{5,4},{6,7},{7,6},{8,9},{9,8},{10,11... | collective-permute-start | bytes 393224 | tf_op jit(solution)/shard_map/ppermute | solution.py:362
  8.1 4.4 %collective-permute-start.1 = (bf16[2,64,256]{2,1,0:T(8,128)(2,1)S(1)}, bf16[2,64,256]{2,1,0:T(8,128)(2,1)S(1)}, u32[]{:S(2)}, u32[]{:S(2)}) collective-permute-start(bf16[2,64,256]{2,1,0:T(8,128)(2,1)S(1)} %get-tuple-element.57), channel_id=1, source_target_pairs={{0,3},{1,2},{2,1},{3,0},{4,7},{5,6},{6,5},{7,4},{8,11},{9,10},{10,... | collective-permute-start | bytes 196616 | tf_op jit(solution)/shard_map/ppermute | solution.py:362
  12.4 1.7 %copy-start.1 = (bf16[2,1,8,256,256]{4,3,2,1,0:T(8,128)(2,1)S(1)}, bf16[2,1,8,256,256]{4,3,2,1,0:T(8,128)(2,1)}, u32[]{:S(2)}) copy-start(bf16[2,1,8,256,256]{4,3,2,1,0:T(8,128)(2,1)} %param.16) | copy-start | bytes 6291460
  12.4 1.9 %copy-start.2 = (bf16[2,2,512,256]{3,2,1,0:T(8,128)(2,1)S(1)}, bf16[2,2,512,256]{3,2,1,0:T(8,128)(2,1)}, u32[]{:S(2)}) copy-start(bf16[2,2,512,256]{3,2,1,0:T(8,128)(2,1)} %r.7) | copy-start | bytes 3145732
  12.4 1.9 %copy-start.4 = (bf16[2,1,256,256]{3,2,1,0:T(8,128)(2,1)S(1)}, bf16[2,1,256,256]{3,2,1,0:T(8,128)(2,1)}, u32[]{:S(2)}) copy-start(bf16[2,1,256,256]{3,2,1,0:T(8,128)(2,1)} %bl.3) | copy-start | bytes 786436
  12.6 5.3 %collective-permute-start.2 = (bf16[2,32,256]{2,1,0:T(8,128)(2,1)S(1)}, bf16[2,32,256]{2,1,0:T(8,128)(2,1)S(1)}, u32[]{:S(2)}, u32[]{:S(2)}) collective-permute-start(bf16[2,32,256]{2,1,0:T(8,128)(2,1)S(1)} %get-tuple-element.61), channel_id=1, source_target_pairs={{0,5},{1,4},{2,7},{3,6},{4,1},{5,0},{6,3},{7,2},{8,13},{9,12},{10,... | collective-permute-start | bytes 98312 | tf_op jit(solution)/shard_map/ppermute | solution.py:362
  18.1 5.7 %collective-permute-start.3 = (bf16[2,32,256]{2,1,0:T(8,128)(2,1)S(1)}, bf16[2,32,256]{2,1,0:T(8,128)(2,1)S(1)}, u32[]{:S(2)}, u32[]{:S(2)}) collective-permute-start(bf16[2,32,256]{2,1,0:T(8,128)(2,1)S(1)} %climb_2.1.q3), channel_id=1, source_target_pairs={{0,13},{1,12},{2,15},{3,14},{4,9},{5,8},{6,11},{7,10},{8,5},{9,4},... | collective-permute-start | bytes 98312 | tf_op jit(solution)/shard_map/ppermute | solution.py:362
  24.0 3.5 %collective-permute-start.5 = (bf16[2,32,256]{2,1,0:T(8,128)(2,1)S(1)}, bf16[2,32,256]{2,1,0:T(8,128)(2,1)S(1)}, u32[]{:S(2)}, u32[]{:S(2)}) collective-permute-start(bf16[2,32,256]{2,1,0:T(8,128)(2,1)S(1)} %climb_3.1.q4), channel_id=1, source_target_pairs={{0,17},{1,16},{2,19},{3,18},{4,21},{5,20},{6,23},{7,22},{8,25},{9,... | collective-permute-start | bytes 98312 | tf_op jit(solution)/shard_map/ppermute | solution.py:362
  27.7 4.7 %collective-permute-start.6 = (bf16[2,32,256]{2,1,0:T(8,128)(2,1)S(1)}, bf16[2,32,256]{2,1,0:T(8,128)(2,1)S(1)}, u32[]{:S(2)}, u32[]{:S(2)}) collective-permute-start(bf16[2,32,256]{2,1,0:T(8,128)(2,1)S(1)} %climb_4.1.q5), channel_id=1, source_target_pairs={{0,49},{1,48},{2,51},{3,50},{4,53},{5,52},{6,55},{7,54},{8,57},{9,... | collective-permute-start | bytes 98312 | tf_op jit(solution)/shard_map/ppermute | solution.py:362
  32.5 3.5 %collective-permute-start.7 = (bf16[2,32,256]{2,1,0:T(8,128)(2,1)S(1)}, bf16[2,32,256]{2,1,0:T(8,128)(2,1)S(1)}, u32[]{:S(2)}, u32[]{:S(2)}) collective-permute-start(bf16[2,32,256]{2,1,0:T(8,128)(2,1)S(1)} %climb_5.1.q6), channel_id=1, source_target_pairs={{0,65},{1,64},{2,67},{3,66},{4,69},{5,68},{6,71},{7,70},{8,73},{9,... | collective-permute-start | bytes 98312 | tf_op jit(solution)/shard_map/ppermute | solution.py:362
  36.2 4.9 %collective-permute-start.8 = (bf16[2,32,256]{2,1,0:T(8,128)(2,1)S(1)}, bf16[2,32,256]{2,1,0:T(8,128)(2,1)S(1)}, u32[]{:S(2)}, u32[]{:S(2)}) collective-permute-start(bf16[2,32,256]{2,1,0:T(8,128)(2,1)S(1)} %climb_6.1), channel_id=1, source_target_pairs={{0,193},{1,192},{2,195},{3,194},{4,197},{5,196},{6,199},{7,198},{8... | collective-permute-start | bytes 98312 | tf_op jit(solution)/shard_map/ppermute | solution.py:362
  41.4 4.4 %collective-permute-start.10 = (bf16[2,32,256]{2,1,0:T(8,128)(2,1)S(1)}, bf16[2,32,256]{2,1,0:T(8,128)(2,1)S(1)}, u32[]{:S(2)}, u32[]{:S(2)}) collective-permute-start(bf16[2,32,256]{2,1,0:T(8,128)(2,1)S(1)} %get-tuple-element.89), channel_id=1, source_target_pairs={{0,5},{1,4},{2,7},{3,6},{4,1},{5,0},{6,3},{7,2},{8,13},{9,12},{10,... | collective-permute-start | bytes 98312 | tf_op jit(solution)/shard_map/ppermute | solution.py:362
  43.6 4.8 %collective-permute-start.12 = (bf16[2,32,256]{2,1,0:T(8,128)(2,1)S(1)}, bf16[2,32,256]{2,1,0:T(8,128)(2,1)S(1)}, u32[]{:S(2)}, u32[]{:S(2)}) collective-permute-start(bf16[2,32,256]{2,1,0:T(8,128)(2,1)S(1)} %get-tuple-element.88), channel_id=1, source_target_pairs={{0,2},{1,3},{2,0},{3,1},{4,6},{5,7},{6,4},{7,5},{8,10},{9,11},{10,... | collective-permute-start | bytes 98312 | tf_op jit(solution)/shard_map/ppermute | solution.py:362
  44.2 4.5 %collective-permute-start.9 = (bf16[2,32,256]{2,1,0:T(8,128)(2,1)S(1)}, bf16[2,32,256]{2,1,0:T(8,128)(2,1)S(1)}, u32[]{:S(2)}, u32[]{:S(2)}) collective-permute-start(bf16[2,32,256]{2,1,0:T(8,128)(2,1)S(1)} %get-tuple-element.88), channel_id=1, source_target_pairs={{0,3},{1,2},{2,1},{3,0},{4,7},{5,6},{6,5},{7,4},{8,11},{9,10},{10,... | collective-permute-start | bytes 98312 | tf_op jit(solution)/shard_map/ppermute | solution.py:362
  45.5 3.2 %collective-permute-start.14 = (bf16[2,32,256]{2,1,0:T(8,128)(2,1)S(1)}, bf16[2,32,256]{2,1,0:T(8,128)(2,1)S(1)}, u32[]{:S(2)}, u32[]{:S(2)}) collective-permute-start(bf16[2,32,256]{2,1,0:T(8,128)(2,1)S(1)} %get-tuple-element.94.mine), channel_id=1, source_target_pairs={{0,1},{1,0},{2,3},{3,2},{4,5},{5,4},{6,7},{7,6},{8,9},{9,8},{10,11... | collective-permute-start | bytes 98312 | tf_op jit(solution)/shard_map/ppermute | solution.py:362
  46.1 2.7 %collective-permute-start.15 = (bf16[2,32,256]{2,1,0:T(8,128)(2,1)S(1)}, bf16[2,32,256]{2,1,0:T(8,128)(2,1)S(1)}, u32[]{:S(2)}, u32[]{:S(2)}) collective-permute-start(bf16[2,32,256]{2,1,0:T(8,128)(2,1)S(1)} %get-tuple-element.95.got), channel_id=1, source_target_pairs={{0,1},{1,0},{2,3},{3,2},{4,5},{5,4},{6,7},{7,6},{8,9},{9,8},{10,11... | collective-permute-start | bytes 98312 | tf_op jit(solution)/shard_map/ppermute | solution.py:362
  46.5 4.4 %collective-permute-start.13 = (bf16[2,32,256]{2,1,0:T(8,128)(2,1)S(1)}, bf16[2,32,256]{2,1,0:T(8,128)(2,1)S(1)}, u32[]{:S(2)}, u32[]{:S(2)}) collective-permute-start(bf16[2,32,256]{2,1,0:T(8,128)(2,1)S(1)} %get-tuple-element.90), channel_id=1, source_target_pairs={{0,2},{1,3},{2,0},{3,1},{4,6},{5,7},{6,4},{7,5},{8,10},{9,11},{10,... | collective-permute-start | bytes 98312 | tf_op jit(solution)/shard_map/ppermute | solution.py:362
  48.4 4.0 %collective-permute-start.11 = (bf16[2,32,256]{2,1,0:T(8,128)(2,1)S(1)}, bf16[2,32,256]{2,1,0:T(8,128)(2,1)S(1)}, u32[]{:S(2)}, u32[]{:S(2)}) collective-permute-start(bf16[2,32,256]{2,1,0:T(8,128)(2,1)S(1)} %get-tuple-element.90), channel_id=1, source_target_pairs={{0,3},{1,2},{2,1},{3,0},{4,7},{5,6},{6,5},{7,4},{8,11},{9,10},{10,... | collective-permute-start | bytes 98312 | tf_op jit(solution)/shard_map/ppermute | solution.py:362

commit v10 on v7

--- a/solution.py
+++ b/solution.py
@@ -106,14 +106,17 @@
         at = pl.ds(block * size, size)
         return pltpu.make_async_copy(x.at[:, at], x_v.at[:, at], sems.at[block])
 
-    order_copy = pltpu.make_async_copy(order, order_s, sems.at[2])
-    u_copy = pltpu.make_async_copy(u, u_v, sems.at[3])
-    wl_copy = pltpu.make_async_copy(wl, wl_v, sems.at[4])
-    w_copy = pltpu.make_async_copy(w.at[:, 0], w0.at[:, 0], sems.at[5])
+    def u_copy(leaf):
+        return pltpu.make_async_copy(u.at[:, leaf], u_v.at[:, leaf], sems.at[2 + leaf])
+
+    order_copy = pltpu.make_async_copy(order, order_s, sems.at[4])
+    wl_copy = pltpu.make_async_copy(wl, wl_v, sems.at[5])
+    w_copy = pltpu.make_async_copy(w.at[:, 0], w0.at[:, 0], sems.at[6])
     x_copy(0).start()
     x_copy(1).start()
     order_copy.start()
-    u_copy.start()
+    u_copy(0).start()
+    u_copy(1).start()
     wl_copy.start()
     w_copy.start()
     keep = side(pos, 0)
@@ -125,31 +128,32 @@
             out[block, :half] = x_v[0, at, lanes].T
             out[block, half:] = x_v[1, at, lanes].T
     order_copy.wait()
-    u_copy.wait()
-    for block in range(2):
-        leaf = order_s[0, 0] ^ block
+    for leaf in range(2):
+        u_copy(leaf).wait()
+        block = order_s[0, leaf]
         qleaf[leaf] = times(xs[block], u_v[0, leaf], u_v[1, leaf]).astype(BF)
     wl_copy.wait()
     put(send, parent(qleaf, wl_v))
     w_copy.wait()
 
 
-def keep_kernel(pos, order, xt, u, wl, w0, qleaf, keep, own):
-    for block in range(2):
-        leaf = order[0, 0] ^ block
+def keep_kernel(pos, order, xt, u, wl, qleaf, keep):
+    for leaf in range(2):
+        block = order[0, leaf]
         qleaf[leaf] = times(xt[block], u[0, leaf], u[1, leaf]).astype(BF)
-    q = parent(qleaf, wl)
-    put(keep, q)
-    put(own, lift(q, w0, pos, 0))
+    put(keep, parent(qleaf, wl))
+
+
+def first_climb(pos, got, q, w, keep, send):
+    c = bit(pos, 0)
+    pair = jnp.concatenate([widen(rows(q)), widen(rows(got))], axis=1)
+    mats = jnp.concatenate([w[0, 0, c], w[1, 0, c], w[0, 0, 1 - c], w[1, 0, 1 - c]], axis=0)
+    split(dot(pair, mats).astype(BF), side(pos, 1), keep, send)
 
 
 def climb_kernel(level):
-    def kernel(pos, got, own, w, *outs):
-        q = (rows(own) + lift(rows(got), w, pos, level, 1)).astype(BF)
-        if len(outs) == 2:
-            split(q, side(pos, level + 1), *outs)
-        else:
-            put(outs[0], q)
+    def kernel(pos, got, own, w, out):
+        put(out, rows(own) + lift(rows(got), w, pos, level, 1))
 
     return kernel
 
@@ -164,8 +168,14 @@
     out[1] = dot(jnp.concatenate([im, re], axis=1), xs)
 
 
-def shadow_1(pos, order, keep, w, x, d, own, part):
+def stack(w, level, child):
+    return jnp.concatenate([w[0, level, child], w[1, level, child]], axis=0)
+
+
+def shadow_1(pos, order, keep, w, w0, wl, x, d, own, part, paths):
     put(own, lift(rows(keep), w, pos, 1))
+    for leaf in range(2):
+        put(paths.at[leaf], lift(stack(wl, 0, leaf), w0, pos, 0))
     direct(order, 0, x, d, part)
 
 
@@ -208,34 +218,37 @@
     set_base(pos, order, 0, r, cleaf, (part_0, part_1), base)
 
 
-def product(r, wl, leaf, out):
-    put(out, times(jnp.concatenate([r[0, leaf], r[1, leaf]], axis=0), wl[0, 0, leaf], wl[1, 0, leaf]))
-
-
-def shadow_5(pos, q5, got4, w, b, r, wl, top, own, top_out, path, rw):
+def product(r, paths, leaf, out):
+    put(out, times(rows(r.at[:, leaf]), paths[leaf, 0], paths[leaf, 1]))
+
+
+def shadow_5(pos, q5, got4, w, b, r, paths, top, keep1, got1, own, top_out, path, g, c1, c1_oth):
     put(own, lift(rows(q5), w, pos, 5))
     c4 = couple(rows(got4), b, pos, 4).astype(BF)
     put(top_out, rows(top) + lower(c4, w, pos, 3))
-    w3 = bit(pos, 3)
-    put(path, lift(jnp.concatenate([w[0, 3, w3], w[1, 3, w3]], axis=0), w, pos, 4))
-    product(r, wl, 0, rw)
-
-
-def shadow_6(pos, q6, got5, w, b, r, wl, top, path, own, top_out, path_out, rw):
+    put(path, lift(stack(w, 3, bit(pos, 3)), w, pos, 4))
+    product(r, paths, 0, g)
+    put(c1, couple(rows(got1), b, pos, 1))
+    put(c1_oth, couple(rows(keep1), b, pos, 1, 1))
+
+
+def shadow_6(pos, q6, got5, w, b, r, paths, top, path, own, top_out, path_6, path_7, g):
     put(own, lift(rows(q6), w, pos, 6))
     c5 = couple(rows(got5), b, pos, 5).astype(BF)
     put(top_out, rows(top) + times_t(c5, path[0], path[1]))
-    put(path_out, lift(rows(path), w, pos, 5))
-    product(r, wl, 1, rw)
-
-
-def shadow_7(pos, got6, w, b, top, path, keep2, got2, top_out, path_out, c2, c2_oth):
+    longer = lift(rows(path), w, pos, 5).astype(BF)
+    put(path_6, longer)
+    put(path_7, lift(longer, w, pos, 6))
+    product(r, paths, 1, g)
+
+
+def shadow_7(pos, got6, w, b, top, path_6, path_7, got2, const, path_out):
     c6 = couple(rows(got6), b, pos, 6).astype(BF)
-    put(top_out, rows(top) + times_t(c6, path[0], path[1]))
-    longer = lift(rows(path), w, pos, 6).astype(BF)
-    put(path_out, couple_path(longer, b, pos))
-    put(c2, couple(rows(got2), b, pos, 2))
-    put(c2_oth, couple(rows(keep2), b, pos, 2, 1))
+    h = (rows(top) + times_t(c6, path_6[0], path_6[1])).astype(BF)
+    put(const, couple(rows(got2), b, pos, 2) + lower(h, w, pos, 2))
+    path = couple_path(rows(path_7), b, pos).astype(BF)
+    half = path.shape[0] // 2
+    put(path_out, times(stack(w, 2, bit(pos, 2)), path[:half], path[half:]))
 
 
 def couple_path(path, b, pos):
@@ -246,23 +259,10 @@
     )
 
 
-def top_kernel(pos, got, top, path, c_own, c_oth, w, own, send):
-    h = (rows(top) + times_t(rows(got), path[0], path[1])).astype(BF)
-    put(own, rows(c_own) + lower(h, w, pos, 2))
-    put(send, rows(c_oth) + lower(h, w, pos, 2, 1))
-
-
-def shadow_8(pos, mine, keep1, got1, b, w0, rw0, rw1, c1, c1_oth, g0, g1):
-    put(c1, couple(rows(got1), b, pos, 1))
-    put(c1_oth, couple(rows(keep1), b, pos, 1, 1))
-    put(g0, lift(rows(rw0), w0, pos, 0))
-    put(g1, lift(rows(rw1), w0, pos, 0))
-
-
-def down_kernel(pos, mine, got, c_own, c_oth, w, own, send):
-    h = join(mine, got, side(pos, 2))
+def top_kernel(pos, got, const, path, c_own, c_oth, w, own, send):
+    h = (rows(const) + times_t(rows(got), path[0], path[1])).astype(BF)
+    put(send, rows(c_oth) + lower(h, w, pos, 1, 1))
     put(own, rows(c_own) + lower(h, w, pos, 1))
-    put(send, rows(c_oth) + lower(h, w, pos, 1, 1))
 
 
 def shadow_9(pos, order, mine, r, cleaf, part_0, part_1, base):
@@ -347,7 +347,7 @@
         return ((2, columns, rank), dtype)
 
     mac = 8 * rank * rank
-    half, quarter, eighth = n // 2, n // 4, n // 8
+    half, quarter = n // 2, n // 4
     qleaf_shape = ((2, n, rank), BF)
     hbm = [pltpu.with_memory_space_constraint(a, pltpu.HBM) for a in (order, rhs, col_basis, wl, w)]
     q_other, send, xt, x, u, wl, w0 = call(
@@ -358,99 +358,87 @@
         scratch=(
             pltpu.SMEM(order.shape, jnp.int32),
             pltpu.VMEM((2, n, size), BF),
-            pltpu.SemaphoreType.DMA((6,)),
+            pltpu.SemaphoreType.DMA((7,)),
         ),
         flops=mac * n * 3,
     )
     got0 = swap(send, 1)
-    q_mine, keep0, own = call(
-        "keep_half", keep_kernel, "ssvvvv", [qleaf_shape, block(half), block(half, F32)],
-        pos, order, xt, u, wl, w0, flops=mac * n * 3,
-    )
+    q_mine, keep0 = call(
+        "keep_half", keep_kernel, "ssvvv", [qleaf_shape, block(half)],
+        pos, order, xt, u, wl, flops=mac * n * 3,
+    )
+    keep1, send = call(
+        "climb_0", first_climb, "svvv", [block(quarter), block(quarter)],
+        pos, got0, keep0, w0, flops=mac * n,
+    )
+    got1 = swap(send, 3)
+    keep0, keep1 = lax.optimization_barrier((keep0, keep1))
     got0_other = swap(keep0, 1)
-    keep1, send = call(
-        "climb_0", climb_kernel(0), "svvv", [block(quarter), block(quarter)],
-        pos, got0, own, w0, flops=mac * half,
-    )
-    got1 = swap(send, 3)
-    own, part_0 = call(
-        "shadow_1", shadow_1, "ssvvvv", [block(quarter, F32), ((2, size, n), F32)],
-        pos, order, keep1, w, x, diag, flops=mac * n * 5,
-    )
-    keep2, send = call(
-        "climb_1", climb_kernel(1), "svvv", [block(eighth), block(eighth)],
-        pos, got1, own, w, flops=mac * quarter,
-    )
-    got2 = swap(send, 5)
-    cleaf_shape = ((2, n, rank), BF)
-    own, part_1, cleaf = call(
-        "shadow_2", shadow_2, "ss" + "v" * 9,
-        [block(eighth, F32), ((2, size, n), F32), cleaf_shape],
-        pos, order, keep2, w, x, diag, b, bl, wl, q_mine, got0, flops=mac * n * 8,
+    own, part_0, paths = call(
+        "shadow_1", shadow_1, "ss" + "v" * 6,
+        [block(quarter, F32), ((2, size, n), F32), ((2, 2, rank, rank), BF)],
+        pos, order, keep1, w, w0, wl, x, diag, flops=mac * n * 7,
     )
 
     def climb(level, got, own):
         return call(
-            "climb_%d" % level, climb_kernel(level), "svvv", [block(eighth)],
-            pos, got, own, w, flops=mac * eighth,
+            "climb_%d" % level, climb_kernel(level), "svvv", [block(quarter)],
+            pos, got, own, w, flops=mac * quarter,
         )[0]
 
+    q2 = climb(1, got1, own)
+    got2 = swap(q2, 5)
+    cleaf_shape = ((2, n, rank), BF)
+    top_shape = block(quarter, F32)
+    own, part_1, cleaf = call(
+        "shadow_2", shadow_2, "ss" + "v" * 9, [top_shape, ((2, size, n), F32), cleaf_shape],
+        pos, order, q2, w, x, diag, b, bl, wl, q_mine, got0, flops=mac * n * 8,
+    )
     base_shape = ((2, 2 * size, half), F32)
     q3 = climb(2, got2, own)
     got3 = swap(q3, 13)
     own, cleaf_other = call(
-        "shadow_3", shadow_3, "s" + "v" * 7, [block(eighth, F32), cleaf_shape],
+        "shadow_3", shadow_3, "s" + "v" * 7, [top_shape, cleaf_shape],
         pos, q3, w, b, bl, wl, q_other, got0_other, flops=mac * n * 4,
     )
     q4 = climb(3, got3, own)
     got4 = swap(q4, 17)
     own, top, base = call(
         "shadow_4", shadow_4, "ss" + "v" * 8,
-        [block(eighth, F32), block(eighth, F32), base_shape],
+        [top_shape, top_shape, base_shape],
         pos, order, q4, got3, w, b, row_basis, cleaf, part_0, part_1, flops=mac * n * 2,
     )
     q5 = climb(4, got4, own)
     got5 = swap(q5, 49)
-    own, top, path, rw0 = call(
-        "shadow_5", shadow_5, "s" + "v" * 7,
-        [block(eighth, F32), block(eighth, F32), block(rank), block(size)],
-        pos, q5, got4, w, b, row_basis, wl, top, flops=mac * n * 3,
+    own, top, path, g0, c1, c1_oth = call(
+        "shadow_5", shadow_5, "s" + "v" * 9,
+        [top_shape, top_shape, block(rank), block(size), top_shape, top_shape],
+        pos, q5, got4, w, b, row_basis, paths, top, keep1, got1, flops=mac * n * 3,
     )
     q6 = climb(5, got5, own)
     got6 = swap(q6, 65)
-    own, top, path, rw1 = call(
+    own, top, path_6, path_7, g1 = call(
         "shadow_6", shadow_6, "s" + "v" * 8,
-        [block(eighth, F32), block(eighth, F32), block(rank), block(size)],
-        pos, q6, got5, w, b, row_basis, wl, top, path, flops=mac * n * 3,
+        [top_shape, top_shape, block(rank), block(rank), block(size)],
+        pos, q6, got5, w, b, row_basis, paths, top, path, flops=mac * n * 3,
     )
     q7 = climb(6, got6, own)
     got7 = swap(q7, 193)
-    top, path, c2, c2_oth = call(
-        "shadow_7", shadow_7, "s" + "v" * 7,
-        [block(eighth, F32), block(rank), block(eighth, F32), block(eighth, F32)],
-        pos, got6, w, b, top, path, keep2, got2, flops=mac * n * 2,
+    const, path = call(
+        "shadow_7", shadow_7, "s" + "v" * 7, [top_shape, block(rank)],
+        pos, got6, w, b, top, path_6, path_7, got2, flops=mac * n * 2,
     )
     mine, send = call(
-        "top", top_kernel, "s" + "v" * 6, [block(eighth), block(eighth)],
-        pos, got7, top, path, c2, c2_oth, w, flops=mac * eighth * 3,
-    )
-    got = swap(send, 5)
-    c1, c1_oth, g0, g1 = call(
-        "shadow_8", shadow_8, "s" + "v" * 7,
-        [block(quarter, F32), block(quarter, F32), block(size), block(size)],
-        pos, mine, keep1, got1, b, w0, rw0, rw1, flops=mac * n * 5,
-    )
-    mine, send = call(
-        "down", down_kernel, "s" + "v" * 5, [block(quarter), block(quarter)],
-        pos, mine, got, c1, c1_oth, w, flops=mac * quarter * 2,
+        "top", top_kernel, "s" + "v" * 6, [block(quarter), block(quarter)],
+        pos, got7, const, path, c1, c1_oth, w, flops=mac * quarter * 3,
     )
     got = swap(send, 3)
-    mine_other = swap(mine, 1)
     (base_other,) = call(
         "shadow_9", shadow_9, "ss" + "v" * 5, [base_shape],
         pos, order, mine, row_basis, cleaf_other, part_0, part_1, flops=mac * n * 2,
     )
-    got, mine_other, base_other = lax.optimization_barrier((got, mine_other, base_other))
+    late, base_other = lax.optimization_barrier((mine, base_other))
+    mine_other = swap(late, 1)
     got_other = swap(got, 1)
     piece = (2, 2, size, half)
     (done,) = call(

time: 53.1 us -> 54.1 us (1.019)
  waiting for transfers between devices: 7.91 us -> 14.7 us
  starting transfers between devices: 23.9 us -> 18 us
    ppermute x13 -> x12, waiting for transfers between devices: 7.91 us -> 14.7 us  [swap(): return lax.ppermute(value, axes, [(i, i ^ flip) for i in range(devices)])]
    ppermute x13 -> x12, starting transfers between devices: 23.9 us -> 18 us  [swap(): return lax.ppermute(value, axes, [(i, i ^ flip) for i in range(devices)])]
    pallas_call x22 -> x20, Pallas kernels: 20.8 us -> 20.5 us  [call(): pl.pallas_call(kernel, out_shape=[jax.ShapeDtypeStruct(shape, dtype) for...]
  transfers between devices with their start and end apart: 13 -> 12, of which waited for: 9 -> 8; matrix products, arithmetic and copies ran while one was open for 0% -> 0% of each run, Pallas kernels for 27% -> 26%
where the time goes in v10:
time: 54.1 us; the launch traced here: 54 us
  Pallas kernels  20.5 us (38%)
  starting transfers between devices  18 us (33%)
  waiting for transfers between devices  14.7 us (27%)
    pallas_call x20, Pallas kernels, call(): pl.pallas_call(kernel, out_shape=[jax.ShapeDtypeStruct(shape, dtype) for...  20.5 us
    ppermute x12, starting transfers between devices, swap(): return lax.ppermute(value, axes, [(i, i ^ flip) for i in range(devices)])  18 us
    ppermute x12, waiting for transfers between devices, swap(): return lax.ppermute(value, axes, [(i, i ^ flip) for i in range(devices)])  14.7 us
  transfers between devices with their start and end apart: 12, of which 8 were waited for; matrix products, arithmetic and copies ran while one was open for 0% of the time, Pallas kernels for 26%

profile of v10, /device:TPU:1, one launch (start us, length us, event | category | flops | bytes accessed | tf_op | source)
XLA Modules:
  0.0 54.0 jit_solution(296902638873634985)
XLA Ops:
  0.0 0.0 copy-start.5
  0.0 0.0 copy-start
  0.0 2.8 %send_half.1 = (bf16[2,256,256]{2,1,0:T(8,128)(2,1)S(1)}, bf16[2,128,256]{2,1,0:T(8,128)(2,1)S(1)}, bf16[2,256,512]{2,1,0:T(8,128)(2,1)S(1)}, bf16[2,1024,256]{2...) custom-call(s32[1]{0:T(128)} %bitcast.pos, ...), custom_call_target="tpu_custom_call" | custom-call | flops 402653184 | bytes 6815756 | tf_op jit(solution)/shard_map/send_half/pallas_call | solution.py:321
  2.8 0.0 copy-start.3
  2.8 3.3 %collective-permute-start = (bf16[2,128,256]{2,1,0:T(8,128)(2,1)S(1)}, bf16[2,128,256]{2,1,0:T(8,128)(2,1)S(1)}, u32[]{:S(2)}, u32[]{:S(2)}) collective-permute-start(bf16[2,128,256]{2,1,0:T(8,128)(2,1)S(1)} %get-tuple-element.46), channel_id=1, source_target_pairs={{0,1},{1,0},{2,3},{3,2},{4,5},{5,4},{6,7},{7,6},{8,9},{9,8},{10,11... | collective-permute-start | bytes 393224 | tf_op jit(solution)/shard_map/ppermute | solution.py:344
  6.1 0.0 copy-done.5
  6.1 1.4 %keep_half.1 = (bf16[2,256,256]{2,1,0:T(8,128)(2,1)S(1)}, bf16[2,128,256]{2,1,0:T(8,128)(2,1)S(1)}) custom-call(s32[1]{0:T(128)} %bitcast.pos, s32[1,2]{1,0:T(1,128)S(1)} %copy-done.5, bf16[2,256,512]{2,1,0:T(8,128)(2,1)S(1)} %get-tuple-element.47.xt, bf16[2,2,512,256]{3,2,1,0:T(8,128)(2,1)S(1)} %get-tuple-element.48.u, ...), custom_call_target="tpu_custom_call" | custom-call | flops 402653184 | bytes 2097164 | tf_op jit(solution)/shard_map/keep_half/pallas_call | solution.py:321
  7.6 0.0 collective-permute-done.got.got0
  7.6 0.3 climb_0.1
  7.9 0.1 collective-permute-start.1
  8.0 0.3 collective-permute-start.4
  8.3 0.0 copy-done
  8.3 0.0 copy-done.3
  8.3 1.6 %shadow_1.1 = (f32[2,64,256]{2,1,0:T(8,128)S(1)}, f32[2,512,256]{2,1,0:T(8,128)S(1)}, bf16[2,2,256,256]{3,2,1,0:T(8,128)(2,1)S(1)}) custom-call(s32[1]{0:T(128)} %bitcast.pos, s32[1,2]{1,0:T(1,128)S(1)} %copy-done.5, bf16[2,64,256]{2,1,0:T(8,128)(2,1)S(1)} %get-tuple-element.54.keep.keep1, bf16[2,8,2,256,256]{4,3,2,1,0:T(8,128)(2,1)S(1)} %bitcast.4, ...), custom_call_target="tpu_custom_call" | custom-call | flops 939524096 | bytes 8454156 | tf_op jit(solution)/shard_map/shadow_1/pallas_call | solution.py:321
  9.9 1.9 %collective-permute-done.1.got.got1 = bf16[2,64,256]{2,1,0:T(8,128)(2,1)S(1)} collective-permute-done((bf16[2,64,256]{2,1,0:T(8,128)(2,1)S(1)}, bf16[2,64,256]{2,1,0:T(8,128)(2,1)S(1)}, u32[]{:S(2)}, u32[]{:S(2)}) %collective-permute-start.1) | collective-permute-done | bytes 65568 | tf_op jit(solution)/shard_map/ppermute | solution.py:344
  11.7 0.0 copy-start.1
  11.7 0.0 copy-start.4
  11.7 0.2 climb_1.1.keep
  11.9 1.9 %collective-permute-start.2 = (bf16[2,64,256]{2,1,0:T(8,128)(2,1)S(1)}, bf16[2,64,256]{2,1,0:T(8,128)(2,1)S(1)}, u32[]{:S(2)}, u32[]{:S(2)}) collective-permute-start(bf16[2,64,256]{2,1,0:T(8,128)(2,1)S(1)} %climb_1.1.keep), channel_id=1, source_target_pairs={{0,5},{1,4},{2,7},{3,6},{4,1},{5,0},{6,3},{7,2},{8,13},{9,12},{10,... | collective-permute-start | bytes 196616 | tf_op jit(solution)/shard_map/ppermute | solution.py:344
  13.8 0.0 copy-done.1
  13.8 0.0 copy-done.4
  13.8 2.0 %shadow_2.1 = (f32[2,64,256]{2,1,0:T(8,128)S(1)}, f32[2,512,256]{2,1,0:T(8,128)S(1)}, bf16[2,256,256]{2,1,0:T(8,128)(2,1)S(1)}) custom-call(s32[1]{0:T(128)} %bitcast.pos, s32[1,2]{1,0:T(1,128)S(1)} %copy-done.5, bf16[2,64,256]{2,1,0:T(8,128)(2,1)S(1)} %climb_1.1.keep, bf16[2,8,2,256,256]{4,3,2,1,0:T(8,128)(2,1)S(1)} %bitcast.6, ...), custom_call_target="tpu_custom_call" | custom-call | flops 1073741824 | bytes 10682380 | tf_op jit(solution)/shard_map/shadow_2/pallas_call | solution.py:321
  15.8 2.3 %collective-permute-done.2.got.got2 = bf16[2,64,256]{2,1,0:T(8,128)(2,1)S(1)} collective-permute-done((bf16[2,64,256]{2,1,0:T(8,128)(2,1)S(1)}, bf16[2,64,256]{2,1,0:T(8,128)(2,1)S(1)}, u32[]{:S(2)}, u32[]{:S(2)}) %collective-permute-start.2) | collective-permute-done | bytes 65568 | tf_op jit(solution)/shard_map/ppermute | solution.py:344
  18.1 0.2 climb_2.1.q3
  18.3 3.1 %collective-permute-start.3 = (bf16[2,64,256]{2,1,0:T(8,128)(2,1)S(1)}, bf16[2,64,256]{2,1,0:T(8,128)(2,1)S(1)}, u32[]{:S(2)}, u32[]{:S(2)}) collective-permute-start(bf16[2,64,256]{2,1,0:T(8,128)(2,1)S(1)} %climb_2.1.q3), channel_id=1, source_target_pairs={{0,13},{1,12},{2,15},{3,14},{4,9},{5,8},{6,11},{7,10},{8,5},{9,4},... | collective-permute-start | bytes 196616 | tf_op jit(solution)/shard_map/ppermute | solution.py:344
  21.4 0.0 collective-permute-done.4.got0_other
  21.4 0.9 %shadow_3.1 = (f32[2,64,256]{2,1,0:T(8,128)S(1)}, bf16[2,256,256]{2,1,0:T(8,128)(2,1)S(1)}) custom-call(s32[1]{0:T(128)} %bitcast.pos, bf16[2,64,256]{2,1,0:T(8,128)(2,1)S(1)} %climb_2.1.q3, bf16[2,8,2,256,256]{4,3,2,1,0:T(8,128)(2,1)S(1)} %bitcast.8, bf16[2,8,256,256]{3,2,1,0:T(8,128)(2,1)S(1)} %bitcast.19, bf16[2,1,256,256]{3,2,1,0:T(8,128)(2,1)S(1)} %copy-done.4, ...), custom_call_target="tpu_custom_call" | custom-call | flops 536870912 | bytes 7536644 | tf_op jit(solution)/shard_map/shadow_3/pallas_call | solution.py:321
  22.3 2.3 %collective-permute-done.3.got.got3 = bf16[2,64,256]{2,1,0:T(8,128)(2,1)S(1)} collective-permute-done((bf16[2,64,256]{2,1,0:T(8,128)(2,1)S(1)}, bf16[2,64,256]{2,1,0:T(8,128)(2,1)S(1)}, u32[]{:S(2)}, u32[]{:S(2)}) %collective-permute-start.3) | collective-permute-done | bytes 65568 | tf_op jit(solution)/shard_map/ppermute | solution.py:344
  24.6 0.0 copy-start.2
  24.6 0.2 climb_3.1.q4
  24.8 0.7 %collective-permute-start.5 = (bf16[2,64,256]{2,1,0:T(8,128)(2,1)S(1)}, bf16[2,64,256]{2,1,0:T(8,128)(2,1)S(1)}, u32[]{:S(2)}, u32[]{:S(2)}) collective-permute-start(bf16[2,64,256]{2,1,0:T(8,128)(2,1)S(1)} %climb_3.1.q4), channel_id=1, source_target_pairs={{0,17},{1,16},{2,19},{3,18},{4,21},{5,20},{6,23},{7,22},{8,25},{9,... | collective-permute-start | bytes 196616 | tf_op jit(solution)/shard_map/ppermute | solution.py:344
  25.6 0.3 copy-done.2
  25.9 1.4 %shadow_4.1 = (f32[2,64,256]{2,1,0:T(8,128)S(1)}, f32[2,64,256]{2,1,0:T(8,128)S(1)}, f32[2,1024,128]{2,1,0:T(8,128)S(1)}) custom-call(s32[1]{0:T(128)} %bitcast.pos, s32[1,2]{1,0:T(1,128)S(1)} %copy-done.5, bf16[2,64,256]{2,1,0:T(8,128)(2,1)S(1)} %climb_3.1.q4, bf16[2,64,256]{2,1,0:T(8,128)(2,1)S(1)} %collective-permute-done.3.got.got3, ...), custom_call_target="tpu_custom_call" | custom-call | flops 268435456 | bytes 9830412 | tf_op jit(solution)/shard_map/shadow_4/pallas_call | solution.py:321
  27.3 1.7 %collective-permute-done.5.got.got4 = bf16[2,64,256]{2,1,0:T(8,128)(2,1)S(1)} collective-permute-done((bf16[2,64,256]{2,1,0:T(8,128)(2,1)S(1)}, bf16[2,64,256]{2,1,0:T(8,128)(2,1)S(1)}, u32[]{:S(2)}, u32[]{:S(2)}) %collective-permute-start.5) | collective-permute-done | bytes 65568 | tf_op jit(solution)/shard_map/ppermute | solution.py:344
  29.0 0.2 climb_4.1.q5
  29.2 2.0 %collective-permute-start.6 = (bf16[2,64,256]{2,1,0:T(8,128)(2,1)S(1)}, bf16[2,64,256]{2,1,0:T(8,128)(2,1)S(1)}, u32[]{:S(2)}, u32[]{:S(2)}) collective-permute-start(bf16[2,64,256]{2,1,0:T(8,128)(2,1)S(1)} %climb_4.1.q5), channel_id=1, source_target_pairs={{0,49},{1,48},{2,51},{3,50},{4,53},{5,52},{6,55},{7,54},{8,57},{9,... | collective-permute-start | bytes 196616 | tf_op jit(solution)/shard_map/ppermute | solution.py:344
  31.2 1.5 %shadow_5.1 = (f32[2,64,256]{2,1,0:T(8,128)S(1)}, f32[2,64,256]{2,1,0:T(8,128)S(1)}, bf16[2,256,256]{2,1,0:T(8,128)(2,1)S(1)}, bf16[2,512,256]{2,1,0:T(8,128)(2,...) custom-call(s32[1]{0:T(128)} %bitcast.pos, bf16[2,64,256]{2,1,0:T(8,128)(2,1)S(1)} %climb_4.1.q5, ...), custom_call_target="tpu_custom_call" | custom-call | flops 402653184 | bytes 8257540 | tf_op jit(solution)/shard_map/shadow_5/pallas_call | solution.py:321
  32.6 2.0 %collective-permute-done.6.got.got5 = bf16[2,64,256]{2,1,0:T(8,128)(2,1)S(1)} collective-permute-done((bf16[2,64,256]{2,1,0:T(8,128)(2,1)S(1)}, bf16[2,64,256]{2,1,0:T(8,128)(2,1)S(1)}, u32[]{:S(2)}, u32[]{:S(2)}) %collective-permute-start.6) | collective-permute-done | bytes 65568 | tf_op jit(solution)/shard_map/ppermute | solution.py:344
  34.6 0.2 climb_5.1.q6
  34.8 0.7 %collective-permute-start.7 = (bf16[2,64,256]{2,1,0:T(8,128)(2,1)S(1)}, bf16[2,64,256]{2,1,0:T(8,128)(2,1)S(1)}, u32[]{:S(2)}, u32[]{:S(2)}) collective-permute-start(bf16[2,64,256]{2,1,0:T(8,128)(2,1)S(1)} %climb_5.1.q6), channel_id=1, source_target_pairs={{0,65},{1,64},{2,67},{3,66},{4,69},{5,68},{6,71},{7,70},{8,73},{9,... | collective-permute-start | bytes 196616 | tf_op jit(solution)/shard_map/ppermute | solution.py:344
  35.5 1.3 %shadow_6.1 = (f32[2,64,256]{2,1,0:T(8,128)S(1)}, f32[2,64,256]{2,1,0:T(8,128)S(1)}, bf16[2,256,256]{2,1,0:T(8,128)(2,1)S(1)}, bf16[2,256,256]{2,1,0:T(8,128)(2,1)S(1)}, bf16[2,512,256]{2,1,0:T(8,128)(2,1)S(1)}) custom-call(s32[1]{0:T(128)} %bitcast.pos, bf16[2,64,256]{2,1,0:T(8,128)(2,1)S(1)} %climb_5.1.q6, ...), custom_call_target="tpu_custom_call" | custom-call | flops 402653184 | bytes 8388612 | tf_op jit(solution)/shard_map/shadow_6/pallas_call | solution.py:321
  36.9 2.1 %collective-permute-done.7.got.got6 = bf16[2,64,256]{2,1,0:T(8,128)(2,1)S(1)} collective-permute-done((bf16[2,64,256]{2,1,0:T(8,128)(2,1)S(1)}, bf16[2,64,256]{2,1,0:T(8,128)(2,1)S(1)}, u32[]{:S(2)}, u32[]{:S(2)}) %collective-permute-start.7) | collective-permute-done | bytes 65568 | tf_op jit(solution)/shard_map/ppermute | solution.py:344
  39.0 0.2 climb_6.1
  39.2 2.4 %collective-permute-start.8 = (bf16[2,64,256]{2,1,0:T(8,128)(2,1)S(1)}, bf16[2,64,256]{2,1,0:T(8,128)(2,1)S(1)}, u32[]{:S(2)}, u32[]{:S(2)}) collective-permute-start(bf16[2,64,256]{2,1,0:T(8,128)(2,1)S(1)} %climb_6.1), channel_id=1, source_target_pairs={{0,193},{1,192},{2,195},{3,194},{4,197},{5,196},{6,199},{7,198},{8... | collective-permute-start | bytes 196616 | tf_op jit(solution)/shard_map/ppermute | solution.py:344
  41.6 1.6 %shadow_7.1 = (f32[2,64,256]{2,1,0:T(8,128)S(1)}, bf16[2,256,256]{2,1,0:T(8,128)(2,1)S(1)}) custom-call(s32[1]{0:T(128)} %bitcast.pos, bf16[2,64,256]{2,1,0:T(8,128)(2,1)S(1)} %collective-permute-done.7.got.got6, bf16[2,8,2,256,256]{4,3,2,1,0:T(8,128)(2,1)S(1)} %bitcast.16, bf16[2,8,256,256]{3,2,1,0:T(8,128)(2,1)S(1)} %bitcast.23, ...), custom_call_target="tpu_custom_call" | custom-call | flops 268435456 | bytes 7077892 | tf_op jit(solution)/shard_map/shadow_7/pallas_call | solution.py:321
  43.1 1.6 %collective-permute-done.8.got = bf16[2,64,256]{2,1,0:T(8,128)(2,1)S(1)} collective-permute-done((bf16[2,64,256]{2,1,0:T(8,128)(2,1)S(1)}, bf16[2,64,256]{2,1,0:T(8,128)(2,1)S(1)}, u32[]{:S(2)}, u32[]{:S(2)}) %collective-permute-start.8) | collective-permute-done | bytes 65568 | tf_op jit(solution)/shard_map/ppermute | solution.py:344
  44.8 0.4 top.1
  45.2 3.1 %collective-permute-start.10 = (bf16[2,64,256]{2,1,0:T(8,128)(2,1)S(1)}, bf16[2,64,256]{2,1,0:T(8,128)(2,1)S(1)}, u32[]{:S(2)}, u32[]{:S(2)}) collective-permute-start(bf16[2,64,256]{2,1,0:T(8,128)(2,1)S(1)} %get-tuple-element.82), channel_id=1, source_target_pairs={{0,3},{1,2},{2,1},{3,0},{4,7},{5,6},{6,5},{7,4},{8,11},{9,10},{10,... | collective-permute-start | bytes 196616 | tf_op jit(solution)/shard_map/ppermute | solution.py:344
  48.3 1.0 %shadow_9.1.base = f32[2,1024,128]{2,1,0:T(8,128)S(1)} custom-call(s32[1]{0:T(128)} %bitcast.pos, s32[1,2]{1,0:T(1,128)S(1)} %copy-done.5, bf16[2,64,256]{2,1,0:T(8,128)(2,1)S(1)} %get-tuple-element.81.mine, bf16[2,2,512,256]{3,2,1,0:T(8,128)(2,1)S(1)} %copy-done.2, bf16[2,256,256]{2,1,0:T(8,128)(2,1)S(1)} %get-tuple-element.80.cleaf, ...), custom_call_target="tpu_custom_call" | custom-call | flops 268435456 | bytes 3473420 | tf_op jit(solution)/shard_map/shadow_9/pallas_call | solution.py:321
  49.3 0.2 collective-permute-start.9
  49.5 0.9 %collective-permute-done.10.got = bf16[2,64,256]{2,1,0:T(8,128)(2,1)S(1)} collective-permute-done((bf16[2,64,256]{2,1,0:T(8,128)(2,1)S(1)}, bf16[2,64,256]{2,1,0:T(8,128)(2,1)S(1)}, u32[]{:S(2)}, u32[]{:S(2)}) %collective-permute-start.10) | collective-permute-done | bytes 65568 | tf_op jit(solution)/shard_map/ppermute | solution.py:344
  50.4 0.2 collective-permute-start.11
  50.6 1.0 %own_columns.1.done = bf16[2,2,512,128]{3,2,1,0:T(8,128)(2,1)S(1)} custom-call(s32[1]{0:T(128)} %bitcast.pos, s32[1,2]{1,0:T(1,128)S(1)} %copy-done.5, bf16[2,64,256]{2,1,0:T(8,128)(2,1)S(1)} %get-tuple-element.81.mine, bf16[2,64,256]{2,1,0:T(8,128)(2,1)S(1)} %collective-permute-done.10.got, f32[2,1024,128]{2,1,0:T(8,128)S(1)} %get-tuple-element.86.base, ...), custom_call_target="tpu_custom_call" | custom-call | flops 268435456 | bytes 2228236 | tf_op jit(solution)/shard_map/own_columns/pallas_call | solution.py:321
  51.6 0.0 collective-permute-done.9.mine
  51.6 0.0 collective-permute-done.11.got
  51.6 2.2 %other_columns.1 = bf16[2,1024,256]{2,1,0:T(8,128)(2,1)} custom-call(s32[1]{0:T(128)} %bitcast.pos, s32[1,2]{1,0:T(1,128)S(1)} %copy-done.5, bf16[2,64,256]{2,1,0:T(8,128)(2,1)S(1)} %collective-permute-done.9.mine, bf16[2,64,256]{2,1,0:T(8,128)(2,1)S(1)} %collective-permute-done.11.got, f32[2,1024,128]{2,1,0:T(8,128)S(1)} %shadow_9.1.base, ...), custom_call_target="tpu_custom_call" | custom-call | flops 268435456 | bytes 2752524 | tf_op jit(solution)/shard_map/other_columns/pallas_call | solution.py:321
Async XLA Ops:
  0.0 6.1 %copy-start.5 = (s32[1,2]{1,0:T(1,128)S(1)}, s32[1,2]{1,0:T(1,128)}, u32[]{:S(2)}) copy-start(s32[1,2]{1,0:T(1,128)} %order.15) | copy-start | bytes 28
  0.0 8.3 %copy-start = (bf16[2,1,8,2,256,256]{5,4,3,2,1,0:T(8,128)(2,1)S(1)}, bf16[2,1,8,2,256,256]{5,4,3,2,1,0:T(8,128)(2,1)}, u32[]{:S(2)}) copy-start(bf16[2,1,8,2,256,256]{5,4,3,2,1,0:T(8,128)(2,1)} %param.15) | copy-start | bytes 12582916
  2.8 5.5 %copy-start.3 = (bf16[2,2,512,512]{3,2,1,0:T(8,128)(2,1)S(1)}, bf16[2,2,512,512]{3,2,1,0:T(8,128)(2,1)}, u32[]{:S(2)}) copy-start(bf16[2,2,512,512]{3,2,1,0:T(8,128)(2,1)} %d.3) | copy-start | bytes 6291460
  2.8 4.8 %collective-permute-start = (bf16[2,128,256]{2,1,0:T(8,128)(2,1)S(1)}, bf16[2,128,256]{2,1,0:T(8,128)(2,1)S(1)}, u32[]{:S(2)}, u32[]{:S(2)}) collective-permute-start(bf16[2,128,256]{2,1,0:T(8,128)(2,1)S(1)} %get-tuple-element.46), channel_id=1, source_target_pairs={{0,1},{1,0},{2,3},{3,2},{4,5},{5,4},{6,7},{7,6},{8,9},{9,8},{10,11... | collective-permute-start | bytes 393224 | tf_op jit(solution)/shard_map/ppermute | solution.py:344
  7.9 3.8 %collective-permute-start.1 = (bf16[2,64,256]{2,1,0:T(8,128)(2,1)S(1)}, bf16[2,64,256]{2,1,0:T(8,128)(2,1)S(1)}, u32[]{:S(2)}, u32[]{:S(2)}) collective-permute-start(bf16[2,64,256]{2,1,0:T(8,128)(2,1)S(1)} %get-tuple-element.52), channel_id=1, source_target_pairs={{0,3},{1,2},{2,1},{3,0},{4,7},{5,6},{6,5},{7,4},{8,11},{9,10},{10,... | collective-permute-start | bytes 196616 | tf_op jit(solution)/shard_map/ppermute | solution.py:344
  8.0 13.4 %collective-permute-start.4 = (bf16[2,128,256]{2,1,0:T(8,128)(2,1)S(1)}, bf16[2,128,256]{2,1,0:T(8,128)(2,1)S(1)}, u32[]{:S(2)}, u32[]{:S(2)}) collective-permute-start(bf16[2,128,256]{2,1,0:T(8,128)(2,1)S(1)} %get-tuple-element.60.q), channel_id=1, source_target_pairs={{0,1},{1,0},{2,3},{3,2},{4,5},{5,4},{6,7},{7,6},{8,9},{9,8},{10,11... | collective-permute-start | bytes 393224 | tf_op jit(solution)/shard_map/ppermute | solution.py:344
  11.7 2.1 %copy-start.1 = (bf16[2,1,8,256,256]{4,3,2,1,0:T(8,128)(2,1)S(1)}, bf16[2,1,8,256,256]{4,3,2,1,0:T(8,128)(2,1)}, u32[]{:S(2)}) copy-start(bf16[2,1,8,256,256]{4,3,2,1,0:T(8,128)(2,1)} %param.16) | copy-start | bytes 6291460
  11.7 2.1 %copy-start.4 = (bf16[2,1,256,256]{3,2,1,0:T(8,128)(2,1)S(1)}, bf16[2,1,256,256]{3,2,1,0:T(8,128)(2,1)}, u32[]{:S(2)}) copy-start(bf16[2,1,256,256]{3,2,1,0:T(8,128)(2,1)} %bl.3) | copy-start | bytes 786436
  11.9 6.2 %collective-permute-start.2 = (bf16[2,64,256]{2,1,0:T(8,128)(2,1)S(1)}, bf16[2,64,256]{2,1,0:T(8,128)(2,1)S(1)}, u32[]{:S(2)}, u32[]{:S(2)}) collective-permute-start(bf16[2,64,256]{2,1,0:T(8,128)(2,1)S(1)} %climb_1.1.keep), channel_id=1, source_target_pairs={{0,5},{1,4},{2,7},{3,6},{4,1},{5,0},{6,3},{7,2},{8,13},{9,12},{10,... | collective-permute-start | bytes 196616 | tf_op jit(solution)/shard_map/ppermute | solution.py:344
  18.3 6.3 %collective-permute-start.3 = (bf16[2,64,256]{2,1,0:T(8,128)(2,1)S(1)}, bf16[2,64,256]{2,1,0:T(8,128)(2,1)S(1)}, u32[]{:S(2)}, u32[]{:S(2)}) collective-permute-start(bf16[2,64,256]{2,1,0:T(8,128)(2,1)S(1)} %climb_2.1.q3), channel_id=1, source_target_pairs={{0,13},{1,12},{2,15},{3,14},{4,9},{5,8},{6,11},{7,10},{8,5},{9,4},... | collective-permute-start | bytes 196616 | tf_op jit(solution)/shard_map/ppermute | solution.py:344
  24.6 1.2 %copy-start.2 = (bf16[2,2,512,256]{3,2,1,0:T(8,128)(2,1)S(1)}, bf16[2,2,512,256]{3,2,1,0:T(8,128)(2,1)}, u32[]{:S(2)}) copy-start(bf16[2,2,512,256]{3,2,1,0:T(8,128)(2,1)} %r.7) | copy-start | bytes 3145732
  24.8 4.2 %collective-permute-start.5 = (bf16[2,64,256]{2,1,0:T(8,128)(2,1)S(1)}, bf16[2,64,256]{2,1,0:T(8,128)(2,1)S(1)}, u32[]{:S(2)}, u32[]{:S(2)}) collective-permute-start(bf16[2,64,256]{2,1,0:T(8,128)(2,1)S(1)} %climb_3.1.q4), channel_id=1, source_target_pairs={{0,17},{1,16},{2,19},{3,18},{4,21},{5,20},{6,23},{7,22},{8,25},{9,... | collective-permute-start | bytes 196616 | tf_op jit(solution)/shard_map/ppermute | solution.py:344
  29.2 5.4 %collective-permute-start.6 = (bf16[2,64,256]{2,1,0:T(8,128)(2,1)S(1)}, bf16[2,64,256]{2,1,0:T(8,128)(2,1)S(1)}, u32[]{:S(2)}, u32[]{:S(2)}) collective-permute-start(bf16[2,64,256]{2,1,0:T(8,128)(2,1)S(1)} %climb_4.1.q5), channel_id=1, source_target_pairs={{0,49},{1,48},{2,51},{3,50},{4,53},{5,52},{6,55},{7,54},{8,57},{9,... | collective-permute-start | bytes 196616 | tf_op jit(solution)/shard_map/ppermute | solution.py:344
  34.8 4.2 %collective-permute-start.7 = (bf16[2,64,256]{2,1,0:T(8,128)(2,1)S(1)}, bf16[2,64,256]{2,1,0:T(8,128)(2,1)S(1)}, u32[]{:S(2)}, u32[]{:S(2)}) collective-permute-start(bf16[2,64,256]{2,1,0:T(8,128)(2,1)S(1)} %climb_5.1.q6), channel_id=1, source_target_pairs={{0,65},{1,64},{2,67},{3,66},{4,69},{5,68},{6,71},{7,70},{8,73},{9,... | collective-permute-start | bytes 196616 | tf_op jit(solution)/shard_map/ppermute | solution.py:344
  39.2 5.6 %collective-permute-start.8 = (bf16[2,64,256]{2,1,0:T(8,128)(2,1)S(1)}, bf16[2,64,256]{2,1,0:T(8,128)(2,1)S(1)}, u32[]{:S(2)}, u32[]{:S(2)}) collective-permute-start(bf16[2,64,256]{2,1,0:T(8,128)(2,1)S(1)} %climb_6.1), channel_id=1, source_target_pairs={{0,193},{1,192},{2,195},{3,194},{4,197},{5,196},{6,199},{7,198},{8... | collective-permute-start | bytes 196616 | tf_op jit(solution)/shard_map/ppermute | solution.py:344
  45.2 5.2 %collective-permute-start.10 = (bf16[2,64,256]{2,1,0:T(8,128)(2,1)S(1)}, bf16[2,64,256]{2,1,0:T(8,128)(2,1)S(1)}, u32[]{:S(2)}, u32[]{:S(2)}) collective-permute-start(bf16[2,64,256]{2,1,0:T(8,128)(2,1)S(1)} %get-tuple-element.82), channel_id=1, source_target_pairs={{0,3},{1,2},{2,1},{3,0},{4,7},{5,6},{6,5},{7,4},{8,11},{9,10},{10,... | collective-permute-start | bytes 196616 | tf_op jit(solution)/shard_map/ppermute | solution.py:344
  49.3 2.3 %collective-permute-start.9 = (bf16[2,64,256]{2,1,0:T(8,128)(2,1)S(1)}, bf16[2,64,256]{2,1,0:T(8,128)(2,1)S(1)}, u32[]{:S(2)}, u32[]{:S(2)}) collective-permute-start(bf16[2,64,256]{2,1,0:T(8,128)(2,1)S(1)} %get-tuple-element.81.mine), channel_id=1, source_target_pairs={{0,1},{1,0},{2,3},{3,2},{4,5},{5,4},{6,7},{7,6},{8,9},{9,8},{10,11... | collective-permute-start | bytes 196616 | tf_op jit(solution)/shard_map/ppermute | solution.py:344
  50.4 1.3 %collective-permute-start.11 = (bf16[2,64,256]{2,1,0:T(8,128)(2,1)S(1)}, bf16[2,64,256]{2,1,0:T(8,128)(2,1)S(1)}, u32[]{:S(2)}, u32[]{:S(2)}) collective-permute-start(bf16[2,64,256]{2,1,0:T(8,128)(2,1)S(1)} %collective-permute-done.10.got), channel_id=1, source_target_pairs={{0,1},{1,0},{2,3},{3,2},{4,5},{5,4},{6,7},{7,6},{8,9},{9,8},{10,11... | collective-permute-start | bytes 196616 | tf_op jit(solution)/shard_map/ppermute | solution.py:344

commit v11 on v10

--- a/solution.py
+++ b/solution.py
@@ -94,8 +94,9 @@
 
 
 def parent(qleaf, wl):
-    q = times(qleaf[0], wl[0, 0, 0], wl[1, 0, 0]) + times(qleaf[1], wl[0, 0, 1], wl[1, 0, 1])
-    return q.astype(BF)
+    pair = jnp.concatenate([widen(qleaf[0]), widen(qleaf[1])], axis=1)
+    mats = jnp.concatenate([wl[0, 0, 0], wl[1, 0, 0], wl[0, 0, 1], wl[1, 0, 1]], axis=0)
+    return dot(pair, mats).astype(BF)
 
 
 def send_kernel(pos, order, x, u, wl, w, qleaf, send, xt, x_v, u_v, wl_v, w0, order_s, xs, sems):
@@ -152,8 +153,12 @@
 
 
 def climb_kernel(level):
-    def kernel(pos, got, own, w, out):
-        put(out, rows(own) + lift(rows(got), w, pos, level, 1))
+    def kernel(pos, got, own, w, *outs):
+        q = (rows(own) + lift(rows(got), w, pos, level, 1)).astype(BF)
+        if len(outs) == 2:
+            split(q, side(pos, level + 1), *outs)
+        else:
+            put(outs[0], q)
 
     return kernel
 
@@ -222,33 +227,31 @@
     put(out, times(rows(r.at[:, leaf]), paths[leaf, 0], paths[leaf, 1]))
 
 
-def shadow_5(pos, q5, got4, w, b, r, paths, top, keep1, got1, own, top_out, path, g, c1, c1_oth):
+def shadow_5(pos, q5, got4, w, b, r, paths, top, own, top_out, path, g):
     put(own, lift(rows(q5), w, pos, 5))
     c4 = couple(rows(got4), b, pos, 4).astype(BF)
     put(top_out, rows(top) + lower(c4, w, pos, 3))
     put(path, lift(stack(w, 3, bit(pos, 3)), w, pos, 4))
     product(r, paths, 0, g)
-    put(c1, couple(rows(got1), b, pos, 1))
-    put(c1_oth, couple(rows(keep1), b, pos, 1, 1))
-
-
-def shadow_6(pos, q6, got5, w, b, r, paths, top, path, own, top_out, path_6, path_7, g):
+
+
+def shadow_6(pos, q6, got5, w, b, r, paths, top, path, own, top_out, path_6, path_8, g):
     put(own, lift(rows(q6), w, pos, 6))
     c5 = couple(rows(got5), b, pos, 5).astype(BF)
     put(top_out, rows(top) + times_t(c5, path[0], path[1]))
     longer = lift(rows(path), w, pos, 5).astype(BF)
     put(path_6, longer)
-    put(path_7, lift(longer, w, pos, 6))
+    put(path_8, couple_path(lift(longer, w, pos, 6).astype(BF), b, pos))
     product(r, paths, 1, g)
 
 
-def shadow_7(pos, got6, w, b, top, path_6, path_7, got2, const, path_out):
+def shadow_7(pos, got6, w, b, top, path_6, path_8, keep2, got2, const, const_oth, path, path_oth):
     c6 = couple(rows(got6), b, pos, 6).astype(BF)
     h = (rows(top) + times_t(c6, path_6[0], path_6[1])).astype(BF)
     put(const, couple(rows(got2), b, pos, 2) + lower(h, w, pos, 2))
-    path = couple_path(rows(path_7), b, pos).astype(BF)
-    half = path.shape[0] // 2
-    put(path_out, times(stack(w, 2, bit(pos, 2)), path[:half], path[half:]))
+    put(const_oth, couple(rows(keep2), b, pos, 2, 1) + lower(h, w, pos, 2, 1))
+    for flip, out in enumerate((path, path_oth)):
+        put(out, times(stack(w, 2, bit(pos, 2) ^ flip), path_8[0], path_8[1]))
 
 
 def couple_path(path, b, pos):
@@ -259,8 +262,19 @@
     )
 
 
-def top_kernel(pos, got, const, path, c_own, c_oth, w, own, send):
-    h = (rows(const) + times_t(rows(got), path[0], path[1])).astype(BF)
+def top_kernel(pos, got, const, const_oth, path, path_oth, own, send):
+    q = widen(rows(got))
+    put(send, rows(const_oth) + dot(q, jnp.concatenate([path_oth[0], path_oth[1]], axis=1), NT))
+    put(own, rows(const) + dot(q, jnp.concatenate([path[0], path[1]], axis=1), NT))
+
+
+def shadow_8(pos, mine, keep1, got1, b, c1, c1_oth):
+    put(c1, couple(rows(got1), b, pos, 1))
+    put(c1_oth, couple(rows(keep1), b, pos, 1, 1))
+
+
+def down_kernel(pos, mine, got, c_own, c_oth, w, own, send):
+    h = join(mine, got, side(pos, 2))
     put(send, rows(c_oth) + lower(h, w, pos, 1, 1))
     put(own, rows(c_own) + lower(h, w, pos, 1))
 
@@ -347,7 +361,7 @@
         return ((2, columns, rank), dtype)
 
     mac = 8 * rank * rank
-    half, quarter = n // 2, n // 4
+    half, quarter, eighth = n // 2, n // 4, n // 8
     qleaf_shape = ((2, n, rank), BF)
     hbm = [pltpu.with_memory_space_constraint(a, pltpu.HBM) for a in (order, rhs, col_basis, wl, w)]
     q_other, send, xt, x, u, wl, w0 = call(
@@ -382,17 +396,20 @@
 
     def climb(level, got, own):
         return call(
-            "climb_%d" % level, climb_kernel(level), "svvv", [block(quarter)],
-            pos, got, own, w, flops=mac * quarter,
+            "climb_%d" % level, climb_kernel(level), "svvv", [block(eighth)],
+            pos, got, own, w, flops=mac * eighth,
         )[0]
 
-    q2 = climb(1, got1, own)
-    got2 = swap(q2, 5)
+    keep2, send = call(
+        "climb_1", climb_kernel(1), "svvv", [block(eighth), block(eighth)],
+        pos, got1, own, w, flops=mac * quarter,
+    )
+    got2 = swap(send, 5)
     cleaf_shape = ((2, n, rank), BF)
-    top_shape = block(quarter, F32)
+    top_shape = block(eighth, F32)
     own, part_1, cleaf = call(
         "shadow_2", shadow_2, "ss" + "v" * 9, [top_shape, ((2, size, n), F32), cleaf_shape],
-        pos, order, q2, w, x, diag, b, bl, wl, q_mine, got0, flops=mac * n * 8,
+        pos, order, keep2, w, x, diag, b, bl, wl, q_mine, got0, flops=mac * n * 8,
     )
     base_shape = ((2, 2 * size, half), F32)
     q3 = climb(2, got2, own)
@@ -410,27 +427,37 @@
     )
     q5 = climb(4, got4, own)
     got5 = swap(q5, 49)
-    own, top, path, g0, c1, c1_oth = call(
-        "shadow_5", shadow_5, "s" + "v" * 9,
-        [top_shape, top_shape, block(rank), block(size), top_shape, top_shape],
-        pos, q5, got4, w, b, row_basis, paths, top, keep1, got1, flops=mac * n * 3,
+    own, top, path, g0 = call(
+        "shadow_5", shadow_5, "s" + "v" * 7,
+        [top_shape, top_shape, block(rank), block(size)],
+        pos, q5, got4, w, b, row_basis, paths, top, flops=mac * n * 3,
     )
     q6 = climb(5, got5, own)
     got6 = swap(q6, 65)
-    own, top, path_6, path_7, g1 = call(
+    own, top, path_6, path_8, g1 = call(
         "shadow_6", shadow_6, "s" + "v" * 8,
         [top_shape, top_shape, block(rank), block(rank), block(size)],
-        pos, q6, got5, w, b, row_basis, paths, top, path, flops=mac * n * 3,
+        pos, q6, got5, w, b, row_basis, paths, top, path, flops=mac * n * 4,
     )
     q7 = climb(6, got6, own)
     got7 = swap(q7, 193)
-    const, path = call(
-        "shadow_7", shadow_7, "s" + "v" * 7, [top_shape, block(rank)],
-        pos, got6, w, b, top, path_6, path_7, got2, flops=mac * n * 2,
+    const, const_oth, path, path_oth = call(
+        "shadow_7", shadow_7, "s" + "v" * 8,
+        [top_shape, top_shape, block(rank), block(rank)],
+        pos, got6, w, b, top, path_6, path_8, keep2, got2, flops=mac * n * 3,
     )
     mine, send = call(
-        "top", top_kernel, "s" + "v" * 6, [block(quarter), block(quarter)],
-        pos, got7, const, path, c1, c1_oth, w, flops=mac * quarter * 3,
+        "top", top_kernel, "s" + "v" * 5, [block(eighth), block(eighth)],
+        pos, got7, const, const_oth, path, path_oth, flops=mac * eighth * 2,
+    )
+    got = swap(send, 5)
+    c1, c1_oth = call(
+        "shadow_8", shadow_8, "s" + "v" * 4, [block(quarter, F32), block(quarter, F32)],
+        pos, mine, keep1, got1, b, flops=mac * half,
+    )
+    mine, send = call(
+        "down", down_kernel, "s" + "v" * 5, [block(quarter), block(quarter)],
+        pos, mine, got, c1, c1_oth, w, flops=mac * quarter * 2,
     )
     got = swap(send, 3)
     (base_other,) = call(

time: 54.1 us -> 53.1 us (0.982)
  waiting for transfers between devices: 14.7 us -> 7.76 us
  starting transfers between devices: 18 us -> 23.9 us
    ppermute x12 -> x13, waiting for transfers between devices: 14.7 us -> 7.76 us  [swap(): return lax.ppermute(value, axes, [(i, i ^ flip) for i in range(devices)])]
    ppermute x12 -> x13, starting transfers between devices: 18 us -> 23.9 us  [swap(): return lax.ppermute(value, axes, [(i, i ^ flip) for i in range(devices)])]
    pallas_call x20 -> x22, Pallas kernels: 20.5 us -> 21 us  [call(): pl.pallas_call(kernel, out_shape=[jax.ShapeDtypeStruct(shape, dtype) for...]
  transfers between devices with their start and end apart: 12 -> 13, of which waited for: 8 -> 8; matrix products, arithmetic and copies ran while one was open for 0% -> 0% of each run, Pallas kernels for 26% -> 27%
where the time goes in v11:
time: 53.1 us; the launch traced here: 53 us
  starting transfers between devices  23.9 us (45%)
  Pallas kernels  21 us (40%)
  waiting for transfers between devices  7.76 us (15%)
    ppermute x13, starting transfers between devices, swap(): return lax.ppermute(value, axes, [(i, i ^ flip) for i in range(devices)])  23.9 us
    pallas_call x22, Pallas kernels, call(): pl.pallas_call(kernel, out_shape=[jax.ShapeDtypeStruct(shape, dtype) for...  21 us
    ppermute x13, waiting for transfers between devices, swap(): return lax.ppermute(value, axes, [(i, i ^ flip) for i in range(devices)])  7.76 us
  transfers between devices with their start and end apart: 13, of which 8 were waited for; matrix products, arithmetic and copies ran while one was open for 0% of the time, Pallas kernels for 27%

profile of v11, /device:TPU:1, one launch (start us, length us, event | category | flops | bytes accessed | tf_op | source)
XLA Modules:
  0.0 53.0 jit_solution(5292507636550844137)
XLA Ops:
  0.0 0.0 copy-start.5
  0.0 0.0 copy-start
  0.0 2.8 %send_half.1 = (bf16[2,256,256]{2,1,0:T(8,128)(2,1)S(1)}, bf16[2,128,256]{2,1,0:T(8,128)(2,1)S(1)}, bf16[2,256,512]{2,1,0:T(8,128)(2,1)S(1)}, bf16[2,1024,256]{2...) custom-call(s32[1]{0:T(128)} %bitcast.pos, ...), custom_call_target="tpu_custom_call" | custom-call | flops 402653184 | bytes 6815756 | tf_op jit(solution)/shard_map/send_half/pallas_call | solution.py:335
  2.8 0.0 copy-start.3
  2.8 3.3 %collective-permute-start = (bf16[2,128,256]{2,1,0:T(8,128)(2,1)S(1)}, bf16[2,128,256]{2,1,0:T(8,128)(2,1)S(1)}, u32[]{:S(2)}, u32[]{:S(2)}) collective-permute-start(bf16[2,128,256]{2,1,0:T(8,128)(2,1)S(1)} %get-tuple-element.52), channel_id=1, source_target_pairs={{0,1},{1,0},{2,3},{3,2},{4,5},{5,4},{6,7},{7,6},{8,9},{9,8},{10,11... | collective-permute-start | bytes 393224 | tf_op jit(solution)/shard_map/ppermute | solution.py:358
  6.1 0.0 copy-done.5
  6.1 1.3 %keep_half.1 = (bf16[2,256,256]{2,1,0:T(8,128)(2,1)S(1)}, bf16[2,128,256]{2,1,0:T(8,128)(2,1)S(1)}) custom-call(s32[1]{0:T(128)} %bitcast.pos, s32[1,2]{1,0:T(1,128)S(1)} %copy-done.5, bf16[2,256,512]{2,1,0:T(8,128)(2,1)S(1)} %get-tuple-element.53.xt, bf16[2,2,512,256]{3,2,1,0:T(8,128)(2,1)S(1)} %get-tuple-element.54.u, ...), custom_call_target="tpu_custom_call" | custom-call | flops 402653184 | bytes 2097164 | tf_op jit(solution)/shard_map/keep_half/pallas_call | solution.py:335
  7.5 0.0 collective-permute-done.got.got0
  7.5 0.3 climb_0.1
  7.8 0.1 collective-permute-start.1
  7.9 0.3 collective-permute-start.4
  8.2 0.0 copy-done
  8.2 0.0 copy-done.3
  8.2 1.6 %shadow_1.1 = (f32[2,64,256]{2,1,0:T(8,128)S(1)}, f32[2,512,256]{2,1,0:T(8,128)S(1)}, bf16[2,2,256,256]{3,2,1,0:T(8,128)(2,1)S(1)}) custom-call(s32[1]{0:T(128)} %bitcast.pos, s32[1,2]{1,0:T(1,128)S(1)} %copy-done.5, bf16[2,64,256]{2,1,0:T(8,128)(2,1)S(1)} %get-tuple-element.60.keep.keep1, bf16[2,8,2,256,256]{4,3,2,1,0:T(8,128)(2,1)S(1)} %bitcast.4, ...), custom_call_target="tpu_custom_call" | custom-call | flops 939524096 | bytes 8454156 | tf_op jit(solution)/shard_map/shadow_1/pallas_call | solution.py:335
  9.7 1.9 %collective-permute-done.1.got.got1 = bf16[2,64,256]{2,1,0:T(8,128)(2,1)S(1)} collective-permute-done((bf16[2,64,256]{2,1,0:T(8,128)(2,1)S(1)}, bf16[2,64,256]{2,1,0:T(8,128)(2,1)S(1)}, u32[]{:S(2)}, u32[]{:S(2)}) %collective-permute-start.1) | collective-permute-done | bytes 65568 | tf_op jit(solution)/shard_map/ppermute | solution.py:358
  11.6 0.0 copy-start.1
  11.6 0.0 copy-start.4
  11.6 0.2 climb_1.1
  11.8 1.9 %collective-permute-start.2 = (bf16[2,32,256]{2,1,0:T(8,128)(2,1)S(1)}, bf16[2,32,256]{2,1,0:T(8,128)(2,1)S(1)}, u32[]{:S(2)}, u32[]{:S(2)}) collective-permute-start(bf16[2,32,256]{2,1,0:T(8,128)(2,1)S(1)} %get-tuple-element.63), channel_id=1, source_target_pairs={{0,5},{1,4},{2,7},{3,6},{4,1},{5,0},{6,3},{7,2},{8,13},{9,12},{10,... | collective-permute-start | bytes 98312 | tf_op jit(solution)/shard_map/ppermute | solution.py:358
  13.7 0.0 copy-done.1
  13.7 0.0 copy-done.4
  13.7 2.0 %shadow_2.1 = (f32[2,32,256]{2,1,0:T(8,128)S(1)}, f32[2,512,256]{2,1,0:T(8,128)S(1)}, bf16[2,256,256]{2,1,0:T(8,128)(2,1)S(1)}) custom-call(s32[1]{0:T(128)} %bitcast.pos, s32[1,2]{1,0:T(1,128)S(1)} %copy-done.5, bf16[2,32,256]{2,1,0:T(8,128)(2,1)S(1)} %get-tuple-element.64.keep.keep2, bf16[2,8,2,256,256]{4,3,2,1,0:T(8,128)(2,1)S(1)} %bitcast.6, ...), custom_call_target="tpu_custom_call" | custom-call | flops 1073741824 | bytes 10649612 | tf_op jit(solution)/shard_map/shadow_2/pallas_call | solution.py:335
  15.7 0.9 %collective-permute-done.2.got.got2 = bf16[2,32,256]{2,1,0:T(8,128)(2,1)S(1)} collective-permute-done((bf16[2,32,256]{2,1,0:T(8,128)(2,1)S(1)}, bf16[2,32,256]{2,1,0:T(8,128)(2,1)S(1)}, u32[]{:S(2)}, u32[]{:S(2)}) %collective-permute-start.2) | collective-permute-done | bytes 32800 | tf_op jit(solution)/shard_map/ppermute | solution.py:358
  16.6 0.2 climb_2.1.q3
  16.7 3.9 %collective-permute-start.3 = (bf16[2,32,256]{2,1,0:T(8,128)(2,1)S(1)}, bf16[2,32,256]{2,1,0:T(8,128)(2,1)S(1)}, u32[]{:S(2)}, u32[]{:S(2)}) collective-permute-start(bf16[2,32,256]{2,1,0:T(8,128)(2,1)S(1)} %climb_2.1.q3), channel_id=1, source_target_pairs={{0,13},{1,12},{2,15},{3,14},{4,9},{5,8},{6,11},{7,10},{8,5},{9,4},... | collective-permute-start | bytes 98312 | tf_op jit(solution)/shard_map/ppermute | solution.py:358
  20.6 0.0 collective-permute-done.4.got0_other
  20.6 0.9 %shadow_3.1 = (f32[2,32,256]{2,1,0:T(8,128)S(1)}, bf16[2,256,256]{2,1,0:T(8,128)(2,1)S(1)}) custom-call(s32[1]{0:T(128)} %bitcast.pos, bf16[2,32,256]{2,1,0:T(8,128)(2,1)S(1)} %climb_2.1.q3, bf16[2,8,2,256,256]{4,3,2,1,0:T(8,128)(2,1)S(1)} %bitcast.8, bf16[2,8,256,256]{3,2,1,0:T(8,128)(2,1)S(1)} %bitcast.19, bf16[2,1,256,256]{3,2,1,0:T(8,128)(2,1)S(1)} %copy-done.4, ...), custom_call_target="tpu_custom_call" | custom-call | flops 536870912 | bytes 7503876 | tf_op jit(solution)/shard_map/shadow_3/pallas_call | solution.py:335
  21.5 0.9 %collective-permute-done.3.got.got3 = bf16[2,32,256]{2,1,0:T(8,128)(2,1)S(1)} collective-permute-done((bf16[2,32,256]{2,1,0:T(8,128)(2,1)S(1)}, bf16[2,32,256]{2,1,0:T(8,128)(2,1)S(1)}, u32[]{:S(2)}, u32[]{:S(2)}) %collective-permute-start.3) | collective-permute-done | bytes 32800 | tf_op jit(solution)/shard_map/ppermute | solution.py:358
  22.4 0.0 copy-start.2
  22.4 0.2 climb_3.1.q4
  22.6 1.6 %collective-permute-start.5 = (bf16[2,32,256]{2,1,0:T(8,128)(2,1)S(1)}, bf16[2,32,256]{2,1,0:T(8,128)(2,1)S(1)}, u32[]{:S(2)}, u32[]{:S(2)}) collective-permute-start(bf16[2,32,256]{2,1,0:T(8,128)(2,1)S(1)} %climb_3.1.q4), channel_id=1, source_target_pairs={{0,17},{1,16},{2,19},{3,18},{4,21},{5,20},{6,23},{7,22},{8,25},{9,... | collective-permute-start | bytes 98312 | tf_op jit(solution)/shard_map/ppermute | solution.py:358
  24.2 0.0 copy-done.2
  24.2 1.4 %shadow_4.1 = (f32[2,32,256]{2,1,0:T(8,128)S(1)}, f32[2,32,256]{2,1,0:T(8,128)S(1)}, f32[2,1024,128]{2,1,0:T(8,128)S(1)}) custom-call(s32[1]{0:T(128)} %bitcast.pos, s32[1,2]{1,0:T(1,128)S(1)} %copy-done.5, bf16[2,32,256]{2,1,0:T(8,128)(2,1)S(1)} %climb_3.1.q4, bf16[2,32,256]{2,1,0:T(8,128)(2,1)S(1)} %collective-permute-done.3.got.got3, ...), custom_call_target="tpu_custom_call" | custom-call | flops 268435456 | bytes 9764876 | tf_op jit(solution)/shard_map/shadow_4/pallas_call | solution.py:335
  25.6 0.5 collective-permute-done.5.got.got4
  26.1 0.2 climb_4.1.q5
  26.3 2.9 %collective-permute-start.6 = (bf16[2,32,256]{2,1,0:T(8,128)(2,1)S(1)}, bf16[2,32,256]{2,1,0:T(8,128)(2,1)S(1)}, u32[]{:S(2)}, u32[]{:S(2)}) collective-permute-start(bf16[2,32,256]{2,1,0:T(8,128)(2,1)S(1)} %climb_4.1.q5), channel_id=1, source_target_pairs={{0,49},{1,48},{2,51},{3,50},{4,53},{5,52},{6,55},{7,54},{8,57},{9,... | collective-permute-start | bytes 98312 | tf_op jit(solution)/shard_map/ppermute | solution.py:358
  29.2 1.0 %shadow_5.1 = (f32[2,32,256]{2,1,0:T(8,128)S(1)}, f32[2,32,256]{2,1,0:T(8,128)S(1)}, bf16[2,256,256]{2,1,0:T(8,128)(2,1)S(1)}, bf16[2,512,256]{2,1,0:T(8,128)(2,1)S(1)}) custom-call(s32[1]{0:T(128)} %bitcast.pos, bf16[2,32,256]{2,1,0:T(8,128)(2,1)S(1)} %climb_4.1.q5, bf16[2,32,256]{2,1,0:T(8,128)(2,1)S(1)} %collective-permute-done.5.got.got4, ...), custom_call_target="tpu_custom_call" | custom-call | flops 402653184 | bytes 7995396 | tf_op jit(solution)/shard_map/shadow_5/pallas_call | solution.py:335
  30.2 0.8 %collective-permute-done.6.got.got5 = bf16[2,32,256]{2,1,0:T(8,128)(2,1)S(1)} collective-permute-done((bf16[2,32,256]{2,1,0:T(8,128)(2,1)S(1)}, bf16[2,32,256]{2,1,0:T(8,128)(2,1)S(1)}, u32[]{:S(2)}, u32[]{:S(2)}) %collective-permute-start.6) | collective-permute-done | bytes 32800 | tf_op jit(solution)/shard_map/ppermute | solution.py:358
  30.9 0.2 climb_5.1.q6
  31.1 1.7 %collective-permute-start.7 = (bf16[2,32,256]{2,1,0:T(8,128)(2,1)S(1)}, bf16[2,32,256]{2,1,0:T(8,128)(2,1)S(1)}, u32[]{:S(2)}, u32[]{:S(2)}) collective-permute-start(bf16[2,32,256]{2,1,0:T(8,128)(2,1)S(1)} %climb_5.1.q6), channel_id=1, source_target_pairs={{0,65},{1,64},{2,67},{3,66},{4,69},{5,68},{6,71},{7,70},{8,73},{9,... | collective-permute-start | bytes 98312 | tf_op jit(solution)/shard_map/ppermute | solution.py:358
  32.8 2.0 %shadow_6.1 = (f32[2,32,256]{2,1,0:T(8,128)S(1)}, f32[2,32,256]{2,1,0:T(8,128)S(1)}, bf16[2,256,256]{2,1,0:T(8,128)(2,1)S(1)}, bf16[2,256,256]{2,1,0:T(8,128)(2,1)S(1)}, bf16[2,512,256]{2,1,0:T(8,128)(2,1)S(1)}) custom-call(s32[1]{0:T(128)} %bitcast.pos, bf16[2,32,256]{2,1,0:T(8,128)(2,1)S(1)} %climb_5.1.q6, ...), custom_call_target="tpu_custom_call" | custom-call | flops 536870912 | bytes 8257540 | tf_op jit(solution)/shard_map/shadow_6/pallas_call | solution.py:335
  34.8 0.0 collective-permute-done.7.got.got6
  34.8 0.2 climb_6.1
  35.0 3.1 %collective-permute-start.8 = (bf16[2,32,256]{2,1,0:T(8,128)(2,1)S(1)}, bf16[2,32,256]{2,1,0:T(8,128)(2,1)S(1)}, u32[]{:S(2)}, u32[]{:S(2)}) collective-permute-start(bf16[2,32,256]{2,1,0:T(8,128)(2,1)S(1)} %climb_6.1), channel_id=1, source_target_pairs={{0,193},{1,192},{2,195},{3,194},{4,197},{5,196},{6,199},{7,198},{8... | collective-permute-start | bytes 98312 | tf_op jit(solution)/shard_map/ppermute | solution.py:358
  38.1 1.5 %shadow_7.1 = (f32[2,32,256]{2,1,0:T(8,128)S(1)}, f32[2,32,256]{2,1,0:T(8,128)S(1)}, bf16[2,256,256]{2,1,0:T(8,128)(2,1)S(1)}, bf16[2,256,256]{2,1,0:T(8,128)(2,1)S(1)}) custom-call(s32[1]{0:T(128)} %bitcast.pos, bf16[2,32,256]{2,1,0:T(8,128)(2,1)S(1)} %collective-permute-done.7.got.got6, bf16[2,8,2,256,256]{4,3,2,1,0:T(8,128)(2,1)S(1)} %bitcast.16, ...), custom_call_target="tpu_custom_call" | custom-call | flops 402653184 | bytes 6979588 | tf_op jit(solution)/shard_map/shadow_7/pallas_call | solution.py:335
  39.6 0.2 collective-permute-done.8.got
  39.8 0.3 top.1
  40.1 2.1 %collective-permute-start.9 = (bf16[2,32,256]{2,1,0:T(8,128)(2,1)S(1)}, bf16[2,32,256]{2,1,0:T(8,128)(2,1)S(1)}, u32[]{:S(2)}, u32[]{:S(2)}) collective-permute-start(bf16[2,32,256]{2,1,0:T(8,128)(2,1)S(1)} %get-tuple-element.88), channel_id=1, source_target_pairs={{0,5},{1,4},{2,7},{3,6},{4,1},{5,0},{6,3},{7,2},{8,13},{9,12},{10,... | collective-permute-start | bytes 98312 | tf_op jit(solution)/shard_map/ppermute | solution.py:358
  42.1 0.4 shadow_8.1
  42.6 1.8 %collective-permute-done.9.got = bf16[2,32,256]{2,1,0:T(8,128)(2,1)S(1)} collective-permute-done((bf16[2,32,256]{2,1,0:T(8,128)(2,1)S(1)}, bf16[2,32,256]{2,1,0:T(8,128)(2,1)S(1)}, u32[]{:S(2)}, u32[]{:S(2)}) %collective-permute-start.9) | collective-permute-done | bytes 32800 | tf_op jit(solution)/shard_map/ppermute | solution.py:358
  44.4 0.3 down.1
  44.7 2.3 %collective-permute-start.11 = (bf16[2,64,256]{2,1,0:T(8,128)(2,1)S(1)}, bf16[2,64,256]{2,1,0:T(8,128)(2,1)S(1)}, u32[]{:S(2)}, u32[]{:S(2)}) collective-permute-start(bf16[2,64,256]{2,1,0:T(8,128)(2,1)S(1)} %get-tuple-element.94), channel_id=1, source_target_pairs={{0,3},{1,2},{2,1},{3,0},{4,7},{5,6},{6,5},{7,4},{8,11},{9,10},{10,... | collective-permute-start | bytes 196616 | tf_op jit(solution)/shard_map/ppermute | solution.py:358
  47.0 1.0 %shadow_9.1.base = f32[2,1024,128]{2,1,0:T(8,128)S(1)} custom-call(s32[1]{0:T(128)} %bitcast.pos, s32[1,2]{1,0:T(1,128)S(1)} %copy-done.5, bf16[2,64,256]{2,1,0:T(8,128)(2,1)S(1)} %get-tuple-element.93.mine, bf16[2,2,512,256]{3,2,1,0:T(8,128)(2,1)S(1)} %copy-done.2, bf16[2,256,256]{2,1,0:T(8,128)(2,1)S(1)} %get-tuple-element.92.cleaf, ...), custom_call_target="tpu_custom_call" | custom-call | flops 268435456 | bytes 3473420 | tf_op jit(solution)/shard_map/shadow_9/pallas_call | solution.py:335
  48.0 0.4 collective-permute-start.10
  48.4 0.9 %collective-permute-done.11.got = bf16[2,64,256]{2,1,0:T(8,128)(2,1)S(1)} collective-permute-done((bf16[2,64,256]{2,1,0:T(8,128)(2,1)S(1)}, bf16[2,64,256]{2,1,0:T(8,128)(2,1)S(1)}, u32[]{:S(2)}, u32[]{:S(2)}) %collective-permute-start.11) | collective-permute-done | bytes 65568 | tf_op jit(solution)/shard_map/ppermute | solution.py:358
  49.3 0.3 collective-permute-start.12
  49.6 1.0 %own_columns.1.done = bf16[2,2,512,128]{3,2,1,0:T(8,128)(2,1)S(1)} custom-call(s32[1]{0:T(128)} %bitcast.pos, s32[1,2]{1,0:T(1,128)S(1)} %copy-done.5, bf16[2,64,256]{2,1,0:T(8,128)(2,1)S(1)} %get-tuple-element.93.mine, bf16[2,64,256]{2,1,0:T(8,128)(2,1)S(1)} %collective-permute-done.11.got, f32[2,1024,128]{2,1,0:T(8,128)S(1)} %get-tuple-element.98.base, ...), custom_call_target="tpu_custom_call" | custom-call | flops 268435456 | bytes 2228236 | tf_op jit(solution)/shard_map/own_columns/pallas_call | solution.py:335
  50.6 0.0 collective-permute-done.10.mine
  50.6 0.0 collective-permute-done.12.got
  50.7 2.2 %other_columns.1 = bf16[2,1024,256]{2,1,0:T(8,128)(2,1)} custom-call(s32[1]{0:T(128)} %bitcast.pos, s32[1,2]{1,0:T(1,128)S(1)} %copy-done.5, bf16[2,64,256]{2,1,0:T(8,128)(2,1)S(1)} %collective-permute-done.10.mine, bf16[2,64,256]{2,1,0:T(8,128)(2,1)S(1)} %collective-permute-done.12.got, f32[2,1024,128]{2,1,0:T(8,128)S(1)} %shadow_9.1.base, ...), custom_call_target="tpu_custom_call" | custom-call | flops 268435456 | bytes 2752524 | tf_op jit(solution)/shard_map/other_columns/pallas_call | solution.py:335
Async XLA Ops:
  0.0 6.1 %copy-start.5 = (s32[1,2]{1,0:T(1,128)S(1)}, s32[1,2]{1,0:T(1,128)}, u32[]{:S(2)}) copy-start(s32[1,2]{1,0:T(1,128)} %order.15) | copy-start | bytes 28
  0.0 8.2 %copy-start = (bf16[2,1,8,2,256,256]{5,4,3,2,1,0:T(8,128)(2,1)S(1)}, bf16[2,1,8,2,256,256]{5,4,3,2,1,0:T(8,128)(2,1)}, u32[]{:S(2)}) copy-start(bf16[2,1,8,2,256,256]{5,4,3,2,1,0:T(8,128)(2,1)} %param.15) | copy-start | bytes 12582916
  2.8 5.4 %copy-start.3 = (bf16[2,2,512,512]{3,2,1,0:T(8,128)(2,1)S(1)}, bf16[2,2,512,512]{3,2,1,0:T(8,128)(2,1)}, u32[]{:S(2)}) copy-start(bf16[2,2,512,512]{3,2,1,0:T(8,128)(2,1)} %d.3) | copy-start | bytes 6291460
  2.8 4.6 %collective-permute-start = (bf16[2,128,256]{2,1,0:T(8,128)(2,1)S(1)}, bf16[2,128,256]{2,1,0:T(8,128)(2,1)S(1)}, u32[]{:S(2)}, u32[]{:S(2)}) collective-permute-start(bf16[2,128,256]{2,1,0:T(8,128)(2,1)S(1)} %get-tuple-element.52), channel_id=1, source_target_pairs={{0,1},{1,0},{2,3},{3,2},{4,5},{5,4},{6,7},{7,6},{8,9},{9,8},{10,11... | collective-permute-start | bytes 393224 | tf_op jit(solution)/shard_map/ppermute | solution.py:358
  7.8 3.8 %collective-permute-start.1 = (bf16[2,64,256]{2,1,0:T(8,128)(2,1)S(1)}, bf16[2,64,256]{2,1,0:T(8,128)(2,1)S(1)}, u32[]{:S(2)}, u32[]{:S(2)}) collective-permute-start(bf16[2,64,256]{2,1,0:T(8,128)(2,1)S(1)} %get-tuple-element.58), channel_id=1, source_target_pairs={{0,3},{1,2},{2,1},{3,0},{4,7},{5,6},{6,5},{7,4},{8,11},{9,10},{10,... | collective-permute-start | bytes 196616 | tf_op jit(solution)/shard_map/ppermute | solution.py:358
  7.9 12.7 %collective-permute-start.4 = (bf16[2,128,256]{2,1,0:T(8,128)(2,1)S(1)}, bf16[2,128,256]{2,1,0:T(8,128)(2,1)S(1)}, u32[]{:S(2)}, u32[]{:S(2)}) collective-permute-start(bf16[2,128,256]{2,1,0:T(8,128)(2,1)S(1)} %get-tuple-element.68.q), channel_id=1, source_target_pairs={{0,1},{1,0},{2,3},{3,2},{4,5},{5,4},{6,7},{7,6},{8,9},{9,8},{10,11... | collective-permute-start | bytes 393224 | tf_op jit(solution)/shard_map/ppermute | solution.py:358
  11.6 2.1 %copy-start.1 = (bf16[2,1,8,256,256]{4,3,2,1,0:T(8,128)(2,1)S(1)}, bf16[2,1,8,256,256]{4,3,2,1,0:T(8,128)(2,1)}, u32[]{:S(2)}) copy-start(bf16[2,1,8,256,256]{4,3,2,1,0:T(8,128)(2,1)} %param.16) | copy-start | bytes 6291460
  11.6 2.1 %copy-start.4 = (bf16[2,1,256,256]{3,2,1,0:T(8,128)(2,1)S(1)}, bf16[2,1,256,256]{3,2,1,0:T(8,128)(2,1)}, u32[]{:S(2)}) copy-start(bf16[2,1,256,256]{3,2,1,0:T(8,128)(2,1)} %bl.3) | copy-start | bytes 786436
  11.8 4.8 %collective-permute-start.2 = (bf16[2,32,256]{2,1,0:T(8,128)(2,1)S(1)}, bf16[2,32,256]{2,1,0:T(8,128)(2,1)S(1)}, u32[]{:S(2)}, u32[]{:S(2)}) collective-permute-start(bf16[2,32,256]{2,1,0:T(8,128)(2,1)S(1)} %get-tuple-element.63), channel_id=1, source_target_pairs={{0,5},{1,4},{2,7},{3,6},{4,1},{5,0},{6,3},{7,2},{8,13},{9,12},{10,... | collective-permute-start | bytes 98312 | tf_op jit(solution)/shard_map/ppermute | solution.py:358
  16.7 5.7 %collective-permute-start.3 = (bf16[2,32,256]{2,1,0:T(8,128)(2,1)S(1)}, bf16[2,32,256]{2,1,0:T(8,128)(2,1)S(1)}, u32[]{:S(2)}, u32[]{:S(2)}) collective-permute-start(bf16[2,32,256]{2,1,0:T(8,128)(2,1)S(1)} %climb_2.1.q3), channel_id=1, source_target_pairs={{0,13},{1,12},{2,15},{3,14},{4,9},{5,8},{6,11},{7,10},{8,5},{9,4},... | collective-permute-start | bytes 98312 | tf_op jit(solution)/shard_map/ppermute | solution.py:358
  22.4 1.8 %copy-start.2 = (bf16[2,2,512,256]{3,2,1,0:T(8,128)(2,1)S(1)}, bf16[2,2,512,256]{3,2,1,0:T(8,128)(2,1)}, u32[]{:S(2)}) copy-start(bf16[2,2,512,256]{3,2,1,0:T(8,128)(2,1)} %r.7) | copy-start | bytes 3145732
  22.6 3.5 %collective-permute-start.5 = (bf16[2,32,256]{2,1,0:T(8,128)(2,1)S(1)}, bf16[2,32,256]{2,1,0:T(8,128)(2,1)S(1)}, u32[]{:S(2)}, u32[]{:S(2)}) collective-permute-start(bf16[2,32,256]{2,1,0:T(8,128)(2,1)S(1)} %climb_3.1.q4), channel_id=1, source_target_pairs={{0,17},{1,16},{2,19},{3,18},{4,21},{5,20},{6,23},{7,22},{8,25},{9,... | collective-permute-start | bytes 98312 | tf_op jit(solution)/shard_map/ppermute | solution.py:358
  26.3 4.7 %collective-permute-start.6 = (bf16[2,32,256]{2,1,0:T(8,128)(2,1)S(1)}, bf16[2,32,256]{2,1,0:T(8,128)(2,1)S(1)}, u32[]{:S(2)}, u32[]{:S(2)}) collective-permute-start(bf16[2,32,256]{2,1,0:T(8,128)(2,1)S(1)} %climb_4.1.q5), channel_id=1, source_target_pairs={{0,49},{1,48},{2,51},{3,50},{4,53},{5,52},{6,55},{7,54},{8,57},{9,... | collective-permute-start | bytes 98312 | tf_op jit(solution)/shard_map/ppermute | solution.py:358
  31.1 3.7 %collective-permute-start.7 = (bf16[2,32,256]{2,1,0:T(8,128)(2,1)S(1)}, bf16[2,32,256]{2,1,0:T(8,128)(2,1)S(1)}, u32[]{:S(2)}, u32[]{:S(2)}) collective-permute-start(bf16[2,32,256]{2,1,0:T(8,128)(2,1)S(1)} %climb_5.1.q6), channel_id=1, source_target_pairs={{0,65},{1,64},{2,67},{3,66},{4,69},{5,68},{6,71},{7,70},{8,73},{9,... | collective-permute-start | bytes 98312 | tf_op jit(solution)/shard_map/ppermute | solution.py:358
  35.0 4.8 %collective-permute-start.8 = (bf16[2,32,256]{2,1,0:T(8,128)(2,1)S(1)}, bf16[2,32,256]{2,1,0:T(8,128)(2,1)S(1)}, u32[]{:S(2)}, u32[]{:S(2)}) collective-permute-start(bf16[2,32,256]{2,1,0:T(8,128)(2,1)S(1)} %climb_6.1), channel_id=1, source_target_pairs={{0,193},{1,192},{2,195},{3,194},{4,197},{5,196},{6,199},{7,198},{8... | collective-permute-start | bytes 98312 | tf_op jit(solution)/shard_map/ppermute | solution.py:358
  40.1 4.3 %collective-permute-start.9 = (bf16[2,32,256]{2,1,0:T(8,128)(2,1)S(1)}, bf16[2,32,256]{2,1,0:T(8,128)(2,1)S(1)}, u32[]{:S(2)}, u32[]{:S(2)}) collective-permute-start(bf16[2,32,256]{2,1,0:T(8,128)(2,1)S(1)} %get-tuple-element.88), channel_id=1, source_target_pairs={{0,5},{1,4},{2,7},{3,6},{4,1},{5,0},{6,3},{7,2},{8,13},{9,12},{10,... | collective-permute-start | bytes 98312 | tf_op jit(solution)/shard_map/ppermute | solution.py:358
  44.7 4.5 %collective-permute-start.11 = (bf16[2,64,256]{2,1,0:T(8,128)(2,1)S(1)}, bf16[2,64,256]{2,1,0:T(8,128)(2,1)S(1)}, u32[]{:S(2)}, u32[]{:S(2)}) collective-permute-start(bf16[2,64,256]{2,1,0:T(8,128)(2,1)S(1)} %get-tuple-element.94), channel_id=1, source_target_pairs={{0,3},{1,2},{2,1},{3,0},{4,7},{5,6},{6,5},{7,4},{8,11},{9,10},{10,... | collective-permute-start | bytes 196616 | tf_op jit(solution)/shard_map/ppermute | solution.py:358
  48.0 2.6 %collective-permute-start.10 = (bf16[2,64,256]{2,1,0:T(8,128)(2,1)S(1)}, bf16[2,64,256]{2,1,0:T(8,128)(2,1)S(1)}, u32[]{:S(2)}, u32[]{:S(2)}) collective-permute-start(bf16[2,64,256]{2,1,0:T(8,128)(2,1)S(1)} %get-tuple-element.93.mine), channel_id=1, source_target_pairs={{0,1},{1,0},{2,3},{3,2},{4,5},{5,4},{6,7},{7,6},{8,9},{9,8},{10,11... | collective-permute-start | bytes 196616 | tf_op jit(solution)/shard_map/ppermute | solution.py:358
  49.3 1.4 %collective-permute-start.12 = (bf16[2,64,256]{2,1,0:T(8,128)(2,1)S(1)}, bf16[2,64,256]{2,1,0:T(8,128)(2,1)S(1)}, u32[]{:S(2)}, u32[]{:S(2)}) collective-permute-start(bf16[2,64,256]{2,1,0:T(8,128)(2,1)S(1)} %collective-permute-done.11.got), channel_id=1, source_target_pairs={{0,1},{1,0},{2,3},{3,2},{4,5},{5,4},{6,7},{7,6},{8,9},{9,8},{10,11... | collective-permute-start | bytes 196616 | tf_op jit(solution)/shard_map/ppermute | solution.py:358

commit v12 on v11

--- a/solution.py
+++ b/solution.py
@@ -235,14 +235,13 @@
     product(r, paths, 0, g)
 
 
-def shadow_6(pos, q6, got5, w, b, r, paths, top, path, own, top_out, path_6, path_8, g):
+def shadow_6(pos, q6, got5, w, b, top, path, own, top_out, path_6, path_8):
     put(own, lift(rows(q6), w, pos, 6))
     c5 = couple(rows(got5), b, pos, 5).astype(BF)
     put(top_out, rows(top) + times_t(c5, path[0], path[1]))
     longer = lift(rows(path), w, pos, 5).astype(BF)
     put(path_6, longer)
     put(path_8, couple_path(lift(longer, w, pos, 6).astype(BF), b, pos))
-    product(r, paths, 1, g)
 
 
 def shadow_7(pos, got6, w, b, top, path_6, path_8, keep2, got2, const, const_oth, path, path_oth):
@@ -268,7 +267,8 @@
     put(own, rows(const) + dot(q, jnp.concatenate([path[0], path[1]], axis=1), NT))
 
 
-def shadow_8(pos, mine, keep1, got1, b, c1, c1_oth):
+def shadow_8(pos, mine, keep1, got1, b, r, paths, c1, c1_oth, g):
+    product(r, paths, 1, g)
     put(c1, couple(rows(got1), b, pos, 1))
     put(c1_oth, couple(rows(keep1), b, pos, 1, 1))
 
@@ -434,10 +434,9 @@
     )
     q6 = climb(5, got5, own)
     got6 = swap(q6, 65)
-    own, top, path_6, path_8, g1 = call(
-        "shadow_6", shadow_6, "s" + "v" * 8,
-        [top_shape, top_shape, block(rank), block(rank), block(size)],
-        pos, q6, got5, w, b, row_basis, paths, top, path, flops=mac * n * 4,
+    own, top, path_6, path_8 = call(
+        "shadow_6", shadow_6, "s" + "v" * 6, [top_shape, top_shape, block(rank), block(rank)],
+        pos, q6, got5, w, b, top, path, flops=mac * n * 3,
     )
     q7 = climb(6, got6, own)
     got7 = swap(q7, 193)
@@ -451,9 +450,10 @@
         pos, got7, const, const_oth, path, path_oth, flops=mac * eighth * 2,
     )
     got = swap(send, 5)
-    c1, c1_oth = call(
-        "shadow_8", shadow_8, "s" + "v" * 4, [block(quarter, F32), block(quarter, F32)],
-        pos, mine, keep1, got1, b, flops=mac * half,
+    c1, c1_oth, g1 = call(
+        "shadow_8", shadow_8, "s" + "v" * 6,
+        [block(quarter, F32), block(quarter, F32), block(size)],
+        pos, mine, keep1, got1, b, row_basis, paths, flops=mac * n * 2,
     )
     mine, send = call(
         "down", down_kernel, "s" + "v" * 5, [block(quarter), block(quarter)],

time: 53.1 us -> 53 us (level)
  transfers between devices with their start and end apart: 13 -> 13, of which waited for: 8 -> 8; matrix products, arithmetic and copies ran while one was open for 0% -> 0% of each run, Pallas kernels for 27% -> 28%
where the time goes in v12:
time: 53 us; the launch traced here: 52.8 us
  starting transfers between devices  23.9 us (45%)
  Pallas kernels  21.1 us (40%)
  waiting for transfers between devices  7.39 us (14%)
    ppermute x13, starting transfers between devices, swap(): return lax.ppermute(value, axes, [(i, i ^ flip) for i in range(devices)])  23.9 us
    pallas_call x22, Pallas kernels, call(): pl.pallas_call(kernel, out_shape=[jax.ShapeDtypeStruct(shape, dtype) for...  21.1 us
    ppermute x13, waiting for transfers between devices, swap(): return lax.ppermute(value, axes, [(i, i ^ flip) for i in range(devices)])  7.39 us
  transfers between devices with their start and end apart: 13, of which 8 were waited for; matrix products, arithmetic and copies ran while one was open for 0% of the time, Pallas kernels for 28%

profile of v12, /device:TPU:1, one launch (start us, length us, event | category | flops | bytes accessed | tf_op | source)
XLA Modules:
  0.0 52.8 jit_solution(17457842650079983511)
XLA Ops:
  0.0 0.0 copy-start.5
  0.0 0.0 copy-start
  0.0 2.8 %send_half.1 = (bf16[2,256,256]{2,1,0:T(8,128)(2,1)S(1)}, bf16[2,128,256]{2,1,0:T(8,128)(2,1)S(1)}, bf16[2,256,512]{2,1,0:T(8,128)(2,1)S(1)}, bf16[2,1024,256]{2...) custom-call(s32[1]{0:T(128)} %bitcast.pos, ...), custom_call_target="tpu_custom_call" | custom-call | flops 402653184 | bytes 6815756 | tf_op jit(solution)/shard_map/send_half/pallas_call | solution.py:335
  2.8 0.0 copy-start.3
  2.8 3.3 %collective-permute-start = (bf16[2,128,256]{2,1,0:T(8,128)(2,1)S(1)}, bf16[2,128,256]{2,1,0:T(8,128)(2,1)S(1)}, u32[]{:S(2)}, u32[]{:S(2)}) collective-permute-start(bf16[2,128,256]{2,1,0:T(8,128)(2,1)S(1)} %get-tuple-element.52), channel_id=1, source_target_pairs={{0,1},{1,0},{2,3},{3,2},{4,5},{5,4},{6,7},{7,6},{8,9},{9,8},{10,11... | collective-permute-start | bytes 393224 | tf_op jit(solution)/shard_map/ppermute | solution.py:358
  6.2 0.0 copy-done.5
  6.2 1.3 %keep_half.1 = (bf16[2,256,256]{2,1,0:T(8,128)(2,1)S(1)}, bf16[2,128,256]{2,1,0:T(8,128)(2,1)S(1)}) custom-call(s32[1]{0:T(128)} %bitcast.pos, s32[1,2]{1,0:T(1,128)S(1)} %copy-done.5, bf16[2,256,512]{2,1,0:T(8,128)(2,1)S(1)} %get-tuple-element.53.xt, bf16[2,2,512,256]{3,2,1,0:T(8,128)(2,1)S(1)} %get-tuple-element.54.u, ...), custom_call_target="tpu_custom_call" | custom-call | flops 402653184 | bytes 2097164 | tf_op jit(solution)/shard_map/keep_half/pallas_call | solution.py:335
  7.5 0.0 collective-permute-done.got.got0
  7.5 0.3 climb_0.1
  7.8 0.1 collective-permute-start.1
  7.9 0.3 collective-permute-start.4
  8.2 0.0 copy-done
  8.2 0.0 copy-done.3
  8.2 1.6 %shadow_1.1 = (f32[2,64,256]{2,1,0:T(8,128)S(1)}, f32[2,512,256]{2,1,0:T(8,128)S(1)}, bf16[2,2,256,256]{3,2,1,0:T(8,128)(2,1)S(1)}) custom-call(s32[1]{0:T(128)} %bitcast.pos, s32[1,2]{1,0:T(1,128)S(1)} %copy-done.5, bf16[2,64,256]{2,1,0:T(8,128)(2,1)S(1)} %get-tuple-element.60.keep.keep1, bf16[2,8,2,256,256]{4,3,2,1,0:T(8,128)(2,1)S(1)} %bitcast.4, ...), custom_call_target="tpu_custom_call" | custom-call | flops 939524096 | bytes 8454156 | tf_op jit(solution)/shard_map/shadow_1/pallas_call | solution.py:335
  9.7 1.9 %collective-permute-done.1.got.got1 = bf16[2,64,256]{2,1,0:T(8,128)(2,1)S(1)} collective-permute-done((bf16[2,64,256]{2,1,0:T(8,128)(2,1)S(1)}, bf16[2,64,256]{2,1,0:T(8,128)(2,1)S(1)}, u32[]{:S(2)}, u32[]{:S(2)}) %collective-permute-start.1) | collective-permute-done | bytes 65568 | tf_op jit(solution)/shard_map/ppermute | solution.py:358
  11.6 0.0 copy-start.1
  11.6 0.0 copy-start.4
  11.6 0.2 climb_1.1
  11.8 1.9 %collective-permute-start.2 = (bf16[2,32,256]{2,1,0:T(8,128)(2,1)S(1)}, bf16[2,32,256]{2,1,0:T(8,128)(2,1)S(1)}, u32[]{:S(2)}, u32[]{:S(2)}) collective-permute-start(bf16[2,32,256]{2,1,0:T(8,128)(2,1)S(1)} %get-tuple-element.63), channel_id=1, source_target_pairs={{0,5},{1,4},{2,7},{3,6},{4,1},{5,0},{6,3},{7,2},{8,13},{9,12},{10,... | collective-permute-start | bytes 98312 | tf_op jit(solution)/shard_map/ppermute | solution.py:358
  13.7 0.0 copy-done.1
  13.7 0.0 copy-done.4
  13.7 2.0 %shadow_2.1 = (f32[2,32,256]{2,1,0:T(8,128)S(1)}, f32[2,512,256]{2,1,0:T(8,128)S(1)}, bf16[2,256,256]{2,1,0:T(8,128)(2,1)S(1)}) custom-call(s32[1]{0:T(128)} %bitcast.pos, s32[1,2]{1,0:T(1,128)S(1)} %copy-done.5, bf16[2,32,256]{2,1,0:T(8,128)(2,1)S(1)} %get-tuple-element.64.keep.keep2, bf16[2,8,2,256,256]{4,3,2,1,0:T(8,128)(2,1)S(1)} %bitcast.6, ...), custom_call_target="tpu_custom_call" | custom-call | flops 1073741824 | bytes 10649612 | tf_op jit(solution)/shard_map/shadow_2/pallas_call | solution.py:335
  15.7 0.9 %collective-permute-done.2.got.got2 = bf16[2,32,256]{2,1,0:T(8,128)(2,1)S(1)} collective-permute-done((bf16[2,32,256]{2,1,0:T(8,128)(2,1)S(1)}, bf16[2,32,256]{2,1,0:T(8,128)(2,1)S(1)}, u32[]{:S(2)}, u32[]{:S(2)}) %collective-permute-start.2) | collective-permute-done | bytes 32800 | tf_op jit(solution)/shard_map/ppermute | solution.py:358
  16.6 0.2 climb_2.1.q3
  16.7 3.9 %collective-permute-start.3 = (bf16[2,32,256]{2,1,0:T(8,128)(2,1)S(1)}, bf16[2,32,256]{2,1,0:T(8,128)(2,1)S(1)}, u32[]{:S(2)}, u32[]{:S(2)}) collective-permute-start(bf16[2,32,256]{2,1,0:T(8,128)(2,1)S(1)} %climb_2.1.q3), channel_id=1, source_target_pairs={{0,13},{1,12},{2,15},{3,14},{4,9},{5,8},{6,11},{7,10},{8,5},{9,4},... | collective-permute-start | bytes 98312 | tf_op jit(solution)/shard_map/ppermute | solution.py:358
  20.6 0.0 collective-permute-done.4.got0_other
  20.7 0.9 %shadow_3.1 = (f32[2,32,256]{2,1,0:T(8,128)S(1)}, bf16[2,256,256]{2,1,0:T(8,128)(2,1)S(1)}) custom-call(s32[1]{0:T(128)} %bitcast.pos, bf16[2,32,256]{2,1,0:T(8,128)(2,1)S(1)} %climb_2.1.q3, bf16[2,8,2,256,256]{4,3,2,1,0:T(8,128)(2,1)S(1)} %bitcast.8, bf16[2,8,256,256]{3,2,1,0:T(8,128)(2,1)S(1)} %bitcast.19, bf16[2,1,256,256]{3,2,1,0:T(8,128)(2,1)S(1)} %copy-done.4, ...), custom_call_target="tpu_custom_call" | custom-call | flops 536870912 | bytes 7503876 | tf_op jit(solution)/shard_map/shadow_3/pallas_call | solution.py:335
  21.5 0.9 %collective-permute-done.3.got.got3 = bf16[2,32,256]{2,1,0:T(8,128)(2,1)S(1)} collective-permute-done((bf16[2,32,256]{2,1,0:T(8,128)(2,1)S(1)}, bf16[2,32,256]{2,1,0:T(8,128)(2,1)S(1)}, u32[]{:S(2)}, u32[]{:S(2)}) %collective-permute-start.3) | collective-permute-done | bytes 32800 | tf_op jit(solution)/shard_map/ppermute | solution.py:358
  22.4 0.0 copy-start.2
  22.4 0.2 climb_3.1.q4
  22.6 1.6 %collective-permute-start.5 = (bf16[2,32,256]{2,1,0:T(8,128)(2,1)S(1)}, bf16[2,32,256]{2,1,0:T(8,128)(2,1)S(1)}, u32[]{:S(2)}, u32[]{:S(2)}) collective-permute-start(bf16[2,32,256]{2,1,0:T(8,128)(2,1)S(1)} %climb_3.1.q4), channel_id=1, source_target_pairs={{0,17},{1,16},{2,19},{3,18},{4,21},{5,20},{6,23},{7,22},{8,25},{9,... | collective-permute-start | bytes 98312 | tf_op jit(solution)/shard_map/ppermute | solution.py:358
  24.2 0.0 copy-done.2
  24.2 1.4 %shadow_4.1 = (f32[2,32,256]{2,1,0:T(8,128)S(1)}, f32[2,32,256]{2,1,0:T(8,128)S(1)}, f32[2,1024,128]{2,1,0:T(8,128)S(1)}) custom-call(s32[1]{0:T(128)} %bitcast.pos, s32[1,2]{1,0:T(1,128)S(1)} %copy-done.5, bf16[2,32,256]{2,1,0:T(8,128)(2,1)S(1)} %climb_3.1.q4, bf16[2,32,256]{2,1,0:T(8,128)(2,1)S(1)} %collective-permute-done.3.got.got3, ...), custom_call_target="tpu_custom_call" | custom-call | flops 268435456 | bytes 9764876 | tf_op jit(solution)/shard_map/shadow_4/pallas_call | solution.py:335
  25.6 0.5 collective-permute-done.5.got.got4
  26.1 0.2 climb_4.1.q5
  26.3 2.9 %collective-permute-start.6 = (bf16[2,32,256]{2,1,0:T(8,128)(2,1)S(1)}, bf16[2,32,256]{2,1,0:T(8,128)(2,1)S(1)}, u32[]{:S(2)}, u32[]{:S(2)}) collective-permute-start(bf16[2,32,256]{2,1,0:T(8,128)(2,1)S(1)} %climb_4.1.q5), channel_id=1, source_target_pairs={{0,49},{1,48},{2,51},{3,50},{4,53},{5,52},{6,55},{7,54},{8,57},{9,... | collective-permute-start | bytes 98312 | tf_op jit(solution)/shard_map/ppermute | solution.py:358
  29.2 1.0 %shadow_5.1 = (f32[2,32,256]{2,1,0:T(8,128)S(1)}, f32[2,32,256]{2,1,0:T(8,128)S(1)}, bf16[2,256,256]{2,1,0:T(8,128)(2,1)S(1)}, bf16[2,512,256]{2,1,0:T(8,128)(2,1)S(1)}) custom-call(s32[1]{0:T(128)} %bitcast.pos, bf16[2,32,256]{2,1,0:T(8,128)(2,1)S(1)} %climb_4.1.q5, bf16[2,32,256]{2,1,0:T(8,128)(2,1)S(1)} %collective-permute-done.5.got.got4, ...), custom_call_target="tpu_custom_call" | custom-call | flops 402653184 | bytes 7995396 | tf_op jit(solution)/shard_map/shadow_5/pallas_call | solution.py:335
  30.2 0.8 %collective-permute-done.6.got.got5 = bf16[2,32,256]{2,1,0:T(8,128)(2,1)S(1)} collective-permute-done((bf16[2,32,256]{2,1,0:T(8,128)(2,1)S(1)}, bf16[2,32,256]{2,1,0:T(8,128)(2,1)S(1)}, u32[]{:S(2)}, u32[]{:S(2)}) %collective-permute-start.6) | collective-permute-done | bytes 32800 | tf_op jit(solution)/shard_map/ppermute | solution.py:358
  31.0 0.2 climb_5.1.q6
  31.1 1.7 %collective-permute-start.7 = (bf16[2,32,256]{2,1,0:T(8,128)(2,1)S(1)}, bf16[2,32,256]{2,1,0:T(8,128)(2,1)S(1)}, u32[]{:S(2)}, u32[]{:S(2)}) collective-permute-start(bf16[2,32,256]{2,1,0:T(8,128)(2,1)S(1)} %climb_5.1.q6), channel_id=1, source_target_pairs={{0,65},{1,64},{2,67},{3,66},{4,69},{5,68},{6,71},{7,70},{8,73},{9,... | collective-permute-start | bytes 98312 | tf_op jit(solution)/shard_map/ppermute | solution.py:358
  32.9 1.5 %shadow_6.1 = (f32[2,32,256]{2,1,0:T(8,128)S(1)}, f32[2,32,256]{2,1,0:T(8,128)S(1)}, bf16[2,256,256]{2,1,0:T(8,128)(2,1)S(1)}, bf16[2,256,256]{2,1,0:T(8,128)(2,1)S(1)}) custom-call(s32[1]{0:T(128)} %bitcast.pos, bf16[2,32,256]{2,1,0:T(8,128)(2,1)S(1)} %climb_5.1.q6, bf16[2,32,256]{2,1,0:T(8,128)(2,1)S(1)} %collective-permute-done.6.got.got5, ...), custom_call_target="tpu_custom_call" | custom-call | flops 402653184 | bytes 6684676 | tf_op jit(solution)/shard_map/shadow_6/pallas_call | solution.py:335
  34.4 0.2 collective-permute-done.7.got.got6
  34.6 0.2 climb_6.1
  34.8 3.2 %collective-permute-start.8 = (bf16[2,32,256]{2,1,0:T(8,128)(2,1)S(1)}, bf16[2,32,256]{2,1,0:T(8,128)(2,1)S(1)}, u32[]{:S(2)}, u32[]{:S(2)}) collective-permute-start(bf16[2,32,256]{2,1,0:T(8,128)(2,1)S(1)} %climb_6.1), channel_id=1, source_target_pairs={{0,193},{1,192},{2,195},{3,194},{4,197},{5,196},{6,199},{7,198},{8... | collective-permute-start | bytes 98312 | tf_op jit(solution)/shard_map/ppermute | solution.py:358
  38.0 1.7 %shadow_7.1 = (f32[2,32,256]{2,1,0:T(8,128)S(1)}, f32[2,32,256]{2,1,0:T(8,128)S(1)}, bf16[2,256,256]{2,1,0:T(8,128)(2,1)S(1)}, bf16[2,256,256]{2,1,0:T(8,128)(2,1)S(1)}) custom-call(s32[1]{0:T(128)} %bitcast.pos, bf16[2,32,256]{2,1,0:T(8,128)(2,1)S(1)} %collective-permute-done.7.got.got6, bf16[2,8,2,256,256]{4,3,2,1,0:T(8,128)(2,1)S(1)} %bitcast.16, ...), custom_call_target="tpu_custom_call" | custom-call | flops 402653184 | bytes 6979588 | tf_op jit(solution)/shard_map/shadow_7/pallas_call | solution.py:335
  39.7 0.0 collective-permute-done.8.got
  39.7 0.3 top.1
  40.0 2.0 %collective-permute-start.9 = (bf16[2,32,256]{2,1,0:T(8,128)(2,1)S(1)}, bf16[2,32,256]{2,1,0:T(8,128)(2,1)S(1)}, u32[]{:S(2)}, u32[]{:S(2)}) collective-permute-start(bf16[2,32,256]{2,1,0:T(8,128)(2,1)S(1)} %get-tuple-element.88), channel_id=1, source_target_pairs={{0,5},{1,4},{2,7},{3,6},{4,1},{5,0},{6,3},{7,2},{8,13},{9,12},{10,... | collective-permute-start | bytes 98312 | tf_op jit(solution)/shard_map/ppermute | solution.py:358
  42.0 0.9 %shadow_8.1 = (f32[2,64,256]{2,1,0:T(8,128)S(1)}, f32[2,64,256]{2,1,0:T(8,128)S(1)}, bf16[2,512,256]{2,1,0:T(8,128)(2,1)S(1)}) custom-call(s32[1]{0:T(128)} %bitcast.pos, bf16[2,32,256]{2,1,0:T(8,128)(2,1)S(1)} %get-tuple-element.87.mine, bf16[2,64,256]{2,1,0:T(8,128)(2,1)S(1)} %get-tuple-element.60.keep.keep1, ...), custom_call_target="tpu_custom_call" | custom-call | flops 268435456 | bytes 3833860 | tf_op jit(solution)/shard_map/shadow_8/pallas_call | solution.py:335
  42.8 1.4 %collective-permute-done.9.got = bf16[2,32,256]{2,1,0:T(8,128)(2,1)S(1)} collective-permute-done((bf16[2,32,256]{2,1,0:T(8,128)(2,1)S(1)}, bf16[2,32,256]{2,1,0:T(8,128)(2,1)S(1)}, u32[]{:S(2)}, u32[]{:S(2)}) %collective-permute-start.9) | collective-permute-done | bytes 32800 | tf_op jit(solution)/shard_map/ppermute | solution.py:358
  44.3 0.3 down.1
  44.6 2.2 %collective-permute-start.11 = (bf16[2,64,256]{2,1,0:T(8,128)(2,1)S(1)}, bf16[2,64,256]{2,1,0:T(8,128)(2,1)S(1)}, u32[]{:S(2)}, u32[]{:S(2)}) collective-permute-start(bf16[2,64,256]{2,1,0:T(8,128)(2,1)S(1)} %get-tuple-element.94), channel_id=1, source_target_pairs={{0,3},{1,2},{2,1},{3,0},{4,7},{5,6},{6,5},{7,4},{8,11},{9,10},{10,... | collective-permute-start | bytes 196616 | tf_op jit(solution)/shard_map/ppermute | solution.py:358
  46.8 1.0 %shadow_9.1.base = f32[2,1024,128]{2,1,0:T(8,128)S(1)} custom-call(s32[1]{0:T(128)} %bitcast.pos, s32[1,2]{1,0:T(1,128)S(1)} %copy-done.5, bf16[2,64,256]{2,1,0:T(8,128)(2,1)S(1)} %get-tuple-element.93.mine, bf16[2,2,512,256]{3,2,1,0:T(8,128)(2,1)S(1)} %copy-done.2, bf16[2,256,256]{2,1,0:T(8,128)(2,1)S(1)} %get-tuple-element.92.cleaf, ...), custom_call_target="tpu_custom_call" | custom-call | flops 268435456 | bytes 3473420 | tf_op jit(solution)/shard_map/shadow_9/pallas_call | solution.py:335
  47.8 0.4 collective-permute-start.10
  48.2 0.9 %collective-permute-done.11.got = bf16[2,64,256]{2,1,0:T(8,128)(2,1)S(1)} collective-permute-done((bf16[2,64,256]{2,1,0:T(8,128)(2,1)S(1)}, bf16[2,64,256]{2,1,0:T(8,128)(2,1)S(1)}, u32[]{:S(2)}, u32[]{:S(2)}) %collective-permute-start.11) | collective-permute-done | bytes 65568 | tf_op jit(solution)/shard_map/ppermute | solution.py:358
  49.1 0.4 collective-permute-start.12
  49.5 1.0 %own_columns.1.done = bf16[2,2,512,128]{3,2,1,0:T(8,128)(2,1)S(1)} custom-call(s32[1]{0:T(128)} %bitcast.pos, s32[1,2]{1,0:T(1,128)S(1)} %copy-done.5, bf16[2,64,256]{2,1,0:T(8,128)(2,1)S(1)} %get-tuple-element.93.mine, bf16[2,64,256]{2,1,0:T(8,128)(2,1)S(1)} %collective-permute-done.11.got, f32[2,1024,128]{2,1,0:T(8,128)S(1)} %get-tuple-element.98.base, ...), custom_call_target="tpu_custom_call" | custom-call | flops 268435456 | bytes 2228236 | tf_op jit(solution)/shard_map/own_columns/pallas_call | solution.py:335
  50.5 0.0 collective-permute-done.10.mine
  50.5 0.0 collective-permute-done.12.got
  50.5 2.2 %other_columns.1 = bf16[2,1024,256]{2,1,0:T(8,128)(2,1)} custom-call(s32[1]{0:T(128)} %bitcast.pos, s32[1,2]{1,0:T(1,128)S(1)} %copy-done.5, bf16[2,64,256]{2,1,0:T(8,128)(2,1)S(1)} %collective-permute-done.10.mine, bf16[2,64,256]{2,1,0:T(8,128)(2,1)S(1)} %collective-permute-done.12.got, f32[2,1024,128]{2,1,0:T(8,128)S(1)} %shadow_9.1.base, ...), custom_call_target="tpu_custom_call" | custom-call | flops 268435456 | bytes 2752524 | tf_op jit(solution)/shard_map/other_columns/pallas_call | solution.py:335
Async XLA Ops:
  0.0 6.2 %copy-start.5 = (s32[1,2]{1,0:T(1,128)S(1)}, s32[1,2]{1,0:T(1,128)}, u32[]{:S(2)}) copy-start(s32[1,2]{1,0:T(1,128)} %order.15) | copy-start | bytes 28
  0.0 8.2 %copy-start = (bf16[2,1,8,2,256,256]{5,4,3,2,1,0:T(8,128)(2,1)S(1)}, bf16[2,1,8,2,256,256]{5,4,3,2,1,0:T(8,128)(2,1)}, u32[]{:S(2)}) copy-start(bf16[2,1,8,2,256,256]{5,4,3,2,1,0:T(8,128)(2,1)} %param.15) | copy-start | bytes 12582916
  2.8 5.4 %copy-start.3 = (bf16[2,2,512,512]{3,2,1,0:T(8,128)(2,1)S(1)}, bf16[2,2,512,512]{3,2,1,0:T(8,128)(2,1)}, u32[]{:S(2)}) copy-start(bf16[2,2,512,512]{3,2,1,0:T(8,128)(2,1)} %d.3) | copy-start | bytes 6291460
  2.8 4.6 %collective-permute-start = (bf16[2,128,256]{2,1,0:T(8,128)(2,1)S(1)}, bf16[2,128,256]{2,1,0:T(8,128)(2,1)S(1)}, u32[]{:S(2)}, u32[]{:S(2)}) collective-permute-start(bf16[2,128,256]{2,1,0:T(8,128)(2,1)S(1)} %get-tuple-element.52), channel_id=1, source_target_pairs={{0,1},{1,0},{2,3},{3,2},{4,5},{5,4},{6,7},{7,6},{8,9},{9,8},{10,11... | collective-permute-start | bytes 393224 | tf_op jit(solution)/shard_map/ppermute | solution.py:358
  7.8 3.8 %collective-permute-start.1 = (bf16[2,64,256]{2,1,0:T(8,128)(2,1)S(1)}, bf16[2,64,256]{2,1,0:T(8,128)(2,1)S(1)}, u32[]{:S(2)}, u32[]{:S(2)}) collective-permute-start(bf16[2,64,256]{2,1,0:T(8,128)(2,1)S(1)} %get-tuple-element.58), channel_id=1, source_target_pairs={{0,3},{1,2},{2,1},{3,0},{4,7},{5,6},{6,5},{7,4},{8,11},{9,10},{10,... | collective-permute-start | bytes 196616 | tf_op jit(solution)/shard_map/ppermute | solution.py:358
  7.9 12.8 %collective-permute-start.4 = (bf16[2,128,256]{2,1,0:T(8,128)(2,1)S(1)}, bf16[2,128,256]{2,1,0:T(8,128)(2,1)S(1)}, u32[]{:S(2)}, u32[]{:S(2)}) collective-permute-start(bf16[2,128,256]{2,1,0:T(8,128)(2,1)S(1)} %get-tuple-element.68.q), channel_id=1, source_target_pairs={{0,1},{1,0},{2,3},{3,2},{4,5},{5,4},{6,7},{7,6},{8,9},{9,8},{10,11... | collective-permute-start | bytes 393224 | tf_op jit(solution)/shard_map/ppermute | solution.py:358
  11.6 2.1 %copy-start.1 = (bf16[2,1,8,256,256]{4,3,2,1,0:T(8,128)(2,1)S(1)}, bf16[2,1,8,256,256]{4,3,2,1,0:T(8,128)(2,1)}, u32[]{:S(2)}) copy-start(bf16[2,1,8,256,256]{4,3,2,1,0:T(8,128)(2,1)} %param.16) | copy-start | bytes 6291460
  11.6 2.1 %copy-start.4 = (bf16[2,1,256,256]{3,2,1,0:T(8,128)(2,1)S(1)}, bf16[2,1,256,256]{3,2,1,0:T(8,128)(2,1)}, u32[]{:S(2)}) copy-start(bf16[2,1,256,256]{3,2,1,0:T(8,128)(2,1)} %bl.3) | copy-start | bytes 786436
  11.8 4.8 %collective-permute-start.2 = (bf16[2,32,256]{2,1,0:T(8,128)(2,1)S(1)}, bf16[2,32,256]{2,1,0:T(8,128)(2,1)S(1)}, u32[]{:S(2)}, u32[]{:S(2)}) collective-permute-start(bf16[2,32,256]{2,1,0:T(8,128)(2,1)S(1)} %get-tuple-element.63), channel_id=1, source_target_pairs={{0,5},{1,4},{2,7},{3,6},{4,1},{5,0},{6,3},{7,2},{8,13},{9,12},{10,... | collective-permute-start | bytes 98312 | tf_op jit(solution)/shard_map/ppermute | solution.py:358
  16.7 5.7 %collective-permute-start.3 = (bf16[2,32,256]{2,1,0:T(8,128)(2,1)S(1)}, bf16[2,32,256]{2,1,0:T(8,128)(2,1)S(1)}, u32[]{:S(2)}, u32[]{:S(2)}) collective-permute-start(bf16[2,32,256]{2,1,0:T(8,128)(2,1)S(1)} %climb_2.1.q3), channel_id=1, source_target_pairs={{0,13},{1,12},{2,15},{3,14},{4,9},{5,8},{6,11},{7,10},{8,5},{9,4},... | collective-permute-start | bytes 98312 | tf_op jit(solution)/shard_map/ppermute | solution.py:358
  22.4 1.8 %copy-start.2 = (bf16[2,2,512,256]{3,2,1,0:T(8,128)(2,1)S(1)}, bf16[2,2,512,256]{3,2,1,0:T(8,128)(2,1)}, u32[]{:S(2)}) copy-start(bf16[2,2,512,256]{3,2,1,0:T(8,128)(2,1)} %r.7) | copy-start | bytes 3145732
  22.6 3.5 %collective-permute-start.5 = (bf16[2,32,256]{2,1,0:T(8,128)(2,1)S(1)}, bf16[2,32,256]{2,1,0:T(8,128)(2,1)S(1)}, u32[]{:S(2)}, u32[]{:S(2)}) collective-permute-start(bf16[2,32,256]{2,1,0:T(8,128)(2,1)S(1)} %climb_3.1.q4), channel_id=1, source_target_pairs={{0,17},{1,16},{2,19},{3,18},{4,21},{5,20},{6,23},{7,22},{8,25},{9,... | collective-permute-start | bytes 98312 | tf_op jit(solution)/shard_map/ppermute | solution.py:358
  26.3 4.7 %collective-permute-start.6 = (bf16[2,32,256]{2,1,0:T(8,128)(2,1)S(1)}, bf16[2,32,256]{2,1,0:T(8,128)(2,1)S(1)}, u32[]{:S(2)}, u32[]{:S(2)}) collective-permute-start(bf16[2,32,256]{2,1,0:T(8,128)(2,1)S(1)} %climb_4.1.q5), channel_id=1, source_target_pairs={{0,49},{1,48},{2,51},{3,50},{4,53},{5,52},{6,55},{7,54},{8,57},{9,... | collective-permute-start | bytes 98312 | tf_op jit(solution)/shard_map/ppermute | solution.py:358
  31.1 3.5 %collective-permute-start.7 = (bf16[2,32,256]{2,1,0:T(8,128)(2,1)S(1)}, bf16[2,32,256]{2,1,0:T(8,128)(2,1)S(1)}, u32[]{:S(2)}, u32[]{:S(2)}) collective-permute-start(bf16[2,32,256]{2,1,0:T(8,128)(2,1)S(1)} %climb_5.1.q6), channel_id=1, source_target_pairs={{0,65},{1,64},{2,67},{3,66},{4,69},{5,68},{6,71},{7,70},{8,73},{9,... | collective-permute-start | bytes 98312 | tf_op jit(solution)/shard_map/ppermute | solution.py:358
  34.8 4.9 %collective-permute-start.8 = (bf16[2,32,256]{2,1,0:T(8,128)(2,1)S(1)}, bf16[2,32,256]{2,1,0:T(8,128)(2,1)S(1)}, u32[]{:S(2)}, u32[]{:S(2)}) collective-permute-start(bf16[2,32,256]{2,1,0:T(8,128)(2,1)S(1)} %climb_6.1), channel_id=1, source_target_pairs={{0,193},{1,192},{2,195},{3,194},{4,197},{5,196},{6,199},{7,198},{8... | collective-permute-start | bytes 98312 | tf_op jit(solution)/shard_map/ppermute | solution.py:358
  40.0 4.3 %collective-permute-start.9 = (bf16[2,32,256]{2,1,0:T(8,128)(2,1)S(1)}, bf16[2,32,256]{2,1,0:T(8,128)(2,1)S(1)}, u32[]{:S(2)}, u32[]{:S(2)}) collective-permute-start(bf16[2,32,256]{2,1,0:T(8,128)(2,1)S(1)} %get-tuple-element.88), channel_id=1, source_target_pairs={{0,5},{1,4},{2,7},{3,6},{4,1},{5,0},{6,3},{7,2},{8,13},{9,12},{10,... | collective-permute-start | bytes 98312 | tf_op jit(solution)/shard_map/ppermute | solution.py:358
  44.6 4.5 %collective-permute-start.11 = (bf16[2,64,256]{2,1,0:T(8,128)(2,1)S(1)}, bf16[2,64,256]{2,1,0:T(8,128)(2,1)S(1)}, u32[]{:S(2)}, u32[]{:S(2)}) collective-permute-start(bf16[2,64,256]{2,1,0:T(8,128)(2,1)S(1)} %get-tuple-element.94), channel_id=1, source_target_pairs={{0,3},{1,2},{2,1},{3,0},{4,7},{5,6},{6,5},{7,4},{8,11},{9,10},{10,... | collective-permute-start | bytes 196616 | tf_op jit(solution)/shard_map/ppermute | solution.py:358
  47.8 2.6 %collective-permute-start.10 = (bf16[2,64,256]{2,1,0:T(8,128)(2,1)S(1)}, bf16[2,64,256]{2,1,0:T(8,128)(2,1)S(1)}, u32[]{:S(2)}, u32[]{:S(2)}) collective-permute-start(bf16[2,64,256]{2,1,0:T(8,128)(2,1)S(1)} %get-tuple-element.93.mine), channel_id=1, source_target_pairs={{0,1},{1,0},{2,3},{3,2},{4,5},{5,4},{6,7},{7,6},{8,9},{9,8},{10,11... | collective-permute-start | bytes 196616 | tf_op jit(solution)/shard_map/ppermute | solution.py:358
  49.1 1.4 %collective-permute-start.12 = (bf16[2,64,256]{2,1,0:T(8,128)(2,1)S(1)}, bf16[2,64,256]{2,1,0:T(8,128)(2,1)S(1)}, u32[]{:S(2)}, u32[]{:S(2)}) collective-permute-start(bf16[2,64,256]{2,1,0:T(8,128)(2,1)S(1)} %collective-permute-done.11.got), channel_id=1, source_target_pairs={{0,1},{1,0},{2,3},{3,2},{4,5},{5,4},{6,7},{7,6},{8,9},{9,8},{10,11... | collective-permute-start | bytes 196616 | tf_op jit(solution)/shard_map/ppermute | solution.py:358

commit v13 on v12

--- a/solution.py
+++ b/solution.py
@@ -198,8 +198,10 @@
     leaf_coupled(pos, q_mine, got0, b, bl, wl, cleaf)
 
 
-def shadow_3(pos, q3, w, b, bl, wl, q_other, got0_other, own, cleaf):
+def shadow_3(pos, q3, w, b, bl, wl, q_other, got0_other, keep2, got2, own, cleaf, c2, c2_oth):
     put(own, lift(rows(q3), w, pos, 3))
+    put(c2, couple(rows(got2), b, pos, 2))
+    put(c2_oth, couple(rows(keep2), b, pos, 2, 1))
     leaf_coupled(pos, q_other, got0_other, b, bl, wl, cleaf)
 
 
@@ -244,11 +246,11 @@
     put(path_8, couple_path(lift(longer, w, pos, 6).astype(BF), b, pos))
 
 
-def shadow_7(pos, got6, w, b, top, path_6, path_8, keep2, got2, const, const_oth, path, path_oth):
+def shadow_7(pos, got6, w, b, top, path_6, path_8, c2, c2_oth, const, const_oth, path, path_oth):
     c6 = couple(rows(got6), b, pos, 6).astype(BF)
     h = (rows(top) + times_t(c6, path_6[0], path_6[1])).astype(BF)
-    put(const, couple(rows(got2), b, pos, 2) + lower(h, w, pos, 2))
-    put(const_oth, couple(rows(keep2), b, pos, 2, 1) + lower(h, w, pos, 2, 1))
+    put(const, rows(c2) + lower(h, w, pos, 2))
+    put(const_oth, rows(c2_oth) + lower(h, w, pos, 2, 1))
     for flip, out in enumerate((path, path_oth)):
         put(out, times(stack(w, 2, bit(pos, 2) ^ flip), path_8[0], path_8[1]))
 
@@ -414,9 +416,9 @@
     base_shape = ((2, 2 * size, half), F32)
     q3 = climb(2, got2, own)
     got3 = swap(q3, 13)
-    own, cleaf_other = call(
-        "shadow_3", shadow_3, "s" + "v" * 7, [top_shape, cleaf_shape],
-        pos, q3, w, b, bl, wl, q_other, got0_other, flops=mac * n * 4,
+    own, cleaf_other, c2, c2_oth = call(
+        "shadow_3", shadow_3, "s" + "v" * 9, [top_shape, cleaf_shape, top_shape, top_shape],
+        pos, q3, w, b, bl, wl, q_other, got0_other, keep2, got2, flops=mac * n * 4,
     )
     q4 = climb(3, got3, own)
     got4 = swap(q4, 17)
@@ -443,7 +445,7 @@
     const, const_oth, path, path_oth = call(
         "shadow_7", shadow_7, "s" + "v" * 8,
         [top_shape, top_shape, block(rank), block(rank)],
-        pos, got6, w, b, top, path_6, path_8, keep2, got2, flops=mac * n * 3,
+        pos, got6, w, b, top, path_6, path_8, c2, c2_oth, flops=mac * n * 3,
     )
     mine, send = call(
         "top", top_kernel, "s" + "v" * 5, [block(eighth), block(eighth)],

time: 53 us -> 52.9 us (level)
  transfers between devices with their start and end apart: 13 -> 13, of which waited for: 8 -> 9; matrix products, arithmetic and copies ran while one was open for 0% -> 0% of each run, Pallas kernels for 28% -> 27%
where the time goes in v13:
time: 52.9 us; the launch traced here: 52.8 us
  starting transfers between devices  24.1 us (46%)
  Pallas kernels  20.7 us (39%)
  waiting for transfers between devices  7.58 us (14%)
    ppermute x13, starting transfers between devices, swap(): return lax.ppermute(value, axes, [(i, i ^ flip) for i in range(devices)])  24.1 us
    pallas_call x22, Pallas kernels, call(): pl.pallas_call(kernel, out_shape=[jax.ShapeDtypeStruct(shape, dtype) for...  20.7 us
    ppermute x13, waiting for transfers between devices, swap(): return lax.ppermute(value, axes, [(i, i ^ flip) for i in range(devices)])  7.58 us
  transfers between devices with their start and end apart: 13, of which 9 were waited for; matrix products, arithmetic and copies ran while one was open for 0% of the time, Pallas kernels for 27%

profile of v13, /device:TPU:1, one launch (start us, length us, event | category | flops | bytes accessed | tf_op | source)
XLA Modules:
  0.0 52.8 jit_solution(16890244989436515345)
XLA Ops:
  0.0 0.0 copy-start.5
  0.0 0.0 copy-start
  0.0 2.8 %send_half.1 = (bf16[2,256,256]{2,1,0:T(8,128)(2,1)S(1)}, bf16[2,128,256]{2,1,0:T(8,128)(2,1)S(1)}, bf16[2,256,512]{2,1,0:T(8,128)(2,1)S(1)}, bf16[2,1024,256]{2...) custom-call(s32[1]{0:T(128)} %bitcast.pos, ...), custom_call_target="tpu_custom_call" | custom-call | flops 402653184 | bytes 6815756 | tf_op jit(solution)/shard_map/send_half/pallas_call | solution.py:337
  2.8 0.0 copy-start.3
  2.8 3.3 %collective-permute-start = (bf16[2,128,256]{2,1,0:T(8,128)(2,1)S(1)}, bf16[2,128,256]{2,1,0:T(8,128)(2,1)S(1)}, u32[]{:S(2)}, u32[]{:S(2)}) collective-permute-start(bf16[2,128,256]{2,1,0:T(8,128)(2,1)S(1)} %get-tuple-element.54), channel_id=1, source_target_pairs={{0,1},{1,0},{2,3},{3,2},{4,5},{5,4},{6,7},{7,6},{8,9},{9,8},{10,11... | collective-permute-start | bytes 393224 | tf_op jit(solution)/shard_map/ppermute | solution.py:360
  6.1 0.0 copy-done.5
  6.1 1.3 %keep_half.1 = (bf16[2,256,256]{2,1,0:T(8,128)(2,1)S(1)}, bf16[2,128,256]{2,1,0:T(8,128)(2,1)S(1)}) custom-call(s32[1]{0:T(128)} %bitcast.pos, s32[1,2]{1,0:T(1,128)S(1)} %copy-done.5, bf16[2,256,512]{2,1,0:T(8,128)(2,1)S(1)} %get-tuple-element.55.xt, bf16[2,2,512,256]{3,2,1,0:T(8,128)(2,1)S(1)} %get-tuple-element.56.u, ...), custom_call_target="tpu_custom_call" | custom-call | flops 402653184 | bytes 2097164 | tf_op jit(solution)/shard_map/keep_half/pallas_call | solution.py:337
  7.5 0.0 collective-permute-done.got.got0
  7.5 0.3 climb_0.1
  7.8 0.1 collective-permute-start.1
  7.9 0.3 collective-permute-start.4
  8.2 0.0 copy-done
  8.2 0.0 copy-done.3
  8.2 1.6 %shadow_1.1 = (f32[2,64,256]{2,1,0:T(8,128)S(1)}, f32[2,512,256]{2,1,0:T(8,128)S(1)}, bf16[2,2,256,256]{3,2,1,0:T(8,128)(2,1)S(1)}) custom-call(s32[1]{0:T(128)} %bitcast.pos, s32[1,2]{1,0:T(1,128)S(1)} %copy-done.5, bf16[2,64,256]{2,1,0:T(8,128)(2,1)S(1)} %get-tuple-element.62.keep.keep1, bf16[2,8,2,256,256]{4,3,2,1,0:T(8,128)(2,1)S(1)} %bitcast.4, ...), custom_call_target="tpu_custom_call" | custom-call | flops 939524096 | bytes 8454156 | tf_op jit(solution)/shard_map/shadow_1/pallas_call | solution.py:337
  9.7 1.9 %collective-permute-done.1.got.got1 = bf16[2,64,256]{2,1,0:T(8,128)(2,1)S(1)} collective-permute-done((bf16[2,64,256]{2,1,0:T(8,128)(2,1)S(1)}, bf16[2,64,256]{2,1,0:T(8,128)(2,1)S(1)}, u32[]{:S(2)}, u32[]{:S(2)}) %collective-permute-start.1) | collective-permute-done | bytes 65568 | tf_op jit(solution)/shard_map/ppermute | solution.py:360
  11.6 0.0 copy-start.1
  11.6 0.0 copy-start.4
  11.6 0.2 climb_1.1
  11.8 1.9 %collective-permute-start.2 = (bf16[2,32,256]{2,1,0:T(8,128)(2,1)S(1)}, bf16[2,32,256]{2,1,0:T(8,128)(2,1)S(1)}, u32[]{:S(2)}, u32[]{:S(2)}) collective-permute-start(bf16[2,32,256]{2,1,0:T(8,128)(2,1)S(1)} %get-tuple-element.65), channel_id=1, source_target_pairs={{0,5},{1,4},{2,7},{3,6},{4,1},{5,0},{6,3},{7,2},{8,13},{9,12},{10,... | collective-permute-start | bytes 98312 | tf_op jit(solution)/shard_map/ppermute | solution.py:360
  13.7 0.0 copy-done.1
  13.7 0.0 copy-done.4
  13.7 2.0 %shadow_2.1 = (f32[2,32,256]{2,1,0:T(8,128)S(1)}, f32[2,512,256]{2,1,0:T(8,128)S(1)}, bf16[2,256,256]{2,1,0:T(8,128)(2,1)S(1)}) custom-call(s32[1]{0:T(128)} %bitcast.pos, s32[1,2]{1,0:T(1,128)S(1)} %copy-done.5, bf16[2,32,256]{2,1,0:T(8,128)(2,1)S(1)} %get-tuple-element.66.keep.keep2, bf16[2,8,2,256,256]{4,3,2,1,0:T(8,128)(2,1)S(1)} %bitcast.6, ...), custom_call_target="tpu_custom_call" | custom-call | flops 1073741824 | bytes 10649612 | tf_op jit(solution)/shard_map/shadow_2/pallas_call | solution.py:337
  15.7 0.9 %collective-permute-done.2.got.got2 = bf16[2,32,256]{2,1,0:T(8,128)(2,1)S(1)} collective-permute-done((bf16[2,32,256]{2,1,0:T(8,128)(2,1)S(1)}, bf16[2,32,256]{2,1,0:T(8,128)(2,1)S(1)}, u32[]{:S(2)}, u32[]{:S(2)}) %collective-permute-start.2) | collective-permute-done | bytes 32800 | tf_op jit(solution)/shard_map/ppermute | solution.py:360
  16.6 0.2 climb_2.1.q3
  16.7 3.9 %collective-permute-start.3 = (bf16[2,32,256]{2,1,0:T(8,128)(2,1)S(1)}, bf16[2,32,256]{2,1,0:T(8,128)(2,1)S(1)}, u32[]{:S(2)}, u32[]{:S(2)}) collective-permute-start(bf16[2,32,256]{2,1,0:T(8,128)(2,1)S(1)} %climb_2.1.q3), channel_id=1, source_target_pairs={{0,13},{1,12},{2,15},{3,14},{4,9},{5,8},{6,11},{7,10},{8,5},{9,4},... | collective-permute-start | bytes 98312 | tf_op jit(solution)/shard_map/ppermute | solution.py:360
  20.6 0.0 collective-permute-done.4.got0_other
  20.6 1.3 %shadow_3.1 = (f32[2,32,256]{2,1,0:T(8,128)S(1)}, bf16[2,256,256]{2,1,0:T(8,128)(2,1)S(1)}, f32[2,32,256]{2,1,0:T(8,128)S(1)}, f32[2,32,256]{2,1,0:T(8,128)S(1)}) custom-call(s32[1]{0:T(128)} %bitcast.pos, bf16[2,32,256]{2,1,0:T(8,128)(2,1)S(1)} %climb_2.1.q3, bf16[2,8,2,256,256]{4,3,2,1,0:T(8,128)(2,1)S(1)} %bitcast.8, ...), custom_call_target="tpu_custom_call" | custom-call | flops 536870912 | bytes 7569412 | tf_op jit(solution)/shard_map/shadow_3/pallas_call | solution.py:337
  21.9 0.5 collective-permute-done.3.got.got3
  22.4 0.0 copy-start.2
  22.4 0.2 climb_3.1.q4
  22.6 1.6 %collective-permute-start.5 = (bf16[2,32,256]{2,1,0:T(8,128)(2,1)S(1)}, bf16[2,32,256]{2,1,0:T(8,128)(2,1)S(1)}, u32[]{:S(2)}, u32[]{:S(2)}) collective-permute-start(bf16[2,32,256]{2,1,0:T(8,128)(2,1)S(1)} %climb_3.1.q4), channel_id=1, source_target_pairs={{0,17},{1,16},{2,19},{3,18},{4,21},{5,20},{6,23},{7,22},{8,25},{9,... | collective-permute-start | bytes 98312 | tf_op jit(solution)/shard_map/ppermute | solution.py:360
  24.2 0.0 copy-done.2
  24.2 1.4 %shadow_4.1 = (f32[2,32,256]{2,1,0:T(8,128)S(1)}, f32[2,32,256]{2,1,0:T(8,128)S(1)}, f32[2,1024,128]{2,1,0:T(8,128)S(1)}) custom-call(s32[1]{0:T(128)} %bitcast.pos, s32[1,2]{1,0:T(1,128)S(1)} %copy-done.5, bf16[2,32,256]{2,1,0:T(8,128)(2,1)S(1)} %climb_3.1.q4, bf16[2,32,256]{2,1,0:T(8,128)(2,1)S(1)} %collective-permute-done.3.got.got3, ...), custom_call_target="tpu_custom_call" | custom-call | flops 268435456 | bytes 9764876 | tf_op jit(solution)/shard_map/shadow_4/pallas_call | solution.py:337
  25.6 0.5 collective-permute-done.5.got.got4
  26.1 0.2 climb_4.1.q5
  26.3 2.9 %collective-permute-start.6 = (bf16[2,32,256]{2,1,0:T(8,128)(2,1)S(1)}, bf16[2,32,256]{2,1,0:T(8,128)(2,1)S(1)}, u32[]{:S(2)}, u32[]{:S(2)}) collective-permute-start(bf16[2,32,256]{2,1,0:T(8,128)(2,1)S(1)} %climb_4.1.q5), channel_id=1, source_target_pairs={{0,49},{1,48},{2,51},{3,50},{4,53},{5,52},{6,55},{7,54},{8,57},{9,... | collective-permute-start | bytes 98312 | tf_op jit(solution)/shard_map/ppermute | solution.py:360
  29.2 1.0 %shadow_5.1 = (f32[2,32,256]{2,1,0:T(8,128)S(1)}, f32[2,32,256]{2,1,0:T(8,128)S(1)}, bf16[2,256,256]{2,1,0:T(8,128)(2,1)S(1)}, bf16[2,512,256]{2,1,0:T(8,128)(2,1)S(1)}) custom-call(s32[1]{0:T(128)} %bitcast.pos, bf16[2,32,256]{2,1,0:T(8,128)(2,1)S(1)} %climb_4.1.q5, bf16[2,32,256]{2,1,0:T(8,128)(2,1)S(1)} %collective-permute-done.5.got.got4, ...), custom_call_target="tpu_custom_call" | custom-call | flops 402653184 | bytes 7995396 | tf_op jit(solution)/shard_map/shadow_5/pallas_call | solution.py:337
  30.2 0.8 %collective-permute-done.6.got.got5 = bf16[2,32,256]{2,1,0:T(8,128)(2,1)S(1)} collective-permute-done((bf16[2,32,256]{2,1,0:T(8,128)(2,1)S(1)}, bf16[2,32,256]{2,1,0:T(8,128)(2,1)S(1)}, u32[]{:S(2)}, u32[]{:S(2)}) %collective-permute-start.6) | collective-permute-done | bytes 32800 | tf_op jit(solution)/shard_map/ppermute | solution.py:360
  30.9 0.2 climb_5.1.q6
  31.1 1.7 %collective-permute-start.7 = (bf16[2,32,256]{2,1,0:T(8,128)(2,1)S(1)}, bf16[2,32,256]{2,1,0:T(8,128)(2,1)S(1)}, u32[]{:S(2)}, u32[]{:S(2)}) collective-permute-start(bf16[2,32,256]{2,1,0:T(8,128)(2,1)S(1)} %climb_5.1.q6), channel_id=1, source_target_pairs={{0,65},{1,64},{2,67},{3,66},{4,69},{5,68},{6,71},{7,70},{8,73},{9,... | collective-permute-start | bytes 98312 | tf_op jit(solution)/shard_map/ppermute | solution.py:360
  32.8 1.5 %shadow_6.1 = (f32[2,32,256]{2,1,0:T(8,128)S(1)}, f32[2,32,256]{2,1,0:T(8,128)S(1)}, bf16[2,256,256]{2,1,0:T(8,128)(2,1)S(1)}, bf16[2,256,256]{2,1,0:T(8,128)(2,1)S(1)}) custom-call(s32[1]{0:T(128)} %bitcast.pos, bf16[2,32,256]{2,1,0:T(8,128)(2,1)S(1)} %climb_5.1.q6, bf16[2,32,256]{2,1,0:T(8,128)(2,1)S(1)} %collective-permute-done.6.got.got5, ...), custom_call_target="tpu_custom_call" | custom-call | flops 402653184 | bytes 6684676 | tf_op jit(solution)/shard_map/shadow_6/pallas_call | solution.py:337
  34.4 0.2 collective-permute-done.7.got.got6
  34.6 0.2 climb_6.1
  34.8 3.4 %collective-permute-start.8 = (bf16[2,32,256]{2,1,0:T(8,128)(2,1)S(1)}, bf16[2,32,256]{2,1,0:T(8,128)(2,1)S(1)}, u32[]{:S(2)}, u32[]{:S(2)}) collective-permute-start(bf16[2,32,256]{2,1,0:T(8,128)(2,1)S(1)} %climb_6.1), channel_id=1, source_target_pairs={{0,193},{1,192},{2,195},{3,194},{4,197},{5,196},{6,199},{7,198},{8... | collective-permute-start | bytes 98312 | tf_op jit(solution)/shard_map/ppermute | solution.py:360
  38.1 0.9 %shadow_7.1 = (f32[2,32,256]{2,1,0:T(8,128)S(1)}, f32[2,32,256]{2,1,0:T(8,128)S(1)}, bf16[2,256,256]{2,1,0:T(8,128)(2,1)S(1)}, bf16[2,256,256]{2,1,0:T(8,128)(2,1)S(1)}) custom-call(s32[1]{0:T(128)} %bitcast.pos, bf16[2,32,256]{2,1,0:T(8,128)(2,1)S(1)} %collective-permute-done.7.got.got6, bf16[2,8,2,256,256]{4,3,2,1,0:T(8,128)(2,1)S(1)} %bitcast.16, ...), custom_call_target="tpu_custom_call" | custom-call | flops 402653184 | bytes 7045124 | tf_op jit(solution)/shard_map/shadow_7/pallas_call | solution.py:337
  39.0 0.7 %collective-permute-done.8.got = bf16[2,32,256]{2,1,0:T(8,128)(2,1)S(1)} collective-permute-done((bf16[2,32,256]{2,1,0:T(8,128)(2,1)S(1)}, bf16[2,32,256]{2,1,0:T(8,128)(2,1)S(1)}, u32[]{:S(2)}, u32[]{:S(2)}) %collective-permute-start.8) | collective-permute-done | bytes 32800 | tf_op jit(solution)/shard_map/ppermute | solution.py:360
  39.7 0.3 top.1
  40.0 2.1 %collective-permute-start.9 = (bf16[2,32,256]{2,1,0:T(8,128)(2,1)S(1)}, bf16[2,32,256]{2,1,0:T(8,128)(2,1)S(1)}, u32[]{:S(2)}, u32[]{:S(2)}) collective-permute-start(bf16[2,32,256]{2,1,0:T(8,128)(2,1)S(1)} %get-tuple-element.92), channel_id=1, source_target_pairs={{0,5},{1,4},{2,7},{3,6},{4,1},{5,0},{6,3},{7,2},{8,13},{9,12},{10,... | collective-permute-start | bytes 98312 | tf_op jit(solution)/shard_map/ppermute | solution.py:360
  42.1 0.9 %shadow_8.1 = (f32[2,64,256]{2,1,0:T(8,128)S(1)}, f32[2,64,256]{2,1,0:T(8,128)S(1)}, bf16[2,512,256]{2,1,0:T(8,128)(2,1)S(1)}) custom-call(s32[1]{0:T(128)} %bitcast.pos, bf16[2,32,256]{2,1,0:T(8,128)(2,1)S(1)} %get-tuple-element.91.mine, bf16[2,64,256]{2,1,0:T(8,128)(2,1)S(1)} %get-tuple-element.62.keep.keep1, ...), custom_call_target="tpu_custom_call" | custom-call | flops 268435456 | bytes 3833860 | tf_op jit(solution)/shard_map/shadow_8/pallas_call | solution.py:337
  43.0 1.3 %collective-permute-done.9.got = bf16[2,32,256]{2,1,0:T(8,128)(2,1)S(1)} collective-permute-done((bf16[2,32,256]{2,1,0:T(8,128)(2,1)S(1)}, bf16[2,32,256]{2,1,0:T(8,128)(2,1)S(1)}, u32[]{:S(2)}, u32[]{:S(2)}) %collective-permute-start.9) | collective-permute-done | bytes 32800 | tf_op jit(solution)/shard_map/ppermute | solution.py:360
  44.3 0.3 down.1
  44.6 2.4 %collective-permute-start.11 = (bf16[2,64,256]{2,1,0:T(8,128)(2,1)S(1)}, bf16[2,64,256]{2,1,0:T(8,128)(2,1)S(1)}, u32[]{:S(2)}, u32[]{:S(2)}) collective-permute-start(bf16[2,64,256]{2,1,0:T(8,128)(2,1)S(1)} %get-tuple-element.98), channel_id=1, source_target_pairs={{0,3},{1,2},{2,1},{3,0},{4,7},{5,6},{6,5},{7,4},{8,11},{9,10},{10,... | collective-permute-start | bytes 196616 | tf_op jit(solution)/shard_map/ppermute | solution.py:360
  47.0 1.0 %shadow_9.1.base = f32[2,1024,128]{2,1,0:T(8,128)S(1)} custom-call(s32[1]{0:T(128)} %bitcast.pos, s32[1,2]{1,0:T(1,128)S(1)} %copy-done.5, bf16[2,64,256]{2,1,0:T(8,128)(2,1)S(1)} %get-tuple-element.97.mine, bf16[2,2,512,256]{3,2,1,0:T(8,128)(2,1)S(1)} %copy-done.2, bf16[2,256,256]{2,1,0:T(8,128)(2,1)S(1)} %get-tuple-element.96.cleaf, ...), custom_call_target="tpu_custom_call" | custom-call | flops 268435456 | bytes 3473420 | tf_op jit(solution)/shard_map/shadow_9/pallas_call | solution.py:337
  48.0 0.3 collective-permute-start.10
  48.3 0.9 %collective-permute-done.11.got = bf16[2,64,256]{2,1,0:T(8,128)(2,1)S(1)} collective-permute-done((bf16[2,64,256]{2,1,0:T(8,128)(2,1)S(1)}, bf16[2,64,256]{2,1,0:T(8,128)(2,1)S(1)}, u32[]{:S(2)}, u32[]{:S(2)}) %collective-permute-start.11) | collective-permute-done | bytes 65568 | tf_op jit(solution)/shard_map/ppermute | solution.py:360
  49.2 0.3 collective-permute-start.12
  49.4 1.0 %own_columns.1.done = bf16[2,2,512,128]{3,2,1,0:T(8,128)(2,1)S(1)} custom-call(s32[1]{0:T(128)} %bitcast.pos, s32[1,2]{1,0:T(1,128)S(1)} %copy-done.5, bf16[2,64,256]{2,1,0:T(8,128)(2,1)S(1)} %get-tuple-element.97.mine, bf16[2,64,256]{2,1,0:T(8,128)(2,1)S(1)} %collective-permute-done.11.got, f32[2,1024,128]{2,1,0:T(8,128)S(1)} %get-tuple-element.102.base, ...), custom_call_target="tpu_custom_call" | custom-call | flops 268435456 | bytes 2228236 | tf_op jit(solution)/shard_map/own_columns/pallas_call | solution.py:337
  50.4 0.0 collective-permute-done.10.mine
  50.4 0.0 collective-permute-done.12.got
  50.5 2.2 %other_columns.1 = bf16[2,1024,256]{2,1,0:T(8,128)(2,1)} custom-call(s32[1]{0:T(128)} %bitcast.pos, s32[1,2]{1,0:T(1,128)S(1)} %copy-done.5, bf16[2,64,256]{2,1,0:T(8,128)(2,1)S(1)} %collective-permute-done.10.mine, bf16[2,64,256]{2,1,0:T(8,128)(2,1)S(1)} %collective-permute-done.12.got, f32[2,1024,128]{2,1,0:T(8,128)S(1)} %shadow_9.1.base, ...), custom_call_target="tpu_custom_call" | custom-call | flops 268435456 | bytes 2752524 | tf_op jit(solution)/shard_map/other_columns/pallas_call | solution.py:337
Async XLA Ops:
  0.0 6.1 %copy-start.5 = (s32[1,2]{1,0:T(1,128)S(1)}, s32[1,2]{1,0:T(1,128)}, u32[]{:S(2)}) copy-start(s32[1,2]{1,0:T(1,128)} %order.15) | copy-start | bytes 28
  0.0 8.2 %copy-start = (bf16[2,1,8,2,256,256]{5,4,3,2,1,0:T(8,128)(2,1)S(1)}, bf16[2,1,8,2,256,256]{5,4,3,2,1,0:T(8,128)(2,1)}, u32[]{:S(2)}) copy-start(bf16[2,1,8,2,256,256]{5,4,3,2,1,0:T(8,128)(2,1)} %param.15) | copy-start | bytes 12582916
  2.8 5.4 %copy-start.3 = (bf16[2,2,512,512]{3,2,1,0:T(8,128)(2,1)S(1)}, bf16[2,2,512,512]{3,2,1,0:T(8,128)(2,1)}, u32[]{:S(2)}) copy-start(bf16[2,2,512,512]{3,2,1,0:T(8,128)(2,1)} %d.3) | copy-start | bytes 6291460
  2.8 4.6 %collective-permute-start = (bf16[2,128,256]{2,1,0:T(8,128)(2,1)S(1)}, bf16[2,128,256]{2,1,0:T(8,128)(2,1)S(1)}, u32[]{:S(2)}, u32[]{:S(2)}) collective-permute-start(bf16[2,128,256]{2,1,0:T(8,128)(2,1)S(1)} %get-tuple-element.54), channel_id=1, source_target_pairs={{0,1},{1,0},{2,3},{3,2},{4,5},{5,4},{6,7},{7,6},{8,9},{9,8},{10,11... | collective-permute-start | bytes 393224 | tf_op jit(solution)/shard_map/ppermute | solution.py:360
  7.8 3.8 %collective-permute-start.1 = (bf16[2,64,256]{2,1,0:T(8,128)(2,1)S(1)}, bf16[2,64,256]{2,1,0:T(8,128)(2,1)S(1)}, u32[]{:S(2)}, u32[]{:S(2)}) collective-permute-start(bf16[2,64,256]{2,1,0:T(8,128)(2,1)S(1)} %get-tuple-element.60), channel_id=1, source_target_pairs={{0,3},{1,2},{2,1},{3,0},{4,7},{5,6},{6,5},{7,4},{8,11},{9,10},{10,... | collective-permute-start | bytes 196616 | tf_op jit(solution)/shard_map/ppermute | solution.py:360
  7.9 12.7 %collective-permute-start.4 = (bf16[2,128,256]{2,1,0:T(8,128)(2,1)S(1)}, bf16[2,128,256]{2,1,0:T(8,128)(2,1)S(1)}, u32[]{:S(2)}, u32[]{:S(2)}) collective-permute-start(bf16[2,128,256]{2,1,0:T(8,128)(2,1)S(1)} %get-tuple-element.70.q), channel_id=1, source_target_pairs={{0,1},{1,0},{2,3},{3,2},{4,5},{5,4},{6,7},{7,6},{8,9},{9,8},{10,11... | collective-permute-start | bytes 393224 | tf_op jit(solution)/shard_map/ppermute | solution.py:360
  11.6 2.1 %copy-start.1 = (bf16[2,1,8,256,256]{4,3,2,1,0:T(8,128)(2,1)S(1)}, bf16[2,1,8,256,256]{4,3,2,1,0:T(8,128)(2,1)}, u32[]{:S(2)}) copy-start(bf16[2,1,8,256,256]{4,3,2,1,0:T(8,128)(2,1)} %param.16) | copy-start | bytes 6291460
  11.6 2.1 %copy-start.4 = (bf16[2,1,256,256]{3,2,1,0:T(8,128)(2,1)S(1)}, bf16[2,1,256,256]{3,2,1,0:T(8,128)(2,1)}, u32[]{:S(2)}) copy-start(bf16[2,1,256,256]{3,2,1,0:T(8,128)(2,1)} %bl.3) | copy-start | bytes 786436
  11.8 4.8 %collective-permute-start.2 = (bf16[2,32,256]{2,1,0:T(8,128)(2,1)S(1)}, bf16[2,32,256]{2,1,0:T(8,128)(2,1)S(1)}, u32[]{:S(2)}, u32[]{:S(2)}) collective-permute-start(bf16[2,32,256]{2,1,0:T(8,128)(2,1)S(1)} %get-tuple-element.65), channel_id=1, source_target_pairs={{0,5},{1,4},{2,7},{3,6},{4,1},{5,0},{6,3},{7,2},{8,13},{9,12},{10,... | collective-permute-start | bytes 98312 | tf_op jit(solution)/shard_map/ppermute | solution.py:360
  16.7 5.7 %collective-permute-start.3 = (bf16[2,32,256]{2,1,0:T(8,128)(2,1)S(1)}, bf16[2,32,256]{2,1,0:T(8,128)(2,1)S(1)}, u32[]{:S(2)}, u32[]{:S(2)}) collective-permute-start(bf16[2,32,256]{2,1,0:T(8,128)(2,1)S(1)} %climb_2.1.q3), channel_id=1, source_target_pairs={{0,13},{1,12},{2,15},{3,14},{4,9},{5,8},{6,11},{7,10},{8,5},{9,4},... | collective-permute-start | bytes 98312 | tf_op jit(solution)/shard_map/ppermute | solution.py:360
  22.4 1.8 %copy-start.2 = (bf16[2,2,512,256]{3,2,1,0:T(8,128)(2,1)S(1)}, bf16[2,2,512,256]{3,2,1,0:T(8,128)(2,1)}, u32[]{:S(2)}) copy-start(bf16[2,2,512,256]{3,2,1,0:T(8,128)(2,1)} %r.7) | copy-start | bytes 3145732
  22.6 3.5 %collective-permute-start.5 = (bf16[2,32,256]{2,1,0:T(8,128)(2,1)S(1)}, bf16[2,32,256]{2,1,0:T(8,128)(2,1)S(1)}, u32[]{:S(2)}, u32[]{:S(2)}) collective-permute-start(bf16[2,32,256]{2,1,0:T(8,128)(2,1)S(1)} %climb_3.1.q4), channel_id=1, source_target_pairs={{0,17},{1,16},{2,19},{3,18},{4,21},{5,20},{6,23},{7,22},{8,25},{9,... | collective-permute-start | bytes 98312 | tf_op jit(solution)/shard_map/ppermute | solution.py:360
  26.3 4.7 %collective-permute-start.6 = (bf16[2,32,256]{2,1,0:T(8,128)(2,1)S(1)}, bf16[2,32,256]{2,1,0:T(8,128)(2,1)S(1)}, u32[]{:S(2)}, u32[]{:S(2)}) collective-permute-start(bf16[2,32,256]{2,1,0:T(8,128)(2,1)S(1)} %climb_4.1.q5), channel_id=1, source_target_pairs={{0,49},{1,48},{2,51},{3,50},{4,53},{5,52},{6,55},{7,54},{8,57},{9,... | collective-permute-start | bytes 98312 | tf_op jit(solution)/shard_map/ppermute | solution.py:360
  31.1 3.5 %collective-permute-start.7 = (bf16[2,32,256]{2,1,0:T(8,128)(2,1)S(1)}, bf16[2,32,256]{2,1,0:T(8,128)(2,1)S(1)}, u32[]{:S(2)}, u32[]{:S(2)}) collective-permute-start(bf16[2,32,256]{2,1,0:T(8,128)(2,1)S(1)} %climb_5.1.q6), channel_id=1, source_target_pairs={{0,65},{1,64},{2,67},{3,66},{4,69},{5,68},{6,71},{7,70},{8,73},{9,... | collective-permute-start | bytes 98312 | tf_op jit(solution)/shard_map/ppermute | solution.py:360
  34.8 5.0 %collective-permute-start.8 = (bf16[2,32,256]{2,1,0:T(8,128)(2,1)S(1)}, bf16[2,32,256]{2,1,0:T(8,128)(2,1)S(1)}, u32[]{:S(2)}, u32[]{:S(2)}) collective-permute-start(bf16[2,32,256]{2,1,0:T(8,128)(2,1)S(1)} %climb_6.1), channel_id=1, source_target_pairs={{0,193},{1,192},{2,195},{3,194},{4,197},{5,196},{6,199},{7,198},{8... | collective-permute-start | bytes 98312 | tf_op jit(solution)/shard_map/ppermute | solution.py:360
  40.0 4.3 %collective-permute-start.9 = (bf16[2,32,256]{2,1,0:T(8,128)(2,1)S(1)}, bf16[2,32,256]{2,1,0:T(8,128)(2,1)S(1)}, u32[]{:S(2)}, u32[]{:S(2)}) collective-permute-start(bf16[2,32,256]{2,1,0:T(8,128)(2,1)S(1)} %get-tuple-element.92), channel_id=1, source_target_pairs={{0,5},{1,4},{2,7},{3,6},{4,1},{5,0},{6,3},{7,2},{8,13},{9,12},{10,... | collective-permute-start | bytes 98312 | tf_op jit(solution)/shard_map/ppermute | solution.py:360
  44.6 4.5 %collective-permute-start.11 = (bf16[2,64,256]{2,1,0:T(8,128)(2,1)S(1)}, bf16[2,64,256]{2,1,0:T(8,128)(2,1)S(1)}, u32[]{:S(2)}, u32[]{:S(2)}) collective-permute-start(bf16[2,64,256]{2,1,0:T(8,128)(2,1)S(1)} %get-tuple-element.98), channel_id=1, source_target_pairs={{0,3},{1,2},{2,1},{3,0},{4,7},{5,6},{6,5},{7,4},{8,11},{9,10},{10,... | collective-permute-start | bytes 196616 | tf_op jit(solution)/shard_map/ppermute | solution.py:360
  48.0 2.4 %collective-permute-start.10 = (bf16[2,64,256]{2,1,0:T(8,128)(2,1)S(1)}, bf16[2,64,256]{2,1,0:T(8,128)(2,1)S(1)}, u32[]{:S(2)}, u32[]{:S(2)}) collective-permute-start(bf16[2,64,256]{2,1,0:T(8,128)(2,1)S(1)} %get-tuple-element.97.mine), channel_id=1, source_target_pairs={{0,1},{1,0},{2,3},{3,2},{4,5},{5,4},{6,7},{7,6},{8,9},{9,8},{10,11... | collective-permute-start | bytes 196616 | tf_op jit(solution)/shard_map/ppermute | solution.py:360
  49.2 1.3 %collective-permute-start.12 = (bf16[2,64,256]{2,1,0:T(8,128)(2,1)S(1)}, bf16[2,64,256]{2,1,0:T(8,128)(2,1)S(1)}, u32[]{:S(2)}, u32[]{:S(2)}) collective-permute-start(bf16[2,64,256]{2,1,0:T(8,128)(2,1)S(1)} %collective-permute-done.11.got), channel_id=1, source_target_pairs={{0,1},{1,0},{2,3},{3,2},{4,5},{5,4},{6,7},{7,6},{8,9},{9,8},{10,11... | collective-permute-start | bytes 196616 | tf_op jit(solution)/shard_map/ppermute | solution.py:360

commit v14 on v13

--- a/solution.py
+++ b/solution.py
@@ -286,7 +286,7 @@
 
 
 def finish(pos, order, mine, got, base, gs, out, tile):
-    hw = widen(join(mine, got, side(pos, 1)))
+    hw = widen(join(mine, got, side(pos, 1))).T
     n = base.shape[2]
     for leaf, g in enumerate(gs):
         size = g.shape[1]
@@ -294,7 +294,7 @@
             here = pl.ds(step * tile, tile)
             start = (order[0, 0] ^ leaf) * size + step * tile
             at = pl.ds(pl.multiple_of(start, tile), tile)
-            add = dot(jnp.concatenate([g[0, here], g[1, here]], axis=1), hw, NT)
+            add = dot(jnp.concatenate([g[0, here], g[1, here]], axis=1), hw)
             for c in range(2):
                 out[leaf, c, here] = (base[c, at] + add[:, c * n : (c + 1) * n]).astype(BF)
             yield leaf, here, at

time: 52.9 us -> 52.9 us (level)
  no operation moved by 1% of the time
where the time goes in v14:
time: 52.9 us; the launch traced here: 52.8 us
  starting transfers between devices  24.1 us (46%)
  Pallas kernels  20.7 us (39%)
  waiting for transfers between devices  7.58 us (14%)
    ppermute x13, starting transfers between devices, swap(): return lax.ppermute(value, axes, [(i, i ^ flip) for i in range(devices)])  24.1 us
    pallas_call x22, Pallas kernels, call(): pl.pallas_call(kernel, out_shape=[jax.ShapeDtypeStruct(shape, dtype) for...  20.7 us
    ppermute x13, waiting for transfers between devices, swap(): return lax.ppermute(value, axes, [(i, i ^ flip) for i in range(devices)])  7.58 us
  transfers between devices with their start and end apart: 13, of which 9 were waited for; matrix products, arithmetic and copies ran while one was open for 0% of the time, Pallas kernels for 27%

profile of v14, /device:TPU:1, one launch (start us, length us, event | category | flops | bytes accessed | tf_op | source)
XLA Modules:
  0.0 52.8 jit_solution(16890244989436515345)
XLA Ops:
  0.0 0.0 copy-start.5
  0.0 0.0 copy-start
  0.0 2.8 %send_half.1 = (bf16[2,256,256]{2,1,0:T(8,128)(2,1)S(1)}, bf16[2,128,256]{2,1,0:T(8,128)(2,1)S(1)}, bf16[2,256,512]{2,1,0:T(8,128)(2,1)S(1)}, bf16[2,1024,256]{2...) custom-call(s32[1]{0:T(128)} %bitcast.pos, ...), custom_call_target="tpu_custom_call" | custom-call | flops 402653184 | bytes 6815756 | tf_op jit(solution)/shard_map/send_half/pallas_call | solution.py:337
  2.8 0.0 copy-start.3
  2.8 3.3 %collective-permute-start = (bf16[2,128,256]{2,1,0:T(8,128)(2,1)S(1)}, bf16[2,128,256]{2,1,0:T(8,128)(2,1)S(1)}, u32[]{:S(2)}, u32[]{:S(2)}) collective-permute-start(bf16[2,128,256]{2,1,0:T(8,128)(2,1)S(1)} %get-tuple-element.54), channel_id=1, source_target_pairs={{0,1},{1,0},{2,3},{3,2},{4,5},{5,4},{6,7},{7,6},{8,9},{9,8},{10,11... | collective-permute-start | bytes 393224 | tf_op jit(solution)/shard_map/ppermute | solution.py:360
  6.1 0.0 copy-done.5
  6.1 1.3 %keep_half.1 = (bf16[2,256,256]{2,1,0:T(8,128)(2,1)S(1)}, bf16[2,128,256]{2,1,0:T(8,128)(2,1)S(1)}) custom-call(s32[1]{0:T(128)} %bitcast.pos, s32[1,2]{1,0:T(1,128)S(1)} %copy-done.5, bf16[2,256,512]{2,1,0:T(8,128)(2,1)S(1)} %get-tuple-element.55.xt, bf16[2,2,512,256]{3,2,1,0:T(8,128)(2,1)S(1)} %get-tuple-element.56.u, ...), custom_call_target="tpu_custom_call" | custom-call | flops 402653184 | bytes 2097164 | tf_op jit(solution)/shard_map/keep_half/pallas_call | solution.py:337
  7.5 0.0 collective-permute-done.got.got0
  7.5 0.3 climb_0.1
  7.8 0.1 collective-permute-start.1
  7.9 0.3 collective-permute-start.4
  8.2 0.0 copy-done
  8.2 0.0 copy-done.3
  8.2 1.6 %shadow_1.1 = (f32[2,64,256]{2,1,0:T(8,128)S(1)}, f32[2,512,256]{2,1,0:T(8,128)S(1)}, bf16[2,2,256,256]{3,2,1,0:T(8,128)(2,1)S(1)}) custom-call(s32[1]{0:T(128)} %bitcast.pos, s32[1,2]{1,0:T(1,128)S(1)} %copy-done.5, bf16[2,64,256]{2,1,0:T(8,128)(2,1)S(1)} %get-tuple-element.62.keep.keep1, bf16[2,8,2,256,256]{4,3,2,1,0:T(8,128)(2,1)S(1)} %bitcast.4, ...), custom_call_target="tpu_custom_call" | custom-call | flops 939524096 | bytes 8454156 | tf_op jit(solution)/shard_map/shadow_1/pallas_call | solution.py:337
  9.7 1.9 %collective-permute-done.1.got.got1 = bf16[2,64,256]{2,1,0:T(8,128)(2,1)S(1)} collective-permute-done((bf16[2,64,256]{2,1,0:T(8,128)(2,1)S(1)}, bf16[2,64,256]{2,1,0:T(8,128)(2,1)S(1)}, u32[]{:S(2)}, u32[]{:S(2)}) %collective-permute-start.1) | collective-permute-done | bytes 65568 | tf_op jit(solution)/shard_map/ppermute | solution.py:360
  11.6 0.0 copy-start.1
  11.6 0.0 copy-start.4
  11.6 0.2 climb_1.1
  11.8 1.9 %collective-permute-start.2 = (bf16[2,32,256]{2,1,0:T(8,128)(2,1)S(1)}, bf16[2,32,256]{2,1,0:T(8,128)(2,1)S(1)}, u32[]{:S(2)}, u32[]{:S(2)}) collective-permute-start(bf16[2,32,256]{2,1,0:T(8,128)(2,1)S(1)} %get-tuple-element.65), channel_id=1, source_target_pairs={{0,5},{1,4},{2,7},{3,6},{4,1},{5,0},{6,3},{7,2},{8,13},{9,12},{10,... | collective-permute-start | bytes 98312 | tf_op jit(solution)/shard_map/ppermute | solution.py:360
  13.7 0.0 copy-done.1
  13.7 0.0 copy-done.4
  13.7 2.0 %shadow_2.1 = (f32[2,32,256]{2,1,0:T(8,128)S(1)}, f32[2,512,256]{2,1,0:T(8,128)S(1)}, bf16[2,256,256]{2,1,0:T(8,128)(2,1)S(1)}) custom-call(s32[1]{0:T(128)} %bitcast.pos, s32[1,2]{1,0:T(1,128)S(1)} %copy-done.5, bf16[2,32,256]{2,1,0:T(8,128)(2,1)S(1)} %get-tuple-element.66.keep.keep2, bf16[2,8,2,256,256]{4,3,2,1,0:T(8,128)(2,1)S(1)} %bitcast.6, ...), custom_call_target="tpu_custom_call" | custom-call | flops 1073741824 | bytes 10649612 | tf_op jit(solution)/shard_map/shadow_2/pallas_call | solution.py:337
  15.7 0.9 %collective-permute-done.2.got.got2 = bf16[2,32,256]{2,1,0:T(8,128)(2,1)S(1)} collective-permute-done((bf16[2,32,256]{2,1,0:T(8,128)(2,1)S(1)}, bf16[2,32,256]{2,1,0:T(8,128)(2,1)S(1)}, u32[]{:S(2)}, u32[]{:S(2)}) %collective-permute-start.2) | collective-permute-done | bytes 32800 | tf_op jit(solution)/shard_map/ppermute | solution.py:360
  16.6 0.2 climb_2.1.q3
  16.7 3.9 %collective-permute-start.3 = (bf16[2,32,256]{2,1,0:T(8,128)(2,1)S(1)}, bf16[2,32,256]{2,1,0:T(8,128)(2,1)S(1)}, u32[]{:S(2)}, u32[]{:S(2)}) collective-permute-start(bf16[2,32,256]{2,1,0:T(8,128)(2,1)S(1)} %climb_2.1.q3), channel_id=1, source_target_pairs={{0,13},{1,12},{2,15},{3,14},{4,9},{5,8},{6,11},{7,10},{8,5},{9,4},... | collective-permute-start | bytes 98312 | tf_op jit(solution)/shard_map/ppermute | solution.py:360
  20.6 0.0 collective-permute-done.4.got0_other
  20.6 1.3 %shadow_3.1 = (f32[2,32,256]{2,1,0:T(8,128)S(1)}, bf16[2,256,256]{2,1,0:T(8,128)(2,1)S(1)}, f32[2,32,256]{2,1,0:T(8,128)S(1)}, f32[2,32,256]{2,1,0:T(8,128)S(1)}) custom-call(s32[1]{0:T(128)} %bitcast.pos, bf16[2,32,256]{2,1,0:T(8,128)(2,1)S(1)} %climb_2.1.q3, bf16[2,8,2,256,256]{4,3,2,1,0:T(8,128)(2,1)S(1)} %bitcast.8, ...), custom_call_target="tpu_custom_call" | custom-call | flops 536870912 | bytes 7569412 | tf_op jit(solution)/shard_map/shadow_3/pallas_call | solution.py:337
  21.9 0.5 collective-permute-done.3.got.got3
  22.4 0.0 copy-start.2
  22.4 0.2 climb_3.1.q4
  22.6 1.6 %collective-permute-start.5 = (bf16[2,32,256]{2,1,0:T(8,128)(2,1)S(1)}, bf16[2,32,256]{2,1,0:T(8,128)(2,1)S(1)}, u32[]{:S(2)}, u32[]{:S(2)}) collective-permute-start(bf16[2,32,256]{2,1,0:T(8,128)(2,1)S(1)} %climb_3.1.q4), channel_id=1, source_target_pairs={{0,17},{1,16},{2,19},{3,18},{4,21},{5,20},{6,23},{7,22},{8,25},{9,... | collective-permute-start | bytes 98312 | tf_op jit(solution)/shard_map/ppermute | solution.py:360
  24.2 0.0 copy-done.2
  24.2 1.4 %shadow_4.1 = (f32[2,32,256]{2,1,0:T(8,128)S(1)}, f32[2,32,256]{2,1,0:T(8,128)S(1)}, f32[2,1024,128]{2,1,0:T(8,128)S(1)}) custom-call(s32[1]{0:T(128)} %bitcast.pos, s32[1,2]{1,0:T(1,128)S(1)} %copy-done.5, bf16[2,32,256]{2,1,0:T(8,128)(2,1)S(1)} %climb_3.1.q4, bf16[2,32,256]{2,1,0:T(8,128)(2,1)S(1)} %collective-permute-done.3.got.got3, ...), custom_call_target="tpu_custom_call" | custom-call | flops 268435456 | bytes 9764876 | tf_op jit(solution)/shard_map/shadow_4/pallas_call | solution.py:337
  25.6 0.5 collective-permute-done.5.got.got4
  26.1 0.2 climb_4.1.q5
  26.3 2.9 %collective-permute-start.6 = (bf16[2,32,256]{2,1,0:T(8,128)(2,1)S(1)}, bf16[2,32,256]{2,1,0:T(8,128)(2,1)S(1)}, u32[]{:S(2)}, u32[]{:S(2)}) collective-permute-start(bf16[2,32,256]{2,1,0:T(8,128)(2,1)S(1)} %climb_4.1.q5), channel_id=1, source_target_pairs={{0,49},{1,48},{2,51},{3,50},{4,53},{5,52},{6,55},{7,54},{8,57},{9,... | collective-permute-start | bytes 98312 | tf_op jit(solution)/shard_map/ppermute | solution.py:360
  29.2 1.0 %shadow_5.1 = (f32[2,32,256]{2,1,0:T(8,128)S(1)}, f32[2,32,256]{2,1,0:T(8,128)S(1)}, bf16[2,256,256]{2,1,0:T(8,128)(2,1)S(1)}, bf16[2,512,256]{2,1,0:T(8,128)(2,1)S(1)}) custom-call(s32[1]{0:T(128)} %bitcast.pos, bf16[2,32,256]{2,1,0:T(8,128)(2,1)S(1)} %climb_4.1.q5, bf16[2,32,256]{2,1,0:T(8,128)(2,1)S(1)} %collective-permute-done.5.got.got4, ...), custom_call_target="tpu_custom_call" | custom-call | flops 402653184 | bytes 7995396 | tf_op jit(solution)/shard_map/shadow_5/pallas_call | solution.py:337
  30.2 0.8 %collective-permute-done.6.got.got5 = bf16[2,32,256]{2,1,0:T(8,128)(2,1)S(1)} collective-permute-done((bf16[2,32,256]{2,1,0:T(8,128)(2,1)S(1)}, bf16[2,32,256]{2,1,0:T(8,128)(2,1)S(1)}, u32[]{:S(2)}, u32[]{:S(2)}) %collective-permute-start.6) | collective-permute-done | bytes 32800 | tf_op jit(solution)/shard_map/ppermute | solution.py:360
  30.9 0.2 climb_5.1.q6
  31.1 1.7 %collective-permute-start.7 = (bf16[2,32,256]{2,1,0:T(8,128)(2,1)S(1)}, bf16[2,32,256]{2,1,0:T(8,128)(2,1)S(1)}, u32[]{:S(2)}, u32[]{:S(2)}) collective-permute-start(bf16[2,32,256]{2,1,0:T(8,128)(2,1)S(1)} %climb_5.1.q6), channel_id=1, source_target_pairs={{0,65},{1,64},{2,67},{3,66},{4,69},{5,68},{6,71},{7,70},{8,73},{9,... | collective-permute-start | bytes 98312 | tf_op jit(solution)/shard_map/ppermute | solution.py:360
  32.8 1.5 %shadow_6.1 = (f32[2,32,256]{2,1,0:T(8,128)S(1)}, f32[2,32,256]{2,1,0:T(8,128)S(1)}, bf16[2,256,256]{2,1,0:T(8,128)(2,1)S(1)}, bf16[2,256,256]{2,1,0:T(8,128)(2,1)S(1)}) custom-call(s32[1]{0:T(128)} %bitcast.pos, bf16[2,32,256]{2,1,0:T(8,128)(2,1)S(1)} %climb_5.1.q6, bf16[2,32,256]{2,1,0:T(8,128)(2,1)S(1)} %collective-permute-done.6.got.got5, ...), custom_call_target="tpu_custom_call" | custom-call | flops 402653184 | bytes 6684676 | tf_op jit(solution)/shard_map/shadow_6/pallas_call | solution.py:337
  34.4 0.2 collective-permute-done.7.got.got6
  34.6 0.2 climb_6.1
  34.8 3.4 %collective-permute-start.8 = (bf16[2,32,256]{2,1,0:T(8,128)(2,1)S(1)}, bf16[2,32,256]{2,1,0:T(8,128)(2,1)S(1)}, u32[]{:S(2)}, u32[]{:S(2)}) collective-permute-start(bf16[2,32,256]{2,1,0:T(8,128)(2,1)S(1)} %climb_6.1), channel_id=1, source_target_pairs={{0,193},{1,192},{2,195},{3,194},{4,197},{5,196},{6,199},{7,198},{8... | collective-permute-start | bytes 98312 | tf_op jit(solution)/shard_map/ppermute | solution.py:360
  38.1 0.9 %shadow_7.1 = (f32[2,32,256]{2,1,0:T(8,128)S(1)}, f32[2,32,256]{2,1,0:T(8,128)S(1)}, bf16[2,256,256]{2,1,0:T(8,128)(2,1)S(1)}, bf16[2,256,256]{2,1,0:T(8,128)(2,1)S(1)}) custom-call(s32[1]{0:T(128)} %bitcast.pos, bf16[2,32,256]{2,1,0:T(8,128)(2,1)S(1)} %collective-permute-done.7.got.got6, bf16[2,8,2,256,256]{4,3,2,1,0:T(8,128)(2,1)S(1)} %bitcast.16, ...), custom_call_target="tpu_custom_call" | custom-call | flops 402653184 | bytes 7045124 | tf_op jit(solution)/shard_map/shadow_7/pallas_call | solution.py:337
  39.0 0.7 %collective-permute-done.8.got = bf16[2,32,256]{2,1,0:T(8,128)(2,1)S(1)} collective-permute-done((bf16[2,32,256]{2,1,0:T(8,128)(2,1)S(1)}, bf16[2,32,256]{2,1,0:T(8,128)(2,1)S(1)}, u32[]{:S(2)}, u32[]{:S(2)}) %collective-permute-start.8) | collective-permute-done | bytes 32800 | tf_op jit(solution)/shard_map/ppermute | solution.py:360
  39.7 0.3 top.1
  40.0 2.1 %collective-permute-start.9 = (bf16[2,32,256]{2,1,0:T(8,128)(2,1)S(1)}, bf16[2,32,256]{2,1,0:T(8,128)(2,1)S(1)}, u32[]{:S(2)}, u32[]{:S(2)}) collective-permute-start(bf16[2,32,256]{2,1,0:T(8,128)(2,1)S(1)} %get-tuple-element.92), channel_id=1, source_target_pairs={{0,5},{1,4},{2,7},{3,6},{4,1},{5,0},{6,3},{7,2},{8,13},{9,12},{10,... | collective-permute-start | bytes 98312 | tf_op jit(solution)/shard_map/ppermute | solution.py:360
  42.1 0.9 %shadow_8.1 = (f32[2,64,256]{2,1,0:T(8,128)S(1)}, f32[2,64,256]{2,1,0:T(8,128)S(1)}, bf16[2,512,256]{2,1,0:T(8,128)(2,1)S(1)}) custom-call(s32[1]{0:T(128)} %bitcast.pos, bf16[2,32,256]{2,1,0:T(8,128)(2,1)S(1)} %get-tuple-element.91.mine, bf16[2,64,256]{2,1,0:T(8,128)(2,1)S(1)} %get-tuple-element.62.keep.keep1, ...), custom_call_target="tpu_custom_call" | custom-call | flops 268435456 | bytes 3833860 | tf_op jit(solution)/shard_map/shadow_8/pallas_call | solution.py:337
  43.0 1.3 %collective-permute-done.9.got = bf16[2,32,256]{2,1,0:T(8,128)(2,1)S(1)} collective-permute-done((bf16[2,32,256]{2,1,0:T(8,128)(2,1)S(1)}, bf16[2,32,256]{2,1,0:T(8,128)(2,1)S(1)}, u32[]{:S(2)}, u32[]{:S(2)}) %collective-permute-start.9) | collective-permute-done | bytes 32800 | tf_op jit(solution)/shard_map/ppermute | solution.py:360
  44.3 0.3 down.1
  44.6 2.4 %collective-permute-start.11 = (bf16[2,64,256]{2,1,0:T(8,128)(2,1)S(1)}, bf16[2,64,256]{2,1,0:T(8,128)(2,1)S(1)}, u32[]{:S(2)}, u32[]{:S(2)}) collective-permute-start(bf16[2,64,256]{2,1,0:T(8,128)(2,1)S(1)} %get-tuple-element.98), channel_id=1, source_target_pairs={{0,3},{1,2},{2,1},{3,0},{4,7},{5,6},{6,5},{7,4},{8,11},{9,10},{10,... | collective-permute-start | bytes 196616 | tf_op jit(solution)/shard_map/ppermute | solution.py:360
  47.0 1.0 %shadow_9.1.base = f32[2,1024,128]{2,1,0:T(8,128)S(1)} custom-call(s32[1]{0:T(128)} %bitcast.pos, s32[1,2]{1,0:T(1,128)S(1)} %copy-done.5, bf16[2,64,256]{2,1,0:T(8,128)(2,1)S(1)} %get-tuple-element.97.mine, bf16[2,2,512,256]{3,2,1,0:T(8,128)(2,1)S(1)} %copy-done.2, bf16[2,256,256]{2,1,0:T(8,128)(2,1)S(1)} %get-tuple-element.96.cleaf, ...), custom_call_target="tpu_custom_call" | custom-call | flops 268435456 | bytes 3473420 | tf_op jit(solution)/shard_map/shadow_9/pallas_call | solution.py:337
  48.0 0.3 collective-permute-start.10
  48.3 0.9 %collective-permute-done.11.got = bf16[2,64,256]{2,1,0:T(8,128)(2,1)S(1)} collective-permute-done((bf16[2,64,256]{2,1,0:T(8,128)(2,1)S(1)}, bf16[2,64,256]{2,1,0:T(8,128)(2,1)S(1)}, u32[]{:S(2)}, u32[]{:S(2)}) %collective-permute-start.11) | collective-permute-done | bytes 65568 | tf_op jit(solution)/shard_map/ppermute | solution.py:360
  49.2 0.3 collective-permute-start.12
  49.4 1.0 %own_columns.1.done = bf16[2,2,512,128]{3,2,1,0:T(8,128)(2,1)S(1)} custom-call(s32[1]{0:T(128)} %bitcast.pos, s32[1,2]{1,0:T(1,128)S(1)} %copy-done.5, bf16[2,64,256]{2,1,0:T(8,128)(2,1)S(1)} %get-tuple-element.97.mine, bf16[2,64,256]{2,1,0:T(8,128)(2,1)S(1)} %collective-permute-done.11.got, f32[2,1024,128]{2,1,0:T(8,128)S(1)} %get-tuple-element.102.base, ...), custom_call_target="tpu_custom_call" | custom-call | flops 268435456 | bytes 2228236 | tf_op jit(solution)/shard_map/own_columns/pallas_call | solution.py:337
  50.4 0.0 collective-permute-done.10.mine
  50.4 0.0 collective-permute-done.12.got
  50.5 2.2 %other_columns.1 = bf16[2,1024,256]{2,1,0:T(8,128)(2,1)} custom-call(s32[1]{0:T(128)} %bitcast.pos, s32[1,2]{1,0:T(1,128)S(1)} %copy-done.5, bf16[2,64,256]{2,1,0:T(8,128)(2,1)S(1)} %collective-permute-done.10.mine, bf16[2,64,256]{2,1,0:T(8,128)(2,1)S(1)} %collective-permute-done.12.got, f32[2,1024,128]{2,1,0:T(8,128)S(1)} %shadow_9.1.base, ...), custom_call_target="tpu_custom_call" | custom-call | flops 268435456 | bytes 2752524 | tf_op jit(solution)/shard_map/other_columns/pallas_call | solution.py:337
Async XLA Ops:
  0.0 6.1 %copy-start.5 = (s32[1,2]{1,0:T(1,128)S(1)}, s32[1,2]{1,0:T(1,128)}, u32[]{:S(2)}) copy-start(s32[1,2]{1,0:T(1,128)} %order.15) | copy-start | bytes 28
  0.0 8.2 %copy-start = (bf16[2,1,8,2,256,256]{5,4,3,2,1,0:T(8,128)(2,1)S(1)}, bf16[2,1,8,2,256,256]{5,4,3,2,1,0:T(8,128)(2,1)}, u32[]{:S(2)}) copy-start(bf16[2,1,8,2,256,256]{5,4,3,2,1,0:T(8,128)(2,1)} %param.15) | copy-start | bytes 12582916
  2.8 5.4 %copy-start.3 = (bf16[2,2,512,512]{3,2,1,0:T(8,128)(2,1)S(1)}, bf16[2,2,512,512]{3,2,1,0:T(8,128)(2,1)}, u32[]{:S(2)}) copy-start(bf16[2,2,512,512]{3,2,1,0:T(8,128)(2,1)} %d.3) | copy-start | bytes 6291460
  2.8 4.6 %collective-permute-start = (bf16[2,128,256]{2,1,0:T(8,128)(2,1)S(1)}, bf16[2,128,256]{2,1,0:T(8,128)(2,1)S(1)}, u32[]{:S(2)}, u32[]{:S(2)}) collective-permute-start(bf16[2,128,256]{2,1,0:T(8,128)(2,1)S(1)} %get-tuple-element.54), channel_id=1, source_target_pairs={{0,1},{1,0},{2,3},{3,2},{4,5},{5,4},{6,7},{7,6},{8,9},{9,8},{10,11... | collective-permute-start | bytes 393224 | tf_op jit(solution)/shard_map/ppermute | solution.py:360
  7.8 3.8 %collective-permute-start.1 = (bf16[2,64,256]{2,1,0:T(8,128)(2,1)S(1)}, bf16[2,64,256]{2,1,0:T(8,128)(2,1)S(1)}, u32[]{:S(2)}, u32[]{:S(2)}) collective-permute-start(bf16[2,64,256]{2,1,0:T(8,128)(2,1)S(1)} %get-tuple-element.60), channel_id=1, source_target_pairs={{0,3},{1,2},{2,1},{3,0},{4,7},{5,6},{6,5},{7,4},{8,11},{9,10},{10,... | collective-permute-start | bytes 196616 | tf_op jit(solution)/shard_map/ppermute | solution.py:360
  7.9 12.7 %collective-permute-start.4 = (bf16[2,128,256]{2,1,0:T(8,128)(2,1)S(1)}, bf16[2,128,256]{2,1,0:T(8,128)(2,1)S(1)}, u32[]{:S(2)}, u32[]{:S(2)}) collective-permute-start(bf16[2,128,256]{2,1,0:T(8,128)(2,1)S(1)} %get-tuple-element.70.q), channel_id=1, source_target_pairs={{0,1},{1,0},{2,3},{3,2},{4,5},{5,4},{6,7},{7,6},{8,9},{9,8},{10,11... | collective-permute-start | bytes 393224 | tf_op jit(solution)/shard_map/ppermute | solution.py:360
  11.6 2.1 %copy-start.1 = (bf16[2,1,8,256,256]{4,3,2,1,0:T(8,128)(2,1)S(1)}, bf16[2,1,8,256,256]{4,3,2,1,0:T(8,128)(2,1)}, u32[]{:S(2)}) copy-start(bf16[2,1,8,256,256]{4,3,2,1,0:T(8,128)(2,1)} %param.16) | copy-start | bytes 6291460
  11.6 2.1 %copy-start.4 = (bf16[2,1,256,256]{3,2,1,0:T(8,128)(2,1)S(1)}, bf16[2,1,256,256]{3,2,1,0:T(8,128)(2,1)}, u32[]{:S(2)}) copy-start(bf16[2,1,256,256]{3,2,1,0:T(8,128)(2,1)} %bl.3) | copy-start | bytes 786436
  11.8 4.8 %collective-permute-start.2 = (bf16[2,32,256]{2,1,0:T(8,128)(2,1)S(1)}, bf16[2,32,256]{2,1,0:T(8,128)(2,1)S(1)}, u32[]{:S(2)}, u32[]{:S(2)}) collective-permute-start(bf16[2,32,256]{2,1,0:T(8,128)(2,1)S(1)} %get-tuple-element.65), channel_id=1, source_target_pairs={{0,5},{1,4},{2,7},{3,6},{4,1},{5,0},{6,3},{7,2},{8,13},{9,12},{10,... | collective-permute-start | bytes 98312 | tf_op jit(solution)/shard_map/ppermute | solution.py:360
  16.7 5.7 %collective-permute-start.3 = (bf16[2,32,256]{2,1,0:T(8,128)(2,1)S(1)}, bf16[2,32,256]{2,1,0:T(8,128)(2,1)S(1)}, u32[]{:S(2)}, u32[]{:S(2)}) collective-permute-start(bf16[2,32,256]{2,1,0:T(8,128)(2,1)S(1)} %climb_2.1.q3), channel_id=1, source_target_pairs={{0,13},{1,12},{2,15},{3,14},{4,9},{5,8},{6,11},{7,10},{8,5},{9,4},... | collective-permute-start | bytes 98312 | tf_op jit(solution)/shard_map/ppermute | solution.py:360
  22.4 1.8 %copy-start.2 = (bf16[2,2,512,256]{3,2,1,0:T(8,128)(2,1)S(1)}, bf16[2,2,512,256]{3,2,1,0:T(8,128)(2,1)}, u32[]{:S(2)}) copy-start(bf16[2,2,512,256]{3,2,1,0:T(8,128)(2,1)} %r.7) | copy-start | bytes 3145732
  22.6 3.5 %collective-permute-start.5 = (bf16[2,32,256]{2,1,0:T(8,128)(2,1)S(1)}, bf16[2,32,256]{2,1,0:T(8,128)(2,1)S(1)}, u32[]{:S(2)}, u32[]{:S(2)}) collective-permute-start(bf16[2,32,256]{2,1,0:T(8,128)(2,1)S(1)} %climb_3.1.q4), channel_id=1, source_target_pairs={{0,17},{1,16},{2,19},{3,18},{4,21},{5,20},{6,23},{7,22},{8,25},{9,... | collective-permute-start | bytes 98312 | tf_op jit(solution)/shard_map/ppermute | solution.py:360
  26.3 4.7 %collective-permute-start.6 = (bf16[2,32,256]{2,1,0:T(8,128)(2,1)S(1)}, bf16[2,32,256]{2,1,0:T(8,128)(2,1)S(1)}, u32[]{:S(2)}, u32[]{:S(2)}) collective-permute-start(bf16[2,32,256]{2,1,0:T(8,128)(2,1)S(1)} %climb_4.1.q5), channel_id=1, source_target_pairs={{0,49},{1,48},{2,51},{3,50},{4,53},{5,52},{6,55},{7,54},{8,57},{9,... | collective-permute-start | bytes 98312 | tf_op jit(solution)/shard_map/ppermute | solution.py:360
  31.1 3.5 %collective-permute-start.7 = (bf16[2,32,256]{2,1,0:T(8,128)(2,1)S(1)}, bf16[2,32,256]{2,1,0:T(8,128)(2,1)S(1)}, u32[]{:S(2)}, u32[]{:S(2)}) collective-permute-start(bf16[2,32,256]{2,1,0:T(8,128)(2,1)S(1)} %climb_5.1.q6), channel_id=1, source_target_pairs={{0,65},{1,64},{2,67},{3,66},{4,69},{5,68},{6,71},{7,70},{8,73},{9,... | collective-permute-start | bytes 98312 | tf_op jit(solution)/shard_map/ppermute | solution.py:360
  34.8 5.0 %collective-permute-start.8 = (bf16[2,32,256]{2,1,0:T(8,128)(2,1)S(1)}, bf16[2,32,256]{2,1,0:T(8,128)(2,1)S(1)}, u32[]{:S(2)}, u32[]{:S(2)}) collective-permute-start(bf16[2,32,256]{2,1,0:T(8,128)(2,1)S(1)} %climb_6.1), channel_id=1, source_target_pairs={{0,193},{1,192},{2,195},{3,194},{4,197},{5,196},{6,199},{7,198},{8... | collective-permute-start | bytes 98312 | tf_op jit(solution)/shard_map/ppermute | solution.py:360
  40.0 4.3 %collective-permute-start.9 = (bf16[2,32,256]{2,1,0:T(8,128)(2,1)S(1)}, bf16[2,32,256]{2,1,0:T(8,128)(2,1)S(1)}, u32[]{:S(2)}, u32[]{:S(2)}) collective-permute-start(bf16[2,32,256]{2,1,0:T(8,128)(2,1)S(1)} %get-tuple-element.92), channel_id=1, source_target_pairs={{0,5},{1,4},{2,7},{3,6},{4,1},{5,0},{6,3},{7,2},{8,13},{9,12},{10,... | collective-permute-start | bytes 98312 | tf_op jit(solution)/shard_map/ppermute | solution.py:360
  44.6 4.5 %collective-permute-start.11 = (bf16[2,64,256]{2,1,0:T(8,128)(2,1)S(1)}, bf16[2,64,256]{2,1,0:T(8,128)(2,1)S(1)}, u32[]{:S(2)}, u32[]{:S(2)}) collective-permute-start(bf16[2,64,256]{2,1,0:T(8,128)(2,1)S(1)} %get-tuple-element.98), channel_id=1, source_target_pairs={{0,3},{1,2},{2,1},{3,0},{4,7},{5,6},{6,5},{7,4},{8,11},{9,10},{10,... | collective-permute-start | bytes 196616 | tf_op jit(solution)/shard_map/ppermute | solution.py:360
  48.0 2.4 %collective-permute-start.10 = (bf16[2,64,256]{2,1,0:T(8,128)(2,1)S(1)}, bf16[2,64,256]{2,1,0:T(8,128)(2,1)S(1)}, u32[]{:S(2)}, u32[]{:S(2)}) collective-permute-start(bf16[2,64,256]{2,1,0:T(8,128)(2,1)S(1)} %get-tuple-element.97.mine), channel_id=1, source_target_pairs={{0,1},{1,0},{2,3},{3,2},{4,5},{5,4},{6,7},{7,6},{8,9},{9,8},{10,11... | collective-permute-start | bytes 196616 | tf_op jit(solution)/shard_map/ppermute | solution.py:360
  49.2 1.3 %collective-permute-start.12 = (bf16[2,64,256]{2,1,0:T(8,128)(2,1)S(1)}, bf16[2,64,256]{2,1,0:T(8,128)(2,1)S(1)}, u32[]{:S(2)}, u32[]{:S(2)}) collective-permute-start(bf16[2,64,256]{2,1,0:T(8,128)(2,1)S(1)} %collective-permute-done.11.got), channel_id=1, source_target_pairs={{0,1},{1,0},{2,3},{3,2},{4,5},{5,4},{6,7},{7,6},{8,9},{9,8},{10,11... | collective-permute-start | bytes 196616 | tf_op jit(solution)/shard_map/ppermute | solution.py:360

commit v15 on v11

--- a/solution.py
+++ b/solution.py
@@ -295,7 +295,7 @@
             add = dot(jnp.concatenate([g[0, here], g[1, here]], axis=1), hw, NT)
             for c in range(2):
                 out[leaf, c, here] = (base[c, at] + add[:, c * n : (c + 1) * n]).astype(BF)
-            yield leaf, here, at
+                yield leaf, c, here, at
 
 
 def own_kernel(pos, order, mine, got, base, g0, g1, out):
@@ -308,17 +308,18 @@
     n = base.shape[2]
     copies = []
 
-    def store(src, part, at):
+    def store(src, part, c, at):
         lanes = half_lanes(side(pos, 0) ^ part, n)
         sem = sems.at[len(copies)]
-        copies.append(pltpu.make_async_copy(src, out.at[:, at, lanes], sem))
+        copies.append(pltpu.make_async_copy(src, out.at[c, at, lanes], sem))
         copies[-1].start()
 
     for leaf in range(2):
         at = pl.ds(pl.multiple_of((order[0, 0] ^ leaf) * size, size), size)
-        store(done.at[leaf], 0, at)
-    for leaf, here, at in finish(pos, order, mine, got, base, (g0, g1), buf, size):
-        store(buf.at[leaf, :, here], 1, at)
+        for c in range(2):
+            store(done.at[leaf, c], 0, c, at)
+    for leaf, c, here, at in finish(pos, order, mine, got, base, (g0, g1), buf, size):
+        store(buf.at[leaf, c, here], 1, c, at)
     for copy in copies:
         copy.wait()
 
@@ -475,7 +476,7 @@
     (out,) = call(
         "other_columns", last_kernel, "ss" + "v" * 6, [(rhs.shape, BF)],
         pos, order, mine_other, got_other, base_other, g0, g1, done,
-        scratch=(pltpu.VMEM(piece, BF), pltpu.SemaphoreType.DMA((6,))),
+        scratch=(pltpu.VMEM(piece, BF), pltpu.SemaphoreType.DMA((8,))),
         flops=mac * n * 2, out_spec=HBM,
     )
     return out

time: 53.1 us -> 52.9 us (level)
  no operation moved by 1% of the time
where the time goes in v15:
time: 52.9 us; the launch traced here: 52.7 us
  starting transfers between devices  23.9 us (45%)
  Pallas kernels  20.7 us (39%)
  waiting for transfers between devices  7.76 us (15%)
    ppermute x13, starting transfers between devices, swap(): return lax.ppermute(value, axes, [(i, i ^ flip) for i in range(devices)])  23.9 us
    pallas_call x22, Pallas kernels, call(): pl.pallas_call(kernel, out_shape=[jax.ShapeDtypeStruct(shape, dtype) for...  20.7 us
    ppermute x13, waiting for transfers between devices, swap(): return lax.ppermute(value, axes, [(i, i ^ flip) for i in range(devices)])  7.76 us
  transfers between devices with their start and end apart: 13, of which 8 were waited for; matrix products, arithmetic and copies ran while one was open for 0% of the time, Pallas kernels for 27%

profile of v15, /device:TPU:1, one launch (start us, length us, event | category | flops | bytes accessed | tf_op | source)
XLA Modules:
  0.0 52.7 jit_solution(6394484453115462584)
XLA Ops:
  0.0 0.0 copy-start.5
  0.0 0.0 copy-start
  0.0 2.8 %send_half.1 = (bf16[2,256,256]{2,1,0:T(8,128)(2,1)S(1)}, bf16[2,128,256]{2,1,0:T(8,128)(2,1)S(1)}, bf16[2,256,512]{2,1,0:T(8,128)(2,1)S(1)}, bf16[2,1024,256]{2...) custom-call(s32[1]{0:T(128)} %bitcast.pos, ...), custom_call_target="tpu_custom_call" | custom-call | flops 402653184 | bytes 6815756 | tf_op jit(solution)/shard_map/send_half/pallas_call | solution.py:336
  2.8 0.0 copy-start.3
  2.8 3.3 %collective-permute-start = (bf16[2,128,256]{2,1,0:T(8,128)(2,1)S(1)}, bf16[2,128,256]{2,1,0:T(8,128)(2,1)S(1)}, u32[]{:S(2)}, u32[]{:S(2)}) collective-permute-start(bf16[2,128,256]{2,1,0:T(8,128)(2,1)S(1)} %get-tuple-element.52), channel_id=1, source_target_pairs={{0,1},{1,0},{2,3},{3,2},{4,5},{5,4},{6,7},{7,6},{8,9},{9,8},{10,11... | collective-permute-start | bytes 393224 | tf_op jit(solution)/shard_map/ppermute | solution.py:359
  6.1 0.0 copy-done.5
  6.1 1.3 %keep_half.1 = (bf16[2,256,256]{2,1,0:T(8,128)(2,1)S(1)}, bf16[2,128,256]{2,1,0:T(8,128)(2,1)S(1)}) custom-call(s32[1]{0:T(128)} %bitcast.pos, s32[1,2]{1,0:T(1,128)S(1)} %copy-done.5, bf16[2,256,512]{2,1,0:T(8,128)(2,1)S(1)} %get-tuple-element.53.xt, bf16[2,2,512,256]{3,2,1,0:T(8,128)(2,1)S(1)} %get-tuple-element.54.u, ...), custom_call_target="tpu_custom_call" | custom-call | flops 402653184 | bytes 2097164 | tf_op jit(solution)/shard_map/keep_half/pallas_call | solution.py:336
  7.5 0.0 collective-permute-done.got.got0
  7.5 0.3 climb_0.1
  7.8 0.1 collective-permute-start.1
  7.9 0.3 collective-permute-start.4
  8.2 0.0 copy-done
  8.2 0.0 copy-done.3
  8.2 1.6 %shadow_1.1 = (f32[2,64,256]{2,1,0:T(8,128)S(1)}, f32[2,512,256]{2,1,0:T(8,128)S(1)}, bf16[2,2,256,256]{3,2,1,0:T(8,128)(2,1)S(1)}) custom-call(s32[1]{0:T(128)} %bitcast.pos, s32[1,2]{1,0:T(1,128)S(1)} %copy-done.5, bf16[2,64,256]{2,1,0:T(8,128)(2,1)S(1)} %get-tuple-element.60.keep.keep1, bf16[2,8,2,256,256]{4,3,2,1,0:T(8,128)(2,1)S(1)} %bitcast.4, ...), custom_call_target="tpu_custom_call" | custom-call | flops 939524096 | bytes 8454156 | tf_op jit(solution)/shard_map/shadow_1/pallas_call | solution.py:336
  9.7 1.9 %collective-permute-done.1.got.got1 = bf16[2,64,256]{2,1,0:T(8,128)(2,1)S(1)} collective-permute-done((bf16[2,64,256]{2,1,0:T(8,128)(2,1)S(1)}, bf16[2,64,256]{2,1,0:T(8,128)(2,1)S(1)}, u32[]{:S(2)}, u32[]{:S(2)}) %collective-permute-start.1) | collective-permute-done | bytes 65568 | tf_op jit(solution)/shard_map/ppermute | solution.py:359
  11.6 0.0 copy-start.1
  11.6 0.0 copy-start.4
  11.6 0.2 climb_1.1
  11.8 1.9 %collective-permute-start.2 = (bf16[2,32,256]{2,1,0:T(8,128)(2,1)S(1)}, bf16[2,32,256]{2,1,0:T(8,128)(2,1)S(1)}, u32[]{:S(2)}, u32[]{:S(2)}) collective-permute-start(bf16[2,32,256]{2,1,0:T(8,128)(2,1)S(1)} %get-tuple-element.63), channel_id=1, source_target_pairs={{0,5},{1,4},{2,7},{3,6},{4,1},{5,0},{6,3},{7,2},{8,13},{9,12},{10,... | collective-permute-start | bytes 98312 | tf_op jit(solution)/shard_map/ppermute | solution.py:359
  13.7 0.0 copy-done.1
  13.7 0.0 copy-done.4
  13.7 2.0 %shadow_2.1 = (f32[2,32,256]{2,1,0:T(8,128)S(1)}, f32[2,512,256]{2,1,0:T(8,128)S(1)}, bf16[2,256,256]{2,1,0:T(8,128)(2,1)S(1)}) custom-call(s32[1]{0:T(128)} %bitcast.pos, s32[1,2]{1,0:T(1,128)S(1)} %copy-done.5, bf16[2,32,256]{2,1,0:T(8,128)(2,1)S(1)} %get-tuple-element.64.keep.keep2, bf16[2,8,2,256,256]{4,3,2,1,0:T(8,128)(2,1)S(1)} %bitcast.6, ...), custom_call_target="tpu_custom_call" | custom-call | flops 1073741824 | bytes 10649612 | tf_op jit(solution)/shard_map/shadow_2/pallas_call | solution.py:336
  15.7 0.9 %collective-permute-done.2.got.got2 = bf16[2,32,256]{2,1,0:T(8,128)(2,1)S(1)} collective-permute-done((bf16[2,32,256]{2,1,0:T(8,128)(2,1)S(1)}, bf16[2,32,256]{2,1,0:T(8,128)(2,1)S(1)}, u32[]{:S(2)}, u32[]{:S(2)}) %collective-permute-start.2) | collective-permute-done | bytes 32800 | tf_op jit(solution)/shard_map/ppermute | solution.py:359
  16.6 0.2 climb_2.1.q3
  16.7 3.9 %collective-permute-start.3 = (bf16[2,32,256]{2,1,0:T(8,128)(2,1)S(1)}, bf16[2,32,256]{2,1,0:T(8,128)(2,1)S(1)}, u32[]{:S(2)}, u32[]{:S(2)}) collective-permute-start(bf16[2,32,256]{2,1,0:T(8,128)(2,1)S(1)} %climb_2.1.q3), channel_id=1, source_target_pairs={{0,13},{1,12},{2,15},{3,14},{4,9},{5,8},{6,11},{7,10},{8,5},{9,4},... | collective-permute-start | bytes 98312 | tf_op jit(solution)/shard_map/ppermute | solution.py:359
  20.6 0.0 collective-permute-done.4.got0_other
  20.6 0.9 %shadow_3.1 = (f32[2,32,256]{2,1,0:T(8,128)S(1)}, bf16[2,256,256]{2,1,0:T(8,128)(2,1)S(1)}) custom-call(s32[1]{0:T(128)} %bitcast.pos, bf16[2,32,256]{2,1,0:T(8,128)(2,1)S(1)} %climb_2.1.q3, bf16[2,8,2,256,256]{4,3,2,1,0:T(8,128)(2,1)S(1)} %bitcast.8, bf16[2,8,256,256]{3,2,1,0:T(8,128)(2,1)S(1)} %bitcast.19, bf16[2,1,256,256]{3,2,1,0:T(8,128)(2,1)S(1)} %copy-done.4, ...), custom_call_target="tpu_custom_call" | custom-call | flops 536870912 | bytes 7503876 | tf_op jit(solution)/shard_map/shadow_3/pallas_call | solution.py:336
  21.5 0.9 %collective-permute-done.3.got.got3 = bf16[2,32,256]{2,1,0:T(8,128)(2,1)S(1)} collective-permute-done((bf16[2,32,256]{2,1,0:T(8,128)(2,1)S(1)}, bf16[2,32,256]{2,1,0:T(8,128)(2,1)S(1)}, u32[]{:S(2)}, u32[]{:S(2)}) %collective-permute-start.3) | collective-permute-done | bytes 32800 | tf_op jit(solution)/shard_map/ppermute | solution.py:359
  22.4 0.0 copy-start.2
  22.4 0.2 climb_3.1.q4
  22.6 1.6 %collective-permute-start.5 = (bf16[2,32,256]{2,1,0:T(8,128)(2,1)S(1)}, bf16[2,32,256]{2,1,0:T(8,128)(2,1)S(1)}, u32[]{:S(2)}, u32[]{:S(2)}) collective-permute-start(bf16[2,32,256]{2,1,0:T(8,128)(2,1)S(1)} %climb_3.1.q4), channel_id=1, source_target_pairs={{0,17},{1,16},{2,19},{3,18},{4,21},{5,20},{6,23},{7,22},{8,25},{9,... | collective-permute-start | bytes 98312 | tf_op jit(solution)/shard_map/ppermute | solution.py:359
  24.2 0.0 copy-done.2
  24.2 1.4 %shadow_4.1 = (f32[2,32,256]{2,1,0:T(8,128)S(1)}, f32[2,32,256]{2,1,0:T(8,128)S(1)}, f32[2,1024,128]{2,1,0:T(8,128)S(1)}) custom-call(s32[1]{0:T(128)} %bitcast.pos, s32[1,2]{1,0:T(1,128)S(1)} %copy-done.5, bf16[2,32,256]{2,1,0:T(8,128)(2,1)S(1)} %climb_3.1.q4, bf16[2,32,256]{2,1,0:T(8,128)(2,1)S(1)} %collective-permute-done.3.got.got3, ...), custom_call_target="tpu_custom_call" | custom-call | flops 268435456 | bytes 9764876 | tf_op jit(solution)/shard_map/shadow_4/pallas_call | solution.py:336
  25.6 0.5 collective-permute-done.5.got.got4
  26.1 0.2 climb_4.1.q5
  26.3 2.9 %collective-permute-start.6 = (bf16[2,32,256]{2,1,0:T(8,128)(2,1)S(1)}, bf16[2,32,256]{2,1,0:T(8,128)(2,1)S(1)}, u32[]{:S(2)}, u32[]{:S(2)}) collective-permute-start(bf16[2,32,256]{2,1,0:T(8,128)(2,1)S(1)} %climb_4.1.q5), channel_id=1, source_target_pairs={{0,49},{1,48},{2,51},{3,50},{4,53},{5,52},{6,55},{7,54},{8,57},{9,... | collective-permute-start | bytes 98312 | tf_op jit(solution)/shard_map/ppermute | solution.py:359
  29.2 1.0 %shadow_5.1 = (f32[2,32,256]{2,1,0:T(8,128)S(1)}, f32[2,32,256]{2,1,0:T(8,128)S(1)}, bf16[2,256,256]{2,1,0:T(8,128)(2,1)S(1)}, bf16[2,512,256]{2,1,0:T(8,128)(2,1)S(1)}) custom-call(s32[1]{0:T(128)} %bitcast.pos, bf16[2,32,256]{2,1,0:T(8,128)(2,1)S(1)} %climb_4.1.q5, bf16[2,32,256]{2,1,0:T(8,128)(2,1)S(1)} %collective-permute-done.5.got.got4, ...), custom_call_target="tpu_custom_call" | custom-call | flops 402653184 | bytes 7995396 | tf_op jit(solution)/shard_map/shadow_5/pallas_call | solution.py:336
  30.2 0.8 %collective-permute-done.6.got.got5 = bf16[2,32,256]{2,1,0:T(8,128)(2,1)S(1)} collective-permute-done((bf16[2,32,256]{2,1,0:T(8,128)(2,1)S(1)}, bf16[2,32,256]{2,1,0:T(8,128)(2,1)S(1)}, u32[]{:S(2)}, u32[]{:S(2)}) %collective-permute-start.6) | collective-permute-done | bytes 32800 | tf_op jit(solution)/shard_map/ppermute | solution.py:359
  30.9 0.2 climb_5.1.q6
  31.1 1.7 %collective-permute-start.7 = (bf16[2,32,256]{2,1,0:T(8,128)(2,1)S(1)}, bf16[2,32,256]{2,1,0:T(8,128)(2,1)S(1)}, u32[]{:S(2)}, u32[]{:S(2)}) collective-permute-start(bf16[2,32,256]{2,1,0:T(8,128)(2,1)S(1)} %climb_5.1.q6), channel_id=1, source_target_pairs={{0,65},{1,64},{2,67},{3,66},{4,69},{5,68},{6,71},{7,70},{8,73},{9,... | collective-permute-start | bytes 98312 | tf_op jit(solution)/shard_map/ppermute | solution.py:359
  32.8 2.0 %shadow_6.1 = (f32[2,32,256]{2,1,0:T(8,128)S(1)}, f32[2,32,256]{2,1,0:T(8,128)S(1)}, bf16[2,256,256]{2,1,0:T(8,128)(2,1)S(1)}, bf16[2,256,256]{2,1,0:T(8,128)(2,1)S(1)}, bf16[2,512,256]{2,1,0:T(8,128)(2,1)S(1)}) custom-call(s32[1]{0:T(128)} %bitcast.pos, bf16[2,32,256]{2,1,0:T(8,128)(2,1)S(1)} %climb_5.1.q6, ...), custom_call_target="tpu_custom_call" | custom-call | flops 536870912 | bytes 8257540 | tf_op jit(solution)/shard_map/shadow_6/pallas_call | solution.py:336
  34.8 0.0 collective-permute-done.7.got.got6
  34.8 0.2 climb_6.1
  35.0 3.1 %collective-permute-start.8 = (bf16[2,32,256]{2,1,0:T(8,128)(2,1)S(1)}, bf16[2,32,256]{2,1,0:T(8,128)(2,1)S(1)}, u32[]{:S(2)}, u32[]{:S(2)}) collective-permute-start(bf16[2,32,256]{2,1,0:T(8,128)(2,1)S(1)} %climb_6.1), channel_id=1, source_target_pairs={{0,193},{1,192},{2,195},{3,194},{4,197},{5,196},{6,199},{7,198},{8... | collective-permute-start | bytes 98312 | tf_op jit(solution)/shard_map/ppermute | solution.py:359
  38.1 1.5 %shadow_7.1 = (f32[2,32,256]{2,1,0:T(8,128)S(1)}, f32[2,32,256]{2,1,0:T(8,128)S(1)}, bf16[2,256,256]{2,1,0:T(8,128)(2,1)S(1)}, bf16[2,256,256]{2,1,0:T(8,128)(2,1)S(1)}) custom-call(s32[1]{0:T(128)} %bitcast.pos, bf16[2,32,256]{2,1,0:T(8,128)(2,1)S(1)} %collective-permute-done.7.got.got6, bf16[2,8,2,256,256]{4,3,2,1,0:T(8,128)(2,1)S(1)} %bitcast.16, ...), custom_call_target="tpu_custom_call" | custom-call | flops 402653184 | bytes 6979588 | tf_op jit(solution)/shard_map/shadow_7/pallas_call | solution.py:336
  39.6 0.2 collective-permute-done.8.got
  39.8 0.3 top.1
  40.1 2.1 %collective-permute-start.9 = (bf16[2,32,256]{2,1,0:T(8,128)(2,1)S(1)}, bf16[2,32,256]{2,1,0:T(8,128)(2,1)S(1)}, u32[]{:S(2)}, u32[]{:S(2)}) collective-permute-start(bf16[2,32,256]{2,1,0:T(8,128)(2,1)S(1)} %get-tuple-element.88), channel_id=1, source_target_pairs={{0,5},{1,4},{2,7},{3,6},{4,1},{5,0},{6,3},{7,2},{8,13},{9,12},{10,... | collective-permute-start | bytes 98312 | tf_op jit(solution)/shard_map/ppermute | solution.py:359
  42.1 0.4 shadow_8.1
  42.6 1.8 %collective-permute-done.9.got = bf16[2,32,256]{2,1,0:T(8,128)(2,1)S(1)} collective-permute-done((bf16[2,32,256]{2,1,0:T(8,128)(2,1)S(1)}, bf16[2,32,256]{2,1,0:T(8,128)(2,1)S(1)}, u32[]{:S(2)}, u32[]{:S(2)}) %collective-permute-start.9) | collective-permute-done | bytes 32800 | tf_op jit(solution)/shard_map/ppermute | solution.py:359
  44.4 0.3 down.1
  44.7 2.3 %collective-permute-start.11 = (bf16[2,64,256]{2,1,0:T(8,128)(2,1)S(1)}, bf16[2,64,256]{2,1,0:T(8,128)(2,1)S(1)}, u32[]{:S(2)}, u32[]{:S(2)}) collective-permute-start(bf16[2,64,256]{2,1,0:T(8,128)(2,1)S(1)} %get-tuple-element.94), channel_id=1, source_target_pairs={{0,3},{1,2},{2,1},{3,0},{4,7},{5,6},{6,5},{7,4},{8,11},{9,10},{10,... | collective-permute-start | bytes 196616 | tf_op jit(solution)/shard_map/ppermute | solution.py:359
  47.0 1.0 %shadow_9.1.base = f32[2,1024,128]{2,1,0:T(8,128)S(1)} custom-call(s32[1]{0:T(128)} %bitcast.pos, s32[1,2]{1,0:T(1,128)S(1)} %copy-done.5, bf16[2,64,256]{2,1,0:T(8,128)(2,1)S(1)} %get-tuple-element.93.mine, bf16[2,2,512,256]{3,2,1,0:T(8,128)(2,1)S(1)} %copy-done.2, bf16[2,256,256]{2,1,0:T(8,128)(2,1)S(1)} %get-tuple-element.92.cleaf, ...), custom_call_target="tpu_custom_call" | custom-call | flops 268435456 | bytes 3473420 | tf_op jit(solution)/shard_map/shadow_9/pallas_call | solution.py:336
  48.0 0.4 collective-permute-start.10
  48.4 0.9 %collective-permute-done.11.got = bf16[2,64,256]{2,1,0:T(8,128)(2,1)S(1)} collective-permute-done((bf16[2,64,256]{2,1,0:T(8,128)(2,1)S(1)}, bf16[2,64,256]{2,1,0:T(8,128)(2,1)S(1)}, u32[]{:S(2)}, u32[]{:S(2)}) %collective-permute-start.11) | collective-permute-done | bytes 65568 | tf_op jit(solution)/shard_map/ppermute | solution.py:359
  49.3 0.3 collective-permute-start.12
  49.6 1.0 %own_columns.1.done = bf16[2,2,512,128]{3,2,1,0:T(8,128)(2,1)S(1)} custom-call(s32[1]{0:T(128)} %bitcast.pos, s32[1,2]{1,0:T(1,128)S(1)} %copy-done.5, bf16[2,64,256]{2,1,0:T(8,128)(2,1)S(1)} %get-tuple-element.93.mine, bf16[2,64,256]{2,1,0:T(8,128)(2,1)S(1)} %collective-permute-done.11.got, f32[2,1024,128]{2,1,0:T(8,128)S(1)} %get-tuple-element.98.base, ...), custom_call_target="tpu_custom_call" | custom-call | flops 268435456 | bytes 2228236 | tf_op jit(solution)/shard_map/own_columns/pallas_call | solution.py:336
  50.6 0.0 collective-permute-done.10.mine
  50.6 0.0 collective-permute-done.12.got
  50.7 1.9 %other_columns.1 = bf16[2,1024,256]{2,1,0:T(8,128)(2,1)} custom-call(s32[1]{0:T(128)} %bitcast.pos, s32[1,2]{1,0:T(1,128)S(1)} %copy-done.5, bf16[2,64,256]{2,1,0:T(8,128)(2,1)S(1)} %collective-permute-done.10.mine, bf16[2,64,256]{2,1,0:T(8,128)(2,1)S(1)} %collective-permute-done.12.got, f32[2,1024,128]{2,1,0:T(8,128)S(1)} %shadow_9.1.base, ...), custom_call_target="tpu_custom_call" | custom-call | flops 268435456 | bytes 2752524 | tf_op jit(solution)/shard_map/other_columns/pallas_call | solution.py:336
Async XLA Ops:
  0.0 6.1 %copy-start.5 = (s32[1,2]{1,0:T(1,128)S(1)}, s32[1,2]{1,0:T(1,128)}, u32[]{:S(2)}) copy-start(s32[1,2]{1,0:T(1,128)} %order.15) | copy-start | bytes 28
  0.0 8.2 %copy-start = (bf16[2,1,8,2,256,256]{5,4,3,2,1,0:T(8,128)(2,1)S(1)}, bf16[2,1,8,2,256,256]{5,4,3,2,1,0:T(8,128)(2,1)}, u32[]{:S(2)}) copy-start(bf16[2,1,8,2,256,256]{5,4,3,2,1,0:T(8,128)(2,1)} %param.15) | copy-start | bytes 12582916
  2.8 5.4 %copy-start.3 = (bf16[2,2,512,512]{3,2,1,0:T(8,128)(2,1)S(1)}, bf16[2,2,512,512]{3,2,1,0:T(8,128)(2,1)}, u32[]{:S(2)}) copy-start(bf16[2,2,512,512]{3,2,1,0:T(8,128)(2,1)} %d.3) | copy-start | bytes 6291460
  2.8 4.6 %collective-permute-start = (bf16[2,128,256]{2,1,0:T(8,128)(2,1)S(1)}, bf16[2,128,256]{2,1,0:T(8,128)(2,1)S(1)}, u32[]{:S(2)}, u32[]{:S(2)}) collective-permute-start(bf16[2,128,256]{2,1,0:T(8,128)(2,1)S(1)} %get-tuple-element.52), channel_id=1, source_target_pairs={{0,1},{1,0},{2,3},{3,2},{4,5},{5,4},{6,7},{7,6},{8,9},{9,8},{10,11... | collective-permute-start | bytes 393224 | tf_op jit(solution)/shard_map/ppermute | solution.py:359
  7.8 3.8 %collective-permute-start.1 = (bf16[2,64,256]{2,1,0:T(8,128)(2,1)S(1)}, bf16[2,64,256]{2,1,0:T(8,128)(2,1)S(1)}, u32[]{:S(2)}, u32[]{:S(2)}) collective-permute-start(bf16[2,64,256]{2,1,0:T(8,128)(2,1)S(1)} %get-tuple-element.58), channel_id=1, source_target_pairs={{0,3},{1,2},{2,1},{3,0},{4,7},{5,6},{6,5},{7,4},{8,11},{9,10},{10,... | collective-permute-start | bytes 196616 | tf_op jit(solution)/shard_map/ppermute | solution.py:359
  7.9 12.7 %collective-permute-start.4 = (bf16[2,128,256]{2,1,0:T(8,128)(2,1)S(1)}, bf16[2,128,256]{2,1,0:T(8,128)(2,1)S(1)}, u32[]{:S(2)}, u32[]{:S(2)}) collective-permute-start(bf16[2,128,256]{2,1,0:T(8,128)(2,1)S(1)} %get-tuple-element.68.q), channel_id=1, source_target_pairs={{0,1},{1,0},{2,3},{3,2},{4,5},{5,4},{6,7},{7,6},{8,9},{9,8},{10,11... | collective-permute-start | bytes 393224 | tf_op jit(solution)/shard_map/ppermute | solution.py:359
  11.6 2.1 %copy-start.1 = (bf16[2,1,8,256,256]{4,3,2,1,0:T(8,128)(2,1)S(1)}, bf16[2,1,8,256,256]{4,3,2,1,0:T(8,128)(2,1)}, u32[]{:S(2)}) copy-start(bf16[2,1,8,256,256]{4,3,2,1,0:T(8,128)(2,1)} %param.16) | copy-start | bytes 6291460
  11.6 2.1 %copy-start.4 = (bf16[2,1,256,256]{3,2,1,0:T(8,128)(2,1)S(1)}, bf16[2,1,256,256]{3,2,1,0:T(8,128)(2,1)}, u32[]{:S(2)}) copy-start(bf16[2,1,256,256]{3,2,1,0:T(8,128)(2,1)} %bl.3) | copy-start | bytes 786436
  11.8 4.8 %collective-permute-start.2 = (bf16[2,32,256]{2,1,0:T(8,128)(2,1)S(1)}, bf16[2,32,256]{2,1,0:T(8,128)(2,1)S(1)}, u32[]{:S(2)}, u32[]{:S(2)}) collective-permute-start(bf16[2,32,256]{2,1,0:T(8,128)(2,1)S(1)} %get-tuple-element.63), channel_id=1, source_target_pairs={{0,5},{1,4},{2,7},{3,6},{4,1},{5,0},{6,3},{7,2},{8,13},{9,12},{10,... | collective-permute-start | bytes 98312 | tf_op jit(solution)/shard_map/ppermute | solution.py:359
  16.7 5.7 %collective-permute-start.3 = (bf16[2,32,256]{2,1,0:T(8,128)(2,1)S(1)}, bf16[2,32,256]{2,1,0:T(8,128)(2,1)S(1)}, u32[]{:S(2)}, u32[]{:S(2)}) collective-permute-start(bf16[2,32,256]{2,1,0:T(8,128)(2,1)S(1)} %climb_2.1.q3), channel_id=1, source_target_pairs={{0,13},{1,12},{2,15},{3,14},{4,9},{5,8},{6,11},{7,10},{8,5},{9,4},... | collective-permute-start | bytes 98312 | tf_op jit(solution)/shard_map/ppermute | solution.py:359
  22.4 1.8 %copy-start.2 = (bf16[2,2,512,256]{3,2,1,0:T(8,128)(2,1)S(1)}, bf16[2,2,512,256]{3,2,1,0:T(8,128)(2,1)}, u32[]{:S(2)}) copy-start(bf16[2,2,512,256]{3,2,1,0:T(8,128)(2,1)} %r.7) | copy-start | bytes 3145732
  22.6 3.5 %collective-permute-start.5 = (bf16[2,32,256]{2,1,0:T(8,128)(2,1)S(1)}, bf16[2,32,256]{2,1,0:T(8,128)(2,1)S(1)}, u32[]{:S(2)}, u32[]{:S(2)}) collective-permute-start(bf16[2,32,256]{2,1,0:T(8,128)(2,1)S(1)} %climb_3.1.q4), channel_id=1, source_target_pairs={{0,17},{1,16},{2,19},{3,18},{4,21},{5,20},{6,23},{7,22},{8,25},{9,... | collective-permute-start | bytes 98312 | tf_op jit(solution)/shard_map/ppermute | solution.py:359
  26.3 4.7 %collective-permute-start.6 = (bf16[2,32,256]{2,1,0:T(8,128)(2,1)S(1)}, bf16[2,32,256]{2,1,0:T(8,128)(2,1)S(1)}, u32[]{:S(2)}, u32[]{:S(2)}) collective-permute-start(bf16[2,32,256]{2,1,0:T(8,128)(2,1)S(1)} %climb_4.1.q5), channel_id=1, source_target_pairs={{0,49},{1,48},{2,51},{3,50},{4,53},{5,52},{6,55},{7,54},{8,57},{9,... | collective-permute-start | bytes 98312 | tf_op jit(solution)/shard_map/ppermute | solution.py:359
  31.1 3.7 %collective-permute-start.7 = (bf16[2,32,256]{2,1,0:T(8,128)(2,1)S(1)}, bf16[2,32,256]{2,1,0:T(8,128)(2,1)S(1)}, u32[]{:S(2)}, u32[]{:S(2)}) collective-permute-start(bf16[2,32,256]{2,1,0:T(8,128)(2,1)S(1)} %climb_5.1.q6), channel_id=1, source_target_pairs={{0,65},{1,64},{2,67},{3,66},{4,69},{5,68},{6,71},{7,70},{8,73},{9,... | collective-permute-start | bytes 98312 | tf_op jit(solution)/shard_map/ppermute | solution.py:359
  35.0 4.8 %collective-permute-start.8 = (bf16[2,32,256]{2,1,0:T(8,128)(2,1)S(1)}, bf16[2,32,256]{2,1,0:T(8,128)(2,1)S(1)}, u32[]{:S(2)}, u32[]{:S(2)}) collective-permute-start(bf16[2,32,256]{2,1,0:T(8,128)(2,1)S(1)} %climb_6.1), channel_id=1, source_target_pairs={{0,193},{1,192},{2,195},{3,194},{4,197},{5,196},{6,199},{7,198},{8... | collective-permute-start | bytes 98312 | tf_op jit(solution)/shard_map/ppermute | solution.py:359
  40.1 4.3 %collective-permute-start.9 = (bf16[2,32,256]{2,1,0:T(8,128)(2,1)S(1)}, bf16[2,32,256]{2,1,0:T(8,128)(2,1)S(1)}, u32[]{:S(2)}, u32[]{:S(2)}) collective-permute-start(bf16[2,32,256]{2,1,0:T(8,128)(2,1)S(1)} %get-tuple-element.88), channel_id=1, source_target_pairs={{0,5},{1,4},{2,7},{3,6},{4,1},{5,0},{6,3},{7,2},{8,13},{9,12},{10,... | collective-permute-start | bytes 98312 | tf_op jit(solution)/shard_map/ppermute | solution.py:359
  44.7 4.5 %collective-permute-start.11 = (bf16[2,64,256]{2,1,0:T(8,128)(2,1)S(1)}, bf16[2,64,256]{2,1,0:T(8,128)(2,1)S(1)}, u32[]{:S(2)}, u32[]{:S(2)}) collective-permute-start(bf16[2,64,256]{2,1,0:T(8,128)(2,1)S(1)} %get-tuple-element.94), channel_id=1, source_target_pairs={{0,3},{1,2},{2,1},{3,0},{4,7},{5,6},{6,5},{7,4},{8,11},{9,10},{10,... | collective-permute-start | bytes 196616 | tf_op jit(solution)/shard_map/ppermute | solution.py:359
  48.0 2.6 %collective-permute-start.10 = (bf16[2,64,256]{2,1,0:T(8,128)(2,1)S(1)}, bf16[2,64,256]{2,1,0:T(8,128)(2,1)S(1)}, u32[]{:S(2)}, u32[]{:S(2)}) collective-permute-start(bf16[2,64,256]{2,1,0:T(8,128)(2,1)S(1)} %get-tuple-element.93.mine), channel_id=1, source_target_pairs={{0,1},{1,0},{2,3},{3,2},{4,5},{5,4},{6,7},{7,6},{8,9},{9,8},{10,11... | collective-permute-start | bytes 196616 | tf_op jit(solution)/shard_map/ppermute | solution.py:359
  49.3 1.4 %collective-permute-start.12 = (bf16[2,64,256]{2,1,0:T(8,128)(2,1)S(1)}, bf16[2,64,256]{2,1,0:T(8,128)(2,1)S(1)}, u32[]{:S(2)}, u32[]{:S(2)}) collective-permute-start(bf16[2,64,256]{2,1,0:T(8,128)(2,1)S(1)} %collective-permute-done.11.got), channel_id=1, source_target_pairs={{0,1},{1,0},{2,3},{3,2},{4,5},{5,4},{6,7},{7,6},{8,9},{9,8},{10,11... | collective-permute-start | bytes 196616 | tf_op jit(solution)/shard_map/ppermute | solution.py:359
